TPU v7x, 256 devices: a whole 4x4x8 slice. The times are simulated.
256 devices in a mesh: mem: 16 (over y, x_lo, core), lat: 16 (over z, x_hi).
Axes of the slice: x: 4 (x_hi: 2, x_lo: 2; x = x_hi * 2 + x_lo), y: 4, z: 8, core: 2. Of those that a mesh axis runs over, the one named last changes fastest.
Arguments:
- coarse_weights: bfloat16 [128, 64, 8, 256], P('lat', 'mem'), may hold values from -6 to 6
- perturbations: bfloat16 [64, 8, 512, 1024], P('mem', None, 'lat'), may hold values from -6 to 6
- lat_matrix: bfloat16 [512, 128], P('lat'), may hold values from -0.5 to 0.5
- lon_matrix: bfloat16 [256, 1024], replicated, may hold values from -0.375 to 0.375
- wind_field: float32 [2, 512, 1024], P(None, 'lat', 'mem'), may hold values from -0.4 to 0.4
- observed_cell: int32 [4, 8, 512, 128], P(None, None, 'lat', 'mem'), may hold values from 0 to 7
- observed_value: float32 [4, 8, 512, 128], P(None, None, 'lat', 'mem'), may hold values from -6 to 6
- observed_weight: float32 [4, 8, 512, 128], P(None, None, 'lat', 'mem'), may hold values from 0.5 to 4
Outputs:
- gradient: float32 [128, 64, 8, 256], P('lat', 'mem')
- increment: float32 [8, 512, 1024], P(None, 'lat', 'mem')
Inputs may be any that keep to these rules, and one draw needn't show every extreme that they name: `observed_cell`: the observed cell is an offset within its block of 8 longitudes.
All inputs are finite; a program needn't handle non-finite values.
Results may differ from a plain program's by a relative error of at most 0.0003.
Values may be sent and summed in bfloat16 or wider, within the bound.
No kernel may reach another device: no remote copies, remote signals or barrier semaphores. Data moves between devices by JAX's collectives and lax.ppermute only.
A program may use at most 64 MiB of HBM per device.

v0:
```python
import jax
import jax.numpy as jnp
from jax import lax
from jax.sharding import Mesh
from jax.sharding import PartitionSpec as P

STEPS = 4
OBLK = 8
LAT = ("lat_0", "lat_1")


diffusion = 0.2
highest = lax.Precision.HIGHEST


def laid_out(pieces, dim):
    pieces = jnp.moveaxis(pieces, 0, dim)
    shape = pieces.shape
    return pieces.reshape(*shape[:dim], shape[dim] * shape[dim + 1], *shape[dim + 2 :])


def from_everyone(value, axis):
    copies = jnp.broadcast_to(value, (lax.axis_size(axis), *value.shape))
    return lax.all_to_all(copies, axis, split_axis=0, concat_axis=0, tiled=True)


def gathered_copies(value, axis, dim):
    return laid_out(from_everyone(value, axis), dim)


def split_up(value, dim, peers):
    before, after = (value.shape[:dim], value.shape[dim + 1 :])
    return jnp.moveaxis(value.reshape(*before, peers, -1, *after), dim, 0)


def sent_and_summed(value, axis, dim):
    pieces = split_up(value, dim, lax.axis_size(axis))
    arrived = lax.all_to_all(pieces, axis, split_axis=0, concat_axis=0, tiled=True)
    return arrived.sum(axis=0)


def padded_2(value, sides, width):
    for axis, dim in sides:
        peers, length = (lax.axis_size(axis), value.shape[dim])
        up = [(i, (i + 1) % peers) for i in range(peers - 1)]
        down = [(j, i) for i, j in up]
        last = lax.slice_in_dim(value, length - width, length, axis=dim)
        initial = lax.slice_in_dim(value, 0, width, axis=dim)
        before = lax.ppermute(last, axis, up)
        after = lax.ppermute(initial, axis, down)
        value = jnp.concatenate([before, value, after], axis=dim)
    return value


def with_halo(value, sides, width):
    edges = {}
    for axis, dim in sides:
        peers, length = (lax.axis_size(axis), value.shape[dim])
        up = [(i, (i + 1) % peers) for i in range(peers - 1)]
        last = lax.slice_in_dim(value, length - width, length, axis=dim)
        initial = lax.slice_in_dim(value, 0, width, axis=dim)
        edges[dim] = (
            lax.ppermute(last, axis, up),
            lax.ppermute(initial, axis, [(b, a) for a, b in up]),
        )
    done = []
    for _, dim in sides:
        low, high = edges[dim]
        around = [(width, width) if d in done else (0, 0) for d in range(value.ndim)]
        value = jnp.concatenate([jnp.pad(low, around), value, jnp.pad(high, around)], axis=dim)
        done.append(dim)
    return value


def summed_rows(subtotal, axes):
    for axis in axes:
        subtotal = lax.psum_scatter(subtotal, axis, scatter_dimension=0, tiled=True)
    return subtotal


def stencil_parts(padded):
    center = padded[:, 1:-1, 1:-1]
    north_cell = padded[:, 2:, 1:-1]
    south_cell = padded[:, :-2, 1:-1]
    east_cell = padded[:, 1:-1, 2:]
    west_cell = padded[:, 1:-1, :-2]
    return (center, north_cell, south_cell, east_cell, west_cell)


def advance(padded, wind_out):
    center, north_cell, south_cell, east_cell, west_cell = stencil_parts(padded)
    spread = north_cell + south_cell + east_cell + west_cell - 4.0 * center
    return (
        center
        + diffusion * spread
        - 0.5 * wind_out[1] * (north_cell - south_cell)
        - 0.5 * wind_out[0] * (east_cell - west_cell)
    )


def retreat(padded, wind_in):
    center, north_cell, south_cell, east_cell, west_cell = stencil_parts(padded)
    spread = north_cell + south_cell + east_cell + west_cell - 4.0 * center
    along_lon = wind_in[0] * padded
    along_lat = wind_in[1] * padded
    return (
        center
        + diffusion * spread
        + 0.5 * (along_lat[:, 2:, 1:-1] - along_lat[:, :-2, 1:-1])
        + 0.5 * (along_lon[:, 1:-1, 2:] - along_lon[:, 1:-1, :-2])
    )


def observe(tangent, picked, observed, weighting):
    levels, row_count, col_count = tangent.shape
    blocks = tangent.reshape(levels, row_count, col_count // OBLK, OBLK)
    onehot = (picked[..., None] == jnp.arange(OBLK, dtype=jnp.int32)).astype(jnp.float32)
    looked = jnp.sum(blocks * onehot, axis=-1)
    misfit = weighting * (looked - observed)
    return (misfit[..., None] * onehot).reshape(levels, row_count, col_count)


def domain_mask(margin, row_count, col_count):
    lat_start = lax.axis_index(LAT) * row_count - margin
    lon_start = lax.axis_index("mem") * col_count - margin
    row_place = lat_start + jnp.arange(row_count + 2 * margin, dtype=jnp.int32)
    col_place = lon_start + jnp.arange(col_count + 2 * margin, dtype=jnp.int32)
    rows_inside = (row_place >= 0) & (row_place < row_count * lax.axis_size(LAT))
    cols_inside = (col_place >= 0) & (col_place < col_count * lax.axis_size("mem"))
    return (rows_inside[:, None] & cols_inside[None, :]).astype(jnp.float32)


def body(
    coarse_weights,
    perturbations,
    lat_matrix,
    lon_matrix,
    wind_field,
    observed_cell,
    observed_value,
    observed_weight,
):
    members_here, levels, row_count, lon_total = perturbations.shape
    col_count = wind_field.shape[2]
    members_all = members_here * lax.axis_size("mem")
    member_scale = 1.0 / jnp.sqrt(jnp.float32(members_all - 1))
    lat_full = lat_matrix.astype(jnp.float32)
    lon_full = lon_matrix.astype(jnp.float32)
    columns = lat_full
    narrow = jnp.einsum(
        "rc,cmlw->mlrw",
        columns,
        gathered_copies(coarse_weights, LAT, 0).astype(jnp.float32),
        precision=highest,
    )
    localized = jnp.einsum("mlrw,wf->mlrf", narrow, lon_full, precision=highest)
    partial_sum = jnp.sum(localized * perturbations, axis=0)
    increment = sent_and_summed(partial_sum, "mem", 2) * member_scale
    wide_wind = padded_2(wind_field, (("mem", 2), (LAT, 1)), STEPS)

    def wind_margin(margin):
        return wide_wind[
            :,
            STEPS - margin : STEPS + row_count + margin,
            STEPS - margin : STEPS + col_count + margin,
        ]

    forcings = []
    tangent = padded_2(increment, (("mem", 2), (LAT, 1)), STEPS)
    for step_index in range(STEPS):
        margin = STEPS - step_index - 1
        tangent = advance(tangent, wind_margin(margin)) * domain_mask(margin, row_count, col_count)
        inner = tangent[:, margin : margin + row_count, margin : margin + col_count]
        forcings.append(
            observe(
                inner,
                observed_cell[step_index],
                observed_value[step_index],
                observed_weight[step_index],
            )
        )
    adjoint = jnp.zeros_like(increment)
    for step_index in reversed(range(STEPS)):
        padded = with_halo(adjoint + forcings[step_index], (("mem", 2), (LAT, 1)), 1)
        adjoint = retreat(padded, wind_margin(1))
    product = perturbations * gathered_copies(adjoint, "mem", 2)[None]
    projected = jnp.einsum("mlrf,wf->mlrw", product, lon_full, precision=highest)
    columns = lat_full
    banded = summed_rows(jnp.einsum("rc,mlrw->cmlw", columns, projected, precision=highest), LAT)
    gradient = banded * member_scale + coarse_weights.astype(jnp.float32)
    return (gradient, increment)


def solution(mesh):
    split = Mesh(mesh.devices.reshape(mesh.shape["mem"], 8, 2), ("mem", "lat_0", "lat_1"))
    placed = (
        P(LAT, "mem", None, None),
        P("mem", None, LAT, None),
        P(LAT, None),
        P(),
        P(None, LAT, "mem"),
        P(None, None, LAT, "mem"),
        P(None, None, LAT, "mem"),
        P(None, None, LAT, "mem"),
    )
    return jax.shard_map(
        body,
        mesh=split,
        in_specs=placed,
        out_specs=(P(LAT, "mem", None, None), P(None, LAT, "mem")),
        check_vma=False,
    )
```

profile of v0, /device:TPU:2, one launch (start us, length us, event | category | flops | bytes accessed | tf_op | source)
XLA Modules:
  0.0 355.2 jit_solution(15615994501080995483)
XLA Ops:
  9.8 10.3 %all-to-all-start = ((bf16[16,8,4,8,256]{4,1,3,2,0:T(8,128)(2,1)}), bf16[16,8,4,8,256]{4,1,3,2,0:T(8,128)(2,1)}, u32[]{:S(2)}, u32[]{:S(2)}) async-start(bf16[16,8,4,8,256]{4,1,3,2,0:T(8,128)(2,1)} %broadcast_in_dim.4), calls=%async_computation | async-start | bytes 4194304 | tf_op jit(solution)/shard_map/all_to_all | solution.py:24
  22.3 3.6 %collective-permute-start.5 = (f32[2,32,4]{2,1,0:T(8,128)S(1)}, f32[2,32,4]{2,1,0:T(8,128)S(1)}, u32[]{:S(2)}, u32[]{:S(2)}) collective-permute-start(f32[2,32,4]{2,1,0:T(8,128)S(1)} %get-tuple-element.57), channel_id=1, source_target_pairs={{16,0},{32,16},{48,32},{64,48},{80,64},{96,80},{112,96},{128,112},... | collective-permute-start | bytes 3080 | tf_op jit(solution)/shard_map/ppermute | solution.py:50
  26.3 46.0 %all-to-all-done = bf16[16,8,4,8,256]{4,1,3,2,0:T(8,128)(2,1)} async-done(((bf16[16,8,4,8,256]{4,1,3,2,0:T(8,128)(2,1)}), bf16[16,8,4,8,256]{4,1,3,2,0:T(8,128)(2,1)}, u32[]{:S(2)}, u32[]{:S(2)}) %all-to-all-start) | async-done | bytes 2097184 | tf_op jit(solution)/shard_map/all_to_all | solution.py:24
  74.3 3.0 fusion
  81.0 3.4 reshape.267
  84.4 5.9 %all-to-all-start.1 = ((f32[16,1,16384]{2,1,0:T(1,128)}), f32[16,1,16384]{2,1,0:T(1,128)S(1)}, u32[]{:S(2)}, u32[]{:S(2)}) async-start(f32[16,1,16384]{2,1,0:T(1,128)} %reshape.267), calls=%async_computation.1 | async-start | bytes 2097152 | tf_op jit(solution)/shard_map/all_to_all | solution.py:38
  94.7 8.0 %collective-permute-done.6 = f32[2,4,72]{2,1,0:T(4,128)S(1)} collective-permute-done((f32[2,4,72]{2,1,0:T(4,128)S(1)}, f32[2,4,72]{2,1,0:T(4,128)S(1)}, u32[]{:S(2)}, u32[]{:S(2)}) %collective-permute-start.6) | collective-permute-done | bytes 2336 | tf_op jit(solution)/shard_map/ppermute | solution.py:49
  106.2 4.4 %reduce = f32[16,16384]{1,0:T(8,128)} reduce(f32[16,1,16384]{2,1,0:T(1,128)S(1)} %all-to-all-done.1, f32[]{:T(128)} %broadcast.284), dimensions={1}, to_apply=%all_to_all.10.reduce_sub_computation | reduce | bytes 2097156 | tf_op jit(solution)/shard_map/all_to_all | solution.py:38
  115.1 3.5 collective-permute-start.1
  122.9 6.2 %collective-permute-start.2 = (f32[8,4,72]{1,2,0:T(8,128)S(1)}, f32[8,4,72]{1,2,0:T(8,128)S(1)}, u32[]{:S(2)}, u32[]{:S(2)}) collective-permute-start(f32[8,4,72]{1,2,0:T(8,128)S(1)} %copy.330), channel_id=1, source_target_pairs={{0,1},{1,2},{2,3},{3,4},{4,5},{5,6},{6,7},{7,8},{8,9},{9,10},{10,1... | collective-permute-start | bytes 27656 | tf_op jit(solution)/shard_map/ppermute | solution.py:49
  130.0 4.6 %collective-permute-done.3 = f32[8,4,72]{1,2,0:T(8,128)S(1)} collective-permute-done((f32[8,4,72]{1,2,0:T(8,128)S(1)}, f32[8,4,72]{1,2,0:T(8,128)S(1)}, u32[]{:S(2)}, u32[]{:S(2)}) %collective-permute-start.3) | collective-permute-done | bytes 9248 | tf_op jit(solution)/shard_map/ppermute | solution.py:50
  134.6 4.5 %collective-permute-done.2 = f32[8,4,72]{1,2,0:T(8,128)S(1)} collective-permute-done((f32[8,4,72]{1,2,0:T(8,128)S(1)}, f32[8,4,72]{1,2,0:T(8,128)S(1)}, u32[]{:S(2)}, u32[]{:S(2)}) %collective-permute-start.2) | collective-permute-done | bytes 9248 | tf_op jit(solution)/shard_map/ppermute | solution.py:49
  141.6 5.9 %collective-permute-start.11 = (f32[8,1,64]{1,2,0:T(8,128)S(1)}, f32[8,1,64]{1,2,0:T(8,128)S(1)}, u32[]{:S(2)}, u32[]{:S(2)}) collective-permute-start(f32[8,1,64]{1,2,0:T(8,128)S(1)} %get-tuple-element.32), channel_id=1, source_target_pairs={{0,1},{1,2},{2,3},{3,4},{4,5},{5,6},{6,7},{7,8},{8,9},{9,10},{10,1... | collective-permute-start | bytes 6152 | tf_op jit(solution)/shard_map/ppermute | solution.py:63
  150.7 3.6 %collective-permute-start.9 = (f32[8,32,1]{1,2,0:T(1,128)S(1)}, f32[8,32,1]{1,2,0:T(1,128)S(1)}, u32[]{:S(2)}, u32[]{:S(2)}) collective-permute-start(f32[8,32,1]{1,2,0:T(1,128)S(1)} %get-tuple-element.35), channel_id=1, source_target_pairs={{16,0},{32,16},{48,32},{64,48},{80,64},{96,80},{112,96},{128,112},... | collective-permute-start | bytes 3080 | tf_op jit(solution)/shard_map/ppermute | solution.py:64
  154.6 4.4 %collective-permute-done.11 = f32[8,1,64]{1,2,0:T(8,128)S(1)} collective-permute-done((f32[8,1,64]{1,2,0:T(8,128)S(1)}, f32[8,1,64]{1,2,0:T(8,128)S(1)}, u32[]{:S(2)}, u32[]{:S(2)}) %collective-permute-start.11) | collective-permute-done | bytes 2080 | tf_op jit(solution)/shard_map/ppermute | solution.py:63
  160.0 5.9 %collective-permute-start.15 = (f32[8,1,64]{1,2,0:T(8,128)S(1)}, f32[8,1,64]{1,2,0:T(8,128)S(1)}, u32[]{:S(2)}, u32[]{:S(2)}) collective-permute-start(f32[8,1,64]{1,2,0:T(8,128)S(1)} %get-tuple-element.28), channel_id=1, source_target_pairs={{0,1},{1,2},{2,3},{3,4},{4,5},{5,6},{6,7},{7,8},{8,9},{9,10},{10,1... | collective-permute-start | bytes 6152 | tf_op jit(solution)/shard_map/ppermute | solution.py:63
  169.1 3.6 %collective-permute-start.13 = (f32[8,32,1]{1,2,0:T(1,128)S(1)}, f32[8,32,1]{1,2,0:T(1,128)S(1)}, u32[]{:S(2)}, u32[]{:S(2)}) collective-permute-start(f32[8,32,1]{1,2,0:T(1,128)S(1)} %get-tuple-element.31), channel_id=1, source_target_pairs={{16,0},{32,16},{48,32},{64,48},{80,64},{96,80},{112,96},{128,112},... | collective-permute-start | bytes 3080 | tf_op jit(solution)/shard_map/ppermute | solution.py:64
  172.8 4.2 %collective-permute-done.15 = f32[8,1,64]{1,2,0:T(8,128)S(1)} collective-permute-done((f32[8,1,64]{1,2,0:T(8,128)S(1)}, f32[8,1,64]{1,2,0:T(8,128)S(1)}, u32[]{:S(2)}, u32[]{:S(2)}) %collective-permute-start.15) | collective-permute-done | bytes 2080 | tf_op jit(solution)/shard_map/ppermute | solution.py:63
  178.0 5.9 %collective-permute-start.19 = (f32[8,1,64]{1,2,0:T(8,128)S(1)}, f32[8,1,64]{1,2,0:T(8,128)S(1)}, u32[]{:S(2)}, u32[]{:S(2)}) collective-permute-start(f32[8,1,64]{1,2,0:T(8,128)S(1)} %get-tuple-element.24), channel_id=1, source_target_pairs={{0,1},{1,2},{2,3},{3,4},{4,5},{5,6},{6,7},{7,8},{8,9},{9,10},{10,1... | collective-permute-start | bytes 6152 | tf_op jit(solution)/shard_map/ppermute | solution.py:63
  187.2 3.6 %collective-permute-start.17 = (f32[8,32,1]{1,2,0:T(1,128)S(1)}, f32[8,32,1]{1,2,0:T(1,128)S(1)}, u32[]{:S(2)}, u32[]{:S(2)}) collective-permute-start(f32[8,32,1]{1,2,0:T(1,128)S(1)} %get-tuple-element.27), channel_id=1, source_target_pairs={{16,0},{32,16},{48,32},{64,48},{80,64},{96,80},{112,96},{128,112},... | collective-permute-start | bytes 3080 | tf_op jit(solution)/shard_map/ppermute | solution.py:64
  190.8 4.5 %collective-permute-done.19 = f32[8,1,64]{1,2,0:T(8,128)S(1)} collective-permute-done((f32[8,1,64]{1,2,0:T(8,128)S(1)}, f32[8,1,64]{1,2,0:T(8,128)S(1)}, u32[]{:S(2)}, u32[]{:S(2)}) %collective-permute-start.19) | collective-permute-done | bytes 2080 | tf_op jit(solution)/shard_map/ppermute | solution.py:63
  196.3 5.9 %collective-permute-start.23 = (f32[8,1,64]{1,2,0:T(8,128)S(1)}, f32[8,1,64]{1,2,0:T(8,128)S(1)}, u32[]{:S(2)}, u32[]{:S(2)}) collective-permute-start(f32[8,1,64]{1,2,0:T(8,128)S(1)} %get-tuple-element.16), channel_id=1, source_target_pairs={{0,1},{1,2},{2,3},{3,4},{4,5},{5,6},{6,7},{7,8},{8,9},{9,10},{10,1... | collective-permute-start | bytes 6152 | tf_op jit(solution)/shard_map/ppermute | solution.py:63
  205.4 3.6 %collective-permute-start.21 = (f32[8,32,1]{1,2,0:T(1,128)S(1)}, f32[8,32,1]{1,2,0:T(1,128)S(1)}, u32[]{:S(2)}, u32[]{:S(2)}) collective-permute-start(f32[8,32,1]{1,2,0:T(1,128)S(1)} %get-tuple-element.19), channel_id=1, source_target_pairs={{16,0},{32,16},{48,32},{64,48},{80,64},{96,80},{112,96},{128,112},... | collective-permute-start | bytes 3080 | tf_op jit(solution)/shard_map/ppermute | solution.py:64
  209.2 4.5 %collective-permute-done.22 = f32[8,1,64]{1,2,0:T(8,128)S(1)} collective-permute-done((f32[8,1,64]{1,2,0:T(8,128)S(1)}, f32[8,1,64]{1,2,0:T(8,128)S(1)}, u32[]{:S(2)}, u32[]{:S(2)}) %collective-permute-start.22) | collective-permute-done | bytes 2080 | tf_op jit(solution)/shard_map/ppermute | solution.py:64
  217.1 20.9 %all_to_all.15 = f32[16,1,16384]{2,1,0:T(1,128)S(1)} all-to-all(f32[16,1,16384]{2,1,0:T(1,128)} %reshape.269), channel_id=1, replica_groups=mesh['mem'=16,'lat_0'=8,'lat_1'=2] {'mem'}, dimensions={0} | all-to-all | bytes 2097152 | tf_op jit(solution)/shard_map/all_to_all | solution.py:24
  237.9 4.4 %reduce.1 = f32[16,16384]{1,0:T(8,128)} reduce(f32[16,1,16384]{2,1,0:T(1,128)S(1)} %all_to_all.15, f32[]{:T(128)} %broadcast.284), dimensions={1}, to_apply=%all_to_all.11.reduce_sub_computation | reduce | bytes 2097156 | tf_op jit(solution)/shard_map/all_to_all | solution.py:24
  246.9 2.9 mul.521
  249.9 3.5 fusion.1
  253.3 5.0 %convolution_bitcast_fusion = f32[128,4,8,256]{0,3,2,1:T(8,128)} fusion(f32[4,8,32,256]{3,2,1,0:T(8,128)S(1)} %fusion.1, bf16[32,128]{1,0:T(8,128)(2,1)S(1)} %copy-done.9), kind=kOutput, calls=%fused_computation.4 | convolution fusion | flops 402653184 | bytes 5251072 | tf_op jit(solution)/shard_map/rc,mlrw->cmlw/dot_general | solution.py:189
  258.3 5.5 %copy.345 = f32[128,4,8,256]{3,2,1,0:T(8,128)} copy(f32[128,4,8,256]{0,3,2,1:T(8,128)} %convolution_bitcast_fusion) | data formatting | bytes 8388608 | tf_op jit(solution)/shard_map/rc,mlrw->cmlw/dot_general | solution.py:189
  263.9 61.4 %reduce-scatter.3.cloned.1.call-done = f32[16,4,8,256]{3,2,1,0:T(8,128)} async-done(((f32[128,4,8,256]{3,2,1,0:T(8,128)}), f32[16,4,8,256]{3,2,1,0:T(8,128)}) %reduce-scatter.3.cloned.1.call-update) | async-done | bytes 524304 | tf_op jit(solution)/shard_map/reduce_scatter | solution.py:77
  325.3 21.4 %reduce-scatter.5.cloned.1.call-done = f32[8,4,8,256]{3,2,1,0:T(8,128)} async-done(((f32[16,4,8,256]{3,2,1,0:T(8,128)}), f32[8,4,8,256]{3,2,1,0:T(8,128)}) %reduce-scatter.5.cloned.1.call-update) | async-done | bytes 262160 | tf_op jit(solution)/shard_map/reduce_scatter | solution.py:77
  (140 shorter events, 56.2 us)
Async XLA Ops:
  7.2 67.1 %copy-start = (bf16[256,1024]{1,0:T(8,128)(2,1)S(1)}, bf16[256,1024]{1,0:T(8,128)(2,1)}, u32[]{:S(2)}) copy-start(bf16[256,1024]{1,0:T(8,128)(2,1)} %param.11) | copy-start | bytes 1572868
  9.8 62.4 %copy-start.9 = (bf16[32,128]{1,0:T(8,128)(2,1)S(1)}, bf16[32,128]{1,0:T(8,128)(2,1)}, u32[]{:S(2)}) copy-start(bf16[32,128]{1,0:T(8,128)(2,1)} %param.10) | copy-start | bytes 24580
  9.8 62.4 %all-to-all-start = ((bf16[16,8,4,8,256]{4,1,3,2,0:T(8,128)(2,1)}), bf16[16,8,4,8,256]{4,1,3,2,0:T(8,128)(2,1)}, u32[]{:S(2)}, u32[]{:S(2)}) async-start(bf16[16,8,4,8,256]{4,1,3,2,0:T(8,128)(2,1)} %broadcast_in_dim.4), calls=%async_computation | async-start | bytes 4194304 | tf_op jit(solution)/shard_map/all_to_all | solution.py:24
  20.1 54.1 %copy-start.1 = (bf16[4,8,32,1024]{3,2,1,0:T(8,128)(2,1)S(1)}, bf16[4,8,32,1024]{3,2,1,0:T(8,128)(2,1)}, u32[]{:S(2)}) copy-start(bf16[4,8,32,1024]{3,2,1,0:T(8,128)(2,1)} %param.9) | copy-start | bytes 6291460
  20.2 70.3 %collective-permute-start.4 = (f32[2,32,4]{2,1,0:T(8,128)S(1)}, f32[2,32,4]{2,1,0:T(8,128)S(1)}, u32[]{:S(2)}, u32[]{:S(2)}) collective-permute-start(f32[2,32,4]{2,1,0:T(8,128)S(1)} %get-tuple-element.56), channel_id=1, source_target_pairs={{0,16},{16,32},{32,48},{48,64},{64,80},{80,96},{96,112},{112,128},... | collective-permute-start | bytes 3080 | tf_op jit(solution)/shard_map/ppermute | solution.py:49
  22.3 68.2 %collective-permute-start.5 = (f32[2,32,4]{2,1,0:T(8,128)S(1)}, f32[2,32,4]{2,1,0:T(8,128)S(1)}, u32[]{:S(2)}, u32[]{:S(2)}) collective-permute-start(f32[2,32,4]{2,1,0:T(8,128)S(1)} %get-tuple-element.57), channel_id=1, source_target_pairs={{16,0},{32,16},{48,32},{64,48},{80,64},{96,80},{112,96},{128,112},... | collective-permute-start | bytes 3080 | tf_op jit(solution)/shard_map/ppermute | solution.py:50
  84.4 21.3 %all-to-all-start.1 = ((f32[16,1,16384]{2,1,0:T(1,128)}), f32[16,1,16384]{2,1,0:T(1,128)S(1)}, u32[]{:S(2)}, u32[]{:S(2)}) async-start(f32[16,1,16384]{2,1,0:T(1,128)} %reshape.267), calls=%async_computation.1 | async-start | bytes 2097152 | tf_op jit(solution)/shard_map/all_to_all | solution.py:38
  90.4 235.0 %reduce-scatter.3.cloned.1.call-start = ((), (), s32[]{:S(2)}) async-start(), calls=%async_computation.5 | async-start | bytes 4718592 | tf_op jit(solution)/shard_map/reduce_scatter | solution.py:77
  90.6 12.0 %collective-permute-start.6 = (f32[2,4,72]{2,1,0:T(4,128)S(1)}, f32[2,4,72]{2,1,0:T(4,128)S(1)}, u32[]{:S(2)}, u32[]{:S(2)}) collective-permute-start(f32[2,4,72]{2,1,0:T(4,128)S(1)} %get-tuple-element.44), channel_id=1, source_target_pairs={{0,1},{1,2},{2,3},{3,4},{4,5},{5,6},{6,7},{7,8},{8,9},{9,10},{10,1... | collective-permute-start | bytes 6920 | tf_op jit(solution)/shard_map/ppermute | solution.py:49
  93.1 10.4 %collective-permute-start.7 = (f32[2,4,72]{2,1,0:T(4,128)S(1)}, f32[2,4,72]{2,1,0:T(4,128)S(1)}, u32[]{:S(2)}, u32[]{:S(2)}) collective-permute-start(f32[2,4,72]{2,1,0:T(4,128)S(1)} %get-tuple-element.45), channel_id=1, source_target_pairs={{1,0},{2,1},{3,2},{4,3},{5,4},{6,5},{7,6},{8,7},{9,8},{10,9},{11,1... | collective-permute-start | bytes 6920 | tf_op jit(solution)/shard_map/ppermute | solution.py:50
  113.1 6.3 %collective-permute-start = (f32[8,32,4]{2,1,0:T(8,128)S(1)}, f32[8,32,4]{2,1,0:T(8,128)S(1)}, u32[]{:S(2)}, u32[]{:S(2)}) collective-permute-start(f32[8,32,4]{2,1,0:T(8,128)S(1)} %get-tuple-element.42), channel_id=1, source_target_pairs={{0,16},{16,32},{32,48},{48,64},{64,80},{80,96},{96,112},{112,128},... | collective-permute-start | bytes 12296 | tf_op jit(solution)/shard_map/ppermute | solution.py:49
  115.1 6.0 %collective-permute-start.1 = (f32[8,32,4]{2,1,0:T(8,128)S(1)}, f32[8,32,4]{2,1,0:T(8,128)S(1)}, u32[]{:S(2)}, u32[]{:S(2)}) collective-permute-start(f32[8,32,4]{2,1,0:T(8,128)S(1)} %get-tuple-element.43), channel_id=1, source_target_pairs={{16,0},{32,16},{48,32},{64,48},{80,64},{96,80},{112,96},{128,112},... | collective-permute-start | bytes 12296 | tf_op jit(solution)/shard_map/ppermute | solution.py:50
  121.6 13.0 %collective-permute-start.3 = (f32[8,4,72]{1,2,0:T(8,128)S(1)}, f32[8,4,72]{1,2,0:T(8,128)S(1)}, u32[]{:S(2)}, u32[]{:S(2)}) collective-permute-start(f32[8,4,72]{1,2,0:T(8,128)S(1)} %copy.331), channel_id=1, source_target_pairs={{1,0},{2,1},{3,2},{4,3},{5,4},{6,5},{7,6},{8,7},{9,8},{10,9},{11,1... | collective-permute-start | bytes 27656 | tf_op jit(solution)/shard_map/ppermute | solution.py:50
  122.9 16.2 %collective-permute-start.2 = (f32[8,4,72]{1,2,0:T(8,128)S(1)}, f32[8,4,72]{1,2,0:T(8,128)S(1)}, u32[]{:S(2)}, u32[]{:S(2)}) collective-permute-start(f32[8,4,72]{1,2,0:T(8,128)S(1)} %copy.330), channel_id=1, source_target_pairs={{0,1},{1,2},{2,3},{3,4},{4,5},{5,6},{6,7},{7,8},{8,9},{9,10},{10,1... | collective-permute-start | bytes 27656 | tf_op jit(solution)/shard_map/ppermute | solution.py:49
  141.6 17.4 %collective-permute-start.11 = (f32[8,1,64]{1,2,0:T(8,128)S(1)}, f32[8,1,64]{1,2,0:T(8,128)S(1)}, u32[]{:S(2)}, u32[]{:S(2)}) collective-permute-start(f32[8,1,64]{1,2,0:T(8,128)S(1)} %get-tuple-element.32), channel_id=1, source_target_pairs={{0,1},{1,2},{2,3},{3,4},{4,5},{5,6},{6,7},{7,8},{8,9},{9,10},{10,1... | collective-permute-start | bytes 6152 | tf_op jit(solution)/shard_map/ppermute | solution.py:63
  147.5 11.5 %collective-permute-start.10 = (f32[8,1,64]{1,2,0:T(8,128)S(1)}, f32[8,1,64]{1,2,0:T(8,128)S(1)}, u32[]{:S(2)}, u32[]{:S(2)}) collective-permute-start(f32[8,1,64]{1,2,0:T(8,128)S(1)} %get-tuple-element.33), channel_id=1, source_target_pairs={{1,0},{2,1},{3,2},{4,3},{5,4},{6,5},{7,6},{8,7},{9,8},{10,9},{11,1... | collective-permute-start | bytes 6152 | tf_op jit(solution)/shard_map/ppermute | solution.py:64
  148.8 10.2 %collective-permute-start.8 = (f32[8,32,1]{1,2,0:T(1,128)S(1)}, f32[8,32,1]{1,2,0:T(1,128)S(1)}, u32[]{:S(2)}, u32[]{:S(2)}) collective-permute-start(f32[8,32,1]{1,2,0:T(1,128)S(1)} %get-tuple-element.34), channel_id=1, source_target_pairs={{0,16},{16,32},{32,48},{48,64},{64,80},{80,96},{96,112},{112,128},... | collective-permute-start | bytes 3080 | tf_op jit(solution)/shard_map/ppermute | solution.py:63
  150.7 8.3 %collective-permute-start.9 = (f32[8,32,1]{1,2,0:T(1,128)S(1)}, f32[8,32,1]{1,2,0:T(1,128)S(1)}, u32[]{:S(2)}, u32[]{:S(2)}) collective-permute-start(f32[8,32,1]{1,2,0:T(1,128)S(1)} %get-tuple-element.35), channel_id=1, source_target_pairs={{16,0},{32,16},{48,32},{64,48},{80,64},{96,80},{112,96},{128,112},... | collective-permute-start | bytes 3080 | tf_op jit(solution)/shard_map/ppermute | solution.py:64
  160.0 17.0 %collective-permute-start.15 = (f32[8,1,64]{1,2,0:T(8,128)S(1)}, f32[8,1,64]{1,2,0:T(8,128)S(1)}, u32[]{:S(2)}, u32[]{:S(2)}) collective-permute-start(f32[8,1,64]{1,2,0:T(8,128)S(1)} %get-tuple-element.28), channel_id=1, source_target_pairs={{0,1},{1,2},{2,3},{3,4},{4,5},{5,6},{6,7},{7,8},{8,9},{9,10},{10,1... | collective-permute-start | bytes 6152 | tf_op jit(solution)/shard_map/ppermute | solution.py:63
  165.9 11.1 %collective-permute-start.14 = (f32[8,1,64]{1,2,0:T(8,128)S(1)}, f32[8,1,64]{1,2,0:T(8,128)S(1)}, u32[]{:S(2)}, u32[]{:S(2)}) collective-permute-start(f32[8,1,64]{1,2,0:T(8,128)S(1)} %get-tuple-element.29), channel_id=1, source_target_pairs={{1,0},{2,1},{3,2},{4,3},{5,4},{6,5},{7,6},{8,7},{9,8},{10,9},{11,1... | collective-permute-start | bytes 6152 | tf_op jit(solution)/shard_map/ppermute | solution.py:64
  167.2 9.9 %collective-permute-start.12 = (f32[8,32,1]{1,2,0:T(1,128)S(1)}, f32[8,32,1]{1,2,0:T(1,128)S(1)}, u32[]{:S(2)}, u32[]{:S(2)}) collective-permute-start(f32[8,32,1]{1,2,0:T(1,128)S(1)} %get-tuple-element.30), channel_id=1, source_target_pairs={{0,16},{16,32},{32,48},{48,64},{64,80},{80,96},{96,112},{112,128},... | collective-permute-start | bytes 3080 | tf_op jit(solution)/shard_map/ppermute | solution.py:63
  169.1 8.0 %collective-permute-start.13 = (f32[8,32,1]{1,2,0:T(1,128)S(1)}, f32[8,32,1]{1,2,0:T(1,128)S(1)}, u32[]{:S(2)}, u32[]{:S(2)}) collective-permute-start(f32[8,32,1]{1,2,0:T(1,128)S(1)} %get-tuple-element.31), channel_id=1, source_target_pairs={{16,0},{32,16},{48,32},{64,48},{80,64},{96,80},{112,96},{128,112},... | collective-permute-start | bytes 3080 | tf_op jit(solution)/shard_map/ppermute | solution.py:64
  178.0 17.3 %collective-permute-start.19 = (f32[8,1,64]{1,2,0:T(8,128)S(1)}, f32[8,1,64]{1,2,0:T(8,128)S(1)}, u32[]{:S(2)}, u32[]{:S(2)}) collective-permute-start(f32[8,1,64]{1,2,0:T(8,128)S(1)} %get-tuple-element.24), channel_id=1, source_target_pairs={{0,1},{1,2},{2,3},{3,4},{4,5},{5,6},{6,7},{7,8},{8,9},{9,10},{10,1... | collective-permute-start | bytes 6152 | tf_op jit(solution)/shard_map/ppermute | solution.py:63
  183.9 11.4 %collective-permute-start.18 = (f32[8,1,64]{1,2,0:T(8,128)S(1)}, f32[8,1,64]{1,2,0:T(8,128)S(1)}, u32[]{:S(2)}, u32[]{:S(2)}) collective-permute-start(f32[8,1,64]{1,2,0:T(8,128)S(1)} %get-tuple-element.25), channel_id=1, source_target_pairs={{1,0},{2,1},{3,2},{4,3},{5,4},{6,5},{7,6},{8,7},{9,8},{10,9},{11,1... | collective-permute-start | bytes 6152 | tf_op jit(solution)/shard_map/ppermute | solution.py:64
  185.2 10.1 %collective-permute-start.16 = (f32[8,32,1]{1,2,0:T(1,128)S(1)}, f32[8,32,1]{1,2,0:T(1,128)S(1)}, u32[]{:S(2)}, u32[]{:S(2)}) collective-permute-start(f32[8,32,1]{1,2,0:T(1,128)S(1)} %get-tuple-element.26), channel_id=1, source_target_pairs={{0,16},{16,32},{32,48},{48,64},{64,80},{80,96},{96,112},{112,128},... | collective-permute-start | bytes 3080 | tf_op jit(solution)/shard_map/ppermute | solution.py:63
  187.2 8.2 %collective-permute-start.17 = (f32[8,32,1]{1,2,0:T(1,128)S(1)}, f32[8,32,1]{1,2,0:T(1,128)S(1)}, u32[]{:S(2)}, u32[]{:S(2)}) collective-permute-start(f32[8,32,1]{1,2,0:T(1,128)S(1)} %get-tuple-element.27), channel_id=1, source_target_pairs={{16,0},{32,16},{48,32},{64,48},{80,64},{96,80},{112,96},{128,112},... | collective-permute-start | bytes 3080 | tf_op jit(solution)/shard_map/ppermute | solution.py:64
  196.3 12.8 %collective-permute-start.23 = (f32[8,1,64]{1,2,0:T(8,128)S(1)}, f32[8,1,64]{1,2,0:T(8,128)S(1)}, u32[]{:S(2)}, u32[]{:S(2)}) collective-permute-start(f32[8,1,64]{1,2,0:T(8,128)S(1)} %get-tuple-element.16), channel_id=1, source_target_pairs={{0,1},{1,2},{2,3},{3,4},{4,5},{5,6},{6,7},{7,8},{8,9},{9,10},{10,1... | collective-permute-start | bytes 6152 | tf_op jit(solution)/shard_map/ppermute | solution.py:63
  202.2 11.4 %collective-permute-start.22 = (f32[8,1,64]{1,2,0:T(8,128)S(1)}, f32[8,1,64]{1,2,0:T(8,128)S(1)}, u32[]{:S(2)}, u32[]{:S(2)}) collective-permute-start(f32[8,1,64]{1,2,0:T(8,128)S(1)} %get-tuple-element.17), channel_id=1, source_target_pairs={{1,0},{2,1},{3,2},{4,3},{5,4},{6,5},{7,6},{8,7},{9,8},{10,9},{11,1... | collective-permute-start | bytes 6152 | tf_op jit(solution)/shard_map/ppermute | solution.py:64
  203.5 10.1 %collective-permute-start.20 = (f32[8,32,1]{1,2,0:T(1,128)S(1)}, f32[8,32,1]{1,2,0:T(1,128)S(1)}, u32[]{:S(2)}, u32[]{:S(2)}) collective-permute-start(f32[8,32,1]{1,2,0:T(1,128)S(1)} %get-tuple-element.18), channel_id=1, source_target_pairs={{0,16},{16,32},{32,48},{48,64},{64,80},{80,96},{96,112},{112,128},... | collective-permute-start | bytes 3080 | tf_op jit(solution)/shard_map/ppermute | solution.py:63
  205.4 8.2 %collective-permute-start.21 = (f32[8,32,1]{1,2,0:T(1,128)S(1)}, f32[8,32,1]{1,2,0:T(1,128)S(1)}, u32[]{:S(2)}, u32[]{:S(2)}) collective-permute-start(f32[8,32,1]{1,2,0:T(1,128)S(1)} %get-tuple-element.19), channel_id=1, source_target_pairs={{16,0},{32,16},{48,32},{64,48},{80,64},{96,80},{112,96},{128,112},... | collective-permute-start | bytes 3080 | tf_op jit(solution)/shard_map/ppermute | solution.py:64
  263.8 82.9 %copy-start.5 = (bf16[8,4,8,256]{3,2,1,0:T(8,128)(2,1)S(1)}, bf16[8,4,8,256]{3,2,1,0:T(8,128)(2,1)}, u32[]{:S(2)}) copy-start(bf16[8,4,8,256]{3,2,1,0:T(8,128)(2,1)} %param.8) | copy-start | bytes 393220
  263.8 82.9 %reduce-scatter.5.cloned.1.call-start = ((), (), s32[]{:S(2)}) async-start(), calls=%async_computation.6 | async-start | bytes 786432 | tf_op jit(solution)/shard_map/reduce_scatter | solution.py:77
  (6 other events, 58.7 us)
Sparse Core Ops, SparseCore 0:
  264.0 61.3 reduce-scatter.2
  327.8 18.8 reduce-scatter.4
where the time goes:
time: 358 us; the launch traced here: 355 us
  waiting for transfers between devices  169 us (47%)
  starting transfers between devices  89.9 us (25%)
  local copies, waits for them, and re-layouts  30.5 us (9%)
  blocking collectives  20.9 us (6%)
  other arithmetic  16.8 us (5%)
  between operations  14.8 us (4%)
  matrix products  13.5 us (4%)
    reduce_scatter x2, waiting for transfers between devices, summed_rows(): subtotal = lax.psum_scatter(subtotal, axis, scatter_dimension=0, tiled=True)  82.8 us
    all_to_all x1, waiting for transfers between devices, from_everyone(): return lax.all_to_all(copies, axis, split_axis=0, concat_axis=0, tiled=True)  46 us
    ppermute x8, starting transfers between devices, with_halo(): lax.ppermute(last, axis, up)  31.3 us
    all_to_all x1, blocking collectives, from_everyone(): return lax.all_to_all(copies, axis, split_axis=0, concat_axis=0, tiled=True)  20.9 us
    ppermute x8, starting transfers between devices, with_halo(): lax.ppermute(initial, axis, [(b, a) for a, b in up])  19.7 us
    ppermute x4, waiting for transfers between devices, padded_2(): before = lax.ppermute(last, axis, up)  13.1 us
    ppermute x8, waiting for transfers between devices, with_halo(): lax.ppermute(last, axis, up)  13.1 us
    ppermute x4, starting transfers between devices, padded_2(): before = lax.ppermute(last, axis, up)  12.8 us
  transfers between devices with their start and end apart: 28, of which 14 were waited for; matrix products, arithmetic and copies ran while one was open for 4% of the time, Pallas kernels for 0%

commit v1 on v0

v1 whole, which is shorter than its diff:
```python
import jax
import jax.numpy as jnp
from jax import lax
from jax.experimental import pallas as pl
from jax.experimental.pallas import tpu as pltpu
from jax.sharding import Mesh
from jax.sharding import PartitionSpec as P

STEPS = 4
OBLK = 8
HALO = 8
LAT = ("lat_0", "lat_1")
ALL = ("mem", "lat_0", "lat_1")

highest = lax.Precision.HIGHEST


def swapped(value, axis, dim):
    return lax.all_to_all(value, axis, split_axis=dim, concat_axis=dim, tiled=True)


def ring_blocks(block, axis):
    size = lax.axis_size(axis)
    up = [(i, (i + 1) % size) for i in range(size)]
    down = [(j, i) for i, j in up]
    blocks = {0: block}
    rising = falling = block
    for hop in range(1, size // 2 + 1):
        rising = lax.ppermute(rising, axis, up)
        blocks[(-hop) % size] = rising
        if hop < size - hop:
            falling = lax.ppermute(falling, axis, down)
            blocks[hop] = falling
    return blocks


def stencil_kernel(place_ref, own_ref, inner_ref, outer_ref, wind_ref, gain_ref, value_ref, adjoint_ref):
    rows, cols = wind_ref.shape[1:]
    half = place_ref[0]
    first_row = place_ref[1]
    last_row = place_ref[2]
    inner = inner_ref[...]
    outer = outer_ref[...]
    lower = half == 0
    state = jnp.concatenate(
        [jnp.where(lower, outer, inner), own_ref[...], jnp.where(lower, inner, outer)], axis=0
    )
    row = lax.broadcasted_iota(jnp.int32, (rows, cols), 0) + first_row
    col = lax.broadcasted_iota(jnp.int32, (rows, cols), 1)
    inside = ((row >= 0) & (row < last_row)).astype(jnp.float32)
    not_first = (col > 0).astype(jnp.float32)
    not_last = (col < cols - 1).astype(jnp.float32)
    lon_wind = 0.5 * wind_ref[0]
    lat_wind = 0.5 * wind_ref[1]

    def north(x):
        return pltpu.roll(x, rows - 1, 0)

    def south(x):
        return pltpu.roll(x, 1, 0)

    def east(x):
        return pltpu.roll(x, cols - 1, 1)

    def west(x):
        return pltpu.roll(x, 1, 1)

    from_north = (0.2 - lat_wind) * inside
    from_south = (0.2 + lat_wind) * inside
    from_east = (0.2 - lon_wind) * inside * not_last
    from_west = (0.2 + lon_wind) * inside * not_first
    centre = 0.2 * inside
    forcings = []
    for step in range(STEPS):
        state = (
            centre * state
            + from_north * north(state)
            + from_south * south(state)
            + from_east * east(state)
            + from_west * west(state)
        )
        forcings.append(gain_ref[step] * (state - value_ref[step]))
    to_south = 0.2 + lat_wind
    to_north = 0.2 - lat_wind
    to_west = (0.2 + lon_wind) * not_first
    to_east = (0.2 - lon_wind) * not_last
    adjoint = None
    for step in reversed(range(STEPS)):
        pushed = forcings[step] if adjoint is None else adjoint + forcings[step]
        adjoint = inside * (
            0.2 * pushed
            + north(to_south * pushed)
            + south(to_north * pushed)
            + east(to_west * pushed)
            + west(to_east * pushed)
        )
    adjoint_ref[...] = adjoint[HALO : rows - HALO]


def body(
    coarse_weights,
    perturbations,
    lat_matrix,
    lon_matrix,
    wind_field,
    observed_cell,
    observed_value,
    observed_weight,
):
    members_here, levels, row_count, lon_total = perturbations.shape
    coarse_rows, _, _, coarse_lons = coarse_weights.shape
    col_count = wind_field.shape[2]
    peers = lax.axis_size("mem")
    bands = lax.axis_size(LAT)
    rings = lax.axis_size("lat_0")
    pairs = members_here * levels
    halves = peers // levels
    own_rows = row_count // halves
    member_scale = 1.0 / jnp.sqrt(jnp.float32(members_here * peers - 1))
    lon_full = lon_matrix.astype(jnp.float32)
    half = lax.axis_index("mem") % halves
    band = lax.axis_index(LAT)
    lower = half == 0

    beside = [(m, m ^ 1) for m in range(peers)]
    beyond = []
    for m in range(peers):
        for b in range(bands):
            if m % 2 == 0 and b > 0:
                beyond.append((m * bands + b, (m + 1) * bands + b - 1))
            if m % 2 == 1 and b < bands - 1:
                beyond.append((m * bands + b, (m - 1) * bands + b + 1))

    other = lax.ppermute(coarse_weights, "lat_1", [(0, 1), (1, 0)])
    both = jnp.concatenate([coarse_weights, other], axis=0)
    blocks = ring_blocks(both, "lat_0")
    columns = lat_matrix.reshape(row_count, rings, 2, coarse_rows)
    columns = jnp.where(lax.axis_index("lat_1") == 0, columns, columns[:, :, ::-1])
    columns = columns.reshape(row_count, rings, 2 * coarse_rows)
    columns = lax.dynamic_slice_in_dim(
        jnp.concatenate([columns, columns], axis=1), lax.axis_index("lat_0"), rings, axis=1
    ).reshape(row_count, rings * 2 * coarse_rows)

    packed = jnp.concatenate(
        [observed_cell.astype(jnp.float32), observed_value, observed_weight], axis=0
    )
    kinds, _, _, block_count = packed.shape
    packed = jnp.transpose(packed, (1, 2, 0, 3)).reshape(levels, row_count, kinds * block_count)
    winds = jnp.transpose(wind_field, (1, 0, 2)).reshape(1, row_count, 2 * col_count)
    winds = jnp.broadcast_to(winds, (levels, row_count, 2 * col_count))
    filler = jnp.zeros((levels, row_count, 256 - kinds * block_count - 2 * col_count), jnp.float32)
    packed = jnp.concatenate([winds, packed, filler], axis=2)
    packed = jnp.broadcast_to(packed[:, None], (levels, halves, row_count, 256))
    packed = swapped(packed.reshape(peers, row_count, 256), "mem", 0)
    winds = packed[:, :, : 2 * col_count].reshape(peers, row_count, 2, col_count)
    winds = jnp.transpose(winds, (1, 2, 0, 3)).reshape(row_count, 2 * lon_total)
    sights = packed[:, :, 2 * col_count : 2 * col_count + kinds * block_count]
    sights = sights.reshape(peers, row_count, kinds, block_count)
    sights = jnp.transpose(sights, (1, 2, 0, 3)).reshape(row_count, kinds * peers * block_count)
    local = jnp.concatenate([winds, sights], axis=1)
    outgoing = jnp.where(lower, local[:HALO], local[-HALO:])
    margin = lax.ppermute(outgoing, ALL, beyond)
    local = jnp.where(
        lower,
        jnp.concatenate([margin, local[: row_count - HALO]], axis=0),
        jnp.concatenate([local[HALO:], margin], axis=0),
    )
    wide_rows = own_rows + 2 * HALO
    wide_wind = jnp.transpose(local[:, : 2 * lon_total].reshape(wide_rows, 2, lon_total), (1, 0, 2))
    sights = local[:, 2 * lon_total :].reshape(wide_rows, kinds, peers * block_count)
    sights = jnp.transpose(sights, (1, 0, 2))
    spread = jnp.arange(lon_total)[None, :] // OBLK == jnp.arange(lon_total // OBLK)[:, None]
    sights = jnp.einsum("krb,bf->krf", sights, spread.astype(jnp.float32), precision=highest)
    cells = sights[:STEPS]
    values = sights[STEPS : 2 * STEPS]
    offset = (jnp.arange(lon_total) % OBLK).astype(jnp.float32)
    gains = jnp.where(jnp.abs(cells - offset) < 0.5, sights[2 * STEPS :], 0.0)

    lat_all = lax.all_gather(lat_matrix, LAT, axis=0, tiled=True)

    order = [0] + [d for d in blocks if d != 0]
    gathered = jnp.concatenate([blocks[d] for d in order], axis=0)
    columns = columns.reshape(row_count, rings, 2 * coarse_rows)
    columns = jnp.concatenate([columns[:, d] for d in order], axis=1)
    narrow = jnp.einsum(
        "rc,cmlw->mlrw", columns, gathered, preferred_element_type=jnp.float32
    )
    localized = jnp.einsum("mlrw,wf->mlrf", narrow, lon_full, precision=highest)
    partial_sum = jnp.sum(localized * perturbations, axis=0)
    arrived = swapped(partial_sum.reshape(peers, own_rows, lon_total), "mem", 0)
    own = arrived.sum(axis=0) * member_scale

    inner = lax.ppermute(jnp.where(lower, own[-HALO:], own[:HALO]), "mem", beside)
    outer = lax.ppermute(jnp.where(lower, own[:HALO], own[-HALO:]), ALL, beyond)
    place = jnp.stack(
        [half, band * row_count + half * own_rows - HALO, jnp.int32(row_count * bands)]
    ).astype(jnp.int32)
    whole = pl.BlockSpec(memory_space=pltpu.VMEM)
    adjoint = pl.pallas_call(
        stencil_kernel,
        out_shape=jax.ShapeDtypeStruct((own_rows, lon_total), jnp.float32),
        in_specs=[pl.BlockSpec(memory_space=pltpu.SMEM)] + [whole] * 6,
        out_specs=whole,
        compiler_params=pltpu.CompilerParams(vmem_limit_bytes=32 * 1024 * 1024),
    )(place, own, inner, outer, wide_wind, gains, values)

    copies = jnp.broadcast_to(adjoint, (peers, own_rows, lon_total))
    adjoint_all = swapped(copies, "mem", 0).reshape(levels, row_count, lon_total)
    product = perturbations * adjoint_all[None]
    projected = jnp.einsum("mlrf,wf->mlrw", product, lon_full, precision=highest)
    by_pair = projected.reshape(bands, pairs // bands, row_count, coarse_lons)
    by_pair = swapped(by_pair, LAT, 0)
    full = jnp.einsum(
        "bqrw,brc->qcw",
        by_pair,
        lat_all.reshape(bands, row_count, bands * coarse_rows).astype(jnp.float32),
        precision=highest,
    )
    full = full.reshape(pairs // bands, bands, coarse_rows, coarse_lons)
    full = swapped(jnp.transpose(full, (1, 0, 2, 3)), LAT, 0)
    full = full.reshape(members_here, levels, coarse_rows, coarse_lons)
    full = jnp.transpose(full, (2, 0, 1, 3))
    gradient = full * member_scale + coarse_weights.astype(jnp.float32)

    tiles = jnp.transpose(own.reshape(own_rows, peers, col_count), (1, 0, 2))
    increment = swapped(tiles, "mem", 0).reshape(levels, row_count, col_count)
    return (gradient, increment)


def solution(mesh):
    split = Mesh(mesh.devices.reshape(mesh.shape["mem"], 8, 2), ("mem", "lat_0", "lat_1"))
    placed = (
        P(LAT, "mem", None, None),
        P("mem", None, LAT, None),
        P(LAT, None),
        P(),
        P(None, LAT, "mem"),
        P(None, None, LAT, "mem"),
        P(None, None, LAT, "mem"),
        P(None, None, LAT, "mem"),
    )
    return jax.shard_map(
        body,
        mesh=split,
        in_specs=placed,
        out_specs=(P(LAT, "mem", None, None), P(None, LAT, "mem")),
        check_vma=False,
    )
```

time: 358 us -> 211 us (0.59)
  waiting for transfers between devices: 169 us -> 42.8 us
  blocking collectives: 20.9 us -> 80.5 us
  starting transfers between devices: 89.9 us -> 48 us
  local copies, waits for them, and re-layouts: 30.5 us -> 16.6 us
  between operations: 14.8 us -> 0.94 us
  other arithmetic: 16.8 us -> 8.24 us
    reduce_scatter x2 -> x0, waiting for transfers between devices: 82.8 us -> none  [summed_rows(): subtotal = lax.psum_scatter(subtotal, axis, scatter_dimension=0, tiled=True)]
    all_gather x0 -> x1, blocking collectives: none -> 57.4 us  [body(): lat_all = lax.all_gather(lat_matrix, LAT, axis=0, tiled=True)]
    ppermute x24 -> x11, starting transfers between devices: 73.6 us -> 17.5 us  [the longest x3 11.3 us: ring_blocks(): falling = lax.ppermute(falling, axis, down)]
    ppermute x24 -> x11, waiting for transfers between devices: 37.9 us -> 15.1 us  [the longest x4 14.1 us: ring_blocks(): rising = lax.ppermute(rising, axis, up)]
    all_to_all x2 -> x5, waiting for transfers between devices: 48 us -> 27.8 us  [swapped(): lax.all_to_all(value, axis, split_axis=dim, concat_axis=dim, tiled=True)]
    all_to_all x2 -> x5, starting transfers between devices: 16.3 us -> 30.5 us  [swapped(): lax.all_to_all(value, axis, split_axis=dim, concat_axis=dim, tiled=True)]
    all_to_all x2 -> x1, other arithmetic: 8.78 us -> 0.8 us  [swapped(): lax.all_to_all(value, axis, split_axis=dim, concat_axis=dim, tiled=True)]
    dot_general x1 -> x0, local copies, waits for them, and re-layouts: 5.47 us -> none  [body(): jnp.einsum('rc,mlrw->cmlw', columns, projected, precision=highest)]
  transfers between devices with their start and end apart: 28 -> 16, of which waited for: 14 -> 8; matrix products, arithmetic and copies ran while one was open for 4% -> 14% of each run, Pallas kernels for 0% -> 0%
where the time goes in v1:
time: 211 us; the launch traced here: 210 us
  blocking collectives  80.5 us (38%)
  starting transfers between devices  48 us (23%)
  waiting for transfers between devices  42.8 us (20%)
  local copies, waits for them, and re-layouts  16.6 us (8%)
  matrix products  10.9 us (5%)
  other arithmetic  8.24 us (4%)
    all_gather x1, blocking collectives, body(): lat_all = lax.all_gather(lat_matrix, LAT, axis=0, tiled=True)  57.4 us
    all_to_all x5, starting transfers between devices, swapped(): lax.all_to_all(value, axis, split_axis=dim, concat_axis=dim, tiled=True)  30.5 us
    all_to_all x5, waiting for transfers between devices, swapped(): lax.all_to_all(value, axis, split_axis=dim, concat_axis=dim, tiled=True)  27.8 us
    all_to_all x1, blocking collectives, swapped(): lax.all_to_all(value, axis, split_axis=dim, concat_axis=dim, tiled=True)  23.1 us
    ppermute x4, waiting for transfers between devices, ring_blocks(): rising = lax.ppermute(rising, axis, up)  14.1 us
    ppermute x3, starting transfers between devices, ring_blocks(): falling = lax.ppermute(falling, axis, down)  11.3 us
    unnamed x21, local copies, waits for them, and re-layouts  11.1 us
  transfers between devices with their start and end apart: 16, of which 8 were waited for; matrix products, arithmetic and copies ran while one was open for 14% of the time, Pallas kernels for 0%

profile of v1, /device:TPU:2, one launch (start us, length us, event | category | flops | bytes accessed | tf_op | source)
XLA Modules:
  0.0 209.7 jit_solution(12162460254936993449)
XLA Ops:
  0.7 1.7 constant_dynamic-update-slice_fusion.1
  2.4 2.1 %collective-permute-start = (bf16[8,4,8,256]{3,0,2,1:T(8,128)(2,1)S(1)}, bf16[8,4,8,256]{3,0,2,1:T(8,128)(2,1)S(1)}, u32[]{:S(2)}, u32[]{:S(2)}) collective-permute-start(bf16[8,4,8,256]{3,0,2,1:T(8,128)(2,1)S(1)} %get-tuple-element.8), channel_id=1, source_target_pairs={{0,1},{1,0},{2,3},{3,2},{4,5},{5,4},{6,7},{7,6},{8,9},{9,8},{10,11... | collective-permute-start | bytes 393224 | tf_op jit(solution)/shard_map/ppermute | solution.py:134
  7.7 5.9 %all-to-all-start.1 = ((f32[16,32,256]{2,1,0:T(8,128)}), f32[16,32,256]{2,1,0:T(8,128)S(1)}, u32[]{:S(2)}, u32[]{:S(2)}) async-start(f32[16,32,256]{2,1,0:T(8,128)} %bitcast.21), calls=%async_computation.1 | async-start | bytes 1048576 | tf_op jit(solution)/shard_map/all_to_all | solution.py:19
  14.7 1.9 collective-permute-start.1
  16.6 4.0 %collective-permute-start.2 = (bf16[16,4,8,256]{3,0,2,1:T(8,128)(2,1)S(1)}, bf16[16,4,8,256]{3,0,2,1:T(8,128)(2,1)}, u32[]{:S(2)}, u32[]{:S(2)}) collective-permute-start(bf16[16,4,8,256]{3,0,2,1:T(8,128)(2,1)S(1)} %get-tuple-element.4), channel_id=1, source_target_pairs={{2,0},{4,2},{6,4},{8,6},{10,8},{12,10},{14,12},{0,14},{3,1},{5,3},... | collective-permute-start | bytes 786440 | tf_op jit(solution)/shard_map/ppermute | solution.py:32
  21.2 5.9 %collective-permute-done.1 = bf16[16,4,8,256]{3,0,2,1:T(8,128)(2,1)S(1)} collective-permute-done((bf16[16,4,8,256]{3,0,2,1:T(8,128)(2,1)S(1)}, bf16[16,4,8,256]{3,0,2,1:T(8,128)(2,1)S(1)}, u32[]{:S(2)}, u32[]{:S(2)}) %collective-permute-start.1) | collective-permute-done | bytes 262176 | tf_op jit(solution)/shard_map/ppermute | solution.py:29
  27.3 3.3 %collective-permute-start.4 = (bf16[16,4,8,256]{3,0,2,1:T(8,128)(2,1)}, bf16[16,4,8,256]{3,0,2,1:T(8,128)(2,1)}, u32[]{:S(2)}, u32[]{:S(2)}) collective-permute-start(bf16[16,4,8,256]{3,0,2,1:T(8,128)(2,1)} %collective-permute-done.2), channel_id=1, source_target_pairs={{2,0},{4,2},{6,4},{8,6},{10,8},{12,10},{14,12},{0,14},{3,1},{5,3},... | collective-permute-start | bytes 786440 | tf_op jit(solution)/shard_map/ppermute | solution.py:32
  31.4 1.7 constant_dynamic-update-slice_fusion.7
  34.6 1.7 collective-permute-done.3
  36.3 1.3 collective-permute-start.10
  37.6 3.9 %collective-permute-start.6 = (bf16[16,4,8,256]{3,0,2,1:T(8,128)(2,1)}, bf16[16,4,8,256]{3,0,2,1:T(8,128)(2,1)S(1)}, u32[]{:S(2)}, u32[]{:S(2)}) collective-permute-start(bf16[16,4,8,256]{3,0,2,1:T(8,128)(2,1)} %collective-permute-done.4), channel_id=1, source_target_pairs={{2,0},{4,2},{6,4},{8,6},{10,8},{12,10},{14,12},{0,14},{3,1},{5,3},... | collective-permute-start | bytes 786440 | tf_op jit(solution)/shard_map/ppermute | solution.py:32
  41.6 1.7 constant_dynamic-update-slice_fusion.6
  43.3 1.4 collective-permute-done.5
  44.7 1.7 constant_dynamic-update-slice_fusion.5
  48.9 5.1 %collective-permute-done.7 = bf16[16,4,8,256]{3,0,2,1:T(8,128)(2,1)S(1)} collective-permute-done((bf16[16,4,8,256]{3,0,2,1:T(8,128)(2,1)S(1)}, bf16[16,4,8,256]{3,0,2,1:T(8,128)(2,1)S(1)}, u32[]{:S(2)}, u32[]{:S(2)}) %collective-permute-start.7) | collective-permute-done | bytes 262176 | tf_op jit(solution)/shard_map/ppermute | solution.py:29
  54.7 2.0 convolution_bitcast_fusion
  56.7 3.1 %fusion = f32[8,32,1024]{2,1,0:T(8,128)} fusion(bf16[4,8,32,1024]{3,2,1,0:T(8,128)(2,1)S(1)} %copy-done.1, f32[4,8,32,256]{3,2,1,0:T(8,128)S(1)} %convolution_bitcast_fusion, bf16[256,1024]{1,0:T(8,128)(2,1)S(1)} %copy-done), kind=kOutput, calls=%fused_computation.2 | convolution fusion | flops 3224109056 | bytes 4718592 | tf_op jit(solution)/shard_map/mlrw,wf->mlrf/dot_general | solution.py:188
  59.8 5.7 %all-to-all-start = ((f32[16,16,1024]{2,1,0:T(8,128)}), f32[16,16,1024]{2,1,0:T(8,128)}, u32[]{:S(2)}, u32[]{:S(2)}) async-start(f32[16,16,1024]{2,1,0:T(8,128)} %bitcast.98), calls=%async_computation | async-start | bytes 2097152 | tf_op jit(solution)/shard_map/all_to_all | solution.py:19
  65.6 1.0 fusion.11
  66.6 1.9 fusion.8
  68.6 12.4 %all-to-all-done = f32[16,16,1024]{2,1,0:T(8,128)} async-done(((f32[16,16,1024]{2,1,0:T(8,128)}), f32[16,16,1024]{2,1,0:T(8,128)}, u32[]{:S(2)}, u32[]{:S(2)}) %all-to-all-start) | async-done | bytes 1048608 | tf_op jit(solution)/shard_map/all_to_all | solution.py:19
  81.0 1.3 reduce_sum.19
  83.2 1.5 fusion.29
  84.8 1.6 shard_map.95
  86.6 23.1 %all_to_all.30 = f32[16,16,1024]{2,1,0:T(8,128)S(1)} all-to-all(f32[16,16,1024]{2,1,0:T(8,128)S(1)} %broadcast_in_dim.31), channel_id=1, replica_groups=mesh['mem'=16,'lat_0'=8,'lat_1'=2] {'mem'}, dimensions={0} | all-to-all | bytes 2097152 | tf_op jit(solution)/shard_map/all_to_all | solution.py:19
  109.7 3.3 %fusion.1 = f32[4,8,32,256]{3,2,1,0:T(8,128)} fusion(bf16[4,8,32,1024]{3,2,1,0:T(8,128)(2,1)S(1)} %copy-done.1, f32[8,32,1024]{2,1,0:T(8,128)S(1)} %bitcast.100, bf16[256,1024]{1,0:T(8,128)(2,1)S(1)} %copy-done), kind=kOutput, calls=%fused_computation.3 | convolution fusion | flops 3223322624 | bytes 4718592 | tf_op jit(solution)/shard_map/mlrf,wf->mlrw/dot_general | solution.py:210
  113.0 7.9 %all-to-all-start.3 = ((f32[16,2,32,256]{3,2,1,0:T(8,128)}), f32[16,2,32,256]{3,2,1,0:T(8,128)S(1)}, u32[]{:S(2)}, u32[]{:S(2)}) async-start(f32[16,2,32,256]{3,2,1,0:T(8,128)} %bitcast.99), calls=%async_computation.3 | async-start | bytes 2097152 | tf_op jit(solution)/shard_map/all_to_all | solution.py:19
  120.9 57.4 %all_gather.3 = bf16[512,128]{1,0:T(8,128)(2,1)S(1)} all-gather(bf16[32,128]{1,0:T(8,128)(2,1)S(1)} %copy-done.3), channel_id=1, replica_groups=mesh['mem'=16,'lat_0'=8,'lat_1'=2] {'lat_0','lat_1'}, dimensions={0}, use_global_device_ids=true | all-gather | bytes 139264 | tf_op jit(solution)/shard_map/all_gather | solution.py:179
  179.2 3.8 %all-to-all-start.5 = ((f32[16,1,1024]{2,1,0:T(1,128)}), f32[16,1,1024]{2,1,0:T(1,128)S(1)}, u32[]{:S(2)}, u32[]{:S(2)}) async-start(f32[16,1,1024]{2,1,0:T(1,128)} %reshape.127), calls=%async_computation.5 | async-start | bytes 131072 | tf_op jit(solution)/shard_map/all_to_all | solution.py:19
  184.2 3.6 %all-to-all-done.5 = f32[16,1,1024]{2,1,0:T(1,128)S(1)} async-done(((f32[16,1,1024]{2,1,0:T(1,128)}), f32[16,1,1024]{2,1,0:T(1,128)S(1)}, u32[]{:S(2)}, u32[]{:S(2)}) %all-to-all-start.5) | async-done | bytes 65568 | tf_op jit(solution)/shard_map/all_to_all | solution.py:19
  187.9 7.2 %all-to-all-start.4 = ((f32[16,2,8,256]{3,2,1,0:T(8,128)}), f32[16,2,8,256]{3,2,1,0:T(8,128)S(1)}, u32[]{:S(2)}, u32[]{:S(2)}) async-start(f32[16,2,8,256]{3,2,1,0:T(8,128)} %bitcast.95), calls=%async_computation.4 | async-start | bytes 524288 | tf_op jit(solution)/shard_map/all_to_all | solution.py:19
  197.1 11.7 %all-to-all-done.4 = f32[16,2,8,256]{3,2,1,0:T(8,128)S(1)} async-done(((f32[16,2,8,256]{3,2,1,0:T(8,128)}), f32[16,2,8,256]{3,2,1,0:T(8,128)S(1)}, u32[]{:S(2)}, u32[]{:S(2)}) %all-to-all-start.4) | async-done | bytes 262176 | tf_op jit(solution)/shard_map/all_to_all | solution.py:19
  (73 shorter events, 16.4 us)
Async XLA Ops:
  0.6 56.1 %copy-start = (bf16[256,1024]{1,0:T(8,128)(2,1)S(1)}, bf16[256,1024]{1,0:T(8,128)(2,1)}, u32[]{:S(2)}) copy-start(bf16[256,1024]{1,0:T(8,128)(2,1)} %param.11) | copy-start | bytes 1572868
  0.6 5.9 %copy-start.4 = (f32[2,32,64]{2,1,0:T(8,128)S(1)}, f32[2,32,64]{2,1,0:T(8,128)}, u32[]{:S(2)}) copy-start(f32[2,32,64]{2,1,0:T(8,128)} %param.12) | copy-start | bytes 49156
  2.4 11.3 %copy-start.3 = (bf16[32,128]{1,0:T(8,128)(2,1)S(1)}, bf16[32,128]{1,0:T(8,128)(2,1)}, u32[]{:S(2)}) copy-start(bf16[32,128]{1,0:T(8,128)(2,1)} %param.10) | copy-start | bytes 24580
  2.4 11.6 %collective-permute-start = (bf16[8,4,8,256]{3,0,2,1:T(8,128)(2,1)S(1)}, bf16[8,4,8,256]{3,0,2,1:T(8,128)(2,1)S(1)}, u32[]{:S(2)}, u32[]{:S(2)}) collective-permute-start(bf16[8,4,8,256]{3,0,2,1:T(8,128)(2,1)S(1)} %get-tuple-element.8), channel_id=1, source_target_pairs={{0,1},{1,0},{2,3},{3,2},{4,5},{5,4},{6,7},{7,6},{8,9},{9,8},{10,11... | collective-permute-start | bytes 393224 | tf_op jit(solution)/shard_map/ppermute | solution.py:134
  7.7 25.5 %all-to-all-start.1 = ((f32[16,32,256]{2,1,0:T(8,128)}), f32[16,32,256]{2,1,0:T(8,128)S(1)}, u32[]{:S(2)}, u32[]{:S(2)}) async-start(f32[16,32,256]{2,1,0:T(8,128)} %bitcast.21), calls=%async_computation.1 | async-start | bytes 1048576 | tf_op jit(solution)/shard_map/all_to_all | solution.py:19
  14.7 12.5 %collective-permute-start.1 = (bf16[16,4,8,256]{3,0,2,1:T(8,128)(2,1)S(1)}, bf16[16,4,8,256]{3,0,2,1:T(8,128)(2,1)S(1)}, u32[]{:S(2)}, u32[]{:S(2)}) collective-permute-start(bf16[16,4,8,256]{3,0,2,1:T(8,128)(2,1)S(1)} %get-tuple-element.4), channel_id=1, source_target_pairs={{0,2},{2,4},{4,6},{6,8},{8,10},{10,12},{12,14},{14,0},{1,3},{3,5},... | collective-permute-start | bytes 786440 | tf_op jit(solution)/shard_map/ppermute | solution.py:29
  16.6 10.7 %collective-permute-start.2 = (bf16[16,4,8,256]{3,0,2,1:T(8,128)(2,1)S(1)}, bf16[16,4,8,256]{3,0,2,1:T(8,128)(2,1)}, u32[]{:S(2)}, u32[]{:S(2)}) collective-permute-start(bf16[16,4,8,256]{3,0,2,1:T(8,128)(2,1)S(1)} %get-tuple-element.4), channel_id=1, source_target_pairs={{2,0},{4,2},{6,4},{8,6},{10,8},{12,10},{14,12},{0,14},{3,1},{5,3},... | collective-permute-start | bytes 786440 | tf_op jit(solution)/shard_map/ppermute | solution.py:32
  27.2 9.2 %collective-permute-start.3 = (bf16[16,4,8,256]{3,0,2,1:T(8,128)(2,1)S(1)}, bf16[16,4,8,256]{3,0,2,1:T(8,128)(2,1)}, u32[]{:S(2)}, u32[]{:S(2)}) collective-permute-start(bf16[16,4,8,256]{3,0,2,1:T(8,128)(2,1)S(1)} %collective-permute-done.1), channel_id=1, source_target_pairs={{0,2},{2,4},{4,6},{6,8},{8,10},{10,12},{12,14},{14,0},{1,3},{3,5},... | collective-permute-start | bytes 786440 | tf_op jit(solution)/shard_map/ppermute | solution.py:29
  27.3 10.3 %collective-permute-start.4 = (bf16[16,4,8,256]{3,0,2,1:T(8,128)(2,1)}, bf16[16,4,8,256]{3,0,2,1:T(8,128)(2,1)}, u32[]{:S(2)}, u32[]{:S(2)}) collective-permute-start(bf16[16,4,8,256]{3,0,2,1:T(8,128)(2,1)} %collective-permute-done.2), channel_id=1, source_target_pairs={{2,0},{4,2},{6,4},{8,6},{10,8},{12,10},{14,12},{0,14},{3,1},{5,3},... | collective-permute-start | bytes 786440 | tf_op jit(solution)/shard_map/ppermute | solution.py:32
  36.3 8.4 %collective-permute-start.5 = (bf16[16,4,8,256]{3,0,2,1:T(8,128)(2,1)}, bf16[16,4,8,256]{3,0,2,1:T(8,128)(2,1)S(1)}, u32[]{:S(2)}, u32[]{:S(2)}) collective-permute-start(bf16[16,4,8,256]{3,0,2,1:T(8,128)(2,1)} %collective-permute-done.3), channel_id=1, source_target_pairs={{0,2},{2,4},{4,6},{6,8},{8,10},{10,12},{12,14},{14,0},{1,3},{3,5},... | collective-permute-start | bytes 786440 | tf_op jit(solution)/shard_map/ppermute | solution.py:29
  36.3 29.2 %collective-permute-start.10 = (f32[8,3584]{1,0:T(8,128)S(1)}, f32[8,3584]{1,0:T(8,128)}, u32[]{:S(2)}, u32[]{:S(2)}) collective-permute-start(f32[8,3584]{1,0:T(8,128)S(1)} %fusion.16), channel_id=1, source_target_pairs={{1,16},{2,17},{3,18},{4,19},{5,20},{6,21},{7,22},{8,23},{9,24},{10... | collective-permute-start | bytes 344072 | tf_op jit(solution)/shard_map/ppermute | solution.py:162
  37.6 10.5 %collective-permute-start.6 = (bf16[16,4,8,256]{3,0,2,1:T(8,128)(2,1)}, bf16[16,4,8,256]{3,0,2,1:T(8,128)(2,1)S(1)}, u32[]{:S(2)}, u32[]{:S(2)}) collective-permute-start(bf16[16,4,8,256]{3,0,2,1:T(8,128)(2,1)} %collective-permute-done.4), channel_id=1, source_target_pairs={{2,0},{4,2},{6,4},{8,6},{10,8},{12,10},{14,12},{0,14},{3,1},{5,3},... | collective-permute-start | bytes 786440 | tf_op jit(solution)/shard_map/ppermute | solution.py:32
  44.7 9.3 %collective-permute-start.7 = (bf16[16,4,8,256]{3,0,2,1:T(8,128)(2,1)S(1)}, bf16[16,4,8,256]{3,0,2,1:T(8,128)(2,1)S(1)}, u32[]{:S(2)}, u32[]{:S(2)}) collective-permute-start(bf16[16,4,8,256]{3,0,2,1:T(8,128)(2,1)S(1)} %collective-permute-done.5), channel_id=1, source_target_pairs={{0,2},{2,4},{4,6},{6,8},{8,10},{10,12},{12,14},{14,0},{1,3},{3,5},... | collective-permute-start | bytes 786440 | tf_op jit(solution)/shard_map/ppermute | solution.py:29
  47.2 9.5 %copy-start.1 = (bf16[4,8,32,1024]{3,2,1,0:T(8,128)(2,1)S(1)}, bf16[4,8,32,1024]{3,2,1,0:T(8,128)(2,1)}, u32[]{:S(2)}) copy-start(bf16[4,8,32,1024]{3,2,1,0:T(8,128)(2,1)} %param.9) | copy-start | bytes 6291460
  59.8 21.2 %all-to-all-start = ((f32[16,16,1024]{2,1,0:T(8,128)}), f32[16,16,1024]{2,1,0:T(8,128)}, u32[]{:S(2)}, u32[]{:S(2)}) async-start(f32[16,16,1024]{2,1,0:T(8,128)} %bitcast.98), calls=%async_computation | async-start | bytes 2097152 | tf_op jit(solution)/shard_map/all_to_all | solution.py:19
  82.3 2.5 %collective-permute-start.8 = (f32[8,1024]{1,0:T(8,128)S(1)}, f32[8,1024]{1,0:T(8,128)S(1)}, u32[]{:S(2)}, u32[]{:S(2)}) collective-permute-start(f32[8,1024]{1,0:T(8,128)S(1)} %get-tuple-element.10), channel_id=1, source_target_pairs={{0,16},{16,0},{32,48},{48,32},{64,80},{80,64},{96,112},{112,96},{1... | collective-permute-start | bytes 98312 | tf_op jit(solution)/shard_map/ppermute | solution.py:193
  82.5 2.3 %collective-permute-start.9 = (f32[8,1024]{1,0:T(8,128)S(1)}, f32[8,1024]{1,0:T(8,128)S(1)}, u32[]{:S(2)}, u32[]{:S(2)}) collective-permute-start(f32[8,1024]{1,0:T(8,128)S(1)} %get-tuple-element.9), channel_id=1, source_target_pairs={{1,16},{2,17},{3,18},{4,19},{5,20},{6,21},{7,22},{8,23},{9,24},{10... | collective-permute-start | bytes 98312 | tf_op jit(solution)/shard_map/ppermute | solution.py:194
  113.0 66.2 %all-to-all-start.3 = ((f32[16,2,32,256]{3,2,1,0:T(8,128)}), f32[16,2,32,256]{3,2,1,0:T(8,128)S(1)}, u32[]{:S(2)}, u32[]{:S(2)}) async-start(f32[16,2,32,256]{3,2,1,0:T(8,128)} %bitcast.99), calls=%async_computation.3 | async-start | bytes 2097152 | tf_op jit(solution)/shard_map/all_to_all | solution.py:19
  178.3 30.6 %copy-start.2 = (bf16[8,4,8,256]{3,2,1,0:T(8,128)(2,1)S(1)}, bf16[8,4,8,256]{3,2,1,0:T(8,128)(2,1)}, u32[]{:S(2)}) copy-start(bf16[8,4,8,256]{3,2,1,0:T(8,128)(2,1)} %param.8) | copy-start | bytes 393220
  179.2 8.7 %all-to-all-start.5 = ((f32[16,1,1024]{2,1,0:T(1,128)}), f32[16,1,1024]{2,1,0:T(1,128)S(1)}, u32[]{:S(2)}, u32[]{:S(2)}) async-start(f32[16,1,1024]{2,1,0:T(1,128)} %reshape.127), calls=%async_computation.5 | async-start | bytes 131072 | tf_op jit(solution)/shard_map/all_to_all | solution.py:19
  187.9 21.0 %all-to-all-start.4 = ((f32[16,2,8,256]{3,2,1,0:T(8,128)}), f32[16,2,8,256]{3,2,1,0:T(8,128)S(1)}, u32[]{:S(2)}, u32[]{:S(2)}) async-start(f32[16,2,8,256]{3,2,1,0:T(8,128)} %bitcast.95), calls=%async_computation.4 | async-start | bytes 524288 | tf_op jit(solution)/shard_map/all_to_all | solution.py:19

commit v2 on v1

v2 whole, which is shorter than its diff:
```python
import jax
import jax.numpy as jnp
from jax import lax
from jax.experimental import pallas as pl
from jax.experimental.pallas import tpu as pltpu
from jax.sharding import Mesh
from jax.sharding import PartitionSpec as P

STEPS = 4
OBLK = 8
HALO = 8
LAT = ("lat_0", "lat_1")
ALL = ("mem", "lat_0", "lat_1")

highest = lax.Precision.HIGHEST


def swapped(value, axis, dim):
    return lax.all_to_all(value, axis, split_axis=dim, concat_axis=dim, tiled=True)


def ring_blocks(block, axis):
    size = lax.axis_size(axis)
    up = [(i, (i + 1) % size) for i in range(size)]
    down = [(j, i) for i, j in up]
    blocks = {0: block}
    rising = falling = block
    for hop in range(1, size // 2 + 1):
        rising = lax.ppermute(rising, axis, up)
        blocks[(-hop) % size] = rising
        if hop < size - hop:
            falling = lax.ppermute(falling, axis, down)
            blocks[hop] = falling
    return blocks


def stencil_kernel(place_ref, own_ref, before_ref, after_ref, wind_ref, gain_ref, value_ref, adjoint_ref):
    rows, cols = wind_ref.shape[1:]
    first_row = place_ref[0]
    last_row = place_ref[1]
    state = jnp.concatenate([before_ref[...], own_ref[...], after_ref[...]], axis=0)
    row = lax.broadcasted_iota(jnp.int32, (rows, cols), 0) + first_row
    col = lax.broadcasted_iota(jnp.int32, (rows, cols), 1)
    inside = ((row >= 0) & (row < last_row)).astype(jnp.float32)
    not_first = (col > 0).astype(jnp.float32)
    not_last = (col < cols - 1).astype(jnp.float32)
    lon_wind = 0.5 * wind_ref[0]
    lat_wind = 0.5 * wind_ref[1]

    def north(x):
        return pltpu.roll(x, rows - 1, 0)

    def south(x):
        return pltpu.roll(x, 1, 0)

    def east(x):
        return pltpu.roll(x, cols - 1, 1)

    def west(x):
        return pltpu.roll(x, 1, 1)

    from_north = (0.2 - lat_wind) * inside
    from_south = (0.2 + lat_wind) * inside
    from_east = (0.2 - lon_wind) * inside * not_last
    from_west = (0.2 + lon_wind) * inside * not_first
    centre = 0.2 * inside
    forcings = []
    for step in range(STEPS):
        state = (
            centre * state
            + from_north * north(state)
            + from_south * south(state)
            + from_east * east(state)
            + from_west * west(state)
        )
        forcings.append(gain_ref[step] * (state - value_ref[step]))
    to_south = 0.2 + lat_wind
    to_north = 0.2 - lat_wind
    to_west = (0.2 + lon_wind) * not_first
    to_east = (0.2 - lon_wind) * not_last
    adjoint = None
    for step in reversed(range(STEPS)):
        pushed = forcings[step] if adjoint is None else adjoint + forcings[step]
        adjoint = inside * (
            0.2 * pushed
            + north(to_south * pushed)
            + south(to_north * pushed)
            + east(to_west * pushed)
            + west(to_east * pushed)
        )
    adjoint_ref[...] = adjoint[HALO : rows - HALO]


def body(
    coarse_weights,
    perturbations,
    lat_matrix,
    lon_matrix,
    wind_field,
    observed_cell,
    observed_value,
    observed_weight,
):
    members_here, levels, row_count, lon_total = perturbations.shape
    coarse_rows, _, _, coarse_lons = coarse_weights.shape
    col_count = wind_field.shape[2]
    peers = lax.axis_size("mem")
    rings = lax.axis_size("lat_0")
    sides = lax.axis_size("lat_1")
    bands = rings * sides
    levels_here = levels // sides
    wide_count = row_count * sides
    pairs = members_here * levels_here
    quarters = peers // levels_here
    own_rows = wide_count // quarters
    member_scale = 1.0 / jnp.sqrt(jnp.float32(members_here * peers - 1))
    lon_full = lon_matrix.astype(jnp.float32)
    quarter = lax.axis_index("mem") % quarters
    ring = lax.axis_index("lat_0")
    first = lax.axis_index("lat_1") == 0
    across = [(0, 1), (1, 0)]

    forward = []
    for m in range(peers):
        for z in range(rings):
            for x in range(sides):
                here = (m * rings + z) * sides + x
                if m % quarters < quarters - 1:
                    forward.append((here, here + bands))
                elif z < rings - 1:
                    forward.append((here, here - (quarters - 1) * bands + sides))
    backward = [(b, a) for a, b in forward]

    def halves(value, dim):
        low = lax.slice_in_dim(value, 0, levels_here, axis=dim)
        high = lax.slice_in_dim(value, levels_here, levels, axis=dim)
        return jnp.where(first, low, high), jnp.where(first, high, low)

    def in_order(mine, theirs, dim):
        return jnp.where(
            first, jnp.concatenate([mine, theirs], dim), jnp.concatenate([theirs, mine], dim)
        )

    mine, theirs = halves(coarse_weights, 2)
    lat_rows = jnp.concatenate([lat_matrix[: row_count // 2], lat_matrix[row_count // 2 :]], axis=1)

    def with_lat(value):
        value = value.reshape(coarse_rows, pairs, coarse_lons)
        return jnp.concatenate([value, lat_rows[None]], axis=0)[None]

    from_side = lax.ppermute(with_lat(theirs), "lat_1", across)
    both = in_order(with_lat(mine), from_side, 0)
    blocks = ring_blocks(both, "lat_0")

    def lat_of(block):
        rows = block[:, coarse_rows]
        rows = jnp.concatenate([rows[..., : bands * coarse_rows], rows[..., bands * coarse_rows :]], 1)
        return rows.reshape(1, wide_count, bands * coarse_rows)

    lat_ring = jnp.concatenate([lat_of(blocks[d]) for d in range(rings)], axis=0)
    lat_all = lax.dynamic_slice_in_dim(
        jnp.concatenate([lat_ring, lat_ring], axis=0), rings - ring, rings, axis=0
    )
    columns = lat_of(both)[0].reshape(wide_count, rings, sides * coarse_rows)
    columns = lax.dynamic_slice_in_dim(
        jnp.concatenate([columns, columns], axis=1), ring, rings, axis=1
    )

    mine, theirs = halves(perturbations, 1)
    members = in_order(mine, lax.ppermute(theirs, "lat_1", across), 2)

    packed = jnp.concatenate(
        [observed_cell.astype(jnp.float32), observed_value, observed_weight], axis=0
    )
    kinds, _, _, block_count = packed.shape
    lanes = 2 * col_count
    packed = jnp.transpose(packed, (1, 2, 0, 3)).reshape(levels, row_count, kinds * block_count)
    packed = jnp.pad(packed, ((0, 0), (0, 0), (0, lanes - kinds * block_count)))
    winds = jnp.transpose(wind_field, (1, 0, 2)).reshape(1, row_count, lanes)
    mine, theirs = halves(packed, 0)
    from_side = lax.ppermute(jnp.concatenate([theirs, winds], axis=0), "lat_1", across)
    packed = in_order(jnp.concatenate([mine, winds], axis=0), from_side, 1)
    packed = packed.reshape(levels_here + 1, quarters, own_rows, lanes)
    winds = jnp.broadcast_to(packed[levels_here:], (levels_here, quarters, own_rows, lanes))
    packed = jnp.stack([packed[:levels_here], winds], axis=2)
    packed = swapped(packed.reshape(peers, 2, own_rows, lanes), "mem", 0)
    winds = packed[:, 1].reshape(peers, own_rows, 2, col_count)
    winds = jnp.transpose(winds, (1, 2, 0, 3)).reshape(own_rows, 2 * lon_total)
    sights = packed[:, 0, :, : kinds * block_count].reshape(peers, own_rows, kinds, block_count)
    sights = jnp.transpose(sights, (1, 2, 0, 3)).reshape(own_rows, kinds * peers * block_count)
    local = jnp.concatenate([winds, sights], axis=1)
    before = lax.ppermute(local[-HALO:], ALL, forward)
    after = lax.ppermute(local[:HALO], ALL, backward)
    local = jnp.concatenate([before, local, after], axis=0)
    wide_rows = own_rows + 2 * HALO
    wide_wind = jnp.transpose(local[:, : 2 * lon_total].reshape(wide_rows, 2, lon_total), (1, 0, 2))
    sights = local[:, 2 * lon_total :].reshape(wide_rows, kinds, peers * block_count)
    sights = jnp.transpose(sights, (1, 0, 2))
    spread = jnp.arange(lon_total)[None, :] // OBLK == jnp.arange(lon_total // OBLK)[:, None]
    sights = jnp.einsum("krb,bf->krf", sights, spread.astype(jnp.float32), precision=highest)
    cells = sights[:STEPS]
    values = sights[STEPS : 2 * STEPS]
    offset = (jnp.arange(lon_total) % OBLK).astype(jnp.float32)
    gains = jnp.where(jnp.abs(cells - offset) < 0.5, sights[2 * STEPS :], 0.0)

    def narrowed(parts):
        chosen = jnp.concatenate([columns[:, d] for d in parts], axis=1)
        weights = jnp.concatenate(
            [blocks[d][:, :coarse_rows].reshape(-1, pairs, coarse_lons) for d in parts], axis=0
        )
        return jnp.einsum("rc,cpw->prw", chosen, weights, preferred_element_type=jnp.float32)

    narrow = narrowed(range(rings))
    localized = jnp.einsum("prw,wf->prf", narrow, lon_full, precision=highest)
    localized = localized.reshape(members_here, levels_here, wide_count, lon_total)
    partial_sum = jnp.sum(localized * members, axis=0)
    arrived = swapped(partial_sum.reshape(peers, own_rows, lon_total), "mem", 0)
    own = arrived.sum(axis=0) * member_scale

    before = lax.ppermute(own[-HALO:], ALL, forward)
    after = lax.ppermute(own[:HALO], ALL, backward)
    place = jnp.stack(
        [ring * wide_count + quarter * own_rows - HALO, jnp.int32(row_count * bands)]
    ).astype(jnp.int32)
    whole = pl.BlockSpec(memory_space=pltpu.VMEM)
    adjoint = pl.pallas_call(
        stencil_kernel,
        out_shape=jax.ShapeDtypeStruct((own_rows, lon_total), jnp.float32),
        in_specs=[pl.BlockSpec(memory_space=pltpu.SMEM)] + [whole] * 6,
        out_specs=whole,
        compiler_params=pltpu.CompilerParams(vmem_limit_bytes=32 * 1024 * 1024),
    )(place, own, before, after, wide_wind, gains, values)

    copies = jnp.broadcast_to(adjoint, (peers, own_rows, lon_total))
    adjoint_all = swapped(copies, "mem", 0).reshape(levels_here, wide_count, lon_total)
    product = members * adjoint_all[None]
    projected = jnp.einsum("mlrf,wf->mlrw", product, lon_full, precision=highest)
    by_pair = projected.reshape(rings, pairs // rings, wide_count, coarse_lons)
    by_pair = swapped(by_pair, "lat_0", 0)
    full = jnp.einsum(
        "zqrw,zrc->qcw", by_pair, lat_all.astype(jnp.float32), precision=highest
    )
    full = full.reshape(pairs // rings, bands, coarse_rows, coarse_lons)
    full = swapped(jnp.transpose(full, (1, 0, 2, 3)), LAT, 0)
    full = full.reshape(
        members_here, rings // members_here, sides, pairs // rings, coarse_rows, coarse_lons
    )
    full = jnp.transpose(full, (4, 0, 2, 1, 3, 5)).reshape(coarse_weights.shape)
    gradient = full * member_scale + coarse_weights.astype(jnp.float32)

    tiles = jnp.transpose(own.reshape(own_rows, peers, col_count), (1, 0, 2))
    tiles = swapped(tiles, "mem", 0).reshape(levels_here, sides, row_count, col_count)
    kept = jnp.where(first, tiles[:, 0], tiles[:, 1])
    sent = jnp.where(first, tiles[:, 1], tiles[:, 0])
    increment = in_order(kept, lax.ppermute(sent, "lat_1", across), 0)
    return (gradient, increment)


def solution(mesh):
    split = Mesh(mesh.devices.reshape(mesh.shape["mem"], 8, 2), ("mem", "lat_0", "lat_1"))
    placed = (
        P(LAT, "mem", None, None),
        P("mem", None, LAT, None),
        P(LAT, None),
        P(),
        P(None, LAT, "mem"),
        P(None, None, LAT, "mem"),
        P(None, None, LAT, "mem"),
        P(None, None, LAT, "mem"),
    )
    return jax.shard_map(
        body,
        mesh=split,
        in_specs=placed,
        out_specs=(P(LAT, "mem", None, None), P(None, LAT, "mem")),
        check_vma=False,
    )
```

time: 211 us -> 204 us (0.967)
  blocking collectives: 80.5 us -> 0 us
  waiting for transfers between devices: 42.8 us -> 78.2 us
  starting transfers between devices: 48 us -> 67.1 us
  local copies, waits for them, and re-layouts: 16.6 us -> 30.5 us
  other arithmetic: 8.24 us -> 13.4 us
    all_gather x1 -> x0, blocking collectives: 57.4 us -> none  [body(): lat_all = lax.all_gather(lat_matrix, LAT, axis=0, tiled=True)]
    all_to_all x5 -> x6, waiting for transfers between devices: 27.8 us -> 59.6 us  [swapped(): lax.all_to_all(value, axis, split_axis=dim, concat_axis=dim, tiled=True)]
    all_to_all x1 -> x0, blocking collectives: 23.1 us -> none  [swapped(): lax.all_to_all(value, axis, split_axis=dim, concat_axis=dim, tiled=True)]
    ppermute x4 -> x8, starting transfers between devices: 4.28 us -> 19.3 us  [the longest x1 3.39 us: body(): increment = in_order(kept, lax.ppermute(sent, 'lat_1', across), 0)]
    slice x2 -> x40, local copies, waits for them, and re-layouts: 0.04 us -> 12.3 us  [the longest x8 6.5 us: lat_of(): rows = block[:, coarse_rows]]
    ppermute x4 -> x8, waiting for transfers between devices: 0.01 us -> 4.68 us  [the longest x1 2.51 us: body(): increment = in_order(kept, lax.ppermute(sent, 'lat_1', across), 0)]
    reduce_sum x0 -> x1, other arithmetic: none -> 3.61 us  [body(): partial_sum = jnp.sum(localized * members, axis=0)]
    select_n x3 -> x8, other arithmetic: 1.06 us -> 3.5 us  [the longest x3 2.73 us: halves(): return (jnp.where(first, low, high), jnp.where(first, high, low))]
  transfers between devices with their start and end apart: 16 -> 21, of which waited for: 8 -> 9; matrix products, arithmetic and copies ran while one was open for 14% -> 24% of each run, Pallas kernels for 0% -> 0%
where the time goes in v2:
time: 204 us; the launch traced here: 203 us
  waiting for transfers between devices  78.2 us (38%)
  starting transfers between devices  67.1 us (33%)
  local copies, waits for them, and re-layouts  30.5 us (15%)
  other arithmetic  13.4 us (7%)
  matrix products  10.7 us (5%)
    all_to_all x6, waiting for transfers between devices, swapped(): lax.all_to_all(value, axis, split_axis=dim, concat_axis=dim, tiled=True)  59.6 us
    all_to_all x6, starting transfers between devices, swapped(): lax.all_to_all(value, axis, split_axis=dim, concat_axis=dim, tiled=True)  32.1 us
    ppermute x4, waiting for transfers between devices, ring_blocks(): rising = lax.ppermute(rising, axis, up)  13.9 us
    ppermute x3, starting transfers between devices, ring_blocks(): falling = lax.ppermute(falling, axis, down)  11.3 us
    unnamed x63, local copies, waits for them, and re-layouts  10.2 us
    slice x8, local copies, waits for them, and re-layouts, lat_of(): rows = block[:, coarse_rows]  6.5 us
    dot_general x1, matrix products, body(): jnp.einsum('mlrf,wf->mlrw', product, lon_full, precision=highest)  5.17 us
    ppermute x4, starting transfers between devices, ring_blocks(): rising = lax.ppermute(rising, axis, up)  4.34 us
  transfers between devices with their start and end apart: 21, of which 9 were waited for; matrix products, arithmetic and copies ran while one was open for 24% of the time, Pallas kernels for 0%

profile of v2, /device:TPU:2, one launch (start us, length us, event | category | flops | bytes accessed | tf_op | source)
XLA Modules:
  0.0 202.9 jit_solution(14047678106538819282)
XLA Ops:
  2.6 2.2 %collective-permute-start = (bf16[1,9,16,256]{3,1,2,0:T(8,128)(2,1)S(1)}, bf16[1,9,16,256]{3,1,2,0:T(8,128)(2,1)S(1)}, u32[]{:S(2)}, u32[]{:S(2)}) collective-permute-start(bf16[1,9,16,256]{3,1,2,0:T(8,128)(2,1)S(1)} %get-tuple-element.41), channel_id=1, source_target_pairs={{0,1},{1,0},{2,3},{3,2},{4,5},{5,4},{6,7},{7,6},{8,9},{9,8},{10,11... | collective-permute-start | bytes 221192 | tf_op jit(solution)/shard_map/ppermute | solution.py:151
  9.2 2.6 %broadcast_select_fusion = (bf16[4,4,32,1024]{3,2,1,0:T(8,128)(2,1)}, bf16[4,4,32,1024]{3,2,1,0:T(8,128)(2,1)S(1)}) fusion(pred[]{:T(512)S(6)} %eq.20, bf16[4,8,32,1024]{3,2,1,0:T(8,128)(2,1)} %param.9), kind=kLoop, calls=%fused_computation.8 | loop fusion | flops 1048576 | bytes 4194305 | tf_op jit(solution)/shard_map/jit(_where)/select_n | solution.py:137
  11.9 2.1 %collective-permute-start.8 = (bf16[4,4,32,1024]{3,2,1,0:T(8,128)(2,1)}, bf16[4,4,32,1024]{3,2,1,0:T(8,128)(2,1)}, u32[]{:S(2)}, u32[]{:S(2)}) collective-permute-start(bf16[4,4,32,1024]{3,2,1,0:T(8,128)(2,1)} %get-tuple-element.2), channel_id=1, source_target_pairs={{0,1},{1,0},{2,3},{3,2},{4,5},{5,4},{6,7},{7,6},{8,9},{9,8},{10,11... | collective-permute-start | bytes 3145736 | tf_op jit(solution)/shard_map/ppermute | solution.py:170
  14.3 2.0 collective-permute-start.4
  16.3 4.0 %collective-permute-start.1 = (bf16[2,9,16,256]{3,1,2,0:T(8,128)(2,1)S(1)}, bf16[2,9,16,256]{3,1,2,0:T(8,128)(2,1)}, u32[]{:S(2)}, u32[]{:S(2)}) collective-permute-start(bf16[2,9,16,256]{3,1,2,0:T(8,128)(2,1)S(1)} %maximum_select_fusion.2), channel_id=1, source_target_pairs={{2,0},{4,2},{6,4},{8,6},{10,8},{12,10},{14,12},{0,14},{3,1},{5,3},... | collective-permute-start | bytes 442376 | tf_op jit(solution)/shard_map/ppermute | solution.py:32
  24.4 5.9 %all-to-all-start.1 = ((f32[16,2,16,128]{3,2,1,0:T(8,128)}), f32[16,2,16,128]{3,2,1,0:T(8,128)S(1)}, u32[]{:S(2)}, u32[]{:S(2)}) async-start(f32[16,2,16,128]{3,2,1,0:T(8,128)} %copy.162), calls=%async_computation.1 | async-start | bytes 524288 | tf_op jit(solution)/shard_map/all_to_all | solution.py:19
  36.1 3.2 %collective-permute-start.2 = (bf16[2,9,16,256]{3,1,2,0:T(8,128)(2,1)}, bf16[2,9,16,256]{3,1,2,0:T(8,128)(2,1)}, u32[]{:S(2)}, u32[]{:S(2)}) collective-permute-start(bf16[2,9,16,256]{3,1,2,0:T(8,128)(2,1)} %collective-permute-done.1), channel_id=1, source_target_pairs={{2,0},{4,2},{6,4},{8,6},{10,8},{12,10},{14,12},{0,14},{3,1},{5,3},... | collective-permute-start | bytes 442376 | tf_op jit(solution)/shard_map/ppermute | solution.py:32
  40.0 2.4 %all-to-all-done.1 = f32[16,2,16,128]{3,2,1,0:T(8,128)S(1)} async-done(((f32[16,2,16,128]{3,2,1,0:T(8,128)}), f32[16,2,16,128]{3,2,1,0:T(8,128)S(1)}, u32[]{:S(2)}, u32[]{:S(2)}) %all-to-all-start.1) | async-done | bytes 262176 | tf_op jit(solution)/shard_map/all_to_all | solution.py:19
  43.5 2.4 %collective-permute-start.12 = (f32[8,3584]{1,0:T(8,128)S(1)}, f32[8,3584]{1,0:T(8,128)S(1)}, u32[]{:S(2)}, u32[]{:S(2)}) collective-permute-start(f32[8,3584]{1,0:T(8,128)S(1)} %get-tuple-element.8), channel_id=1, source_target_pairs={{0,16},{1,17},{2,18},{3,19},{4,20},{5,21},{6,22},{7,23},{8,24},{9,... | collective-permute-start | bytes 344072 | tf_op jit(solution)/shard_map/ppermute | solution.py:192
  45.9 3.1 %collective-permute-start.13 = (f32[8,3584]{1,0:T(8,128)S(1)}, f32[8,3584]{1,0:T(8,128)}, u32[]{:S(2)}, u32[]{:S(2)}) collective-permute-start(f32[8,3584]{1,0:T(8,128)S(1)} %get-tuple-element.9), channel_id=1, source_target_pairs={{16,0},{17,1},{18,2},{19,3},{20,4},{21,5},{22,6},{23,7},{24,8},{25... | collective-permute-start | bytes 344072 | tf_op jit(solution)/shard_map/ppermute | solution.py:193
  51.9 2.0 collective-permute-start.6
  53.9 4.0 %collective-permute-start.3 = (bf16[2,9,16,256]{3,1,2,0:T(8,128)(2,1)}, bf16[2,9,16,256]{3,1,2,0:T(8,128)(2,1)S(1)}, u32[]{:S(2)}, u32[]{:S(2)}) collective-permute-start(bf16[2,9,16,256]{3,1,2,0:T(8,128)(2,1)} %collective-permute-done.2), channel_id=1, source_target_pairs={{2,0},{4,2},{6,4},{8,6},{10,8},{12,10},{14,12},{0,14},{3,1},{5,3},... | collective-permute-start | bytes 442376 | tf_op jit(solution)/shard_map/ppermute | solution.py:32
  58.6 5.8 %collective-permute-done.6 = bf16[2,9,16,256]{3,1,2,0:T(8,128)(2,1)S(1)} collective-permute-done((bf16[2,9,16,256]{3,1,2,0:T(8,128)(2,1)}, bf16[2,9,16,256]{3,1,2,0:T(8,128)(2,1)S(1)}, u32[]{:S(2)}, u32[]{:S(2)}) %collective-permute-start.6) | collective-permute-done | bytes 147488 | tf_op jit(solution)/shard_map/ppermute | solution.py:29
  66.2 8.1 %collective-permute-done.7 = bf16[2,9,16,256]{3,1,2,0:T(8,128)(2,1)S(1)} collective-permute-done((bf16[2,9,16,256]{3,1,2,0:T(8,128)(2,1)S(1)}, bf16[2,9,16,256]{3,1,2,0:T(8,128)(2,1)S(1)}, u32[]{:S(2)}, u32[]{:S(2)}) %collective-permute-start.7) | collective-permute-done | bytes 147488 | tf_op jit(solution)/shard_map/ppermute | solution.py:29
  78.8 1.9 fusion.6
  80.7 3.6 %fusion = f32[4,64,1024]{2,1,0:T(8,128)} fusion(f32[4,4,64,1024]{3,2,1,0:T(8,128)S(1)} %bitcast.190, bf16[4,4,32,1024]{3,2,1,0:T(8,128)(2,1)S(1)} %get-tuple-element.3, bf16[4,4,32,1024]{3,2,1,0:T(8,128)(2,1)} %collective-permute-done.8, pred[]{:T(512)S(6)} %eq.20), kind=kLoop, calls=%fused_computation.2 | loop fusion | flops 12320768 | bytes 7340033 | tf_op jit(solution)/shard_map/reduce_sum | solution.py:216
  84.3 4.9 %all-to-all-start = ((f32[16,16,1024]{2,1,0:T(8,128)}), f32[16,16,1024]{2,1,0:T(8,128)S(1)}, u32[]{:S(2)}, u32[]{:S(2)}) async-start(f32[16,16,1024]{2,1,0:T(8,128)} %bitcast.35), calls=%async_computation | async-start | bytes 2097152 | tf_op jit(solution)/shard_map/all_to_all | solution.py:19
  91.7 1.7 pad_maximum_fusion
  93.5 11.1 %all-to-all-done = f32[16,16,1024]{2,1,0:T(8,128)S(1)} async-done(((f32[16,16,1024]{2,1,0:T(8,128)}), f32[16,16,1024]{2,1,0:T(8,128)S(1)}, u32[]{:S(2)}, u32[]{:S(2)}) %all-to-all-start) | async-done | bytes 1048608 | tf_op jit(solution)/shard_map/all_to_all | solution.py:19
  104.6 2.5 %collective-permute-start.10 = (f32[8,1024]{1,0:T(8,128)S(1)}, f32[8,1024]{1,0:T(8,128)S(1)}, u32[]{:S(2)}, u32[]{:S(2)}) collective-permute-start(f32[8,1024]{1,0:T(8,128)S(1)} %get-tuple-element.14), channel_id=1, source_target_pairs={{16,0},{17,1},{18,2},{19,3},{20,4},{21,5},{22,6},{23,7},{24,8},{25... | collective-permute-start | bytes 98312 | tf_op jit(solution)/shard_map/ppermute | solution.py:221
  107.1 2.1 %collective-permute-start.9 = (f32[8,1024]{1,0:T(8,128)S(1)}, f32[8,1024]{1,0:T(8,128)S(1)}, u32[]{:S(2)}, u32[]{:S(2)}) collective-permute-start(f32[8,1024]{1,0:T(8,128)S(1)} %get-tuple-element.15), channel_id=1, source_target_pairs={{0,16},{1,17},{2,18},{3,19},{4,20},{5,21},{6,22},{7,23},{8,24},{9,... | collective-permute-start | bytes 98312 | tf_op jit(solution)/shard_map/ppermute | solution.py:220
  110.3 2.2 %collective-permute-done.9.before_ref = f32[8,1024]{1,0:T(8,128)S(1)} collective-permute-done((f32[8,1024]{1,0:T(8,128)S(1)}, f32[8,1024]{1,0:T(8,128)S(1)}, u32[]{:S(2)}, u32[]{:S(2)}) %collective-permute-start.9) | collective-permute-done | bytes 32800 | tf_op jit(solution)/shard_map/ppermute | solution.py:220
  115.2 3.7 %all-to-all-start.2 = ((f32[16,16,1024]{2,1,0:T(8,128)}), f32[16,16,1024]{2,1,0:T(8,128)S(1)}, u32[]{:S(2)}, u32[]{:S(2)}) async-start(f32[16,16,1024]{2,1,0:T(8,128)} %broadcast_in_dim.24), calls=%async_computation.2 | async-start | bytes 2097152 | tf_op jit(solution)/shard_map/all_to_all | solution.py:19
  122.3 11.9 %all-to-all-done.2 = f32[16,16,1024]{2,1,0:T(8,128)S(1)} async-done(((f32[16,16,1024]{2,1,0:T(8,128)}), f32[16,16,1024]{2,1,0:T(8,128)S(1)}, u32[]{:S(2)}, u32[]{:S(2)}) %all-to-all-start.2) | async-done | bytes 1048608 | tf_op jit(solution)/shard_map/all_to_all | solution.py:19
  134.2 4.6 %all-to-all-start.5 = ((f32[16,1,1024]{2,1,0:T(1,128)}), f32[16,1,1024]{2,1,0:T(1,128)S(1)}, u32[]{:S(2)}, u32[]{:S(2)}) async-start(f32[16,1,1024]{2,1,0:T(1,128)} %reshape.204), calls=%async_computation.5 | async-start | bytes 131072 | tf_op jit(solution)/shard_map/all_to_all | solution.py:19
  138.9 5.2 %fusion.1 = f32[4,4,64,256]{3,2,1,0:T(8,128)} fusion(f32[4,64,1024]{2,1,0:T(8,128)S(1)} %bitcast.195, bf16[256,1024]{1,0:T(8,128)(2,1)S(1)} %copy-done, bf16[4,4,32,1024]{3,2,1,0:T(8,128)(2,1)} %collective-permute-done.8, bf16[4,4,32,1024]{3,2,1,0:T(8,128)(2,1)S(1)} %copy-done.2, pred[]{:T(512)S(6)} %eq.20), kind=kOutput, calls=%fused_computation.3 | convolution fusion | flops 3232759808 | bytes 4718593 | tf_op jit(solution)/shard_map/mlrf,wf->mlrw/dot_general | solution.py:237
  144.1 9.4 %all-to-all-start.3 = ((f32[8,2,64,256]{3,2,1,0:T(8,128)}), f32[8,2,64,256]{3,2,1,0:T(8,128)S(1)}, u32[]{:S(2)}, u32[]{:S(2)}) async-start(f32[8,2,64,256]{3,2,1,0:T(8,128)} %bitcast.52), calls=%async_computation.3 | async-start | bytes 2097152 | tf_op jit(solution)/shard_map/all_to_all | solution.py:19
  156.1 26.5 %all-to-all-done.3 = f32[8,2,64,256]{3,2,1,0:T(8,128)S(1)} async-done(((f32[8,2,64,256]{3,2,1,0:T(8,128)}), f32[8,2,64,256]{3,2,1,0:T(8,128)S(1)}, u32[]{:S(2)}, u32[]{:S(2)}) %all-to-all-start.3) | async-done | bytes 1048608 | tf_op jit(solution)/shard_map/all_to_all | solution.py:19
  183.9 3.5 %all-to-all-start.4 = ((f32[16,2,8,256]{3,2,1,0:T(8,128)}), f32[16,2,8,256]{3,2,1,0:T(8,128)S(1)}, u32[]{:S(2)}, u32[]{:S(2)}) async-start(f32[16,2,8,256]{3,2,1,0:T(8,128)} %bitcast.162), calls=%async_computation.4 | async-start | bytes 524288 | tf_op jit(solution)/shard_map/all_to_all | solution.py:19
  187.4 3.4 %collective-permute-start.14 = (f32[4,32,64]{2,1,0:T(8,128)S(1)}, f32[4,32,64]{2,1,0:T(8,128)S(1)}, u32[]{:S(2)}, u32[]{:S(2)}) collective-permute-start(f32[4,32,64]{2,1,0:T(8,128)S(1)} %select_bitcast_fusion), channel_id=1, source_target_pairs={{0,1},{1,0},{2,3},{3,2},{4,5},{5,4},{6,7},{7,6},{8,9},{9,8},{10,11... | collective-permute-start | bytes 98312 | tf_op jit(solution)/shard_map/ppermute | solution.py:255
  190.8 2.5 %collective-permute-done.14 = f32[4,32,64]{2,1,0:T(8,128)S(1)} collective-permute-done((f32[4,32,64]{2,1,0:T(8,128)S(1)}, f32[4,32,64]{2,1,0:T(8,128)S(1)}, u32[]{:S(2)}, u32[]{:S(2)}) %collective-permute-start.14) | collective-permute-done | bytes 32800 | tf_op jit(solution)/shard_map/ppermute | solution.py:255
  194.0 7.8 %all-to-all-done.4 = f32[16,2,8,256]{3,2,1,0:T(8,128)S(1)} async-done(((f32[16,2,8,256]{3,2,1,0:T(8,128)}), f32[16,2,8,256]{3,2,1,0:T(8,128)S(1)}, u32[]{:S(2)}, u32[]{:S(2)}) %all-to-all-start.4) | async-done | bytes 262176 | tf_op jit(solution)/shard_map/all_to_all | solution.py:19
  (180 shorter events, 43.0 us)
Async XLA Ops:
  0.6 78.1 %copy-start = (bf16[256,1024]{1,0:T(8,128)(2,1)S(1)}, bf16[256,1024]{1,0:T(8,128)(2,1)}, u32[]{:S(2)}) copy-start(bf16[256,1024]{1,0:T(8,128)(2,1)} %param.11) | copy-start | bytes 1572868
  2.6 11.6 %collective-permute-start = (bf16[1,9,16,256]{3,1,2,0:T(8,128)(2,1)S(1)}, bf16[1,9,16,256]{3,1,2,0:T(8,128)(2,1)S(1)}, u32[]{:S(2)}, u32[]{:S(2)}) collective-permute-start(bf16[1,9,16,256]{3,1,2,0:T(8,128)(2,1)S(1)} %get-tuple-element.41), channel_id=1, source_target_pairs={{0,1},{1,0},{2,3},{3,2},{4,5},{5,4},{6,7},{7,6},{8,9},{9,8},{10,11... | collective-permute-start | bytes 221192 | tf_op jit(solution)/shard_map/ppermute | solution.py:151
  7.7 15.8 %collective-permute-start.11 = (f32[5,32,128]{2,1,0:T(8,128)S(1)}, f32[5,32,128]{2,1,0:T(8,128)S(1)}, u32[]{:S(2)}, u32[]{:S(2)}) collective-permute-start(f32[5,32,128]{2,1,0:T(8,128)S(1)} %pad_maximum_fusion.5), channel_id=1, source_target_pairs={{0,1},{1,0},{2,3},{3,2},{4,5},{5,4},{6,7},{7,6},{8,9},{9,8},{10,11... | collective-permute-start | bytes 245768 | tf_op jit(solution)/shard_map/ppermute | solution.py:181
  11.9 68.8 %copy-start.1 = (bf16[4,4,32,1024]{3,2,1,0:T(8,128)(2,1)}, bf16[4,4,32,1024]{3,2,1,0:T(8,128)(2,1)S(1)}, u32[]{:S(2)}) copy-start(bf16[4,4,32,1024]{3,2,1,0:T(8,128)(2,1)S(1)} %get-tuple-element.3) | copy-start | bytes 3145732
  11.9 68.8 %collective-permute-start.8 = (bf16[4,4,32,1024]{3,2,1,0:T(8,128)(2,1)}, bf16[4,4,32,1024]{3,2,1,0:T(8,128)(2,1)}, u32[]{:S(2)}, u32[]{:S(2)}) collective-permute-start(bf16[4,4,32,1024]{3,2,1,0:T(8,128)(2,1)} %get-tuple-element.2), channel_id=1, source_target_pairs={{0,1},{1,0},{2,3},{3,2},{4,5},{5,4},{6,7},{7,6},{8,9},{9,8},{10,11... | collective-permute-start | bytes 3145736 | tf_op jit(solution)/shard_map/ppermute | solution.py:170
  14.3 16.0 %collective-permute-start.4 = (bf16[2,9,16,256]{3,1,2,0:T(8,128)(2,1)S(1)}, bf16[2,9,16,256]{3,1,2,0:T(8,128)(2,1)}, u32[]{:S(2)}, u32[]{:S(2)}) collective-permute-start(bf16[2,9,16,256]{3,1,2,0:T(8,128)(2,1)S(1)} %maximum_select_fusion.2), channel_id=1, source_target_pairs={{0,2},{2,4},{4,6},{6,8},{8,10},{10,12},{12,14},{14,0},{1,3},{3,5},... | collective-permute-start | bytes 442376 | tf_op jit(solution)/shard_map/ppermute | solution.py:29
  16.3 15.0 %collective-permute-start.1 = (bf16[2,9,16,256]{3,1,2,0:T(8,128)(2,1)S(1)}, bf16[2,9,16,256]{3,1,2,0:T(8,128)(2,1)}, u32[]{:S(2)}, u32[]{:S(2)}) collective-permute-start(bf16[2,9,16,256]{3,1,2,0:T(8,128)(2,1)S(1)} %maximum_select_fusion.2), channel_id=1, source_target_pairs={{2,0},{4,2},{6,4},{8,6},{10,8},{12,10},{14,12},{0,14},{3,1},{5,3},... | collective-permute-start | bytes 442376 | tf_op jit(solution)/shard_map/ppermute | solution.py:32
  24.4 18.0 %all-to-all-start.1 = ((f32[16,2,16,128]{3,2,1,0:T(8,128)}), f32[16,2,16,128]{3,2,1,0:T(8,128)S(1)}, u32[]{:S(2)}, u32[]{:S(2)}) async-start(f32[16,2,16,128]{3,2,1,0:T(8,128)} %copy.162), calls=%async_computation.1 | async-start | bytes 524288 | tf_op jit(solution)/shard_map/all_to_all | solution.py:19
  32.9 0.6 copy-start.5
  36.0 13.1 %collective-permute-start.5 = (bf16[2,9,16,256]{3,1,2,0:T(8,128)(2,1)}, bf16[2,9,16,256]{3,1,2,0:T(8,128)(2,1)}, u32[]{:S(2)}, u32[]{:S(2)}) collective-permute-start(bf16[2,9,16,256]{3,1,2,0:T(8,128)(2,1)} %collective-permute-done.4), channel_id=1, source_target_pairs={{0,2},{2,4},{4,6},{6,8},{8,10},{10,12},{12,14},{14,0},{1,3},{3,5},... | collective-permute-start | bytes 442376 | tf_op jit(solution)/shard_map/ppermute | solution.py:29
  36.1 14.9 %collective-permute-start.2 = (bf16[2,9,16,256]{3,1,2,0:T(8,128)(2,1)}, bf16[2,9,16,256]{3,1,2,0:T(8,128)(2,1)}, u32[]{:S(2)}, u32[]{:S(2)}) collective-permute-start(bf16[2,9,16,256]{3,1,2,0:T(8,128)(2,1)} %collective-permute-done.1), channel_id=1, source_target_pairs={{2,0},{4,2},{6,4},{8,6},{10,8},{12,10},{14,12},{0,14},{3,1},{5,3},... | collective-permute-start | bytes 442376 | tf_op jit(solution)/shard_map/ppermute | solution.py:32
  43.5 46.6 %collective-permute-start.12 = (f32[8,3584]{1,0:T(8,128)S(1)}, f32[8,3584]{1,0:T(8,128)S(1)}, u32[]{:S(2)}, u32[]{:S(2)}) collective-permute-start(f32[8,3584]{1,0:T(8,128)S(1)} %get-tuple-element.8), channel_id=1, source_target_pairs={{0,16},{1,17},{2,18},{3,19},{4,20},{5,21},{6,22},{7,23},{8,24},{9,... | collective-permute-start | bytes 344072 | tf_op jit(solution)/shard_map/ppermute | solution.py:192
  45.9 44.2 %collective-permute-start.13 = (f32[8,3584]{1,0:T(8,128)S(1)}, f32[8,3584]{1,0:T(8,128)}, u32[]{:S(2)}, u32[]{:S(2)}) collective-permute-start(f32[8,3584]{1,0:T(8,128)S(1)} %get-tuple-element.9), channel_id=1, source_target_pairs={{16,0},{17,1},{18,2},{19,3},{20,4},{21,5},{22,6},{23,7},{24,8},{25... | collective-permute-start | bytes 344072 | tf_op jit(solution)/shard_map/ppermute | solution.py:193
  51.9 12.5 %collective-permute-start.6 = (bf16[2,9,16,256]{3,1,2,0:T(8,128)(2,1)}, bf16[2,9,16,256]{3,1,2,0:T(8,128)(2,1)S(1)}, u32[]{:S(2)}, u32[]{:S(2)}) collective-permute-start(bf16[2,9,16,256]{3,1,2,0:T(8,128)(2,1)} %collective-permute-done.5), channel_id=1, source_target_pairs={{0,2},{2,4},{4,6},{6,8},{8,10},{10,12},{12,14},{14,0},{1,3},{3,5},... | collective-permute-start | bytes 442376 | tf_op jit(solution)/shard_map/ppermute | solution.py:29
  53.9 10.6 %collective-permute-start.3 = (bf16[2,9,16,256]{3,1,2,0:T(8,128)(2,1)}, bf16[2,9,16,256]{3,1,2,0:T(8,128)(2,1)S(1)}, u32[]{:S(2)}, u32[]{:S(2)}) collective-permute-start(bf16[2,9,16,256]{3,1,2,0:T(8,128)(2,1)} %collective-permute-done.2), channel_id=1, source_target_pairs={{2,0},{4,2},{6,4},{8,6},{10,8},{12,10},{14,12},{0,14},{3,1},{5,3},... | collective-permute-start | bytes 442376 | tf_op jit(solution)/shard_map/ppermute | solution.py:32
  64.4 16.2 %copy-start.8 = (bf16[2,9,16,256]{3,1,2,0:T(8,128)(2,1)}, bf16[2,9,16,256]{3,1,2,0:T(8,128)(2,1)S(1)}, u32[]{:S(2)}) copy-start(bf16[2,9,16,256]{3,1,2,0:T(8,128)(2,1)S(1)} %collective-permute-done.6) | copy-start | bytes 442372
  64.5 0.7 copy-start.9
  65.3 9.0 %collective-permute-start.7 = (bf16[2,9,16,256]{3,1,2,0:T(8,128)(2,1)S(1)}, bf16[2,9,16,256]{3,1,2,0:T(8,128)(2,1)S(1)}, u32[]{:S(2)}, u32[]{:S(2)}) collective-permute-start(bf16[2,9,16,256]{3,1,2,0:T(8,128)(2,1)S(1)} %collective-permute-done.6), channel_id=1, source_target_pairs={{0,2},{2,4},{4,6},{6,8},{8,10},{10,12},{12,14},{14,0},{1,3},{3,5},... | collective-permute-start | bytes 442376 | tf_op jit(solution)/shard_map/ppermute | solution.py:29
  74.3 6.3 %copy-start.7 = (bf16[2,9,16,256]{3,1,2,0:T(8,128)(2,1)}, bf16[2,9,16,256]{3,1,2,0:T(8,128)(2,1)S(1)}, u32[]{:S(2)}) copy-start(bf16[2,9,16,256]{3,1,2,0:T(8,128)(2,1)S(1)} %collective-permute-done.7) | copy-start | bytes 442372
  84.3 20.2 %all-to-all-start = ((f32[16,16,1024]{2,1,0:T(8,128)}), f32[16,16,1024]{2,1,0:T(8,128)S(1)}, u32[]{:S(2)}, u32[]{:S(2)}) async-start(f32[16,16,1024]{2,1,0:T(8,128)} %bitcast.35), calls=%async_computation | async-start | bytes 2097152 | tf_op jit(solution)/shard_map/all_to_all | solution.py:19
  104.6 5.7 %collective-permute-start.10 = (f32[8,1024]{1,0:T(8,128)S(1)}, f32[8,1024]{1,0:T(8,128)S(1)}, u32[]{:S(2)}, u32[]{:S(2)}) collective-permute-start(f32[8,1024]{1,0:T(8,128)S(1)} %get-tuple-element.14), channel_id=1, source_target_pairs={{16,0},{17,1},{18,2},{19,3},{20,4},{21,5},{22,6},{23,7},{24,8},{25... | collective-permute-start | bytes 98312 | tf_op jit(solution)/shard_map/ppermute | solution.py:221
  107.1 31.8 %copy-start.2 = (bf16[4,4,32,1024]{3,2,1,0:T(8,128)(2,1)S(1)}, bf16[4,4,32,1024]{3,2,1,0:T(8,128)(2,1)}, u32[]{:S(2)}) copy-start(bf16[4,4,32,1024]{3,2,1,0:T(8,128)(2,1)} %copy-done.1) | copy-start | bytes 3145732
  107.1 5.4 %collective-permute-start.9 = (f32[8,1024]{1,0:T(8,128)S(1)}, f32[8,1024]{1,0:T(8,128)S(1)}, u32[]{:S(2)}, u32[]{:S(2)}) collective-permute-start(f32[8,1024]{1,0:T(8,128)S(1)} %get-tuple-element.15), channel_id=1, source_target_pairs={{0,16},{1,17},{2,18},{3,19},{4,20},{5,21},{6,22},{7,23},{8,24},{9,... | collective-permute-start | bytes 98312 | tf_op jit(solution)/shard_map/ppermute | solution.py:220
  115.2 19.1 %all-to-all-start.2 = ((f32[16,16,1024]{2,1,0:T(8,128)}), f32[16,16,1024]{2,1,0:T(8,128)S(1)}, u32[]{:S(2)}, u32[]{:S(2)}) async-start(f32[16,16,1024]{2,1,0:T(8,128)} %broadcast_in_dim.24), calls=%async_computation.2 | async-start | bytes 2097152 | tf_op jit(solution)/shard_map/all_to_all | solution.py:19
  134.2 9.9 %all-to-all-start.5 = ((f32[16,1,1024]{2,1,0:T(1,128)}), f32[16,1,1024]{2,1,0:T(1,128)S(1)}, u32[]{:S(2)}, u32[]{:S(2)}) async-start(f32[16,1,1024]{2,1,0:T(1,128)} %reshape.204), calls=%async_computation.5 | async-start | bytes 131072 | tf_op jit(solution)/shard_map/all_to_all | solution.py:19
  138.9 14.6 %copy-start.10 = (bf16[16,64,128]{2,1,0:T(8,128)(2,1)S(1)}, bf16[16,64,128]{2,1,0:T(8,128)(2,1)}, u32[]{:S(2)}) copy-start(bf16[16,64,128]{2,1,0:T(8,128)(2,1)} %constant_dynamic-update-slice_fusion.13) | copy-start | bytes 786436
  138.9 15.6 %copy-start.4 = (bf16[2,32,128]{2,1,0:T(8,128)(2,1)S(1)}, bf16[2,32,128]{2,1,0:T(8,128)(2,1)}, u32[]{:S(2)}) copy-start(bf16[2,32,128]{2,1,0:T(8,128)(2,1)} %pad_maximum_fusion.13) | copy-start | bytes 49156
  138.9 15.7 %copy-start.6 = (bf16[2,32,128]{2,1,0:T(8,128)(2,1)S(1)}, bf16[2,32,128]{2,1,0:T(8,128)(2,1)}, u32[]{:S(2)}) copy-start(bf16[2,32,128]{2,1,0:T(8,128)(2,1)} %copy-done.5) | copy-start | bytes 49156
  144.1 58.1 %copy-start.3 = (bf16[8,4,8,256]{3,2,1,0:T(8,128)(2,1)S(1)}, bf16[8,4,8,256]{3,2,1,0:T(8,128)(2,1)}, u32[]{:S(2)}) copy-start(bf16[8,4,8,256]{3,2,1,0:T(8,128)(2,1)} %param.8) | copy-start | bytes 393220
  144.1 38.5 %all-to-all-start.3 = ((f32[8,2,64,256]{3,2,1,0:T(8,128)}), f32[8,2,64,256]{3,2,1,0:T(8,128)S(1)}, u32[]{:S(2)}, u32[]{:S(2)}) async-start(f32[8,2,64,256]{3,2,1,0:T(8,128)} %bitcast.52), calls=%async_computation.3 | async-start | bytes 2097152 | tf_op jit(solution)/shard_map/all_to_all | solution.py:19
  183.9 17.9 %all-to-all-start.4 = ((f32[16,2,8,256]{3,2,1,0:T(8,128)}), f32[16,2,8,256]{3,2,1,0:T(8,128)S(1)}, u32[]{:S(2)}, u32[]{:S(2)}) async-start(f32[16,2,8,256]{3,2,1,0:T(8,128)} %bitcast.162), calls=%async_computation.4 | async-start | bytes 524288 | tf_op jit(solution)/shard_map/all_to_all | solution.py:19
  187.4 5.9 %collective-permute-start.14 = (f32[4,32,64]{2,1,0:T(8,128)S(1)}, f32[4,32,64]{2,1,0:T(8,128)S(1)}, u32[]{:S(2)}, u32[]{:S(2)}) collective-permute-start(f32[4,32,64]{2,1,0:T(8,128)S(1)} %select_bitcast_fusion), channel_id=1, source_target_pairs={{0,1},{1,0},{2,3},{3,2},{4,5},{5,4},{6,7},{7,6},{8,9},{9,8},{10,11... | collective-permute-start | bytes 98312 | tf_op jit(solution)/shard_map/ppermute | solution.py:255

commit v3 on v2

--- a/solution.py
+++ b/solution.py
@@ -19,19 +19,67 @@
     return lax.all_to_all(value, axis, split_axis=dim, concat_axis=dim, tiled=True)
 
 
-def ring_blocks(block, axis):
-    size = lax.axis_size(axis)
-    up = [(i, (i + 1) % size) for i in range(size)]
-    down = [(j, i) for i, j in up]
-    blocks = {0: block}
-    rising = falling = block
-    for hop in range(1, size // 2 + 1):
-        rising = lax.ppermute(rising, axis, up)
-        blocks[(-hop) % size] = rising
-        if hop < size - hop:
-            falling = lax.ppermute(falling, axis, down)
-            blocks[hop] = falling
-    return blocks
+def two_terms(value):
+    high = value.astype(jnp.bfloat16)
+    low = (value - high.astype(jnp.float32)).astype(jnp.bfloat16)
+    return jnp.concatenate([high, low], axis=0)
+
+
+def dot(a, b):
+    return jnp.dot(a, b, preferred_element_type=jnp.float32)
+
+
+def member_rows(side, own_ref, other_ref, member, level):
+    levels_here = other_ref.shape[1]
+    own = own_ref[member, side * levels_here + level].astype(jnp.float32)
+    other = other_ref[member, level].astype(jnp.float32)
+    low = jnp.where(side == 0, own, other)
+    high = jnp.where(side == 0, other, own)
+    return jnp.concatenate([low, high], axis=0)
+
+
+def localize_kernel(side_ref, columns_ref, lon_ref, own_ref, other_ref, *refs):
+    block_refs, sum_ref = refs[:-1], refs[-1]
+    members, levels_here, row_count, lon_total = other_ref.shape
+    tall = 2 * row_count
+    side = side_ref[0]
+    per_block = columns_ref.shape[1] // len(block_refs)
+    columns = columns_ref[...]
+    lon = lon_ref[...]
+    for level in range(levels_here):
+        narrow = []
+        for member in range(members):
+            start = (member * levels_here + level) * per_block
+            weights = jnp.concatenate([ref[start : start + per_block] for ref in block_refs], axis=0)
+            narrow.append(dot(columns, weights))
+        localized = dot(two_terms(jnp.concatenate(narrow, axis=0)), lon)
+        total = None
+        for member in range(members):
+            at = member * tall
+            term = localized[at : at + tall] + localized[at + members * tall : at + (members + 1) * tall]
+            term = term * member_rows(side, own_ref, other_ref, member, level)
+            total = term if total is None else total + term
+        count = sum_ref.shape[0] // levels_here
+        sum_ref[level * count : (level + 1) * count] = total.reshape(count, tall // count, lon_total)
+
+
+def project_kernel(side_ref, adjoint_ref, lon_ref, own_ref, other_ref, out_ref):
+    members, levels_here, row_count, lon_total = other_ref.shape
+    tall = 2 * row_count
+    side = side_ref[0]
+    lon = lon_ref[...]
+    count = adjoint_ref.shape[0] // levels_here
+    for level in range(levels_here):
+        adjoint = adjoint_ref[level * count : (level + 1) * count].reshape(tall, lon_total)
+        product = [
+            member_rows(side, own_ref, other_ref, member, level) * adjoint for member in range(members)
+        ]
+        projected = dot(two_terms(jnp.concatenate(product, axis=0)), lon)
+        for member in range(members):
+            at = member * tall
+            out_ref[member * levels_here + level] = (
+                projected[at : at + tall] + projected[at + members * tall : at + (members + 1) * tall]
+            )
 
 
 def stencil_kernel(place_ref, own_ref, before_ref, after_ref, wind_ref, gain_ref, value_ref, adjoint_ref):
@@ -88,7 +136,9 @@
             + east(to_west * pushed)
             + west(to_east * pushed)
         )
-    adjoint_ref[...] = adjoint[HALO : rows - HALO]
+    adjoint = adjoint[HALO : rows - HALO]
+    for copy in range(adjoint_ref.shape[0]):
+        adjoint_ref[copy] = adjoint
 
 
 def body(
@@ -114,7 +164,6 @@
     quarters = peers // levels_here
     own_rows = wide_count // quarters
     member_scale = 1.0 / jnp.sqrt(jnp.float32(members_here * peers - 1))
-    lon_full = lon_matrix.astype(jnp.float32)
     quarter = lax.axis_index("mem") % quarters
     ring = lax.axis_index("lat_0")
     first = lax.axis_index("lat_1") == 0
@@ -141,33 +190,21 @@
             first, jnp.concatenate([mine, theirs], dim), jnp.concatenate([theirs, mine], dim)
         )
 
+    weight_rows = pairs * coarse_rows
+    coarse_total = bands * coarse_rows
     mine, theirs = halves(coarse_weights, 2)
     lat_rows = jnp.concatenate([lat_matrix[: row_count // 2], lat_matrix[row_count // 2 :]], axis=1)
 
-    def with_lat(value):
+    def by_pair_first(value):
         value = value.reshape(coarse_rows, pairs, coarse_lons)
-        return jnp.concatenate([value, lat_rows[None]], axis=0)[None]
-
-    from_side = lax.ppermute(with_lat(theirs), "lat_1", across)
-    both = in_order(with_lat(mine), from_side, 0)
-    blocks = ring_blocks(both, "lat_0")
-
-    def lat_of(block):
-        rows = block[:, coarse_rows]
-        rows = jnp.concatenate([rows[..., : bands * coarse_rows], rows[..., bands * coarse_rows :]], 1)
-        return rows.reshape(1, wide_count, bands * coarse_rows)
-
-    lat_ring = jnp.concatenate([lat_of(blocks[d]) for d in range(rings)], axis=0)
-    lat_all = lax.dynamic_slice_in_dim(
-        jnp.concatenate([lat_ring, lat_ring], axis=0), rings - ring, rings, axis=0
-    )
-    columns = lat_of(both)[0].reshape(wide_count, rings, sides * coarse_rows)
-    columns = lax.dynamic_slice_in_dim(
-        jnp.concatenate([columns, columns], axis=1), ring, rings, axis=1
-    )
-
-    mine, theirs = halves(perturbations, 1)
-    members = in_order(mine, lax.ppermute(theirs, "lat_1", across), 2)
+        return jnp.transpose(value, (1, 0, 2))
+
+    theirs = by_pair_first(theirs).reshape(weight_rows, coarse_lons)
+    from_side = lax.ppermute(jnp.concatenate([theirs, lat_rows], axis=0), "lat_1", across)
+    both = in_order(
+        by_pair_first(mine), from_side[:weight_rows].reshape(pairs, coarse_rows, coarse_lons), 1
+    ).reshape(sides * weight_rows, coarse_lons)
+    both = jnp.concatenate([both, in_order(lat_rows, from_side[weight_rows:], 0)], axis=0)
 
     packed = jnp.concatenate(
         [observed_cell.astype(jnp.float32), observed_value, observed_weight], axis=0
@@ -177,13 +214,54 @@
     packed = jnp.transpose(packed, (1, 2, 0, 3)).reshape(levels, row_count, kinds * block_count)
     packed = jnp.pad(packed, ((0, 0), (0, 0), (0, lanes - kinds * block_count)))
     winds = jnp.transpose(wind_field, (1, 0, 2)).reshape(1, row_count, lanes)
-    mine, theirs = halves(packed, 0)
-    from_side = lax.ppermute(jnp.concatenate([theirs, winds], axis=0), "lat_1", across)
-    packed = in_order(jnp.concatenate([mine, winds], axis=0), from_side, 1)
-    packed = packed.reshape(levels_here + 1, quarters, own_rows, lanes)
-    winds = jnp.broadcast_to(packed[levels_here:], (levels_here, quarters, own_rows, lanes))
-    packed = jnp.stack([packed[:levels_here], winds], axis=2)
-    packed = swapped(packed.reshape(peers, 2, own_rows, lanes), "mem", 0)
+    mine_seen, theirs_seen = halves(packed, 0)
+    mine_seen = jnp.concatenate([mine_seen, winds], axis=0)
+    theirs_seen = lax.ppermute(jnp.concatenate([theirs_seen, winds], axis=0), "lat_1", across)
+
+    side = lax.axis_index("lat_1")
+    up = [(i, (i + 1) % rings) for i in range(rings)]
+    down = [(b, a) for a, b in up]
+    blocks = {0: both}
+    rising = falling = both
+    for hop in range(1, rings // 2 + 1):
+        rising = lax.ppermute(rising, "lat_0", up)
+        if hop < rings - hop:
+            falling = lax.ppermute(falling, "lat_0", down)
+        if hop == 1:
+            rising, falling, perturbed = lax.optimization_barrier((rising, falling, perturbations))
+            other_members = lax.dynamic_slice_in_dim(
+                perturbed, (1 - side) * levels_here, levels_here, axis=1
+            )
+            other_members = lax.ppermute(other_members, "lat_1", across)
+        if hop == 2:
+            rising, falling, mine_seen, theirs_seen = lax.optimization_barrier(
+                (rising, falling, mine_seen, theirs_seen)
+            )
+            packed = in_order(mine_seen, theirs_seen, 1)
+            packed = packed.reshape(levels_here + 1, quarters, own_rows, lanes)
+            winds = jnp.broadcast_to(packed[levels_here:], (levels_here, quarters, own_rows, lanes))
+            packed = jnp.stack([packed[:levels_here], winds], axis=2)
+            packed = swapped(packed.reshape(peers, 2, own_rows, lanes), "mem", 0)
+        blocks[-hop % rings] = rising
+        if hop < rings - hop:
+            blocks[hop] = falling
+    last, packed = lax.optimization_barrier((blocks[rings // 2], packed))
+    blocks[rings // 2] = last
+
+    def lat_of(block):
+        rows = block[sides * weight_rows :].reshape(sides, row_count // 2, coarse_lons)
+        rows = jnp.concatenate([rows[..., :coarse_total], rows[..., coarse_total:]], 1)
+        return rows.reshape(1, wide_count, coarse_total)
+
+    lat_ring = jnp.concatenate([lat_of(blocks[d]) for d in range(rings)], axis=0)
+    lat_all = lax.dynamic_slice_in_dim(
+        jnp.concatenate([lat_ring, lat_ring], axis=0), rings - ring, rings, axis=0
+    )
+    columns = lat_of(both)[0].reshape(wide_count, rings, sides * coarse_rows)
+    columns = lax.dynamic_slice_in_dim(
+        jnp.concatenate([columns, columns], axis=1), ring, rings, axis=1
+    ).reshape(wide_count, coarse_total)
+
     winds = packed[:, 1].reshape(peers, own_rows, 2, col_count)
     winds = jnp.transpose(winds, (1, 2, 0, 3)).reshape(own_rows, 2 * lon_total)
     sights = packed[:, 0, :, : kinds * block_count].reshape(peers, own_rows, kinds, block_count)
@@ -203,18 +281,25 @@
     offset = (jnp.arange(lon_total) % OBLK).astype(jnp.float32)
     gains = jnp.where(jnp.abs(cells - offset) < 0.5, sights[2 * STEPS :], 0.0)
 
-    def narrowed(parts):
-        chosen = jnp.concatenate([columns[:, d] for d in parts], axis=1)
-        weights = jnp.concatenate(
-            [blocks[d][:, :coarse_rows].reshape(-1, pairs, coarse_lons) for d in parts], axis=0
-        )
-        return jnp.einsum("rc,cpw->prw", chosen, weights, preferred_element_type=jnp.float32)
-
-    narrow = narrowed(range(rings))
-    localized = jnp.einsum("prw,wf->prf", narrow, lon_full, precision=highest)
-    localized = localized.reshape(members_here, levels_here, wide_count, lon_total)
-    partial_sum = jnp.sum(localized * members, axis=0)
-    arrived = swapped(partial_sum.reshape(peers, own_rows, lon_total), "mem", 0)
+    scalars = pl.BlockSpec(memory_space=pltpu.SMEM)
+    whole = pl.BlockSpec(memory_space=pltpu.VMEM)
+    roomy = pltpu.CompilerParams(vmem_limit_bytes=48 * 1024 * 1024)
+    where_side = jnp.reshape(side, (1,)).astype(jnp.int32)
+    partial_sum = pl.pallas_call(
+        localize_kernel,
+        out_shape=jax.ShapeDtypeStruct((peers, own_rows, lon_total), jnp.float32),
+        in_specs=[scalars] + [whole] * (4 + rings),
+        out_specs=whole,
+        compiler_params=roomy,
+    )(
+        where_side,
+        columns,
+        lon_matrix,
+        perturbations,
+        other_members,
+        *[blocks[d] for d in range(rings)],
+    )
+    arrived = swapped(partial_sum, "mem", 0)
     own = arrived.sum(axis=0) * member_scale
 
     before = lax.ppermute(own[-HALO:], ALL, forward)
@@ -222,19 +307,22 @@
     place = jnp.stack(
         [ring * wide_count + quarter * own_rows - HALO, jnp.int32(row_count * bands)]
     ).astype(jnp.int32)
-    whole = pl.BlockSpec(memory_space=pltpu.VMEM)
-    adjoint = pl.pallas_call(
+    copies = pl.pallas_call(
         stencil_kernel,
-        out_shape=jax.ShapeDtypeStruct((own_rows, lon_total), jnp.float32),
-        in_specs=[pl.BlockSpec(memory_space=pltpu.SMEM)] + [whole] * 6,
+        out_shape=jax.ShapeDtypeStruct((peers, own_rows, lon_total), jnp.float32),
+        in_specs=[scalars] + [whole] * 6,
         out_specs=whole,
-        compiler_params=pltpu.CompilerParams(vmem_limit_bytes=32 * 1024 * 1024),
+        compiler_params=roomy,
     )(place, own, before, after, wide_wind, gains, values)
 
-    copies = jnp.broadcast_to(adjoint, (peers, own_rows, lon_total))
-    adjoint_all = swapped(copies, "mem", 0).reshape(levels_here, wide_count, lon_total)
-    product = members * adjoint_all[None]
-    projected = jnp.einsum("mlrf,wf->mlrw", product, lon_full, precision=highest)
+    adjoint_all = swapped(copies, "mem", 0)
+    projected = pl.pallas_call(
+        project_kernel,
+        out_shape=jax.ShapeDtypeStruct((pairs, wide_count, coarse_lons), jnp.float32),
+        in_specs=[scalars] + [whole] * 4,
+        out_specs=whole,
+        compiler_params=roomy,
+    )(where_side, adjoint_all, jnp.transpose(lon_matrix), perturbations, other_members)
     by_pair = projected.reshape(rings, pairs // rings, wide_count, coarse_lons)
     by_pair = swapped(by_pair, "lat_0", 0)
     full = jnp.einsum(

time: 204 us -> 199 us (0.975)
  Pallas kernels: 1.61 us -> 9.13 us
  waiting for transfers between devices: 78.2 us -> 70.8 us
  matrix products: 10.7 us -> 3.39 us
  local copies, waits for them, and re-layouts: 30.5 us -> 36 us
  starting transfers between devices: 67.1 us -> 64.4 us
    ppermute x10, waiting for transfers between devices: 13.9 us -> 4.23 us  [the longest x4 4.21 us: body(): rising = lax.ppermute(rising, 'lat_0', up)]
    ppermute x1, waiting for transfers between devices: 0.01 us -> 8.6 us  [body(): before = lax.ppermute(local[-HALO:], ALL, forward)]
    dot_general x3 -> x0, matrix products: 8.55 us -> none  [the longest x1 5.17 us: body(): jnp.einsum('mlrf,wf->mlrw', product, lon_full, precision=highest)]
    pallas_call x1 -> x3, Pallas kernels: 1.61 us -> 9.13 us  [the longest x1 4.07 us: body(): pl.pallas_call(localize_kernel, out_shape=jax.ShapeDtypeStruct((peers, ow...]
    slice x35 -> x17, local copies, waits for them, and re-layouts: 11.5 us -> 7.13 us  [the longest x7 3.63 us: lat_of(): block[sides * weight_rows:].reshape(sides, row_count // 2, coarse_lons)]
    all_to_all x6, waiting for transfers between devices: 59.6 us -> 55.4 us  [swapped(): lax.all_to_all(value, axis, split_axis=dim, concat_axis=dim, tiled=True)]
    reduce_sum x1 -> x0, other arithmetic: 3.61 us -> none  [body(): partial_sum = jnp.sum(localized * members, axis=0)]
    another operation x2, local copies, waits for them, and re-layouts: 0.35 us -> 3.6 us  [body(): winds = packed[:, 1].reshape(peers, own_rows, 2, col_count)]
  transfers between devices with their start and end apart: 21 -> 21, of which waited for: 9 -> 8; matrix products, arithmetic and copies ran while one was open for 24% -> 21% of each run, Pallas kernels for 0% -> 1%
where the time goes in v3:
time: 199 us; the launch traced here: 197 us
  waiting for transfers between devices  70.8 us (36%)
  starting transfers between devices  64.4 us (32%)
  local copies, waits for them, and re-layouts  36 us (18%)
  other arithmetic  12.1 us (6%)
  Pallas kernels  9.13 us (5%)
  matrix products  3.39 us (2%)
    all_to_all x6, waiting for transfers between devices, swapped(): lax.all_to_all(value, axis, split_axis=dim, concat_axis=dim, tiled=True)  55.4 us
    all_to_all x6, starting transfers between devices, swapped(): lax.all_to_all(value, axis, split_axis=dim, concat_axis=dim, tiled=True)  31.3 us
    ppermute x3, starting transfers between devices, body(): falling = lax.ppermute(falling, 'lat_0', down)  9.64 us
    unnamed x58, local copies, waits for them, and re-layouts  9.32 us
    ppermute x1, waiting for transfers between devices, body(): before = lax.ppermute(local[-HALO:], ALL, forward)  8.6 us
    ppermute x4, waiting for transfers between devices, body(): rising = lax.ppermute(rising, 'lat_0', up)  4.21 us
    pallas_call x1, Pallas kernels, body(): pl.pallas_call(localize_kernel, out_shape=jax.ShapeDtypeStruct((peers, ow...  4.07 us
  transfers between devices with their start and end apart: 21, of which 8 were waited for; matrix products, arithmetic and copies ran while one was open for 21% of the time, Pallas kernels for 1%

profile of v3, /device:TPU:2, one launch (start us, length us, event | category | flops | bytes accessed | tf_op | source)
XLA Modules:
  0.0 196.9 jit_solution(9142741120466128396)
XLA Ops:
  3.1 2.1 %collective-permute-start = (bf16[144,256]{1,0:T(8,128)(2,1)}, bf16[144,256]{1,0:T(8,128)(2,1)S(1)}, u32[]{:S(2)}, u32[]{:S(2)}) collective-permute-start(bf16[144,256]{1,0:T(8,128)(2,1)} %maximum_maximum_fusion), channel_id=1, source_target_pairs={{0,1},{1,0},{2,3},{3,2},{4,5},{5,4},{6,7},{7,6},{8,9},{9,8},{10,11... | collective-permute-start | bytes 221192 | tf_op jit(solution)/shard_map/ppermute | solution.py:203
  11.4 2.0 %collective-permute-start.1 = (bf16[288,256]{1,0:T(8,128)(2,1)S(1)}, bf16[288,256]{1,0:T(8,128)(2,1)S(1)}, u32[]{:S(2)}, u32[]{:S(2)}) collective-permute-start(bf16[288,256]{1,0:T(8,128)(2,1)S(1)} %pad_maximum_fusion.2.refs_0_), channel_id=1, source_target_pairs={{0,2},{2,4},{4,6},{6,8},{8,10},{10,12},{12,14},{14,0},{1,3},{3,5},... | collective-permute-start | bytes 442376 | tf_op jit(solution)/shard_map/ppermute | solution.py:227
  13.4 4.0 %collective-permute-start.2 = (bf16[288,256]{1,0:T(8,128)(2,1)S(1)}, bf16[288,256]{1,0:T(8,128)(2,1)}, u32[]{:S(2)}, u32[]{:S(2)}) collective-permute-start(bf16[288,256]{1,0:T(8,128)(2,1)S(1)} %pad_maximum_fusion.2.refs_0_), channel_id=1, source_target_pairs={{2,0},{4,2},{6,4},{8,6},{10,8},{12,10},{14,12},{0,14},{3,1},{5,3},... | collective-permute-start | bytes 442376 | tf_op jit(solution)/shard_map/ppermute | solution.py:229
  18.4 2.2 %collective-permute-done.1.refs_7_ = bf16[288,256]{1,0:T(8,128)(2,1)S(1)} collective-permute-done((bf16[288,256]{1,0:T(8,128)(2,1)S(1)}, bf16[288,256]{1,0:T(8,128)(2,1)S(1)}, u32[]{:S(2)}, u32[]{:S(2)}) %collective-permute-start.1) | collective-permute-done | bytes 147488 | tf_op jit(solution)/shard_map/ppermute | solution.py:227
  20.6 3.3 %collective-permute-start.4 = (bf16[288,256]{1,0:T(8,128)(2,1)}, bf16[288,256]{1,0:T(8,128)(2,1)}, u32[]{:S(2)}, u32[]{:S(2)}) collective-permute-start(bf16[288,256]{1,0:T(8,128)(2,1)} %collective-permute-done.2.refs_1_), channel_id=1, source_target_pairs={{2,0},{4,2},{6,4},{8,6},{10,8},{12,10},{14,12},{0,14},{3,1},{5,3},... | collective-permute-start | bytes 442376 | tf_op jit(solution)/shard_map/ppermute | solution.py:229
  26.3 2.1 %collective-permute-start.9 = (bf16[4,4,32,1024]{3,2,1,0:T(8,128)(2,1)}, bf16[4,4,32,1024]{3,2,1,0:T(8,128)(2,1)S(1)}, u32[]{:S(2)}, u32[]{:S(2)}) collective-permute-start(bf16[4,4,32,1024]{3,2,1,0:T(8,128)(2,1)} %constant_dynamic-slice_fusion), channel_id=1, source_target_pairs={{0,1},{1,0},{2,3},{3,2},{4,5},{5,4},{6,7},{7,6},{8,9},{9,8},{10,11... | collective-permute-start | bytes 3145736 | tf_op jit(solution)/shard_map/ppermute | solution.py:235
  29.0 2.0 %collective-permute-done.3.refs_6_ = bf16[288,256]{1,0:T(8,128)(2,1)} collective-permute-done((bf16[288,256]{1,0:T(8,128)(2,1)S(1)}, bf16[288,256]{1,0:T(8,128)(2,1)}, u32[]{:S(2)}, u32[]{:S(2)}) %collective-permute-start.3) | collective-permute-done | bytes 147488 | tf_op jit(solution)/shard_map/ppermute | solution.py:227
  33.0 5.9 %all-to-all-start = ((f32[16,2,16,128]{3,2,1,0:T(8,128)}), f32[16,2,16,128]{3,2,1,0:T(8,128)}, u32[]{:S(2)}, u32[]{:S(2)}) async-start(f32[16,2,16,128]{3,2,1,0:T(8,128)} %copy.71), calls=%async_computation | async-start | bytes 524288 | tf_op jit(solution)/shard_map/all_to_all | solution.py:19
  41.9 2.4 %collective-permute-start.6 = (bf16[288,256]{1,0:T(8,128)(2,1)}, bf16[288,256]{1,0:T(8,128)(2,1)}, u32[]{:S(2)}, u32[]{:S(2)}) collective-permute-start(bf16[288,256]{1,0:T(8,128)(2,1)} %collective-permute-done.4.refs_2_), channel_id=1, source_target_pairs={{2,0},{4,2},{6,4},{8,6},{10,8},{12,10},{14,12},{0,14},{3,1},{5,3},... | collective-permute-start | bytes 442376 | tf_op jit(solution)/shard_map/ppermute | solution.py:229
  44.9 10.5 %all-to-all-done = f32[16,2,16,128]{3,2,1,0:T(8,128)} async-done(((f32[16,2,16,128]{3,2,1,0:T(8,128)}), f32[16,2,16,128]{3,2,1,0:T(8,128)}, u32[]{:S(2)}, u32[]{:S(2)}) %all-to-all-start) | async-done | bytes 262176 | tf_op jit(solution)/shard_map/all_to_all | solution.py:19
  55.5 2.9 %copy.75 = f32[16,2,16,128]{2,3,0,1:T(8,128)} copy(f32[16,2,16,128]{3,2,1,0:T(8,128)} %all-to-all-done) | data formatting | bytes 524288 | tf_op jit(solution)/shard_map/optimization_barrier | solution.py:248
  62.1 2.0 %copy.77 = f32[16,1536]{1,0:T(8,128)} copy(f32[16,1536]{0,1:T(8,128)} %bitcast.148) | data formatting | bytes 196608 | tf_op jit(solution)/shard_map/reshape | solution.py:268
  65.9 1.8 copy.110
  71.8 4.1 %shard_map.95 = f32[16,16,1024]{2,1,0:T(8,128)} custom-call(s32[1]{0:T(128)} %bitcast.31.side_ref, bf16[64,128]{1,0:T(8,128)(2,1)S(1)} %copy.73.columns_ref, bf16[256,1024]{1,0:T(8,128)(2,1)S(1)} %copy-done.4, bf16[4,8,32,1024]{3,2,1,0:T(8,128)(2,1)S(1)} %copy-done, bf16[4,4,32,1024]{3,2,1,0:T(8,128)(2,1)S(1)} %collective-permute-done.9.other_ref, ...), custom_call_target="tpu_custom_call" | custom-call | tf_op jit(solution)/shard_map/pallas_call | solution.py:288
  75.8 5.0 %all-to-all-start.1 = ((f32[16,16,1024]{2,1,0:T(8,128)}), f32[16,16,1024]{2,1,0:T(8,128)S(1)}, u32[]{:S(2)}, u32[]{:S(2)}) async-start(f32[16,16,1024]{2,1,0:T(8,128)} %shard_map.95), calls=%async_computation.1 | async-start | bytes 2097152 | tf_op jit(solution)/shard_map/all_to_all | solution.py:19
  81.9 2.1 %collective-permute-start.12 = (f32[8,3584]{1,0:T(8,128)S(1)}, f32[8,3584]{1,0:T(8,128)S(1)}, u32[]{:S(2)}, u32[]{:S(2)}) collective-permute-start(f32[8,3584]{1,0:T(8,128)S(1)} %get-tuple-element.24), channel_id=1, source_target_pairs={{0,16},{1,17},{2,18},{3,19},{4,20},{5,21},{6,22},{7,23},{8,24},{9,... | collective-permute-start | bytes 344072 | tf_op jit(solution)/shard_map/ppermute | solution.py:270
  83.9 3.7 %collective-permute-start.13 = (f32[8,3584]{1,0:T(8,128)S(1)}, f32[8,3584]{1,0:T(8,128)S(1)}, u32[]{:S(2)}, u32[]{:S(2)}) collective-permute-start(f32[8,3584]{1,0:T(8,128)S(1)} %get-tuple-element.25), channel_id=1, source_target_pairs={{16,0},{17,1},{18,2},{19,3},{20,4},{21,5},{22,6},{23,7},{24,8},{25... | collective-permute-start | bytes 344072 | tf_op jit(solution)/shard_map/ppermute | solution.py:271
  87.6 8.6 %collective-permute-done.12 = f32[8,3584]{1,0:T(8,128)S(1)} collective-permute-done((f32[8,3584]{1,0:T(8,128)S(1)}, f32[8,3584]{1,0:T(8,128)S(1)}, u32[]{:S(2)}, u32[]{:S(2)}) %collective-permute-start.12) | collective-permute-done | bytes 114720 | tf_op jit(solution)/shard_map/ppermute | solution.py:270
  96.2 2.9 %fusion.3 = f32[12,32,1024]{2,1,0:T(8,128)} fusion(s32[1024]{0:T(1024)S(1)} %copy-done.19, f32[8,3584]{1,0:T(8,128)S(1)} %collective-permute-done.13, f32[8,3584]{1,0:T(8,128)S(1)} %collective-permute-done.12, f32[16,1536]{1,0:T(8,128)} %copy.77, f32[16,2048]{1,0:T(8,128)} %reshape.205), kind=kOutput, calls=%fused_computation.10 | convolution fusion | flops 604258304 | bytes 2035712 | tf_op jit(solution)/shard_map/krb,bf->krf/dot_general | solution.py:278
  100.0 2.1 %collective-permute-start.10 = (f32[8,1024]{1,0:T(8,128)S(1)}, f32[8,1024]{1,0:T(8,128)S(1)}, u32[]{:S(2)}, u32[]{:S(2)}) collective-permute-start(f32[8,1024]{1,0:T(8,128)S(1)} %get-tuple-element.31), channel_id=1, source_target_pairs={{0,16},{1,17},{2,18},{3,19},{4,20},{5,21},{6,22},{7,23},{8,24},{9,... | collective-permute-start | bytes 98312 | tf_op jit(solution)/shard_map/ppermute | solution.py:305
  102.1 3.6 %collective-permute-start.11 = (f32[8,1024]{1,0:T(8,128)S(1)}, f32[8,1024]{1,0:T(8,128)S(1)}, u32[]{:S(2)}, u32[]{:S(2)}) collective-permute-start(f32[8,1024]{1,0:T(8,128)S(1)} %get-tuple-element.30), channel_id=1, source_target_pairs={{16,0},{17,1},{18,2},{19,3},{20,4},{21,5},{22,6},{23,7},{24,8},{25... | collective-permute-start | bytes 98312 | tf_op jit(solution)/shard_map/ppermute | solution.py:306
  107.3 2.7 %shard_map.96 = f32[16,16,1024]{2,1,0:T(8,128)} custom-call(s32[2]{0:T(128)S(1)} %pad_add_fusion.place_ref, f32[16,1024]{1,0:T(8,128)S(1)} %broadcast_multiply_fusion.1.own_ref, f32[8,1024]{1,0:T(8,128)S(1)} %collective-permute-done.10.before_ref, f32[8,1024]{1,0:T(8,128)S(1)} %collective-permute-done.11.after_ref, f32[2,32,1024]{2,1,0:T(8,128)S(1)} %bitcast.147, ...), custom_call_target="tpu_custom_call" | custom-call | tf_op jit(solution)/shard_map/pallas_call | solution.py:310
  110.0 6.2 %all-to-all-start.2 = ((f32[16,16,1024]{2,1,0:T(8,128)}), f32[16,16,1024]{2,1,0:T(8,128)S(1)}, u32[]{:S(2)}, u32[]{:S(2)}) async-start(f32[16,16,1024]{2,1,0:T(8,128)} %shard_map.96), calls=%async_computation.2 | async-start | bytes 2097152 | tf_op jit(solution)/shard_map/all_to_all | solution.py:19
  122.0 9.6 %all-to-all-done.2.adjoint_ref = f32[16,16,1024]{2,1,0:T(8,128)S(1)} async-done(((f32[16,16,1024]{2,1,0:T(8,128)}), f32[16,16,1024]{2,1,0:T(8,128)S(1)}, u32[]{:S(2)}, u32[]{:S(2)}) %all-to-all-start.2) | async-done | bytes 1048608 | tf_op jit(solution)/shard_map/all_to_all | solution.py:19
  131.6 4.6 %all-to-all-start.5 = ((f32[16,1,1024]{2,1,0:T(1,128)}), f32[16,1,1024]{2,1,0:T(1,128)S(1)}, u32[]{:S(2)}, u32[]{:S(2)}) async-start(f32[16,1,1024]{2,1,0:T(1,128)} %reshape.215), calls=%async_computation.5 | async-start | bytes 131072 | tf_op jit(solution)/shard_map/all_to_all | solution.py:19
  139.2 2.4 %shard_map.97 = f32[16,64,256]{2,1,0:T(8,128)} custom-call(s32[1]{0:T(128)} %bitcast.31.side_ref, f32[16,16,1024]{2,1,0:T(8,128)S(1)} %all-to-all-done.2.adjoint_ref, bf16[1024,256]{1,0:T(8,128)(2,1)S(1)} %bitcast.146, bf16[4,8,32,1024]{3,2,1,0:T(8,128)(2,1)S(1)} %copy-done, bf16[4,4,32,1024]{3,2,1,0:T(8,128)(2,1)S(1)} %copy-done.2), custom_call_target="tpu_custom_call" | custom-call | tf_op jit(solution)/shard_map/pallas_call | solution.py:319
  141.6 5.9 %all-to-all-start.3 = ((f32[8,2,64,256]{3,2,1,0:T(8,128)}), f32[8,2,64,256]{3,2,1,0:T(8,128)S(1)}, u32[]{:S(2)}, u32[]{:S(2)}) async-start(f32[8,2,64,256]{3,2,1,0:T(8,128)} %bitcast.42), calls=%async_computation.3 | async-start | bytes 2097152 | tf_op jit(solution)/shard_map/all_to_all | solution.py:19
  149.2 27.4 %all-to-all-done.3 = f32[8,2,64,256]{3,2,1,0:T(8,128)S(1)} async-done(((f32[8,2,64,256]{3,2,1,0:T(8,128)}), f32[8,2,64,256]{3,2,1,0:T(8,128)S(1)}, u32[]{:S(2)}, u32[]{:S(2)}) %all-to-all-start.3) | async-done | bytes 1048608 | tf_op jit(solution)/shard_map/all_to_all | solution.py:19
  177.8 3.5 %all-to-all-start.4 = ((f32[16,2,8,256]{3,2,1,0:T(8,128)}), f32[16,2,8,256]{3,2,1,0:T(8,128)S(1)}, u32[]{:S(2)}, u32[]{:S(2)}) async-start(f32[16,2,8,256]{3,2,1,0:T(8,128)} %bitcast.127), calls=%async_computation.4 | async-start | bytes 524288 | tf_op jit(solution)/shard_map/all_to_all | solution.py:19
  181.4 3.4 %collective-permute-start.14 = (f32[4,32,64]{2,1,0:T(8,128)S(1)}, f32[4,32,64]{2,1,0:T(8,128)S(1)}, u32[]{:S(2)}, u32[]{:S(2)}) collective-permute-start(f32[4,32,64]{2,1,0:T(8,128)S(1)} %select_bitcast_fusion), channel_id=1, source_target_pairs={{0,1},{1,0},{2,3},{3,2},{4,5},{5,4},{6,7},{7,6},{8,9},{9,8},{10,11... | collective-permute-start | bytes 98312 | tf_op jit(solution)/shard_map/ppermute | solution.py:343
  184.8 2.5 %collective-permute-done.14 = f32[4,32,64]{2,1,0:T(8,128)S(1)} collective-permute-done((f32[4,32,64]{2,1,0:T(8,128)S(1)}, f32[4,32,64]{2,1,0:T(8,128)S(1)}, u32[]{:S(2)}, u32[]{:S(2)}) %collective-permute-start.14) | collective-permute-done | bytes 32800 | tf_op jit(solution)/shard_map/ppermute | solution.py:343
  188.0 7.8 %all-to-all-done.4 = f32[16,2,8,256]{3,2,1,0:T(8,128)S(1)} async-done(((f32[16,2,8,256]{3,2,1,0:T(8,128)}), f32[16,2,8,256]{3,2,1,0:T(8,128)S(1)}, u32[]{:S(2)}, u32[]{:S(2)}) %all-to-all-start.4) | async-done | bytes 262176 | tf_op jit(solution)/shard_map/all_to_all | solution.py:19
  (157 shorter events, 44.3 us)
Async XLA Ops:
  0.6 6.8 %copy-start.16 = (f32[2,32,64]{2,1,0:T(8,128)S(1)}, f32[2,32,64]{2,1,0:T(8,128)}, u32[]{:S(2)}) copy-start(f32[2,32,64]{2,1,0:T(8,128)} %param.12) | copy-start | bytes 49156
  0.6 9.6 %copy-start.3 = (bf16[256,1024]{1,0:T(8,128)(2,1)S(1)}, bf16[256,1024]{1,0:T(8,128)(2,1)}, u32[]{:S(2)}) copy-start(bf16[256,1024]{1,0:T(8,128)(2,1)} %lon_ref.1) | copy-start | bytes 1572868
  3.1 8.2 %collective-permute-start = (bf16[144,256]{1,0:T(8,128)(2,1)}, bf16[144,256]{1,0:T(8,128)(2,1)S(1)}, u32[]{:S(2)}, u32[]{:S(2)}) collective-permute-start(bf16[144,256]{1,0:T(8,128)(2,1)} %maximum_maximum_fusion), channel_id=1, source_target_pairs={{0,1},{1,0},{2,3},{3,2},{4,5},{5,4},{6,7},{7,6},{8,9},{9,8},{10,11... | collective-permute-start | bytes 221192 | tf_op jit(solution)/shard_map/ppermute | solution.py:203
  7.2 18.1 %copy-start = (bf16[4,8,32,1024]{3,2,1,0:T(8,128)(2,1)S(1)}, bf16[4,8,32,1024]{3,2,1,0:T(8,128)(2,1)}, u32[]{:S(2)}) copy-start(bf16[4,8,32,1024]{3,2,1,0:T(8,128)(2,1)} %own_ref.3) | copy-start | bytes 6291460
  8.2 20.8 %collective-permute-start.5 = (f32[5,32,128]{2,1,0:T(8,128)}, f32[5,32,128]{2,1,0:T(8,128)}, u32[]{:S(2)}, u32[]{:S(2)}) collective-permute-start(f32[5,32,128]{2,1,0:T(8,128)} %get-tuple-element.46), channel_id=1, source_target_pairs={{0,1},{1,0},{2,3},{3,2},{4,5},{5,4},{6,7},{7,6},{8,9},{9,8},{10,11... | collective-permute-start | bytes 245768 | tf_op jit(solution)/shard_map/ppermute | solution.py:219
  11.4 9.2 %collective-permute-start.1 = (bf16[288,256]{1,0:T(8,128)(2,1)S(1)}, bf16[288,256]{1,0:T(8,128)(2,1)S(1)}, u32[]{:S(2)}, u32[]{:S(2)}) collective-permute-start(bf16[288,256]{1,0:T(8,128)(2,1)S(1)} %pad_maximum_fusion.2.refs_0_), channel_id=1, source_target_pairs={{0,2},{2,4},{4,6},{6,8},{8,10},{10,12},{12,14},{14,0},{1,3},{3,5},... | collective-permute-start | bytes 442376 | tf_op jit(solution)/shard_map/ppermute | solution.py:227
  13.4 7.2 %collective-permute-start.2 = (bf16[288,256]{1,0:T(8,128)(2,1)S(1)}, bf16[288,256]{1,0:T(8,128)(2,1)}, u32[]{:S(2)}, u32[]{:S(2)}) collective-permute-start(bf16[288,256]{1,0:T(8,128)(2,1)S(1)} %pad_maximum_fusion.2.refs_0_), channel_id=1, source_target_pairs={{2,0},{4,2},{6,4},{8,6},{10,8},{12,10},{14,12},{0,14},{3,1},{5,3},... | collective-permute-start | bytes 442376 | tf_op jit(solution)/shard_map/ppermute | solution.py:229
  17.4 7.8 %copy-start.11 = (bf16[2,32,128]{2,1,0:T(8,128)(2,1)}, bf16[2,32,128]{2,1,0:T(8,128)(2,1)S(1)}, u32[]{:S(2)}) copy-start(bf16[2,32,128]{2,1,0:T(8,128)(2,1)S(1)} %pad_maximum_fusion.6) | copy-start | bytes 49156
  20.6 12.4 %copy-start.6 = (bf16[288,256]{1,0:T(8,128)(2,1)}, bf16[288,256]{1,0:T(8,128)(2,1)S(1)}, u32[]{:S(2)}) copy-start(bf16[288,256]{1,0:T(8,128)(2,1)S(1)} %collective-permute-done.1.refs_7_) | copy-start | bytes 442372
  20.6 10.5 %collective-permute-start.4 = (bf16[288,256]{1,0:T(8,128)(2,1)}, bf16[288,256]{1,0:T(8,128)(2,1)}, u32[]{:S(2)}, u32[]{:S(2)}) collective-permute-start(bf16[288,256]{1,0:T(8,128)(2,1)} %collective-permute-done.2.refs_1_), channel_id=1, source_target_pairs={{2,0},{4,2},{6,4},{8,6},{10,8},{12,10},{14,12},{0,14},{3,1},{5,3},... | collective-permute-start | bytes 442376 | tf_op jit(solution)/shard_map/ppermute | solution.py:229
  24.6 6.5 %collective-permute-start.3 = (bf16[288,256]{1,0:T(8,128)(2,1)S(1)}, bf16[288,256]{1,0:T(8,128)(2,1)}, u32[]{:S(2)}, u32[]{:S(2)}) collective-permute-start(bf16[288,256]{1,0:T(8,128)(2,1)S(1)} %collective-permute-done.1.refs_7_), channel_id=1, source_target_pairs={{0,2},{2,4},{4,6},{6,8},{8,10},{10,12},{12,14},{14,0},{1,3},{3,5},... | collective-permute-start | bytes 442376 | tf_op jit(solution)/shard_map/ppermute | solution.py:227
  26.3 43.1 %collective-permute-start.9 = (bf16[4,4,32,1024]{3,2,1,0:T(8,128)(2,1)}, bf16[4,4,32,1024]{3,2,1,0:T(8,128)(2,1)S(1)}, u32[]{:S(2)}, u32[]{:S(2)}) collective-permute-start(bf16[4,4,32,1024]{3,2,1,0:T(8,128)(2,1)} %constant_dynamic-slice_fusion), channel_id=1, source_target_pairs={{0,1},{1,0},{2,3},{3,2},{4,5},{5,4},{6,7},{7,6},{8,9},{9,8},{10,11... | collective-permute-start | bytes 3145736 | tf_op jit(solution)/shard_map/ppermute | solution.py:235
  32.1 9.1 %copy-start.17 = (bf16[2,16,128]{2,1,0:T(8,128)(2,1)S(1)}, bf16[2,16,128]{2,1,0:T(8,128)(2,1)}, u32[]{:S(2)}) copy-start(bf16[2,16,128]{2,1,0:T(8,128)(2,1)} %get-tuple-element.33) | copy-start | bytes 24580
  32.1 7.5 %collective-permute-start.7 = (bf16[288,256]{1,0:T(8,128)(2,1)}, bf16[288,256]{1,0:T(8,128)(2,1)}, u32[]{:S(2)}, u32[]{:S(2)}) collective-permute-start(bf16[288,256]{1,0:T(8,128)(2,1)} %collective-permute-done.3.refs_6_), channel_id=1, source_target_pairs={{0,2},{2,4},{4,6},{6,8},{8,10},{10,12},{12,14},{14,0},{1,3},{3,5},... | collective-permute-start | bytes 442376 | tf_op jit(solution)/shard_map/ppermute | solution.py:227
  33.0 22.5 %all-to-all-start = ((f32[16,2,16,128]{3,2,1,0:T(8,128)}), f32[16,2,16,128]{3,2,1,0:T(8,128)}, u32[]{:S(2)}, u32[]{:S(2)}) async-start(f32[16,2,16,128]{3,2,1,0:T(8,128)} %copy.71), calls=%async_computation | async-start | bytes 524288 | tf_op jit(solution)/shard_map/all_to_all | solution.py:19
  39.6 15.8 %collective-permute-start.8 = (bf16[288,256]{1,0:T(8,128)(2,1)}, bf16[288,256]{1,0:T(8,128)(2,1)S(1)}, u32[]{:S(2)}, u32[]{:S(2)}) collective-permute-start(bf16[288,256]{1,0:T(8,128)(2,1)} %collective-permute-done.7.refs_5_), channel_id=1, source_target_pairs={{0,2},{2,4},{4,6},{6,8},{8,10},{10,12},{12,14},{14,0},{1,3},{3,5},... | collective-permute-start | bytes 442376 | tf_op jit(solution)/shard_map/ppermute | solution.py:227
  41.9 27.6 %collective-permute-start.6 = (bf16[288,256]{1,0:T(8,128)(2,1)}, bf16[288,256]{1,0:T(8,128)(2,1)}, u32[]{:S(2)}, u32[]{:S(2)}) collective-permute-start(bf16[288,256]{1,0:T(8,128)(2,1)} %collective-permute-done.4.refs_2_), channel_id=1, source_target_pairs={{2,0},{4,2},{6,4},{8,6},{10,8},{12,10},{14,12},{0,14},{3,1},{5,3},... | collective-permute-start | bytes 442376 | tf_op jit(solution)/shard_map/ppermute | solution.py:229
  75.8 20.4 %copy-start.19 = (s32[1024]{0:T(1024)S(1)}, s32[1024]{0:T(1024)}, u32[]{:S(2)}) copy-start(s32[1024]{0:T(1024)} %add_select_fusion) | copy-start | bytes 12292
  75.8 24.1 %all-to-all-start.1 = ((f32[16,16,1024]{2,1,0:T(8,128)}), f32[16,16,1024]{2,1,0:T(8,128)S(1)}, u32[]{:S(2)}, u32[]{:S(2)}) async-start(f32[16,16,1024]{2,1,0:T(8,128)} %shard_map.95), calls=%async_computation.1 | async-start | bytes 2097152 | tf_op jit(solution)/shard_map/all_to_all | solution.py:19
  80.9 18.2 %copy-start.8 = (f32[16,2048]{1,0:T(8,128)S(1)}, f32[16,2048]{1,0:T(8,128)}, u32[]{:S(2)}) copy-start(f32[16,2048]{1,0:T(8,128)} %reshape.205) | copy-start | bytes 393220
  80.9 18.2 %copy-start.9 = (f32[16,1536]{1,0:T(8,128)S(1)}, f32[16,1536]{1,0:T(8,128)}, u32[]{:S(2)}) copy-start(f32[16,1536]{1,0:T(8,128)} %copy.77) | copy-start | bytes 294916
  81.9 14.4 %collective-permute-start.12 = (f32[8,3584]{1,0:T(8,128)S(1)}, f32[8,3584]{1,0:T(8,128)S(1)}, u32[]{:S(2)}, u32[]{:S(2)}) collective-permute-start(f32[8,3584]{1,0:T(8,128)S(1)} %get-tuple-element.24), channel_id=1, source_target_pairs={{0,16},{1,17},{2,18},{3,19},{4,20},{5,21},{6,22},{7,23},{8,24},{9,... | collective-permute-start | bytes 344072 | tf_op jit(solution)/shard_map/ppermute | solution.py:270
  83.9 12.3 %collective-permute-start.13 = (f32[8,3584]{1,0:T(8,128)S(1)}, f32[8,3584]{1,0:T(8,128)S(1)}, u32[]{:S(2)}, u32[]{:S(2)}) collective-permute-start(f32[8,3584]{1,0:T(8,128)S(1)} %get-tuple-element.25), channel_id=1, source_target_pairs={{16,0},{17,1},{18,2},{19,3},{20,4},{21,5},{22,6},{23,7},{24,8},{25... | collective-permute-start | bytes 344072 | tf_op jit(solution)/shard_map/ppermute | solution.py:271
  100.0 7.3 %slice-start = ((f32[32,3584]{1,0:T(8,128)}), f32[32,2048]{1,0:T(8,128)S(1)}, s32[]{:S(2)}) async-start(f32[32,3584]{1,0:T(8,128)} %pad_maximum_fusion), calls=%async_computation.6 | async-start | bytes 524288 | tf_op jit(solution)/shard_map/slice | solution.py:274
  100.0 7.3 %collective-permute-start.10 = (f32[8,1024]{1,0:T(8,128)S(1)}, f32[8,1024]{1,0:T(8,128)S(1)}, u32[]{:S(2)}, u32[]{:S(2)}) collective-permute-start(f32[8,1024]{1,0:T(8,128)S(1)} %get-tuple-element.31), channel_id=1, source_target_pairs={{0,16},{1,17},{2,18},{3,19},{4,20},{5,21},{6,22},{7,23},{8,24},{9,... | collective-permute-start | bytes 98312 | tf_op jit(solution)/shard_map/ppermute | solution.py:305
  102.1 5.2 %collective-permute-start.11 = (f32[8,1024]{1,0:T(8,128)S(1)}, f32[8,1024]{1,0:T(8,128)S(1)}, u32[]{:S(2)}, u32[]{:S(2)}) collective-permute-start(f32[8,1024]{1,0:T(8,128)S(1)} %get-tuple-element.30), channel_id=1, source_target_pairs={{16,0},{17,1},{18,2},{19,3},{20,4},{21,5},{22,6},{23,7},{24,8},{25... | collective-permute-start | bytes 98312 | tf_op jit(solution)/shard_map/ppermute | solution.py:306
  110.0 21.6 %all-to-all-start.2 = ((f32[16,16,1024]{2,1,0:T(8,128)}), f32[16,16,1024]{2,1,0:T(8,128)S(1)}, u32[]{:S(2)}, u32[]{:S(2)}) async-start(f32[16,16,1024]{2,1,0:T(8,128)} %shard_map.96), calls=%async_computation.2 | async-start | bytes 2097152 | tf_op jit(solution)/shard_map/all_to_all | solution.py:19
  131.6 10.0 %all-to-all-start.5 = ((f32[16,1,1024]{2,1,0:T(1,128)}), f32[16,1,1024]{2,1,0:T(1,128)S(1)}, u32[]{:S(2)}, u32[]{:S(2)}) async-start(f32[16,1,1024]{2,1,0:T(1,128)} %reshape.215), calls=%async_computation.5 | async-start | bytes 131072 | tf_op jit(solution)/shard_map/all_to_all | solution.py:19
  141.6 35.0 %all-to-all-start.3 = ((f32[8,2,64,256]{3,2,1,0:T(8,128)}), f32[8,2,64,256]{3,2,1,0:T(8,128)S(1)}, u32[]{:S(2)}, u32[]{:S(2)}) async-start(f32[8,2,64,256]{3,2,1,0:T(8,128)} %bitcast.42), calls=%async_computation.3 | async-start | bytes 2097152 | tf_op jit(solution)/shard_map/all_to_all | solution.py:19
  149.2 47.0 %copy-start.10 = (bf16[8,4,8,256]{3,2,1,0:T(8,128)(2,1)S(1)}, bf16[8,4,8,256]{3,2,1,0:T(8,128)(2,1)}, u32[]{:S(2)}) copy-start(bf16[8,4,8,256]{3,2,1,0:T(8,128)(2,1)} %param.8) | copy-start | bytes 393220
  177.8 17.9 %all-to-all-start.4 = ((f32[16,2,8,256]{3,2,1,0:T(8,128)}), f32[16,2,8,256]{3,2,1,0:T(8,128)S(1)}, u32[]{:S(2)}, u32[]{:S(2)}) async-start(f32[16,2,8,256]{3,2,1,0:T(8,128)} %bitcast.127), calls=%async_computation.4 | async-start | bytes 524288 | tf_op jit(solution)/shard_map/all_to_all | solution.py:19
  181.4 5.9 %collective-permute-start.14 = (f32[4,32,64]{2,1,0:T(8,128)S(1)}, f32[4,32,64]{2,1,0:T(8,128)S(1)}, u32[]{:S(2)}, u32[]{:S(2)}) collective-permute-start(f32[4,32,64]{2,1,0:T(8,128)S(1)} %select_bitcast_fusion), channel_id=1, source_target_pairs={{0,1},{1,0},{2,3},{3,2},{4,5},{5,4},{6,7},{7,6},{8,9},{9,8},{10,11... | collective-permute-start | bytes 98312 | tf_op jit(solution)/shard_map/ppermute | solution.py:343
  (10 other events, 37.6 us)

commit v4 on v3

--- a/solution.py
+++ b/solution.py
@@ -80,6 +80,61 @@
             out_ref[member * levels_here + level] = (
                 projected[at : at + tall] + projected[at + members * tall : at + (members + 1) * tall]
             )
+
+
+def arrange_kernel(side_ref, own_ref, other_ref, out_ref):
+    peers, _, row_count, lanes = own_ref.shape
+    side = side_ref[0]
+    is_own = side_ref[1] == 1
+    lane = lax.broadcasted_iota(jnp.int32, (row_count, lanes), 1)
+    width = lanes // 2
+    pick = lambda peer, which, mine: jnp.where(is_own, own_ref[peer, mine], other_ref[peer, which])
+    winds = [pick(peer, 1, 2) for peer in range(peers)]
+    seen = [pick(peer, 0, side) for peer in range(peers)]
+    lon_total = peers * width
+    for at in range(peers // 2):
+        even, odd = winds[2 * at], winds[2 * at + 1]
+        spot = slice(at * lanes, (at + 1) * lanes)
+        out_ref[:, spot] = jnp.where(lane < width, even, pltpu.roll(odd, width, 1))
+        spot = slice(lon_total + at * lanes, lon_total + (at + 1) * lanes)
+        out_ref[:, spot] = jnp.where(lane < width, pltpu.roll(even, width, 1), odd)
+    blocks = lanes // peers
+    kinds = (out_ref.shape[1] - 2 * lon_total) // lanes
+    owner = lane // blocks
+    for kind in range(kinds):
+        total = jnp.zeros((row_count, lanes), jnp.float32)
+        for peer in range(peers):
+            shift = (peer - kind) * blocks % lanes
+            value = seen[peer] if shift == 0 else pltpu.roll(seen[peer], shift, 1)
+            total = jnp.where(owner == peer, value, total)
+        spot = slice(2 * lon_total + kind * lanes, 2 * lon_total + (kind + 1) * lanes)
+        out_ref[:, spot] = total
+
+
+def spread_kernel(before_ref, local_ref, after_ref, wind_ref, gain_ref, value_ref):
+    _, rows, cols = wind_ref.shape
+    lanes = cols // OBLK
+    local = jnp.concatenate([before_ref[...], local_ref[...], after_ref[...]], axis=0)
+    wind_ref[0] = local[:, :cols]
+    wind_ref[1] = local[:, cols : 2 * cols]
+    sights = [local[:, 2 * cols + k * lanes : 2 * cols + (k + 1) * lanes] for k in range(3 * STEPS)]
+    cells = jnp.concatenate(sights[:STEPS], axis=0).astype(jnp.bfloat16)
+    others = jnp.concatenate(sights[STEPS:], axis=0)
+    high = others.astype(jnp.bfloat16)
+    rest = others - high.astype(jnp.float32)
+    middle = rest.astype(jnp.bfloat16)
+    low = (rest - middle.astype(jnp.float32)).astype(jnp.bfloat16)
+    block = lax.broadcasted_iota(jnp.int32, (lanes, cols), 0)
+    spread = (lax.broadcasted_iota(jnp.int32, (lanes, cols), 1) // OBLK == block).astype(jnp.bfloat16)
+    cells = dot(cells, spread)
+    wide = dot(high, spread) + (dot(middle, spread) + dot(low, spread))
+    offset = lax.broadcasted_iota(jnp.int32, (rows, cols), 1) % OBLK
+    offset = offset.astype(jnp.float32)
+    for step in range(STEPS):
+        value_ref[step] = wide[step * rows : (step + 1) * rows]
+        hit = jnp.abs(cells[step * rows : (step + 1) * rows] - offset) < 0.5
+        weight = wide[(STEPS + step) * rows : (STEPS + step + 1) * rows]
+        gain_ref[step] = jnp.where(hit, weight, 0.0)
 
 
 def stencil_kernel(place_ref, own_ref, before_ref, after_ref, wind_ref, gain_ref, value_ref, adjoint_ref):
@@ -214,9 +269,16 @@
     packed = jnp.transpose(packed, (1, 2, 0, 3)).reshape(levels, row_count, kinds * block_count)
     packed = jnp.pad(packed, ((0, 0), (0, 0), (0, lanes - kinds * block_count)))
     winds = jnp.transpose(wind_field, (1, 0, 2)).reshape(1, row_count, lanes)
-    mine_seen, theirs_seen = halves(packed, 0)
-    mine_seen = jnp.concatenate([mine_seen, winds], axis=0)
-    theirs_seen = lax.ppermute(jnp.concatenate([theirs_seen, winds], axis=0), "lat_1", across)
+    parts = row_count // own_rows
+    packed = packed.reshape(sides, levels_here, 1, parts, own_rows, lanes)
+    winds = jnp.broadcast_to(
+        winds.reshape(1, 1, 1, parts, own_rows, lanes), (1, levels_here, 1, parts, own_rows, lanes)
+    )
+    packed = jnp.transpose(jnp.concatenate([packed, winds], axis=0), (1, 2, 3, 0, 4, 5))
+    packed = jnp.broadcast_to(
+        packed, (levels_here, quarters // parts, parts, sides + 1, own_rows, lanes)
+    )
+    packed = swapped(packed.reshape(peers, sides + 1, own_rows, lanes), "mem", 0)
 
     side = lax.axis_index("lat_1")
     up = [(i, (i + 1) % rings) for i in range(rings)]
@@ -234,19 +296,12 @@
             )
             other_members = lax.ppermute(other_members, "lat_1", across)
         if hop == 2:
-            rising, falling, mine_seen, theirs_seen = lax.optimization_barrier(
-                (rising, falling, mine_seen, theirs_seen)
-            )
-            packed = in_order(mine_seen, theirs_seen, 1)
-            packed = packed.reshape(levels_here + 1, quarters, own_rows, lanes)
-            winds = jnp.broadcast_to(packed[levels_here:], (levels_here, quarters, own_rows, lanes))
-            packed = jnp.stack([packed[:levels_here], winds], axis=2)
-            packed = swapped(packed.reshape(peers, 2, own_rows, lanes), "mem", 0)
+            rising, falling, packed = lax.optimization_barrier((rising, falling, packed))
+            passed = jnp.where(first, packed[:, 1:], jnp.stack([packed[:, 0], packed[:, 2]], axis=1))
+            passed = lax.ppermute(passed, "lat_1", across)
         blocks[-hop % rings] = rising
         if hop < rings - hop:
             blocks[hop] = falling
-    last, packed = lax.optimization_barrier((blocks[rings // 2], packed))
-    blocks[rings // 2] = last
 
     def lat_of(block):
         rows = block[sides * weight_rows :].reshape(sides, row_count // 2, coarse_lons)
@@ -261,25 +316,6 @@
     columns = lax.dynamic_slice_in_dim(
         jnp.concatenate([columns, columns], axis=1), ring, rings, axis=1
     ).reshape(wide_count, coarse_total)
-
-    winds = packed[:, 1].reshape(peers, own_rows, 2, col_count)
-    winds = jnp.transpose(winds, (1, 2, 0, 3)).reshape(own_rows, 2 * lon_total)
-    sights = packed[:, 0, :, : kinds * block_count].reshape(peers, own_rows, kinds, block_count)
-    sights = jnp.transpose(sights, (1, 2, 0, 3)).reshape(own_rows, kinds * peers * block_count)
-    local = jnp.concatenate([winds, sights], axis=1)
-    before = lax.ppermute(local[-HALO:], ALL, forward)
-    after = lax.ppermute(local[:HALO], ALL, backward)
-    local = jnp.concatenate([before, local, after], axis=0)
-    wide_rows = own_rows + 2 * HALO
-    wide_wind = jnp.transpose(local[:, : 2 * lon_total].reshape(wide_rows, 2, lon_total), (1, 0, 2))
-    sights = local[:, 2 * lon_total :].reshape(wide_rows, kinds, peers * block_count)
-    sights = jnp.transpose(sights, (1, 0, 2))
-    spread = jnp.arange(lon_total)[None, :] // OBLK == jnp.arange(lon_total // OBLK)[:, None]
-    sights = jnp.einsum("krb,bf->krf", sights, spread.astype(jnp.float32), precision=highest)
-    cells = sights[:STEPS]
-    values = sights[STEPS : 2 * STEPS]
-    offset = (jnp.arange(lon_total) % OBLK).astype(jnp.float32)
-    gains = jnp.where(jnp.abs(cells - offset) < 0.5, sights[2 * STEPS :], 0.0)
 
     scalars = pl.BlockSpec(memory_space=pltpu.SMEM)
     whole = pl.BlockSpec(memory_space=pltpu.VMEM)
@@ -299,7 +335,33 @@
         other_members,
         *[blocks[d] for d in range(rings)],
     )
+    partial_sum, packed, passed = lax.optimization_barrier((partial_sum, packed, passed))
     arrived = swapped(partial_sum, "mem", 0)
+
+    is_own = (quarter // parts == side).astype(jnp.int32)
+    local = pl.pallas_call(
+        arrange_kernel,
+        out_shape=jax.ShapeDtypeStruct(
+            (own_rows, 2 * lon_total + kinds * peers * block_count), jnp.float32
+        ),
+        in_specs=[scalars, whole, whole],
+        out_specs=whole,
+        compiler_params=roomy,
+    )(jnp.stack([side.astype(jnp.int32), is_own]), packed, passed)
+    before = lax.ppermute(local[-HALO:], ALL, forward)
+    after = lax.ppermute(local[:HALO], ALL, backward)
+    wide_rows = own_rows + 2 * HALO
+    wide_wind, gains, values = pl.pallas_call(
+        spread_kernel,
+        out_shape=[
+            jax.ShapeDtypeStruct((count, wide_rows, lon_total), jnp.float32)
+            for count in (2, STEPS, STEPS)
+        ],
+        in_specs=[whole] * 3,
+        out_specs=[whole] * 3,
+        compiler_params=roomy,
+    )(before, local, after)
+
     own = arrived.sum(axis=0) * member_scale
 
     before = lax.ppermute(own[-HALO:], ALL, forward)
@@ -323,6 +385,7 @@
         out_specs=whole,
         compiler_params=roomy,
     )(where_side, adjoint_all, jnp.transpose(lon_matrix), perturbations, other_members)
+    projected, own = lax.optimization_barrier((projected, own))
     by_pair = projected.reshape(rings, pairs // rings, wide_count, coarse_lons)
     by_pair = swapped(by_pair, "lat_0", 0)
     full = jnp.einsum(

time: 199 us -> 196 us (0.985)
  waiting for transfers between devices: 70.8 us -> 90.9 us
  local copies, waits for them, and re-layouts: 36 us -> 22.4 us
  starting transfers between devices: 64.4 us -> 59.2 us
  other arithmetic: 12.1 us -> 8.98 us
  matrix products: 3.39 us -> 0.52 us
    ppermute x1, waiting for transfers between devices: 0.01 us -> 11.1 us  [body(): other_members = lax.ppermute(other_members, 'lat_1', across)]
    ppermute x1, waiting for transfers between devices: 8.6 us -> 0.01 us  [body(): before = lax.ppermute(local[-HALO:], ALL, forward)]
    all_to_all x6, waiting for transfers between devices: 55.4 us -> 63.1 us  [swapped(): lax.all_to_all(value, axis, split_axis=dim, concat_axis=dim, tiled=True)]
    ppermute x4, waiting for transfers between devices: 4.21 us -> 10 us  [body(): rising = lax.ppermute(rising, 'lat_0', up)]
    another operation x4 -> x0, local copies, waits for them, and re-layouts: 4.34 us -> none  [the longest x2 3.6 us: body(): winds = packed[:, 1].reshape(peers, own_rows, 2, col_count)]
    reshape x4 -> x2, local copies, waits for them, and re-layouts: 3.83 us -> 0.13 us  [body(): tiles = jnp.transpose(own.reshape(own_rows, peers, col_count), (1, 0, 2))]
    optimization_barrier x1 -> x0, local copies, waits for them, and re-layouts: 2.92 us -> none  [body(): last, packed = lax.optimization_barrier((blocks[rings // 2], packed))]
    dot_general x1 -> x0, matrix products: 2.87 us -> none  [body(): jnp.einsum('krb,bf->krf', sights, spread.astype(jnp.float32), precision=h...]
  transfers between devices with their start and end apart: 21 -> 21, of which waited for: 8 -> 13; matrix products, arithmetic and copies ran while one was open for 21% -> 10% of each run, Pallas kernels for 1% -> 3%
where the time goes in v4:
time: 196 us; the launch traced here: 194 us
  waiting for transfers between devices  90.9 us (46%)
  starting transfers between devices  59.2 us (30%)
  local copies, waits for them, and re-layouts  22.4 us (11%)
  Pallas kernels  11 us (6%)
  other arithmetic  8.98 us (5%)
    all_to_all x6, waiting for transfers between devices, swapped(): lax.all_to_all(value, axis, split_axis=dim, concat_axis=dim, tiled=True)  63.1 us
    all_to_all x6, starting transfers between devices, swapped(): lax.all_to_all(value, axis, split_axis=dim, concat_axis=dim, tiled=True)  30.6 us
    ppermute x1, waiting for transfers between devices, body(): other_members = lax.ppermute(other_members, 'lat_1', across)  11.1 us
    unnamed x65, local copies, waits for them, and re-layouts  10.2 us
    ppermute x4, waiting for transfers between devices, body(): rising = lax.ppermute(rising, 'lat_0', up)  10 us
    ppermute x3, starting transfers between devices, body(): falling = lax.ppermute(falling, 'lat_0', down)  8.92 us
    pallas_call x1, Pallas kernels, body(): pl.pallas_call(localize_kernel, out_shape=jax.ShapeDtypeStruct((peers, ow...  4.29 us
    slice x9, local copies, waits for them, and re-layouts, lat_of(): block[sides * weight_rows:].reshape(sides, row_count // 2, coarse_lons)  4.21 us
  transfers between devices with their start and end apart: 21, of which 13 were waited for; matrix products, arithmetic and copies ran while one was open for 10% of the time, Pallas kernels for 3%

profile of v4, /device:TPU:2, one launch (start us, length us, event | category | flops | bytes accessed | tf_op | source)
XLA Modules:
  0.0 194.1 jit_solution(7714008838638503454)
XLA Ops:
  2.5 2.2 %collective-permute-start = (bf16[144,256]{1,0:T(8,128)(2,1)S(1)}, bf16[144,256]{1,0:T(8,128)(2,1)S(1)}, u32[]{:S(2)}, u32[]{:S(2)}) collective-permute-start(bf16[144,256]{1,0:T(8,128)(2,1)S(1)} %maximum_maximum_fusion), channel_id=1, source_target_pairs={{0,1},{1,0},{2,3},{3,2},{4,5},{5,4},{6,7},{7,6},{8,9},{9,8},{10,11... | collective-permute-start | bytes 221192 | tf_op jit(solution)/shard_map/ppermute | solution.py:258
  8.6 5.9 %all-to-all-start = ((f32[16,3,16,128]{3,2,1,0:T(8,128)}), f32[16,3,16,128]{3,2,1,0:T(8,128)S(1)}, u32[]{:S(2)}, u32[]{:S(2)}) async-start(f32[16,3,16,128]{3,2,1,0:T(8,128)} %bitcast.18), calls=%async_computation | async-start | bytes 786432 | tf_op jit(solution)/shard_map/all_to_all | solution.py:19
  16.9 5.9 %collective-permute-start.2 = (bf16[288,256]{1,0:T(8,128)(2,1)S(1)}, bf16[288,256]{1,0:T(8,128)(2,1)}, u32[]{:S(2)}, u32[]{:S(2)}) collective-permute-start(bf16[288,256]{1,0:T(8,128)(2,1)S(1)} %pad_maximum_fusion.refs_0_), channel_id=1, source_target_pairs={{2,0},{4,2},{6,4},{8,6},{10,8},{12,10},{14,12},{0,14},{3,1},{5,3},... | collective-permute-start | bytes 442376 | tf_op jit(solution)/shard_map/ppermute | solution.py:291
  23.8 2.4 %collective-permute-done.2.refs_1_ = bf16[288,256]{1,0:T(8,128)(2,1)} collective-permute-done((bf16[288,256]{1,0:T(8,128)(2,1)S(1)}, bf16[288,256]{1,0:T(8,128)(2,1)}, u32[]{:S(2)}, u32[]{:S(2)}) %collective-permute-start.2) | collective-permute-done | bytes 147488 | tf_op jit(solution)/shard_map/ppermute | solution.py:291
  26.2 3.5 %collective-permute-done.1.refs_7_ = bf16[288,256]{1,0:T(8,128)(2,1)} collective-permute-done((bf16[288,256]{1,0:T(8,128)(2,1)S(1)}, bf16[288,256]{1,0:T(8,128)(2,1)}, u32[]{:S(2)}, u32[]{:S(2)}) %collective-permute-start.1) | collective-permute-done | bytes 147488 | tf_op jit(solution)/shard_map/ppermute | solution.py:289
  32.1 1.7 collective-permute-start.3
  34.9 1.4 collective-permute-start.8
  39.3 1.5 collective-permute-start.9
  41.5 2.7 %collective-permute-start.5 = (bf16[288,256]{1,0:T(8,128)(2,1)}, bf16[288,256]{1,0:T(8,128)(2,1)S(1)}, u32[]{:S(2)}, u32[]{:S(2)}) collective-permute-start(bf16[288,256]{1,0:T(8,128)(2,1)} %copy-done.13), channel_id=1, source_target_pairs={{2,0},{4,2},{6,4},{8,6},{10,8},{12,10},{14,12},{0,14},{3,1},{5,3},... | collective-permute-start | bytes 442376 | tf_op jit(solution)/shard_map/ppermute | solution.py:291
  45.3 1.4 pad_maximum_fusion.2
  47.3 4.4 %collective-permute-done.7.refs_4_ = bf16[288,256]{1,0:T(8,128)(2,1)S(1)} collective-permute-done((bf16[288,256]{1,0:T(8,128)(2,1)S(1)}, bf16[288,256]{1,0:T(8,128)(2,1)S(1)}, u32[]{:S(2)}, u32[]{:S(2)}) %collective-permute-start.7) | collective-permute-done | bytes 147488 | tf_op jit(solution)/shard_map/ppermute | solution.py:289
  51.7 11.1 %collective-permute-done.8.other_ref = bf16[4,4,32,1024]{3,2,1,0:T(8,128)(2,1)S(1)} collective-permute-done((bf16[4,4,32,1024]{3,2,1,0:T(8,128)(2,1)}, bf16[4,4,32,1024]{3,2,1,0:T(8,128)(2,1)S(1)}, u32[]{:S(2)}, u32[]{:S(2)}) %collective-permute-start.8) | collective-permute-done | bytes 1048608 | tf_op jit(solution)/shard_map/ppermute | solution.py:297
  65.6 4.3 %shard_map.95 = f32[16,16,1024]{2,1,0:T(8,128)} custom-call(s32[1]{0:T(128)} %bitcast.32.side_ref, bf16[64,128]{1,0:T(8,128)(2,1)S(1)} %copy.40.columns_ref, bf16[256,1024]{1,0:T(8,128)(2,1)S(1)} %copy-done.4, bf16[4,8,32,1024]{3,2,1,0:T(8,128)(2,1)S(1)} %copy-done, bf16[4,4,32,1024]{3,2,1,0:T(8,128)(2,1)S(1)} %collective-permute-done.8.other_ref, ...), custom_call_target="tpu_custom_call" | custom-call | tf_op jit(solution)/shard_map/pallas_call | solution.py:324
  70.7 5.9 %all-to-all-start.1 = ((f32[16,16,1024]{2,1,0:T(8,128)}), f32[16,16,1024]{2,1,0:T(8,128)}, u32[]{:S(2)}, u32[]{:S(2)}) async-start(f32[16,16,1024]{2,1,0:T(8,128)} %shard_map.95), calls=%async_computation.1 | async-start | bytes 2097152 | tf_op jit(solution)/shard_map/all_to_all | solution.py:19
  79.3 2.0 %collective-permute-start.13 = (f32[8,3584]{1,0:T(8,128)S(1)}, f32[8,3584]{1,0:T(8,128)S(1)}, u32[]{:S(2)}, u32[]{:S(2)}) collective-permute-start(f32[8,3584]{1,0:T(8,128)S(1)} %get-tuple-element.32), channel_id=1, source_target_pairs={{16,0},{17,1},{18,2},{19,3},{20,4},{21,5},{22,6},{23,7},{24,8},{25... | collective-permute-start | bytes 344072 | tf_op jit(solution)/shard_map/ppermute | solution.py:352
  81.3 2.3 %collective-permute-start.12 = (f32[8,3584]{1,0:T(8,128)S(1)}, f32[8,3584]{1,0:T(8,128)S(1)}, u32[]{:S(2)}, u32[]{:S(2)}) collective-permute-start(f32[8,3584]{1,0:T(8,128)S(1)} %get-tuple-element.33), channel_id=1, source_target_pairs={{0,16},{1,17},{2,18},{3,19},{4,20},{5,21},{6,22},{7,23},{8,24},{9,... | collective-permute-start | bytes 344072 | tf_op jit(solution)/shard_map/ppermute | solution.py:351
  83.6 8.4 %all-to-all-done.1 = f32[16,16,1024]{2,1,0:T(8,128)} async-done(((f32[16,16,1024]{2,1,0:T(8,128)}), f32[16,16,1024]{2,1,0:T(8,128)}, u32[]{:S(2)}, u32[]{:S(2)}) %all-to-all-start.1) | async-done | bytes 1048608 | tf_op jit(solution)/shard_map/all_to_all | solution.py:19
  93.3 2.5 %collective-permute-start.11 = (f32[8,1024]{1,0:T(8,128)S(1)}, f32[8,1024]{1,0:T(8,128)S(1)}, u32[]{:S(2)}, u32[]{:S(2)}) collective-permute-start(f32[8,1024]{1,0:T(8,128)S(1)} %get-tuple-element.38), channel_id=1, source_target_pairs={{16,0},{17,1},{18,2},{19,3},{20,4},{21,5},{22,6},{23,7},{24,8},{25... | collective-permute-start | bytes 98312 | tf_op jit(solution)/shard_map/ppermute | solution.py:368
  95.8 2.1 %collective-permute-start.10 = (f32[8,1024]{1,0:T(8,128)S(1)}, f32[8,1024]{1,0:T(8,128)S(1)}, u32[]{:S(2)}, u32[]{:S(2)}) collective-permute-start(f32[8,1024]{1,0:T(8,128)S(1)} %get-tuple-element.39), channel_id=1, source_target_pairs={{0,16},{1,17},{2,18},{3,19},{4,20},{5,21},{6,22},{7,23},{8,24},{9,... | collective-permute-start | bytes 98312 | tf_op jit(solution)/shard_map/ppermute | solution.py:367
  99.3 1.7 collective-permute-done.10.before_ref
  101.0 2.7 %shard_map.98 = f32[16,16,1024]{2,1,0:T(8,128)} custom-call(s32[2]{0:T(128)S(1)} %copy-done.16, f32[16,1024]{1,0:T(8,128)S(1)} %broadcast_multiply_fusion.1.own_ref, f32[8,1024]{1,0:T(8,128)S(1)} %collective-permute-done.10.before_ref, f32[8,1024]{1,0:T(8,128)S(1)} %collective-permute-done.11.after_ref, f32[2,32,1024]{2,1,0:T(8,128)S(1)} %get-tuple-element.25.wind_ref, ...), custom_call_target="tpu_custom_call" | custom-call | tf_op jit(solution)/shard_map/pallas_call | solution.py:372
  103.7 4.5 %all-to-all-start.2 = ((f32[16,16,1024]{2,1,0:T(8,128)}), f32[16,16,1024]{2,1,0:T(8,128)S(1)}, u32[]{:S(2)}, u32[]{:S(2)}) async-start(f32[16,16,1024]{2,1,0:T(8,128)} %shard_map.98), calls=%async_computation.2 | async-start | bytes 2097152 | tf_op jit(solution)/shard_map/all_to_all | solution.py:19
  109.0 14.6 %all-to-all-done.2.adjoint_ref = f32[16,16,1024]{2,1,0:T(8,128)S(1)} async-done(((f32[16,16,1024]{2,1,0:T(8,128)}), f32[16,16,1024]{2,1,0:T(8,128)S(1)}, u32[]{:S(2)}, u32[]{:S(2)}) %all-to-all-start.2) | async-done | bytes 1048608 | tf_op jit(solution)/shard_map/all_to_all | solution.py:19
  125.9 2.3 %shard_map.99 = f32[16,64,256]{2,1,0:T(8,128)} custom-call(s32[1]{0:T(128)} %bitcast.32.side_ref, f32[16,16,1024]{2,1,0:T(8,128)S(1)} %all-to-all-done.2.adjoint_ref, bf16[1024,256]{1,0:T(8,128)(2,1)S(1)} %bitcast.118, bf16[4,8,32,1024]{3,2,1,0:T(8,128)(2,1)S(1)} %copy-done, bf16[4,4,32,1024]{3,2,1,0:T(8,128)(2,1)S(1)} %copy-done.2), custom_call_target="tpu_custom_call" | custom-call | tf_op jit(solution)/shard_map/pallas_call | solution.py:381
  129.1 4.6 %all-to-all-start.5 = ((f32[16,1,1024]{2,1,0:T(1,128)}), f32[16,1,1024]{2,1,0:T(1,128)S(1)}, u32[]{:S(2)}, u32[]{:S(2)}) async-start(f32[16,1,1024]{2,1,0:T(1,128)} %reshape.143), calls=%async_computation.5 | async-start | bytes 131072 | tf_op jit(solution)/shard_map/all_to_all | solution.py:19
  133.8 4.9 %all-to-all-done.5 = f32[16,1,1024]{2,1,0:T(1,128)S(1)} async-done(((f32[16,1,1024]{2,1,0:T(1,128)}), f32[16,1,1024]{2,1,0:T(1,128)S(1)}, u32[]{:S(2)}, u32[]{:S(2)}) %all-to-all-start.5) | async-done | bytes 65568 | tf_op jit(solution)/shard_map/all_to_all | solution.py:19
  138.7 6.1 %all-to-all-start.3 = ((f32[8,2,64,256]{3,2,1,0:T(8,128)}), f32[8,2,64,256]{3,2,1,0:T(8,128)S(1)}, u32[]{:S(2)}, u32[]{:S(2)}) async-start(f32[8,2,64,256]{3,2,1,0:T(8,128)} %bitcast.37), calls=%async_computation.3 | async-start | bytes 2097152 | tf_op jit(solution)/shard_map/all_to_all | solution.py:19
  146.4 27.4 %all-to-all-done.3 = f32[8,2,64,256]{3,2,1,0:T(8,128)S(1)} async-done(((f32[8,2,64,256]{3,2,1,0:T(8,128)}), f32[8,2,64,256]{3,2,1,0:T(8,128)S(1)}, u32[]{:S(2)}, u32[]{:S(2)}) %all-to-all-start.3) | async-done | bytes 1048608 | tf_op jit(solution)/shard_map/all_to_all | solution.py:19
  175.1 3.5 %all-to-all-start.4 = ((f32[16,2,8,256]{3,2,1,0:T(8,128)}), f32[16,2,8,256]{3,2,1,0:T(8,128)S(1)}, u32[]{:S(2)}, u32[]{:S(2)}) async-start(f32[16,2,8,256]{3,2,1,0:T(8,128)} %bitcast.100), calls=%async_computation.4 | async-start | bytes 524288 | tf_op jit(solution)/shard_map/all_to_all | solution.py:19
  178.6 3.4 %collective-permute-start.14 = (f32[4,32,64]{2,1,0:T(8,128)S(1)}, f32[4,32,64]{2,1,0:T(8,128)S(1)}, u32[]{:S(2)}, u32[]{:S(2)}) collective-permute-start(f32[4,32,64]{2,1,0:T(8,128)S(1)} %select_bitcast_fusion), channel_id=1, source_target_pairs={{0,1},{1,0},{2,3},{3,2},{4,5},{5,4},{6,7},{7,6},{8,9},{9,8},{10,11... | collective-permute-start | bytes 98312 | tf_op jit(solution)/shard_map/ppermute | solution.py:406
  182.0 2.5 %collective-permute-done.14 = f32[4,32,64]{2,1,0:T(8,128)S(1)} collective-permute-done((f32[4,32,64]{2,1,0:T(8,128)S(1)}, f32[4,32,64]{2,1,0:T(8,128)S(1)}, u32[]{:S(2)}, u32[]{:S(2)}) %collective-permute-start.14) | collective-permute-done | bytes 32800 | tf_op jit(solution)/shard_map/ppermute | solution.py:406
  185.2 7.8 %all-to-all-done.4 = f32[16,2,8,256]{3,2,1,0:T(8,128)S(1)} async-done(((f32[16,2,8,256]{3,2,1,0:T(8,128)}), f32[16,2,8,256]{3,2,1,0:T(8,128)S(1)}, u32[]{:S(2)}, u32[]{:S(2)}) %all-to-all-start.4) | async-done | bytes 262176 | tf_op jit(solution)/shard_map/all_to_all | solution.py:19
  (150 shorter events, 35.2 us)
Async XLA Ops:
  2.5 14.3 %collective-permute-start = (bf16[144,256]{1,0:T(8,128)(2,1)S(1)}, bf16[144,256]{1,0:T(8,128)(2,1)S(1)}, u32[]{:S(2)}, u32[]{:S(2)}) collective-permute-start(bf16[144,256]{1,0:T(8,128)(2,1)S(1)} %maximum_maximum_fusion), channel_id=1, source_target_pairs={{0,1},{1,0},{2,3},{3,2},{4,5},{5,4},{6,7},{7,6},{8,9},{9,8},{10,11... | collective-permute-start | bytes 221192 | tf_op jit(solution)/shard_map/ppermute | solution.py:258
  7.7 26.1 %copy-start = (bf16[4,8,32,1024]{3,2,1,0:T(8,128)(2,1)S(1)}, bf16[4,8,32,1024]{3,2,1,0:T(8,128)(2,1)}, u32[]{:S(2)}) copy-start(bf16[4,8,32,1024]{3,2,1,0:T(8,128)(2,1)} %own_ref.3) | copy-start | bytes 6291460
  8.6 30.2 %all-to-all-start = ((f32[16,3,16,128]{3,2,1,0:T(8,128)}), f32[16,3,16,128]{3,2,1,0:T(8,128)S(1)}, u32[]{:S(2)}, u32[]{:S(2)}) async-start(f32[16,3,16,128]{3,2,1,0:T(8,128)} %bitcast.18), calls=%async_computation | async-start | bytes 786432 | tf_op jit(solution)/shard_map/all_to_all | solution.py:19
  16.8 17.0 %copy-start.6 = (bf16[288,256]{1,0:T(8,128)(2,1)}, bf16[288,256]{1,0:T(8,128)(2,1)S(1)}, u32[]{:S(2)}) copy-start(bf16[288,256]{1,0:T(8,128)(2,1)S(1)} %pad_maximum_fusion.refs_0_) | copy-start | bytes 442372
  16.9 9.4 %collective-permute-start.2 = (bf16[288,256]{1,0:T(8,128)(2,1)S(1)}, bf16[288,256]{1,0:T(8,128)(2,1)}, u32[]{:S(2)}, u32[]{:S(2)}) collective-permute-start(bf16[288,256]{1,0:T(8,128)(2,1)S(1)} %pad_maximum_fusion.refs_0_), channel_id=1, source_target_pairs={{2,0},{4,2},{6,4},{8,6},{10,8},{12,10},{14,12},{0,14},{3,1},{5,3},... | collective-permute-start | bytes 442376 | tf_op jit(solution)/shard_map/ppermute | solution.py:291
  22.8 6.9 %collective-permute-start.1 = (bf16[288,256]{1,0:T(8,128)(2,1)S(1)}, bf16[288,256]{1,0:T(8,128)(2,1)}, u32[]{:S(2)}, u32[]{:S(2)}) collective-permute-start(bf16[288,256]{1,0:T(8,128)(2,1)S(1)} %pad_maximum_fusion.refs_0_), channel_id=1, source_target_pairs={{0,2},{2,4},{4,6},{6,8},{8,10},{10,12},{12,14},{14,0},{1,3},{3,5},... | collective-permute-start | bytes 442376 | tf_op jit(solution)/shard_map/ppermute | solution.py:289
  22.8 11.0 %copy-start.18 = (bf16[2,32,128]{2,1,0:T(8,128)(2,1)}, bf16[2,32,128]{2,1,0:T(8,128)(2,1)S(1)}, u32[]{:S(2)}) copy-start(bf16[2,32,128]{2,1,0:T(8,128)(2,1)S(1)} %pad_maximum_fusion.1) | copy-start | bytes 49156
  30.4 6.5 %collective-permute-start.4 = (bf16[288,256]{1,0:T(8,128)(2,1)}, bf16[288,256]{1,0:T(8,128)(2,1)S(1)}, u32[]{:S(2)}, u32[]{:S(2)}) collective-permute-start(bf16[288,256]{1,0:T(8,128)(2,1)} %collective-permute-done.2.refs_1_), channel_id=1, source_target_pairs={{2,0},{4,2},{6,4},{8,6},{10,8},{12,10},{14,12},{0,14},{3,1},{5,3},... | collective-permute-start | bytes 442376 | tf_op jit(solution)/shard_map/ppermute | solution.py:291
  32.1 6.7 %collective-permute-start.3 = (bf16[288,256]{1,0:T(8,128)(2,1)}, bf16[288,256]{1,0:T(8,128)(2,1)}, u32[]{:S(2)}, u32[]{:S(2)}) collective-permute-start(bf16[288,256]{1,0:T(8,128)(2,1)} %collective-permute-done.1.refs_7_), channel_id=1, source_target_pairs={{0,2},{2,4},{4,6},{6,8},{8,10},{10,12},{12,14},{14,0},{1,3},{3,5},... | collective-permute-start | bytes 442376 | tf_op jit(solution)/shard_map/ppermute | solution.py:289
  34.9 27.8 %collective-permute-start.8 = (bf16[4,4,32,1024]{3,2,1,0:T(8,128)(2,1)}, bf16[4,4,32,1024]{3,2,1,0:T(8,128)(2,1)S(1)}, u32[]{:S(2)}, u32[]{:S(2)}) collective-permute-start(bf16[4,4,32,1024]{3,2,1,0:T(8,128)(2,1)} %constant_dynamic-slice_fusion), channel_id=1, source_target_pairs={{0,1},{1,0},{2,3},{3,2},{4,5},{5,4},{6,7},{7,6},{8,9},{9,8},{10,11... | collective-permute-start | bytes 3145736 | tf_op jit(solution)/shard_map/ppermute | solution.py:297
  38.7 6.6 %collective-permute-start.6 = (bf16[288,256]{1,0:T(8,128)(2,1)}, bf16[288,256]{1,0:T(8,128)(2,1)S(1)}, u32[]{:S(2)}, u32[]{:S(2)}) collective-permute-start(bf16[288,256]{1,0:T(8,128)(2,1)} %collective-permute-done.3.refs_6_), channel_id=1, source_target_pairs={{0,2},{2,4},{4,6},{6,8},{8,10},{10,12},{12,14},{14,0},{1,3},{3,5},... | collective-permute-start | bytes 442376 | tf_op jit(solution)/shard_map/ppermute | solution.py:289
  39.3 30.6 %collective-permute-start.9 = (f32[16,2,16,128]{3,2,1,0:T(8,128)S(1)}, f32[16,2,16,128]{3,2,1,0:T(8,128)S(1)}, u32[]{:S(2)}, u32[]{:S(2)}) collective-permute-start(f32[16,2,16,128]{3,2,1,0:T(8,128)S(1)} %maximum_select_fusion), channel_id=1, source_target_pairs={{0,1},{1,0},{2,3},{3,2},{4,5},{5,4},{6,7},{7,6},{8,9},{9,8},{10,11... | collective-permute-start | bytes 786440 | tf_op jit(solution)/shard_map/ppermute | solution.py:301
  41.5 5.7 %collective-permute-start.5 = (bf16[288,256]{1,0:T(8,128)(2,1)}, bf16[288,256]{1,0:T(8,128)(2,1)S(1)}, u32[]{:S(2)}, u32[]{:S(2)}) collective-permute-start(bf16[288,256]{1,0:T(8,128)(2,1)} %copy-done.13), channel_id=1, source_target_pairs={{2,0},{4,2},{6,4},{8,6},{10,8},{12,10},{14,12},{0,14},{3,1},{5,3},... | collective-permute-start | bytes 442376 | tf_op jit(solution)/shard_map/ppermute | solution.py:291
  45.3 24.6 %copy-start.11 = (bf16[288,256]{1,0:T(8,128)(2,1)}, bf16[288,256]{1,0:T(8,128)(2,1)S(1)}, u32[]{:S(2)}) copy-start(bf16[288,256]{1,0:T(8,128)(2,1)S(1)} %collective-permute-done.6.refs_5_) | copy-start | bytes 442372
  45.3 6.4 %collective-permute-start.7 = (bf16[288,256]{1,0:T(8,128)(2,1)S(1)}, bf16[288,256]{1,0:T(8,128)(2,1)S(1)}, u32[]{:S(2)}, u32[]{:S(2)}) collective-permute-start(bf16[288,256]{1,0:T(8,128)(2,1)S(1)} %collective-permute-done.6.refs_5_), channel_id=1, source_target_pairs={{0,2},{2,4},{4,6},{6,8},{8,10},{10,12},{12,14},{14,0},{1,3},{3,5},... | collective-permute-start | bytes 442376 | tf_op jit(solution)/shard_map/ppermute | solution.py:289
  47.3 22.6 %copy-start.12 = (bf16[288,256]{1,0:T(8,128)(2,1)}, bf16[288,256]{1,0:T(8,128)(2,1)S(1)}, u32[]{:S(2)}) copy-start(bf16[288,256]{1,0:T(8,128)(2,1)S(1)} %collective-permute-done.5.refs_3_) | copy-start | bytes 442372
  51.7 18.3 %copy-start.10 = (bf16[288,256]{1,0:T(8,128)(2,1)}, bf16[288,256]{1,0:T(8,128)(2,1)S(1)}, u32[]{:S(2)}) copy-start(bf16[288,256]{1,0:T(8,128)(2,1)S(1)} %collective-permute-done.7.refs_4_) | copy-start | bytes 442372
  70.7 21.3 %all-to-all-start.1 = ((f32[16,16,1024]{2,1,0:T(8,128)}), f32[16,16,1024]{2,1,0:T(8,128)}, u32[]{:S(2)}, u32[]{:S(2)}) async-start(f32[16,16,1024]{2,1,0:T(8,128)} %shard_map.95), calls=%async_computation.1 | async-start | bytes 2097152 | tf_op jit(solution)/shard_map/all_to_all | solution.py:19
  76.5 24.5 %copy-start.16 = (s32[2]{0:T(128)S(1)}, s32[2]{0:T(128)}, u32[]{:S(2)}) copy-start(s32[2]{0:T(128)} %pad_add_fusion.place_ref) | copy-start | bytes 28
  79.3 19.4 %collective-permute-start.13 = (f32[8,3584]{1,0:T(8,128)S(1)}, f32[8,3584]{1,0:T(8,128)S(1)}, u32[]{:S(2)}, u32[]{:S(2)}) collective-permute-start(f32[8,3584]{1,0:T(8,128)S(1)} %get-tuple-element.32), channel_id=1, source_target_pairs={{16,0},{17,1},{18,2},{19,3},{20,4},{21,5},{22,6},{23,7},{24,8},{25... | collective-permute-start | bytes 344072 | tf_op jit(solution)/shard_map/ppermute | solution.py:352
  81.3 17.3 %collective-permute-start.12 = (f32[8,3584]{1,0:T(8,128)S(1)}, f32[8,3584]{1,0:T(8,128)S(1)}, u32[]{:S(2)}, u32[]{:S(2)}) collective-permute-start(f32[8,3584]{1,0:T(8,128)S(1)} %get-tuple-element.33), channel_id=1, source_target_pairs={{0,16},{1,17},{2,18},{3,19},{4,20},{5,21},{6,22},{7,23},{8,24},{9,... | collective-permute-start | bytes 344072 | tf_op jit(solution)/shard_map/ppermute | solution.py:351
  93.3 6.0 %collective-permute-start.11 = (f32[8,1024]{1,0:T(8,128)S(1)}, f32[8,1024]{1,0:T(8,128)S(1)}, u32[]{:S(2)}, u32[]{:S(2)}) collective-permute-start(f32[8,1024]{1,0:T(8,128)S(1)} %get-tuple-element.38), channel_id=1, source_target_pairs={{16,0},{17,1},{18,2},{19,3},{20,4},{21,5},{22,6},{23,7},{24,8},{25... | collective-permute-start | bytes 98312 | tf_op jit(solution)/shard_map/ppermute | solution.py:368
  95.8 5.2 %collective-permute-start.10 = (f32[8,1024]{1,0:T(8,128)S(1)}, f32[8,1024]{1,0:T(8,128)S(1)}, u32[]{:S(2)}, u32[]{:S(2)}) collective-permute-start(f32[8,1024]{1,0:T(8,128)S(1)} %get-tuple-element.39), channel_id=1, source_target_pairs={{0,16},{1,17},{2,18},{3,19},{4,20},{5,21},{6,22},{7,23},{8,24},{9,... | collective-permute-start | bytes 98312 | tf_op jit(solution)/shard_map/ppermute | solution.py:367
  103.7 19.9 %all-to-all-start.2 = ((f32[16,16,1024]{2,1,0:T(8,128)}), f32[16,16,1024]{2,1,0:T(8,128)S(1)}, u32[]{:S(2)}, u32[]{:S(2)}) async-start(f32[16,16,1024]{2,1,0:T(8,128)} %shard_map.98), calls=%async_computation.2 | async-start | bytes 2097152 | tf_op jit(solution)/shard_map/all_to_all | solution.py:19
  128.2 16.6 %slice-start = ((bf16[288,256]{1,0:T(8,128)(2,1)}), bf16[32,256]{1,0:T(8,128)(2,1)S(1)}, s32[]{:S(2)}) async-start(bf16[288,256]{1,0:T(8,128)(2,1)} %copy-done.10), calls=%async_computation.6 | async-start | bytes 32768 | tf_op jit(solution)/shard_map/slice | solution.py:307
  128.2 16.6 %copy-start.20 = (bf16[2,32,128]{2,1,0:T(8,128)(2,1)S(1)}, bf16[2,32,128]{2,1,0:T(8,128)(2,1)}, u32[]{:S(2)}) copy-start(bf16[2,32,128]{2,1,0:T(8,128)(2,1)} %pad_maximum_fusion.8) | copy-start | bytes 49156
  128.2 16.7 %copy-start.19 = (bf16[2,32,128]{2,1,0:T(8,128)(2,1)S(1)}, bf16[2,32,128]{2,1,0:T(8,128)(2,1)}, u32[]{:S(2)}) copy-start(bf16[2,32,128]{2,1,0:T(8,128)(2,1)} %copy-done.18) | copy-start | bytes 49156
  129.1 9.6 %all-to-all-start.5 = ((f32[16,1,1024]{2,1,0:T(1,128)}), f32[16,1,1024]{2,1,0:T(1,128)S(1)}, u32[]{:S(2)}, u32[]{:S(2)}) async-start(f32[16,1,1024]{2,1,0:T(1,128)} %reshape.143), calls=%async_computation.5 | async-start | bytes 131072 | tf_op jit(solution)/shard_map/all_to_all | solution.py:19
  138.7 35.1 %all-to-all-start.3 = ((f32[8,2,64,256]{3,2,1,0:T(8,128)}), f32[8,2,64,256]{3,2,1,0:T(8,128)S(1)}, u32[]{:S(2)}, u32[]{:S(2)}) async-start(f32[8,2,64,256]{3,2,1,0:T(8,128)} %bitcast.37), calls=%async_computation.3 | async-start | bytes 2097152 | tf_op jit(solution)/shard_map/all_to_all | solution.py:19
  146.4 47.0 %copy-start.17 = (bf16[8,4,8,256]{3,2,1,0:T(8,128)(2,1)S(1)}, bf16[8,4,8,256]{3,2,1,0:T(8,128)(2,1)}, u32[]{:S(2)}) copy-start(bf16[8,4,8,256]{3,2,1,0:T(8,128)(2,1)} %param.8) | copy-start | bytes 393220
  175.1 17.9 %all-to-all-start.4 = ((f32[16,2,8,256]{3,2,1,0:T(8,128)}), f32[16,2,8,256]{3,2,1,0:T(8,128)S(1)}, u32[]{:S(2)}, u32[]{:S(2)}) async-start(f32[16,2,8,256]{3,2,1,0:T(8,128)} %bitcast.100), calls=%async_computation.4 | async-start | bytes 524288 | tf_op jit(solution)/shard_map/all_to_all | solution.py:19
  178.6 5.9 %collective-permute-start.14 = (f32[4,32,64]{2,1,0:T(8,128)S(1)}, f32[4,32,64]{2,1,0:T(8,128)S(1)}, u32[]{:S(2)}, u32[]{:S(2)}) collective-permute-start(f32[4,32,64]{2,1,0:T(8,128)S(1)} %select_bitcast_fusion), channel_id=1, source_target_pairs={{0,1},{1,0},{2,3},{3,2},{4,5},{5,4},{6,7},{7,6},{8,9},{9,8},{10,11... | collective-permute-start | bytes 98312 | tf_op jit(solution)/shard_map/ppermute | solution.py:406
  (14 other events, 47.8 us)

commit v5 on v4

--- a/solution.py
+++ b/solution.py
@@ -1,3 +1,5 @@
+import functools
+
 import jax
 import jax.numpy as jnp
 from jax import lax
@@ -9,11 +11,10 @@
 STEPS = 4
 OBLK = 8
 HALO = 8
+LN2 = 0.6931471805599453
+STEPS_16 = 32767.0
 LAT = ("lat_0", "lat_1")
 ALL = ("mem", "lat_0", "lat_1")
-
-highest = lax.Precision.HIGHEST
-
 
 def swapped(value, axis, dim):
     return lax.all_to_all(value, axis, split_axis=dim, concat_axis=dim, tiled=True)
@@ -63,23 +64,95 @@
         sum_ref[level * count : (level + 1) * count] = total.reshape(count, tall // count, lon_total)
 
 
-def project_kernel(side_ref, adjoint_ref, lon_ref, own_ref, other_ref, out_ref):
+def row_codes(value):
+    largest = jnp.maximum(jnp.max(jnp.abs(value), axis=1, keepdims=True), 1e-30)
+    return jnp.ceil(jnp.log(largest) * (256.0 / LN2)) + 1.0
+
+
+def code_scale(codes):
+    return jnp.exp(codes * (LN2 / 256.0))
+
+
+def project_kernel(side_ref, adjoint_ref, lon_ref, own_ref, other_ref, out_ref, tile_ref):
     members, levels_here, row_count, lon_total = other_ref.shape
+    rings, _, coarse_lons = out_ref.shape
     tall = 2 * row_count
     side = side_ref[0]
     lon = lon_ref[...]
-    count = adjoint_ref.shape[0] // levels_here
+    quarters = adjoint_ref.shape[0] // levels_here
+    row_tiles = tall // quarters // 8
+    lane_tiles = lon_total // 128
+    per_message = members * levels_here // rings
+    row = lax.broadcasted_iota(jnp.int32, (tall, 128), 0)
+    lane = lax.broadcasted_iota(jnp.int32, (tall, 128), 1)
+    tails = [jnp.zeros((1, 128), jnp.float32) for _ in range(rings)]
     for level in range(levels_here):
-        adjoint = adjoint_ref[level * count : (level + 1) * count].reshape(tall, lon_total)
+        strips = []
+        for at in range(lane_tiles):
+            strips.append(
+                jnp.concatenate(
+                    [
+                        adjoint_ref[
+                            level * quarters + q, (t * lane_tiles + at) * 8 : (t * lane_tiles + at + 1) * 8
+                        ]
+                        for q in range(quarters)
+                        for t in range(row_tiles)
+                    ],
+                    axis=0,
+                )
+            )
+        adjoint = jnp.concatenate(strips, axis=1)
         product = [
             member_rows(side, own_ref, other_ref, member, level) * adjoint for member in range(members)
         ]
         projected = dot(two_terms(jnp.concatenate(product, axis=0)), lon)
         for member in range(members):
             at = member * tall
-            out_ref[member * levels_here + level] = (
-                projected[at : at + tall] + projected[at + members * tall : at + (members + 1) * tall]
-            )
+            value = projected[at : at + tall] + projected[at + members * tall : at + (members + 1) * tall]
+            pair = member * levels_here + level
+            ring, place = pair // per_message, pair % per_message
+            codes = row_codes(value)
+            whole = jnp.round(value * (STEPS_16 / code_scale(codes))).astype(jnp.int32)
+            out_ref[ring, place * tall : (place + 1) * tall] = whole.astype(jnp.int16)
+            mark = jnp.where(lane == row + place * tall, codes, 0.0)
+            tails[ring] = tails[ring] + jnp.sum(mark, axis=0, keepdims=True)
+        for q in range(quarters):
+            piece = adjoint_ref[level * quarters + q, row_tiles * lane_tiles * 8 :]
+            band, start = q * row_tiles * 8 // row_count, q * row_tiles * 8 % row_count
+            width = tile_ref.shape[3]
+            tile_ref[band, level, start : start + 8] = piece[:, :width]
+            tile_ref[band, level, start + 8 : start + 16] = piece[:, width:]
+    data = per_message * tall
+    for ring in range(rings):
+        tail = jnp.broadcast_to(tails[ring], (16, 128)).astype(jnp.int32).astype(jnp.int16)
+        out_ref[ring, data : data + 16] = jnp.concatenate([tail] * (coarse_lons // 128), axis=1)
+
+
+def gather_kernel(scale, message_ref, lat_ref, out_ref):
+    rings, rows, lons = message_ref.shape
+    bands, places, coarse_rows, _ = out_ref.shape
+    data = rows - 16
+    coarse = bands * coarse_rows
+    high, low, scales = [], [], []
+    for ring in range(rings):
+        value = message_ref[ring, :data].astype(jnp.int32).astype(jnp.float32)
+        upper = jnp.floor(value * (1.0 / 256.0)) * 256.0
+        high.append(upper.astype(jnp.bfloat16))
+        low.append((value - upper).astype(jnp.bfloat16))
+        codes = message_ref[ring, data:].astype(jnp.int32).astype(jnp.float32)[:1, :data]
+        scales.append(code_scale(codes) * (scale / STEPS_16))
+    high = jnp.concatenate(high, axis=0)
+    low = jnp.concatenate(low, axis=0)
+    lat = lat_ref[...].astype(jnp.float32) * jnp.concatenate(scales, axis=1)
+    place = lax.broadcasted_iota(jnp.int32, lat.shape, 1) % data // (data // places)
+    lat = jnp.concatenate([jnp.where(place == p, lat, 0.0) for p in range(places)], axis=0)
+    terms = two_terms(lat)
+    total = dot(terms, high)
+    total = total[: places * coarse] + (total[places * coarse :] + dot(terms[: places * coarse], low))
+    for band in range(bands):
+        for p in range(places):
+            at = p * coarse + band * coarse_rows
+            out_ref[band, p] = total[at : at + coarse_rows]
 
 
 def arrange_kernel(side_ref, own_ref, other_ref, out_ref):
@@ -192,8 +265,27 @@
             + west(to_east * pushed)
         )
     adjoint = adjoint[HALO : rows - HALO]
-    for copy in range(adjoint_ref.shape[0]):
-        adjoint_ref[copy] = adjoint
+    row_tiles, lane_tiles = (rows - 2 * HALO) // 8, cols // 128
+    packed = jnp.concatenate(
+        [
+            adjoint[t * 8 : (t + 1) * 8, at * 128 : (at + 1) * 128]
+            for t in range(row_tiles)
+            for at in range(lane_tiles)
+        ],
+        axis=0,
+    )
+    count = adjoint_ref.shape[0]
+    width = cols // count
+    lane = lax.broadcasted_iota(jnp.int32, (8, 128), 1)
+    for copy in range(count):
+        adjoint_ref[copy, : row_tiles * lane_tiles * 8] = packed
+        strip = slice(copy * width // 128 * 128, copy * width // 128 * 128 + 128)
+        top, bottom = own_ref[0:8, strip], own_ref[8:16, strip]
+        if copy % 2 == 0:
+            piece = jnp.where(lane < width, top, pltpu.roll(bottom, width, 1))
+        else:
+            piece = jnp.where(lane < width, pltpu.roll(top, width, 1), bottom)
+        adjoint_ref[copy, row_tiles * lane_tiles * 8 :] = piece
 
 
 def body(
@@ -281,6 +373,10 @@
     packed = swapped(packed.reshape(peers, sides + 1, own_rows, lanes), "mem", 0)
 
     side = lax.axis_index("lat_1")
+    other_members = lax.dynamic_slice_in_dim(
+        perturbations, (1 - side) * levels_here, levels_here, axis=1
+    )
+    other_members = lax.ppermute(other_members, "lat_1", across)
     up = [(i, (i + 1) % rings) for i in range(rings)]
     down = [(b, a) for a, b in up]
     blocks = {0: both}
@@ -289,12 +385,6 @@
         rising = lax.ppermute(rising, "lat_0", up)
         if hop < rings - hop:
             falling = lax.ppermute(falling, "lat_0", down)
-        if hop == 1:
-            rising, falling, perturbed = lax.optimization_barrier((rising, falling, perturbations))
-            other_members = lax.dynamic_slice_in_dim(
-                perturbed, (1 - side) * levels_here, levels_here, axis=1
-            )
-            other_members = lax.ppermute(other_members, "lat_1", across)
         if hop == 2:
             rising, falling, packed = lax.optimization_barrier((rising, falling, packed))
             passed = jnp.where(first, packed[:, 1:], jnp.stack([packed[:, 0], packed[:, 2]], axis=1))
@@ -308,10 +398,6 @@
         rows = jnp.concatenate([rows[..., :coarse_total], rows[..., coarse_total:]], 1)
         return rows.reshape(1, wide_count, coarse_total)
 
-    lat_ring = jnp.concatenate([lat_of(blocks[d]) for d in range(rings)], axis=0)
-    lat_all = lax.dynamic_slice_in_dim(
-        jnp.concatenate([lat_ring, lat_ring], axis=0), rings - ring, rings, axis=0
-    )
     columns = lat_of(both)[0].reshape(wide_count, rings, sides * coarse_rows)
     columns = lax.dynamic_slice_in_dim(
         jnp.concatenate([columns, columns], axis=1), ring, rings, axis=1
@@ -348,6 +434,14 @@
         out_specs=whole,
         compiler_params=roomy,
     )(jnp.stack([side.astype(jnp.int32), is_own]), packed, passed)
+    local, *tied = lax.optimization_barrier((local, *[blocks[d] for d in range(rings)]))
+    lat_ring = jnp.concatenate([lat_of(block) for block in tied], axis=0)
+    lat_all = lax.dynamic_slice_in_dim(
+        jnp.concatenate([lat_ring, lat_ring], axis=0), rings - ring, rings, axis=0
+    )
+    repeats = pairs // rings
+    lat_all = jnp.broadcast_to(lat_all[:, None], (rings, repeats, wide_count, coarse_total))
+    lat_all = jnp.transpose(lat_all.reshape(rings * repeats * wide_count, coarse_total))
     before = lax.ppermute(local[-HALO:], ALL, forward)
     after = lax.ppermute(local[:HALO], ALL, backward)
     wide_rows = own_rows + 2 * HALO
@@ -371,38 +465,40 @@
     ).astype(jnp.int32)
     copies = pl.pallas_call(
         stencil_kernel,
-        out_shape=jax.ShapeDtypeStruct((peers, own_rows, lon_total), jnp.float32),
+        out_shape=jax.ShapeDtypeStruct((peers, own_rows * lon_total // 128 + 8, 128), jnp.float32),
         in_specs=[scalars] + [whole] * 6,
         out_specs=whole,
         compiler_params=roomy,
     )(place, own, before, after, wide_wind, gains, values)
 
     adjoint_all = swapped(copies, "mem", 0)
-    projected = pl.pallas_call(
+    projected, tiles = pl.pallas_call(
         project_kernel,
-        out_shape=jax.ShapeDtypeStruct((pairs, wide_count, coarse_lons), jnp.float32),
+        out_shape=[
+            jax.ShapeDtypeStruct((rings, repeats * wide_count + 16, coarse_lons), jnp.int16),
+            jax.ShapeDtypeStruct((sides, levels_here, row_count, col_count), jnp.float32),
+        ],
         in_specs=[scalars] + [whole] * 4,
+        out_specs=[whole] * 2,
+        compiler_params=roomy,
+    )(where_side, adjoint_all, jnp.transpose(lon_matrix), perturbations, other_members)
+    by_pair = swapped(projected, "lat_0", 0)
+    full = pl.pallas_call(
+        functools.partial(gather_kernel, (members_here * peers - 1) ** -0.5),
+        out_shape=jax.ShapeDtypeStruct((bands, repeats, coarse_rows, coarse_lons), jnp.float32),
+        in_specs=[whole] * 2,
         out_specs=whole,
         compiler_params=roomy,
-    )(where_side, adjoint_all, jnp.transpose(lon_matrix), perturbations, other_members)
-    projected, own = lax.optimization_barrier((projected, own))
-    by_pair = projected.reshape(rings, pairs // rings, wide_count, coarse_lons)
-    by_pair = swapped(by_pair, "lat_0", 0)
-    full = jnp.einsum(
-        "zqrw,zrc->qcw", by_pair, lat_all.astype(jnp.float32), precision=highest
-    )
-    full = full.reshape(pairs // rings, bands, coarse_rows, coarse_lons)
-    full = swapped(jnp.transpose(full, (1, 0, 2, 3)), LAT, 0)
+    )(by_pair, lat_all)
+    full = swapped(full, LAT, 0)
     full = full.reshape(
         members_here, rings // members_here, sides, pairs // rings, coarse_rows, coarse_lons
     )
     full = jnp.transpose(full, (4, 0, 2, 1, 3, 5)).reshape(coarse_weights.shape)
-    gradient = full * member_scale + coarse_weights.astype(jnp.float32)
-
-    tiles = jnp.transpose(own.reshape(own_rows, peers, col_count), (1, 0, 2))
-    tiles = swapped(tiles, "mem", 0).reshape(levels_here, sides, row_count, col_count)
-    kept = jnp.where(first, tiles[:, 0], tiles[:, 1])
-    sent = jnp.where(first, tiles[:, 1], tiles[:, 0])
+    gradient = full + coarse_weights.astype(jnp.float32)
+
+    kept = jnp.where(first, tiles[0], tiles[1])
+    sent = jnp.where(first, tiles[1], tiles[0])
     increment = in_order(kept, lax.ppermute(sent, "lat_1", across), 0)
     return (gradient, increment)
 

time: 196 us -> 166 us (0.85)
  waiting for transfers between devices: 90.9 us -> 49.3 us
  local copies, waits for them, and re-layouts: 22.4 us -> 33 us
  starting transfers between devices: 59.2 us -> 61.3 us
    all_to_all x6 -> x5, waiting for transfers between devices: 63.1 us -> 34.7 us  [swapped(): lax.all_to_all(value, axis, split_axis=dim, concat_axis=dim, tiled=True)]
    unnamed x65 -> x39, local copies, waits for them, and re-layouts: 10.2 us -> 17.5 us
    ppermute x4, waiting for transfers between devices: 10 us -> 4.17 us  [body(): rising = lax.ppermute(rising, 'lat_0', up)]
    ppermute x1, waiting for transfers between devices: 11.1 us -> 6.48 us  [body(): other_members = lax.ppermute(other_members, 'lat_1', across)]
    ppermute x3, starting transfers between devices: 8.92 us -> 12.4 us  [body(): falling = lax.ppermute(falling, 'lat_0', down)]
    ppermute x3, waiting for transfers between devices: 2.4 us -> 0.01 us  [body(): falling = lax.ppermute(falling, 'lat_0', down)]
    ppermute x4, starting transfers between devices: 2.28 us -> 0.01 us  [body(): rising = lax.ppermute(rising, 'lat_0', up)]
    all_to_all x6 -> x5, starting transfers between devices: 30.6 us -> 28.5 us  [swapped(): lax.all_to_all(value, axis, split_axis=dim, concat_axis=dim, tiled=True)]
  transfers between devices with their start and end apart: 21 -> 20, of which waited for: 13 -> 11; matrix products, arithmetic and copies ran while one was open for 10% -> 20% of each run, Pallas kernels for 3% -> 3%
where the time goes in v5:
time: 166 us; the launch traced here: 164 us
  starting transfers between devices  61.3 us (37%)
  waiting for transfers between devices  49.3 us (30%)
  local copies, waits for them, and re-layouts  33 us (20%)
  Pallas kernels  10.4 us (6%)
  other arithmetic  8.97 us (5%)
    all_to_all x5, waiting for transfers between devices, swapped(): lax.all_to_all(value, axis, split_axis=dim, concat_axis=dim, tiled=True)  34.7 us
    all_to_all x5, starting transfers between devices, swapped(): lax.all_to_all(value, axis, split_axis=dim, concat_axis=dim, tiled=True)  28.5 us
    unnamed x39, local copies, waits for them, and re-layouts  17.5 us
    ppermute x3, starting transfers between devices, body(): falling = lax.ppermute(falling, 'lat_0', down)  12.4 us
    ppermute x1, waiting for transfers between devices, body(): other_members = lax.ppermute(other_members, 'lat_1', across)  6.48 us
    slice x8, local copies, waits for them, and re-layouts, lat_of(): block[sides * weight_rows:].reshape(sides, row_count // 2, coarse_lons)  5.75 us
    ppermute x4, waiting for transfers between devices, body(): rising = lax.ppermute(rising, 'lat_0', up)  4.17 us
    ppermute x1, starting transfers between devices, body(): after = lax.ppermute(own[:HALO], ALL, backward)  3.72 us
  transfers between devices with their start and end apart: 20, of which 11 were waited for; matrix products, arithmetic and copies ran while one was open for 20% of the time, Pallas kernels for 3%

profile of v5, /device:TPU:2, one launch (start us, length us, event | category | flops | bytes accessed | tf_op | source)
XLA Modules:
  0.0 164.0 jit_solution(18068299414053520950)
XLA Ops:
  2.5 2.2 %collective-permute-start = (bf16[144,256]{1,0:T(8,128)(2,1)S(1)}, bf16[144,256]{1,0:T(8,128)(2,1)S(1)}, u32[]{:S(2)}, u32[]{:S(2)}) collective-permute-start(bf16[144,256]{1,0:T(8,128)(2,1)S(1)} %maximum_maximum_fusion), channel_id=1, source_target_pairs={{0,1},{1,0},{2,3},{3,2},{4,5},{5,4},{6,7},{7,6},{8,9},{9,8},{10,11... | collective-permute-start | bytes 221192 | tf_op jit(solution)/shard_map/ppermute | solution.py:350
  9.1 5.9 %collective-permute-start.2 = (bf16[288,256]{1,0:T(8,128)(2,1)}, bf16[288,256]{1,0:T(8,128)(2,1)}, u32[]{:S(2)}, u32[]{:S(2)}) collective-permute-start(bf16[288,256]{1,0:T(8,128)(2,1)} %pad_maximum_fusion.refs_0_), channel_id=1, source_target_pairs={{2,0},{4,2},{6,4},{8,6},{10,8},{12,10},{14,12},{0,14},{3,1},{5,3},... | collective-permute-start | bytes 442376 | tf_op jit(solution)/shard_map/ppermute | solution.py:387
  15.8 5.9 %all-to-all-start = ((f32[16,3,16,128]{3,2,1,0:T(8,128)}), f32[16,3,16,128]{3,2,1,0:T(8,128)S(1)}, u32[]{:S(2)}, u32[]{:S(2)}) async-start(f32[16,3,16,128]{3,2,1,0:T(8,128)} %bitcast.18), calls=%async_computation | async-start | bytes 786432 | tf_op jit(solution)/shard_map/all_to_all | solution.py:20
  22.9 2.1 %collective-permute-start.1 = (bf16[4,4,32,1024]{3,2,1,0:T(8,128)(2,1)}, bf16[4,4,32,1024]{3,2,1,0:T(8,128)(2,1)S(1)}, u32[]{:S(2)}, u32[]{:S(2)}) collective-permute-start(bf16[4,4,32,1024]{3,2,1,0:T(8,128)(2,1)} %constant_dynamic-slice_fusion.1), channel_id=1, source_target_pairs={{0,1},{1,0},{2,3},{3,2},{4,5},{5,4},{6,7},{7,6},{8,9},{9,8},{10,11... | collective-permute-start | bytes 3145736 | tf_op jit(solution)/shard_map/ppermute | solution.py:379
  25.0 3.3 %collective-permute-start.5 = (bf16[288,256]{1,0:T(8,128)(2,1)}, bf16[288,256]{1,0:T(8,128)(2,1)}, u32[]{:S(2)}, u32[]{:S(2)}) collective-permute-start(bf16[288,256]{1,0:T(8,128)(2,1)} %collective-permute-done.2.refs_1_), channel_id=1, source_target_pairs={{2,0},{4,2},{6,4},{8,6},{10,8},{12,10},{14,12},{0,14},{3,1},{5,3},... | collective-permute-start | bytes 442376 | tf_op jit(solution)/shard_map/ppermute | solution.py:387
  29.0 2.1 %copy.50 = bf16[256,1024]{0,1:T(8,128)(2,1)} copy(bf16[256,1024]{1,0:T(8,128)(2,1)} %lon_ref.1) | data formatting | bytes 1048576 | tf_op args[3]
  33.2 1.4 collective-permute-start.9
  34.6 3.2 %collective-permute-start.6 = (bf16[288,256]{1,0:T(8,128)(2,1)}, bf16[288,256]{1,0:T(8,128)(2,1)}, u32[]{:S(2)}, u32[]{:S(2)}) collective-permute-start(bf16[288,256]{1,0:T(8,128)(2,1)} %collective-permute-done.5.refs_2_), channel_id=1, source_target_pairs={{2,0},{4,2},{6,4},{8,6},{10,8},{12,10},{14,12},{0,14},{3,1},{5,3},... | collective-permute-start | bytes 442376 | tf_op jit(solution)/shard_map/ppermute | solution.py:387
  39.9 1.6 reshape_squeeze_reshape.3
  41.4 1.4 fusion
  43.7 2.1 %collective-permute-done.8.refs_4_ = bf16[288,256]{1,0:T(8,128)(2,1)} collective-permute-done((bf16[288,256]{1,0:T(8,128)(2,1)}, bf16[288,256]{1,0:T(8,128)(2,1)}, u32[]{:S(2)}, u32[]{:S(2)}) %collective-permute-start.8) | collective-permute-done | bytes 147488 | tf_op jit(solution)/shard_map/ppermute | solution.py:385
  45.8 6.5 %collective-permute-done.1.other_ref = bf16[4,4,32,1024]{3,2,1,0:T(8,128)(2,1)S(1)} collective-permute-done((bf16[4,4,32,1024]{3,2,1,0:T(8,128)(2,1)}, bf16[4,4,32,1024]{3,2,1,0:T(8,128)(2,1)S(1)}, u32[]{:S(2)}, u32[]{:S(2)}) %collective-permute-start.1) | collective-permute-done | bytes 1048608 | tf_op jit(solution)/shard_map/ppermute | solution.py:379
  53.3 3.6 %shard_map.95 = f32[16,16,1024]{2,1,0:T(8,128)S(1)} custom-call(s32[1]{0:T(128)} %bitcast.side_ref, bf16[64,128]{1,0:T(8,128)(2,1)S(1)} %copy.49.columns_ref, bf16[256,1024]{1,0:T(8,128)(2,1)S(1)} %copy-done.5, bf16[4,8,32,1024]{3,2,1,0:T(8,128)(2,1)S(1)} %copy-done, bf16[4,4,32,1024]{3,2,1,0:T(8,128)(2,1)S(1)} %collective-permute-done.1.other_ref, ...), custom_call_target="tpu_custom_call" | custom-call | tf_op jit(solution)/shard_map/pallas_call | solution.py:410
  57.9 5.7 %all-to-all-start.1 = ((f32[16,16,1024]{2,1,0:T(8,128)}), f32[16,16,1024]{2,1,0:T(8,128)}, u32[]{:S(2)}, u32[]{:S(2)}) async-start(f32[16,16,1024]{2,1,0:T(8,128)} %copy-done.4), calls=%async_computation.1 | async-start | bytes 2097152 | tf_op jit(solution)/shard_map/all_to_all | solution.py:20
  63.6 1.4 shard_map.96.local_ref
  65.1 2.1 %collective-permute-start.12 = (f32[8,3584]{1,0:T(8,128)S(1)}, f32[8,3584]{1,0:T(8,128)S(1)}, u32[]{:S(2)}, u32[]{:S(2)}) collective-permute-start(f32[8,3584]{1,0:T(8,128)S(1)} %get-tuple-element.45), channel_id=1, source_target_pairs={{0,16},{1,17},{2,18},{3,19},{4,20},{5,21},{6,22},{7,23},{8,24},{9,... | collective-permute-start | bytes 344072 | tf_op jit(solution)/shard_map/ppermute | solution.py:445
  67.2 3.5 %collective-permute-start.13 = (f32[8,3584]{1,0:T(8,128)S(1)}, f32[8,3584]{1,0:T(8,128)S(1)}, u32[]{:S(2)}, u32[]{:S(2)}) collective-permute-start(f32[8,3584]{1,0:T(8,128)S(1)} %get-tuple-element.44), channel_id=1, source_target_pairs={{16,0},{17,1},{18,2},{19,3},{20,4},{21,5},{22,6},{23,7},{24,8},{25... | collective-permute-start | bytes 344072 | tf_op jit(solution)/shard_map/ppermute | solution.py:446
  77.5 1.6 all-to-all-done.1
  79.1 1.3 reduce_sum.9
  80.4 2.0 %collective-permute-start.10 = (f32[8,1024]{1,0:T(8,128)S(1)}, f32[8,1024]{1,0:T(8,128)S(1)}, u32[]{:S(2)}, u32[]{:S(2)}) collective-permute-start(f32[8,1024]{1,0:T(8,128)S(1)} %get-tuple-element.53), channel_id=1, source_target_pairs={{0,16},{1,17},{2,18},{3,19},{4,20},{5,21},{6,22},{7,23},{8,24},{9,... | collective-permute-start | bytes 98312 | tf_op jit(solution)/shard_map/ppermute | solution.py:461
  82.4 3.7 %collective-permute-start.11 = (f32[8,1024]{1,0:T(8,128)S(1)}, f32[8,1024]{1,0:T(8,128)S(1)}, u32[]{:S(2)}, u32[]{:S(2)}) collective-permute-start(f32[8,1024]{1,0:T(8,128)S(1)} %get-tuple-element.52), channel_id=1, source_target_pairs={{16,0},{17,1},{18,2},{19,3},{20,4},{21,5},{22,6},{23,7},{24,8},{25... | collective-permute-start | bytes 98312 | tf_op jit(solution)/shard_map/ppermute | solution.py:462
  87.5 1.7 %shard_map.98 = f32[16,136,128]{2,1,0:T(8,128)S(1)} custom-call(s32[2]{0:T(128)S(1)} %copy-done.9, f32[16,1024]{1,0:T(8,128)S(1)} %broadcast_multiply_fusion.own_ref, f32[8,1024]{1,0:T(8,128)S(1)} %collective-permute-done.10.before_ref, f32[8,1024]{1,0:T(8,128)S(1)} %collective-permute-done.11.after_ref, f32[2,32,1024]{2,1,0:T(8,128)S(1)} %get-tuple-element.29.wind_ref, ...), custom_call_target="tpu_custom_call" | custom-call | tf_op jit(solution)/shard_map/pallas_call | solution.py:466
  90.3 5.7 %all-to-all-start.2 = ((f32[16,136,128]{2,1,0:T(8,128)}), f32[16,136,128]{2,1,0:T(8,128)S(1)}, u32[]{:S(2)}, u32[]{:S(2)}) async-start(f32[16,136,128]{2,1,0:T(8,128)} %copy-done.1), calls=%async_computation.2 | async-start | bytes 2228224 | tf_op jit(solution)/shard_map/all_to_all | solution.py:20
  99.3 12.8 %all-to-all-done.2.adjoint_ref = f32[16,136,128]{2,1,0:T(8,128)S(1)} async-done(((f32[16,136,128]{2,1,0:T(8,128)}), f32[16,136,128]{2,1,0:T(8,128)S(1)}, u32[]{:S(2)}, u32[]{:S(2)}) %all-to-all-start.2) | async-done | bytes 1114144 | tf_op jit(solution)/shard_map/all_to_all | solution.py:20
  114.3 1.7 %shard_map.99 = (s16[8,144,256]{2,1,0:T(8,128)(2,1)S(1)}, f32[2,4,32,64]{3,2,1,0:T(8,128)S(1)}) custom-call(s32[1]{0:T(128)} %bitcast.side_ref, f32[16,136,128]{2,1,0:T(8,128)S(1)} %all-to-all-done.2.adjoint_ref, bf16[1024,256]{1,0:T(8,128)(2,1)S(1)} %bitcast.88, bf16[4,8,32,1024]{3,2,1,0:T(8,128)(2,1)S(1)} %copy-done, bf16[4,4,32,1024]{3,2,1,0:T(8,128)(2,1)S(1)} %copy-done.3), custom_call_target="tpu_custom_call" | custom-call | tf_op jit(solution)/shard_map/pallas_call | solution.py:475
  116.8 7.6 %all-to-all-start.3 = ((s16[8,144,256]{2,1,0:T(8,128)(2,1)}), s16[8,144,256]{2,1,0:T(8,128)(2,1)S(1)}, u32[]{:S(2)}, u32[]{:S(2)}) async-start(s16[8,144,256]{2,1,0:T(8,128)(2,1)} %copy-done.7), calls=%async_computation.3 | async-start | bytes 1179648 | tf_op jit(solution)/shard_map/all_to_all | solution.py:20
  131.0 12.6 %all-to-all-done.3.message_ref = s16[8,144,256]{2,1,0:T(8,128)(2,1)S(1)} async-done(((s16[8,144,256]{2,1,0:T(8,128)(2,1)}), s16[8,144,256]{2,1,0:T(8,128)(2,1)S(1)}, u32[]{:S(2)}, u32[]{:S(2)}) %all-to-all-start.3) | async-done | bytes 589856 | tf_op jit(solution)/shard_map/all_to_all | solution.py:20
  143.5 1.4 shard_map.100
  144.9 3.5 %all-to-all-start.4 = ((f32[16,2,8,256]{3,2,1,0:T(8,128)}), f32[16,2,8,256]{3,2,1,0:T(8,128)S(1)}, u32[]{:S(2)}, u32[]{:S(2)}) async-start(f32[16,2,8,256]{3,2,1,0:T(8,128)} %shard_map.100), calls=%async_computation.4 | async-start | bytes 524288 | tf_op jit(solution)/shard_map/all_to_all | solution.py:20
  148.5 3.4 %collective-permute-start.14 = (f32[4,32,64]{2,1,0:T(8,128)S(1)}, f32[4,32,64]{2,1,0:T(8,128)S(1)}, u32[]{:S(2)}, u32[]{:S(2)}) collective-permute-start(f32[4,32,64]{2,1,0:T(8,128)S(1)} %get-tuple-element.47), channel_id=1, source_target_pairs={{0,1},{1,0},{2,3},{3,2},{4,5},{5,4},{6,7},{7,6},{8,9},{9,8},{10,11... | collective-permute-start | bytes 98312 | tf_op jit(solution)/shard_map/ppermute | solution.py:502
  151.9 2.5 %collective-permute-done.14 = f32[4,32,64]{2,1,0:T(8,128)S(1)} collective-permute-done((f32[4,32,64]{2,1,0:T(8,128)S(1)}, f32[4,32,64]{2,1,0:T(8,128)S(1)}, u32[]{:S(2)}, u32[]{:S(2)}) %collective-permute-start.14) | collective-permute-done | bytes 32800 | tf_op jit(solution)/shard_map/ppermute | solution.py:502
  155.1 7.8 %all-to-all-done.4 = f32[16,2,8,256]{3,2,1,0:T(8,128)S(1)} async-done(((f32[16,2,8,256]{3,2,1,0:T(8,128)}), f32[16,2,8,256]{3,2,1,0:T(8,128)S(1)}, u32[]{:S(2)}, u32[]{:S(2)}) %all-to-all-start.4) | async-done | bytes 262176 | tf_op jit(solution)/shard_map/all_to_all | solution.py:20
  (119 shorter events, 39.7 us)
Async XLA Ops:
  2.5 5.9 %collective-permute-start = (bf16[144,256]{1,0:T(8,128)(2,1)S(1)}, bf16[144,256]{1,0:T(8,128)(2,1)S(1)}, u32[]{:S(2)}, u32[]{:S(2)}) collective-permute-start(bf16[144,256]{1,0:T(8,128)(2,1)S(1)} %maximum_maximum_fusion), channel_id=1, source_target_pairs={{0,1},{1,0},{2,3},{3,2},{4,5},{5,4},{6,7},{7,6},{8,9},{9,8},{10,11... | collective-permute-start | bytes 221192 | tf_op jit(solution)/shard_map/ppermute | solution.py:350
  6.5 15.3 %copy-start = (bf16[4,8,32,1024]{3,2,1,0:T(8,128)(2,1)S(1)}, bf16[4,8,32,1024]{3,2,1,0:T(8,128)(2,1)}, u32[]{:S(2)}) copy-start(bf16[4,8,32,1024]{3,2,1,0:T(8,128)(2,1)} %own_ref.3) | copy-start | bytes 6291460
  9.1 15.9 %collective-permute-start.2 = (bf16[288,256]{1,0:T(8,128)(2,1)}, bf16[288,256]{1,0:T(8,128)(2,1)}, u32[]{:S(2)}, u32[]{:S(2)}) collective-permute-start(bf16[288,256]{1,0:T(8,128)(2,1)} %pad_maximum_fusion.refs_0_), channel_id=1, source_target_pairs={{2,0},{4,2},{6,4},{8,6},{10,8},{12,10},{14,12},{0,14},{3,1},{5,3},... | collective-permute-start | bytes 442376 | tf_op jit(solution)/shard_map/ppermute | solution.py:387
  15.0 10.0 %collective-permute-start.3 = (bf16[288,256]{1,0:T(8,128)(2,1)}, bf16[288,256]{1,0:T(8,128)(2,1)}, u32[]{:S(2)}, u32[]{:S(2)}) collective-permute-start(bf16[288,256]{1,0:T(8,128)(2,1)} %pad_maximum_fusion.refs_0_), channel_id=1, source_target_pairs={{0,2},{2,4},{4,6},{6,8},{8,10},{10,12},{12,14},{14,0},{1,3},{3,5},... | collective-permute-start | bytes 442376 | tf_op jit(solution)/shard_map/ppermute | solution.py:385
  15.8 16.6 %all-to-all-start = ((f32[16,3,16,128]{3,2,1,0:T(8,128)}), f32[16,3,16,128]{3,2,1,0:T(8,128)S(1)}, u32[]{:S(2)}, u32[]{:S(2)}) async-start(f32[16,3,16,128]{3,2,1,0:T(8,128)} %bitcast.18), calls=%async_computation | async-start | bytes 786432 | tf_op jit(solution)/shard_map/all_to_all | solution.py:20
  22.9 29.4 %collective-permute-start.1 = (bf16[4,4,32,1024]{3,2,1,0:T(8,128)(2,1)}, bf16[4,4,32,1024]{3,2,1,0:T(8,128)(2,1)S(1)}, u32[]{:S(2)}, u32[]{:S(2)}) collective-permute-start(bf16[4,4,32,1024]{3,2,1,0:T(8,128)(2,1)} %constant_dynamic-slice_fusion.1), channel_id=1, source_target_pairs={{0,1},{1,0},{2,3},{3,2},{4,5},{5,4},{6,7},{7,6},{8,9},{9,8},{10,11... | collective-permute-start | bytes 3145736 | tf_op jit(solution)/shard_map/ppermute | solution.py:379
  25.0 7.4 %collective-permute-start.4 = (bf16[288,256]{1,0:T(8,128)(2,1)}, bf16[288,256]{1,0:T(8,128)(2,1)}, u32[]{:S(2)}, u32[]{:S(2)}) collective-permute-start(bf16[288,256]{1,0:T(8,128)(2,1)} %collective-permute-done.3.refs_7_), channel_id=1, source_target_pairs={{0,2},{2,4},{4,6},{6,8},{8,10},{10,12},{12,14},{14,0},{1,3},{3,5},... | collective-permute-start | bytes 442376 | tf_op jit(solution)/shard_map/ppermute | solution.py:385
  25.0 7.4 %collective-permute-start.5 = (bf16[288,256]{1,0:T(8,128)(2,1)}, bf16[288,256]{1,0:T(8,128)(2,1)}, u32[]{:S(2)}, u32[]{:S(2)}) collective-permute-start(bf16[288,256]{1,0:T(8,128)(2,1)} %collective-permute-done.2.refs_1_), channel_id=1, source_target_pairs={{2,0},{4,2},{6,4},{8,6},{10,8},{12,10},{14,12},{0,14},{3,1},{5,3},... | collective-permute-start | bytes 442376 | tf_op jit(solution)/shard_map/ppermute | solution.py:387
  32.4 6.7 %collective-permute-start.7 = (bf16[288,256]{1,0:T(8,128)(2,1)}, bf16[288,256]{1,0:T(8,128)(2,1)}, u32[]{:S(2)}, u32[]{:S(2)}) collective-permute-start(bf16[288,256]{1,0:T(8,128)(2,1)} %collective-permute-done.4.refs_6_), channel_id=1, source_target_pairs={{0,2},{2,4},{4,6},{6,8},{8,10},{10,12},{12,14},{14,0},{1,3},{3,5},... | collective-permute-start | bytes 442376 | tf_op jit(solution)/shard_map/ppermute | solution.py:385
  33.2 24.7 %collective-permute-start.9 = (f32[16,2,16,128]{3,2,1,0:T(8,128)}, f32[16,2,16,128]{3,2,1,0:T(8,128)}, u32[]{:S(2)}, u32[]{:S(2)}) collective-permute-start(f32[16,2,16,128]{3,2,1,0:T(8,128)} %maximum_select_fusion), channel_id=1, source_target_pairs={{0,1},{1,0},{2,3},{3,2},{4,5},{5,4},{6,7},{7,6},{8,9},{9,8},{10,11... | collective-permute-start | bytes 786440 | tf_op jit(solution)/shard_map/ppermute | solution.py:391
  34.6 9.0 %collective-permute-start.6 = (bf16[288,256]{1,0:T(8,128)(2,1)}, bf16[288,256]{1,0:T(8,128)(2,1)}, u32[]{:S(2)}, u32[]{:S(2)}) collective-permute-start(bf16[288,256]{1,0:T(8,128)(2,1)} %collective-permute-done.5.refs_2_), channel_id=1, source_target_pairs={{2,0},{4,2},{6,4},{8,6},{10,8},{12,10},{14,12},{0,14},{3,1},{5,3},... | collective-permute-start | bytes 442376 | tf_op jit(solution)/shard_map/ppermute | solution.py:387
  39.1 6.7 %collective-permute-start.8 = (bf16[288,256]{1,0:T(8,128)(2,1)}, bf16[288,256]{1,0:T(8,128)(2,1)}, u32[]{:S(2)}, u32[]{:S(2)}) collective-permute-start(bf16[288,256]{1,0:T(8,128)(2,1)} %collective-permute-done.7.refs_5_), channel_id=1, source_target_pairs={{0,2},{2,4},{4,6},{6,8},{8,10},{10,12},{12,14},{14,0},{1,3},{3,5},... | collective-permute-start | bytes 442376 | tf_op jit(solution)/shard_map/ppermute | solution.py:385
  52.3 1.0 copy-start.5
  53.3 3.6 %copy-start.2 = (bf16[4,4,32,1024]{3,2,1,0:T(8,128)(2,1)}, bf16[4,4,32,1024]{3,2,1,0:T(8,128)(2,1)S(1)}, u32[]{:S(2)}) copy-start(bf16[4,4,32,1024]{3,2,1,0:T(8,128)(2,1)S(1)} %collective-permute-done.1.other_ref) | copy-start | bytes 3145732
  56.9 1.0 copy-start.4
  57.9 5.7 %copy-start.8 = (s32[2]{0:T(128)S(1)}, s32[2]{0:T(128)}, u32[]{:S(2)}) copy-start(s32[2]{0:T(128)} %pad_add_fusion.1.side_ref) | copy-start | bytes 28
  57.9 21.2 %all-to-all-start.1 = ((f32[16,16,1024]{2,1,0:T(8,128)}), f32[16,16,1024]{2,1,0:T(8,128)}, u32[]{:S(2)}, u32[]{:S(2)}) async-start(f32[16,16,1024]{2,1,0:T(8,128)} %copy-done.4), calls=%async_computation.1 | async-start | bytes 2097152 | tf_op jit(solution)/shard_map/all_to_all | solution.py:20
  63.6 23.9 %copy-start.9 = (s32[2]{0:T(128)S(1)}, s32[2]{0:T(128)}, u32[]{:S(2)}) copy-start(s32[2]{0:T(128)} %pad_add_fusion.place_ref) | copy-start | bytes 28
  65.1 21.1 %collective-permute-start.12 = (f32[8,3584]{1,0:T(8,128)S(1)}, f32[8,3584]{1,0:T(8,128)S(1)}, u32[]{:S(2)}, u32[]{:S(2)}) collective-permute-start(f32[8,3584]{1,0:T(8,128)S(1)} %get-tuple-element.45), channel_id=1, source_target_pairs={{0,16},{1,17},{2,18},{3,19},{4,20},{5,21},{6,22},{7,23},{8,24},{9,... | collective-permute-start | bytes 344072 | tf_op jit(solution)/shard_map/ppermute | solution.py:445
  67.2 19.0 %collective-permute-start.13 = (f32[8,3584]{1,0:T(8,128)S(1)}, f32[8,3584]{1,0:T(8,128)S(1)}, u32[]{:S(2)}, u32[]{:S(2)}) collective-permute-start(f32[8,3584]{1,0:T(8,128)S(1)} %get-tuple-element.44), channel_id=1, source_target_pairs={{16,0},{17,1},{18,2},{19,3},{20,4},{21,5},{22,6},{23,7},{24,8},{25... | collective-permute-start | bytes 344072 | tf_op jit(solution)/shard_map/ppermute | solution.py:446
  80.4 6.4 %collective-permute-start.10 = (f32[8,1024]{1,0:T(8,128)S(1)}, f32[8,1024]{1,0:T(8,128)S(1)}, u32[]{:S(2)}, u32[]{:S(2)}) collective-permute-start(f32[8,1024]{1,0:T(8,128)S(1)} %get-tuple-element.53), channel_id=1, source_target_pairs={{0,16},{1,17},{2,18},{3,19},{4,20},{5,21},{6,22},{7,23},{8,24},{9,... | collective-permute-start | bytes 98312 | tf_op jit(solution)/shard_map/ppermute | solution.py:461
  82.4 5.1 %collective-permute-start.11 = (f32[8,1024]{1,0:T(8,128)S(1)}, f32[8,1024]{1,0:T(8,128)S(1)}, u32[]{:S(2)}, u32[]{:S(2)}) collective-permute-start(f32[8,1024]{1,0:T(8,128)S(1)} %get-tuple-element.52), channel_id=1, source_target_pairs={{16,0},{17,1},{18,2},{19,3},{20,4},{21,5},{22,6},{23,7},{24,8},{25... | collective-permute-start | bytes 98312 | tf_op jit(solution)/shard_map/ppermute | solution.py:462
  89.3 1.0 copy-start.1
  90.3 21.8 %all-to-all-start.2 = ((f32[16,136,128]{2,1,0:T(8,128)}), f32[16,136,128]{2,1,0:T(8,128)S(1)}, u32[]{:S(2)}, u32[]{:S(2)}) async-start(f32[16,136,128]{2,1,0:T(8,128)} %copy-done.1), calls=%async_computation.2 | async-start | bytes 2228224 | tf_op jit(solution)/shard_map/all_to_all | solution.py:20
  112.0 1.2 copy-start.3
  113.3 1.0 copy-start.6
  116.0 0.8 copy-start.7
  116.8 26.7 %all-to-all-start.3 = ((s16[8,144,256]{2,1,0:T(8,128)(2,1)}), s16[8,144,256]{2,1,0:T(8,128)(2,1)S(1)}, u32[]{:S(2)}, u32[]{:S(2)}) async-start(s16[8,144,256]{2,1,0:T(8,128)(2,1)} %copy-done.7), calls=%async_computation.3 | async-start | bytes 1179648 | tf_op jit(solution)/shard_map/all_to_all | solution.py:20
  130.7 32.5 %copy-start.10 = (bf16[8,4,8,256]{3,2,1,0:T(8,128)(2,1)S(1)}, bf16[8,4,8,256]{3,2,1,0:T(8,128)(2,1)}, u32[]{:S(2)}) copy-start(bf16[8,4,8,256]{3,2,1,0:T(8,128)(2,1)} %param.8) | copy-start | bytes 393220
  144.9 17.9 %all-to-all-start.4 = ((f32[16,2,8,256]{3,2,1,0:T(8,128)}), f32[16,2,8,256]{3,2,1,0:T(8,128)S(1)}, u32[]{:S(2)}, u32[]{:S(2)}) async-start(f32[16,2,8,256]{3,2,1,0:T(8,128)} %shard_map.100), calls=%async_computation.4 | async-start | bytes 524288 | tf_op jit(solution)/shard_map/all_to_all | solution.py:20
  148.5 5.9 %collective-permute-start.14 = (f32[4,32,64]{2,1,0:T(8,128)S(1)}, f32[4,32,64]{2,1,0:T(8,128)S(1)}, u32[]{:S(2)}, u32[]{:S(2)}) collective-permute-start(f32[4,32,64]{2,1,0:T(8,128)S(1)} %get-tuple-element.47), channel_id=1, source_target_pairs={{0,1},{1,0},{2,3},{3,2},{4,5},{5,4},{6,7},{7,6},{8,9},{9,8},{10,11... | collective-permute-start | bytes 98312 | tf_op jit(solution)/shard_map/ppermute | solution.py:502

commit v6 on v5

--- a/solution.py
+++ b/solution.py
@@ -30,102 +30,203 @@
     return jnp.dot(a, b, preferred_element_type=jnp.float32)
 
 
+def dot_last(a, b):
+    return lax.dot_general(a, b, (((1,), (1,)), ((), ())), preferred_element_type=jnp.float32)
+
+
+def row_codes(value):
+    largest = jnp.maximum(jnp.max(jnp.abs(value), axis=1, keepdims=True), 1e-30)
+    return jnp.ceil(jnp.log(largest) * (256.0 / LN2)) + 1.0
+
+
+def code_scale(codes):
+    return jnp.exp(codes * (LN2 / 256.0))
+
+
+def rounded(value, codes):
+    return jnp.round(value * (STEPS_16 / code_scale(codes)))
+
+
+def to_16(value):
+    return value.astype(jnp.int32).astype(jnp.int16)
+
+
+def from_16(value):
+    return value.astype(jnp.int32).astype(jnp.float32)
+
+
+def as_tiles(value):
+    rows, cols = value.shape
+    return jnp.concatenate(
+        [
+            value[t * 8 : (t + 1) * 8, at * 128 : (at + 1) * 128]
+            for t in range(rows // 8)
+            for at in range(cols // 128)
+        ],
+        axis=0,
+    )
+
+
+def from_tiles(value, row_tiles):
+    lane_tiles = value.shape[0] // 8 // row_tiles
+    rows = []
+    for t in range(row_tiles):
+        start = t * lane_tiles * 8
+        strips = [value[start + at * 8 : start + (at + 1) * 8] for at in range(lane_tiles)]
+        rows.append(jnp.concatenate(strips, axis=1))
+    return jnp.concatenate(rows, axis=0)
+
+
+def tile_scales(codes, lane_tiles):
+    scales = code_scale(codes) * (1.0 / STEPS_16)
+    parts = []
+    for t in range(scales.shape[0] // 8):
+        parts += [scales[t * 8 : (t + 1) * 8]] * lane_tiles
+    return jnp.concatenate(parts, axis=0)
+
+
+def load_members(side, own_hbm, other_hbm, own_ref, other_ref, sems):
+    levels_here = other_hbm.shape[1]
+    copies = []
+    for level in range(levels_here):
+        pair = (
+            pltpu.make_async_copy(
+                own_hbm.at[:, side * levels_here + level], own_ref.at[:, level], sems.at[2 * level]
+            ),
+            pltpu.make_async_copy(
+                other_hbm.at[:, level], other_ref.at[:, level], sems.at[2 * level + 1]
+            ),
+        )
+        for copy in pair:
+            copy.start()
+        copies.append(pair)
+    return copies
+
+
 def member_rows(side, own_ref, other_ref, member, level):
-    levels_here = other_ref.shape[1]
-    own = own_ref[member, side * levels_here + level].astype(jnp.float32)
+    own = own_ref[member, level].astype(jnp.float32)
     other = other_ref[member, level].astype(jnp.float32)
     low = jnp.where(side == 0, own, other)
     high = jnp.where(side == 0, other, own)
     return jnp.concatenate([low, high], axis=0)
 
 
-def localize_kernel(side_ref, columns_ref, lon_ref, own_ref, other_ref, *refs):
-    block_refs, sum_ref = refs[:-1], refs[-1]
+def localize_kernel(side_ref, columns_ref, lon_hbm, own_hbm, other_hbm, *refs):
+    block_refs = refs[:-6]
+    out_hbm, lon_ref, own_ref, other_ref, out_ref, sems = refs[-6:]
     members, levels_here, row_count, lon_total = other_ref.shape
     tall = 2 * row_count
     side = side_ref[0]
+    lon_copy = pltpu.make_async_copy(lon_hbm, lon_ref, sems.at[3 * levels_here])
+    lon_copy.start()
+    loads = load_members(side, own_hbm, other_hbm, own_ref, other_ref, sems)
     per_block = columns_ref.shape[1] // len(block_refs)
     columns = columns_ref[...]
-    lon = lon_ref[...]
+    count = out_ref.shape[0] // levels_here
+    piece_rows = tall // count
+    data = piece_rows * lon_total // 128
+    stores = []
     for level in range(levels_here):
         narrow = []
         for member in range(members):
             start = (member * levels_here + level) * per_block
             weights = jnp.concatenate([ref[start : start + per_block] for ref in block_refs], axis=0)
             narrow.append(dot(columns, weights))
-        localized = dot(two_terms(jnp.concatenate(narrow, axis=0)), lon)
+        if level == 0:
+            lon_copy.wait()
+        localized = dot(two_terms(jnp.concatenate(narrow, axis=0)), lon_ref[...])
+        for copy in loads[level]:
+            copy.wait()
         total = None
         for member in range(members):
             at = member * tall
             term = localized[at : at + tall] + localized[at + members * tall : at + (members + 1) * tall]
             term = term * member_rows(side, own_ref, other_ref, member, level)
             total = term if total is None else total + term
-        count = sum_ref.shape[0] // levels_here
-        sum_ref[level * count : (level + 1) * count] = total.reshape(count, tall // count, lon_total)
-
-
-def row_codes(value):
-    largest = jnp.maximum(jnp.max(jnp.abs(value), axis=1, keepdims=True), 1e-30)
-    return jnp.ceil(jnp.log(largest) * (256.0 / LN2)) + 1.0
-
-
-def code_scale(codes):
-    return jnp.exp(codes * (LN2 / 256.0))
-
-
-def project_kernel(side_ref, adjoint_ref, lon_ref, own_ref, other_ref, out_ref, tile_ref):
+        codes = row_codes(total)
+        total = rounded(total, codes)
+        for piece in range(count):
+            part = slice(piece * piece_rows, (piece + 1) * piece_rows)
+            out_ref[level * count + piece, :data] = to_16(as_tiles(total[part]))
+            out_ref[level * count + piece, data:] = to_16(
+                jnp.broadcast_to(codes[part], (piece_rows, 128))
+            )
+        part = pl.ds(level * count, count)
+        store = pltpu.make_async_copy(
+            out_ref.at[part], out_hbm.at[part], sems.at[2 * levels_here + level]
+        )
+        store.start()
+        stores.append(store)
+    for store in stores:
+        store.wait()
+
+
+def add_kernel(scale, message_ref, out_ref):
+    sources, rows, _ = message_ref.shape
+    own_rows, lon_total = out_ref.shape
+    total = None
+    for source in range(sources):
+        value = from_16(message_ref[source, : rows - own_rows])
+        codes = from_16(message_ref[source, rows - own_rows :])
+        value = value * tile_scales(codes, lon_total // 128)
+        total = value if total is None else total + value
+    out_ref[...] = from_tiles(total, own_rows // 8) * scale
+
+
+def project_kernel(side_ref, message_ref, lon_hbm, own_hbm, other_hbm, out_hbm, tile_ref, lon_ref, own_ref, other_ref, out_ref, sems):
     members, levels_here, row_count, lon_total = other_ref.shape
     rings, _, coarse_lons = out_ref.shape
     tall = 2 * row_count
     side = side_ref[0]
-    lon = lon_ref[...]
-    quarters = adjoint_ref.shape[0] // levels_here
-    row_tiles = tall // quarters // 8
+    lon_copy = pltpu.make_async_copy(lon_hbm, lon_ref, sems.at[2 * levels_here])
+    lon_copy.start()
+    loads = load_members(side, own_hbm, other_hbm, own_ref, other_ref, sems)
+    quarters = message_ref.shape[0] // levels_here
+    own_rows = tall // quarters
     lane_tiles = lon_total // 128
+    data = own_rows * lane_tiles
     per_message = members * levels_here // rings
     row = lax.broadcasted_iota(jnp.int32, (tall, 128), 0)
     lane = lax.broadcasted_iota(jnp.int32, (tall, 128), 1)
     tails = [jnp.zeros((1, 128), jnp.float32) for _ in range(rings)]
+    width = tile_ref.shape[3]
     for level in range(levels_here):
-        strips = []
-        for at in range(lane_tiles):
-            strips.append(
-                jnp.concatenate(
-                    [
-                        adjoint_ref[
-                            level * quarters + q, (t * lane_tiles + at) * 8 : (t * lane_tiles + at + 1) * 8
-                        ]
-                        for q in range(quarters)
-                        for t in range(row_tiles)
-                    ],
-                    axis=0,
-                )
-            )
-        adjoint = jnp.concatenate(strips, axis=1)
+        pieces = []
+        for q in range(quarters):
+            value = from_16(message_ref[level * quarters + q, :data])
+            codes = from_16(message_ref[level * quarters + q, data : data + own_rows])
+            pieces.append(from_tiles(value * tile_scales(codes, lane_tiles), own_rows // 8))
+            tail = from_16(message_ref[level * quarters + q, data + own_rows :])
+            tile = tail[:8] * (code_scale(tail[8:]) * (1.0 / STEPS_16))
+            band, start = q * own_rows // row_count, q * own_rows % row_count
+            tile_ref[band, level, start : start + 8] = tile[:, :width]
+            tile_ref[band, level, start + 8 : start + 16] = tile[:, width:]
+        adjoint = jnp.concatenate(pieces, axis=0)
+        for copy in loads[level]:
+            copy.wait()
         product = [
             member_rows(side, own_ref, other_ref, member, level) * adjoint for member in range(members)
         ]
-        projected = dot(two_terms(jnp.concatenate(product, axis=0)), lon)
+        if level == 0:
+            lon_copy.wait()
+        projected = dot_last(two_terms(jnp.concatenate(product, axis=0)), lon_ref[...])
         for member in range(members):
             at = member * tall
             value = projected[at : at + tall] + projected[at + members * tall : at + (members + 1) * tall]
             pair = member * levels_here + level
             ring, place = pair // per_message, pair % per_message
             codes = row_codes(value)
-            whole = jnp.round(value * (STEPS_16 / code_scale(codes))).astype(jnp.int32)
-            out_ref[ring, place * tall : (place + 1) * tall] = whole.astype(jnp.int16)
+            out_ref[ring, place * tall : (place + 1) * tall] = to_16(rounded(value, codes))
             mark = jnp.where(lane == row + place * tall, codes, 0.0)
             tails[ring] = tails[ring] + jnp.sum(mark, axis=0, keepdims=True)
-        for q in range(quarters):
-            piece = adjoint_ref[level * quarters + q, row_tiles * lane_tiles * 8 :]
-            band, start = q * row_tiles * 8 // row_count, q * row_tiles * 8 % row_count
-            width = tile_ref.shape[3]
-            tile_ref[band, level, start : start + 8] = piece[:, :width]
-            tile_ref[band, level, start + 8 : start + 16] = piece[:, width:]
-    data = per_message * tall
+    stores = []
     for ring in range(rings):
-        tail = jnp.broadcast_to(tails[ring], (16, 128)).astype(jnp.int32).astype(jnp.int16)
-        out_ref[ring, data : data + 16] = jnp.concatenate([tail] * (coarse_lons // 128), axis=1)
+        tail = to_16(jnp.broadcast_to(tails[ring], (16, 128)))
+        start = per_message * tall
+        out_ref[ring, start : start + 16] = jnp.concatenate([tail] * (coarse_lons // 128), axis=1)
+    store = pltpu.make_async_copy(out_ref, out_hbm, sems.at[2 * levels_here + 1])
+    store.start()
+    store.wait()
 
 
 def gather_kernel(scale, message_ref, lat_ref, out_ref):
@@ -135,11 +236,11 @@
     coarse = bands * coarse_rows
     high, low, scales = [], [], []
     for ring in range(rings):
-        value = message_ref[ring, :data].astype(jnp.int32).astype(jnp.float32)
+        value = from_16(message_ref[ring, :data])
         upper = jnp.floor(value * (1.0 / 256.0)) * 256.0
         high.append(upper.astype(jnp.bfloat16))
         low.append((value - upper).astype(jnp.bfloat16))
-        codes = message_ref[ring, data:].astype(jnp.int32).astype(jnp.float32)[:1, :data]
+        codes = from_16(message_ref[ring, data:])[:1, :data]
         scales.append(code_scale(codes) * (scale / STEPS_16))
     high = jnp.concatenate(high, axis=0)
     low = jnp.concatenate(low, axis=0)
@@ -210,7 +311,7 @@
         gain_ref[step] = jnp.where(hit, weight, 0.0)
 
 
-def stencil_kernel(place_ref, own_ref, before_ref, after_ref, wind_ref, gain_ref, value_ref, adjoint_ref):
+def stencil_kernel(place_ref, own_ref, before_ref, after_ref, wind_ref, gain_ref, value_ref, out_hbm, adjoint_ref, piece_ref, sems):
     rows, cols = wind_ref.shape[1:]
     first_row = place_ref[0]
     last_row = place_ref[1]
@@ -265,27 +366,41 @@
             + west(to_east * pushed)
         )
     adjoint = adjoint[HALO : rows - HALO]
-    row_tiles, lane_tiles = (rows - 2 * HALO) // 8, cols // 128
-    packed = jnp.concatenate(
-        [
-            adjoint[t * 8 : (t + 1) * 8, at * 128 : (at + 1) * 128]
-            for t in range(row_tiles)
-            for at in range(lane_tiles)
-        ],
-        axis=0,
-    )
-    count = adjoint_ref.shape[0]
+    own_rows = rows - 2 * HALO
+    data = own_rows * cols // 128
+    codes = row_codes(adjoint)
+    adjoint_ref[:data] = to_16(as_tiles(rounded(adjoint, codes)))
+    adjoint_ref[data:] = to_16(jnp.broadcast_to(codes, (own_rows, 128)))
+    count = out_hbm.shape[0]
+    copies = [
+        pltpu.make_async_copy(
+            adjoint_ref, out_hbm.at[copy, pl.ds(0, data + own_rows)], sems.at[copy]
+        )
+        for copy in range(count)
+    ]
+    for copy in copies:
+        copy.start()
     width = cols // count
     lane = lax.broadcasted_iota(jnp.int32, (8, 128), 1)
+    own = own_ref[...]
+    codes = row_codes(own)
+    own = rounded(own, codes)
+    codes = jnp.where(lane < width, codes[:8], codes[8:])
     for copy in range(count):
-        adjoint_ref[copy, : row_tiles * lane_tiles * 8] = packed
         strip = slice(copy * width // 128 * 128, copy * width // 128 * 128 + 128)
-        top, bottom = own_ref[0:8, strip], own_ref[8:16, strip]
+        top, bottom = own[0:8, strip], own[8:16, strip]
         if copy % 2 == 0:
             piece = jnp.where(lane < width, top, pltpu.roll(bottom, width, 1))
         else:
             piece = jnp.where(lane < width, pltpu.roll(top, width, 1), bottom)
-        adjoint_ref[copy, row_tiles * lane_tiles * 8 :] = piece
+        piece_ref[copy] = to_16(jnp.concatenate([piece, codes], axis=0))
+    last = pltpu.make_async_copy(
+        piece_ref, out_hbm.at[:, pl.ds(data + own_rows, 16)], sems.at[count]
+    )
+    last.start()
+    for copy in copies:
+        copy.wait()
+    last.wait()
 
 
 def body(
@@ -310,7 +425,6 @@
     pairs = members_here * levels_here
     quarters = peers // levels_here
     own_rows = wide_count // quarters
-    member_scale = 1.0 / jnp.sqrt(jnp.float32(members_here * peers - 1))
     quarter = lax.axis_index("mem") % quarters
     ring = lax.axis_index("lat_0")
     first = lax.axis_index("lat_1") == 0
@@ -389,6 +503,10 @@
             rising, falling, packed = lax.optimization_barrier((rising, falling, packed))
             passed = jnp.where(first, packed[:, 1:], jnp.stack([packed[:, 0], packed[:, 2]], axis=1))
             passed = lax.ppermute(passed, "lat_1", across)
+        if hop == 3:
+            rising, falling, other_members = lax.optimization_barrier(
+                (rising, falling, other_members)
+            )
         blocks[-hop % rings] = rising
         if hop < rings - hop:
             blocks[hop] = falling
@@ -407,11 +525,22 @@
     whole = pl.BlockSpec(memory_space=pltpu.VMEM)
     roomy = pltpu.CompilerParams(vmem_limit_bytes=48 * 1024 * 1024)
     where_side = jnp.reshape(side, (1,)).astype(jnp.int32)
+    anywhere = pl.BlockSpec(memory_space=pl.ANY)
+    half_members = pltpu.VMEM((members_here, levels_here, row_count, lon_total), jnp.bfloat16)
+    whole_lon = pltpu.VMEM(lon_matrix.shape, jnp.bfloat16)
+    piece_rows = own_rows * lon_total // 128 + own_rows
     partial_sum = pl.pallas_call(
         localize_kernel,
-        out_shape=jax.ShapeDtypeStruct((peers, own_rows, lon_total), jnp.float32),
-        in_specs=[scalars] + [whole] * (4 + rings),
-        out_specs=whole,
+        out_shape=jax.ShapeDtypeStruct((peers, piece_rows, 128), jnp.int16),
+        in_specs=[scalars, whole] + [anywhere] * 3 + [whole] * rings,
+        out_specs=anywhere,
+        scratch_shapes=[
+            whole_lon,
+            half_members,
+            half_members,
+            pltpu.VMEM((peers, piece_rows, 128), jnp.int16),
+            pltpu.SemaphoreType.DMA((3 * levels_here + 1,)),
+        ],
         compiler_params=roomy,
     )(
         where_side,
@@ -456,7 +585,14 @@
         compiler_params=roomy,
     )(before, local, after)
 
-    own = arrived.sum(axis=0) * member_scale
+    scale = (members_here * peers - 1) ** -0.5
+    own = pl.pallas_call(
+        functools.partial(add_kernel, scale),
+        out_shape=jax.ShapeDtypeStruct((own_rows, lon_total), jnp.float32),
+        in_specs=[whole],
+        out_specs=whole,
+        compiler_params=roomy,
+    )(arrived)
 
     before = lax.ppermute(own[-HALO:], ALL, forward)
     after = lax.ppermute(own[:HALO], ALL, backward)
@@ -465,9 +601,14 @@
     ).astype(jnp.int32)
     copies = pl.pallas_call(
         stencil_kernel,
-        out_shape=jax.ShapeDtypeStruct((peers, own_rows * lon_total // 128 + 8, 128), jnp.float32),
+        out_shape=jax.ShapeDtypeStruct((peers, piece_rows + 16, 128), jnp.int16),
         in_specs=[scalars] + [whole] * 6,
-        out_specs=whole,
+        out_specs=anywhere,
+        scratch_shapes=[
+            pltpu.VMEM((piece_rows, 128), jnp.int16),
+            pltpu.VMEM((peers, 16, 128), jnp.int16),
+            pltpu.SemaphoreType.DMA((peers + 1,)),
+        ],
         compiler_params=roomy,
     )(place, own, before, after, wide_wind, gains, values)
 
@@ -478,13 +619,20 @@
             jax.ShapeDtypeStruct((rings, repeats * wide_count + 16, coarse_lons), jnp.int16),
             jax.ShapeDtypeStruct((sides, levels_here, row_count, col_count), jnp.float32),
         ],
-        in_specs=[scalars] + [whole] * 4,
-        out_specs=[whole] * 2,
+        in_specs=[scalars, whole] + [anywhere] * 3,
+        out_specs=[anywhere, whole],
+        scratch_shapes=[
+            whole_lon,
+            half_members,
+            half_members,
+            pltpu.VMEM((rings, repeats * wide_count + 16, coarse_lons), jnp.int16),
+            pltpu.SemaphoreType.DMA((2 * levels_here + 2,)),
+        ],
         compiler_params=roomy,
-    )(where_side, adjoint_all, jnp.transpose(lon_matrix), perturbations, other_members)
+    )(where_side, adjoint_all, lon_matrix, perturbations, other_members)
     by_pair = swapped(projected, "lat_0", 0)
     full = pl.pallas_call(
-        functools.partial(gather_kernel, (members_here * peers - 1) ** -0.5),
+        functools.partial(gather_kernel, scale),
         out_shape=jax.ShapeDtypeStruct((bands, repeats, coarse_rows, coarse_lons), jnp.float32),
         in_specs=[whole] * 2,
         out_specs=whole,

time: 166 us -> 172 us (1.036)
  Pallas kernels: 10.4 us -> 18.3 us
    all_to_all x5, waiting for transfers between devices: 34.7 us -> 28 us  [swapped(): lax.all_to_all(value, axis, split_axis=dim, concat_axis=dim, tiled=True)]
    pallas_call x3 -> x4, Pallas kernels: 6.68 us -> 11.1 us  [the longest x1 5.63 us: body(): pl.pallas_call(localize_kernel, out_shape=jax.ShapeDtypeStruct((peers, pi...]
    pallas_call x1, Pallas kernels: 1.68 us -> 5.15 us  [body(): pl.pallas_call(project_kernel, out_shape=[jax.ShapeDtypeStruct((rings, re...]
    ppermute x3, waiting for transfers between devices: 0.01 us -> 3.01 us  [body(): falling = lax.ppermute(falling, 'lat_0', down)]
    ppermute x4, waiting for transfers between devices: 4.17 us -> 7.09 us  [body(): rising = lax.ppermute(rising, 'lat_0', up)]
    all_to_all x5, starting transfers between devices: 28.5 us -> 30.3 us  [swapped(): lax.all_to_all(value, axis, split_axis=dim, concat_axis=dim, tiled=True)]
    slice x8 -> x9, local copies, waits for them, and re-layouts: 5.75 us -> 5.08 us  [lat_of(): block[sides * weight_rows:].reshape(sides, row_count // 2, coarse_lons)]
    unnamed x39 -> x42, local copies, waits for them, and re-layouts: 17.5 us -> 16.9 us
  transfers between devices with their start and end apart: 20 -> 20, of which waited for: 11 -> 11; matrix products, arithmetic and copies ran while one was open for 20% -> 17% of each run, Pallas kernels for 3% -> 5%
where the time goes in v6:
time: 172 us; the launch traced here: 171 us
  starting transfers between devices  62.1 us (36%)
  waiting for transfers between devices  49 us (28%)
  local copies, waits for them, and re-layouts  32.5 us (19%)
  Pallas kernels  18.3 us (11%)
  other arithmetic  7.62 us (4%)
    all_to_all x5, starting transfers between devices, swapped(): lax.all_to_all(value, axis, split_axis=dim, concat_axis=dim, tiled=True)  30.3 us
    all_to_all x5, waiting for transfers between devices, swapped(): lax.all_to_all(value, axis, split_axis=dim, concat_axis=dim, tiled=True)  28 us
    unnamed x42, local copies, waits for them, and re-layouts  16.9 us
    ppermute x3, starting transfers between devices, body(): falling = lax.ppermute(falling, 'lat_0', down)  12.8 us
    ppermute x1, waiting for transfers between devices, body(): other_members = lax.ppermute(other_members, 'lat_1', across)  7.44 us
    ppermute x4, waiting for transfers between devices, body(): rising = lax.ppermute(rising, 'lat_0', up)  7.09 us
    pallas_call x1, Pallas kernels, body(): pl.pallas_call(localize_kernel, out_shape=jax.ShapeDtypeStruct((peers, pi...  5.63 us
    pallas_call x1, Pallas kernels, body(): pl.pallas_call(project_kernel, out_shape=[jax.ShapeDtypeStruct((rings, re...  5.15 us
  transfers between devices with their start and end apart: 20, of which 11 were waited for; matrix products, arithmetic and copies ran while one was open for 17% of the time, Pallas kernels for 5%

profile of v6, /device:TPU:2, one launch (start us, length us, event | category | flops | bytes accessed | tf_op | source)
XLA Modules:
  0.0 170.6 jit_solution(11603836866850911363)
XLA Ops:
  2.5 2.2 %collective-permute-start = (bf16[144,256]{1,0:T(8,128)(2,1)S(1)}, bf16[144,256]{1,0:T(8,128)(2,1)S(1)}, u32[]{:S(2)}, u32[]{:S(2)}) collective-permute-start(bf16[144,256]{1,0:T(8,128)(2,1)S(1)} %maximum_maximum_fusion), channel_id=1, source_target_pairs={{0,1},{1,0},{2,3},{3,2},{4,5},{5,4},{6,7},{7,6},{8,9},{9,8},{10,11... | collective-permute-start | bytes 221192 | tf_op jit(solution)/shard_map/ppermute | solution.py:464
  8.7 5.9 %all-to-all-start = ((f32[16,3,16,128]{3,2,1,0:T(8,128)}), f32[16,3,16,128]{3,2,1,0:T(8,128)S(1)}, u32[]{:S(2)}, u32[]{:S(2)}) async-start(f32[16,3,16,128]{3,2,1,0:T(8,128)} %bitcast.18), calls=%async_computation | async-start | bytes 786432 | tf_op jit(solution)/shard_map/all_to_all | solution.py:20
  15.4 5.9 %collective-permute-start.3 = (bf16[288,256]{1,0:T(8,128)(2,1)}, bf16[288,256]{1,0:T(8,128)(2,1)}, u32[]{:S(2)}, u32[]{:S(2)}) collective-permute-start(bf16[288,256]{1,0:T(8,128)(2,1)} %pad_maximum_fusion.refs_0_), channel_id=1, source_target_pairs={{2,0},{4,2},{6,4},{8,6},{10,8},{12,10},{14,12},{0,14},{3,1},{5,3},... | collective-permute-start | bytes 442376 | tf_op jit(solution)/shard_map/ppermute | solution.py:501
  22.3 1.4 collective-permute-start.7
  25.0 3.7 %collective-permute-start.4 = (bf16[288,256]{1,0:T(8,128)(2,1)}, bf16[288,256]{1,0:T(8,128)(2,1)}, u32[]{:S(2)}, u32[]{:S(2)}) collective-permute-start(bf16[288,256]{1,0:T(8,128)(2,1)} %collective-permute-done.3.refs_1_), channel_id=1, source_target_pairs={{2,0},{4,2},{6,4},{8,6},{10,8},{12,10},{14,12},{0,14},{3,1},{5,3},... | collective-permute-start | bytes 442376 | tf_op jit(solution)/shard_map/ppermute | solution.py:501
  29.9 1.8 %collective-permute-done.4.refs_2_ = bf16[288,256]{1,0:T(8,128)(2,1)} collective-permute-done((bf16[288,256]{1,0:T(8,128)(2,1)}, bf16[288,256]{1,0:T(8,128)(2,1)}, u32[]{:S(2)}, u32[]{:S(2)}) %collective-permute-start.4) | collective-permute-done | bytes 147488 | tf_op jit(solution)/shard_map/ppermute | solution.py:501
  31.6 3.7 %collective-permute-done.2.refs_6_ = bf16[288,256]{1,0:T(8,128)(2,1)} collective-permute-done((bf16[288,256]{1,0:T(8,128)(2,1)}, bf16[288,256]{1,0:T(8,128)(2,1)}, u32[]{:S(2)}, u32[]{:S(2)}) %collective-permute-start.2) | collective-permute-done | bytes 147488 | tf_op jit(solution)/shard_map/ppermute | solution.py:499
  35.3 3.2 %collective-permute-start.6 = (bf16[288,256]{1,0:T(8,128)(2,1)}, bf16[288,256]{1,0:T(8,128)(2,1)S(1)}, u32[]{:S(2)}, u32[]{:S(2)}) collective-permute-start(bf16[288,256]{1,0:T(8,128)(2,1)} %collective-permute-done.4.refs_2_), channel_id=1, source_target_pairs={{2,0},{4,2},{6,4},{8,6},{10,8},{12,10},{14,12},{0,14},{3,1},{5,3},... | collective-permute-start | bytes 442376 | tf_op jit(solution)/shard_map/ppermute | solution.py:501
  39.3 1.4 collective-permute-start.9
  40.7 1.3 collective-permute-done.5.refs_5_
  42.6 7.4 %collective-permute-done.7.other_hbm = bf16[4,4,32,1024]{3,2,1,0:T(8,128)(2,1)S(1)} collective-permute-done((bf16[4,4,32,1024]{3,2,1,0:T(8,128)(2,1)}, bf16[4,4,32,1024]{3,2,1,0:T(8,128)(2,1)S(1)}, u32[]{:S(2)}, u32[]{:S(2)}) %collective-permute-start.7) | collective-permute-done | bytes 1048608 | tf_op jit(solution)/shard_map/ppermute | solution.py:493
  50.9 1.5 reshape_squeeze_reshape.3
  52.4 1.4 fusion
  54.6 2.2 %collective-permute-done.8.refs_4_ = bf16[288,256]{1,0:T(8,128)(2,1)} collective-permute-done((bf16[288,256]{1,0:T(8,128)(2,1)}, bf16[288,256]{1,0:T(8,128)(2,1)}, u32[]{:S(2)}, u32[]{:S(2)}) %collective-permute-start.8) | collective-permute-done | bytes 147488 | tf_op jit(solution)/shard_map/ppermute | solution.py:499
  58.8 5.6 %shard_map.95 = s16[16,144,128]{2,1,0:T(8,128)(2,1)S(1)} custom-call(s32[1]{0:T(128)} %bitcast.side_ref, bf16[64,128]{1,0:T(8,128)(2,1)S(1)} %copy.47.columns_ref, bf16[256,1024]{1,0:T(8,128)(2,1)S(1)} %copy-done.3, bf16[4,8,32,1024]{3,2,1,0:T(8,128)(2,1)S(1)} %copy-done, bf16[4,4,32,1024]{3,2,1,0:T(8,128)(2,1)S(1)} %collective-permute-done.7.other_hbm, ...), custom_call_target="tpu_custom_call" | custom-call | tf_op jit(solution)/shard_map/pallas_call | solution.py:532
  65.2 5.9 %all-to-all-start.1 = ((s16[16,144,128]{2,1,0:T(8,128)(2,1)}), s16[16,144,128]{2,1,0:T(8,128)(2,1)}, u32[]{:S(2)}, u32[]{:S(2)}) async-start(s16[16,144,128]{2,1,0:T(8,128)(2,1)} %copy-done.2), calls=%async_computation.1 | async-start | bytes 1179648 | tf_op jit(solution)/shard_map/all_to_all | solution.py:20
  71.7 1.4 shard_map.97.local_ref
  79.0 2.0 %collective-permute-start.13 = (f32[8,3584]{1,0:T(8,128)}, f32[8,3584]{1,0:T(8,128)S(1)}, u32[]{:S(2)}, u32[]{:S(2)}) collective-permute-start(f32[8,3584]{1,0:T(8,128)} %get-tuple-element.50), channel_id=1, source_target_pairs={{16,0},{17,1},{18,2},{19,3},{20,4},{21,5},{22,6},{23,7},{24,8},{25... | collective-permute-start | bytes 344072 | tf_op jit(solution)/shard_map/ppermute | solution.py:575
  81.0 2.3 %collective-permute-start.12 = (f32[8,3584]{1,0:T(8,128)}, f32[8,3584]{1,0:T(8,128)S(1)}, u32[]{:S(2)}, u32[]{:S(2)}) collective-permute-start(f32[8,3584]{1,0:T(8,128)} %get-tuple-element.51), channel_id=1, source_target_pairs={{0,16},{1,17},{2,18},{3,19},{4,20},{5,21},{6,22},{7,23},{8,24},{9,... | collective-permute-start | bytes 344072 | tf_op jit(solution)/shard_map/ppermute | solution.py:574
  85.3 3.3 %collective-permute-start.11 = (f32[8,1024]{1,0:T(8,128)S(1)}, f32[8,1024]{1,0:T(8,128)S(1)}, u32[]{:S(2)}, u32[]{:S(2)}) collective-permute-start(f32[8,1024]{1,0:T(8,128)S(1)} %get-tuple-element.58), channel_id=1, source_target_pairs={{16,0},{17,1},{18,2},{19,3},{20,4},{21,5},{22,6},{23,7},{24,8},{25... | collective-permute-start | bytes 98312 | tf_op jit(solution)/shard_map/ppermute | solution.py:598
  88.5 3.0 %collective-permute-start.10 = (f32[8,1024]{1,0:T(8,128)S(1)}, f32[8,1024]{1,0:T(8,128)S(1)}, u32[]{:S(2)}, u32[]{:S(2)}) collective-permute-start(f32[8,1024]{1,0:T(8,128)S(1)} %get-tuple-element.59), channel_id=1, source_target_pairs={{0,16},{1,17},{2,18},{3,19},{4,20},{5,21},{6,22},{7,23},{8,24},{9,... | collective-permute-start | bytes 98312 | tf_op jit(solution)/shard_map/ppermute | solution.py:597
  94.1 2.8 %shard_map.99 = s16[16,160,128]{2,1,0:T(8,128)(2,1)S(1)} custom-call(s32[2]{0:T(128)S(1)} %copy-done.10, f32[16,1024]{1,0:T(8,128)S(1)} %shard_map.96.own_ref, f32[8,1024]{1,0:T(8,128)S(1)} %collective-permute-done.10.before_ref, f32[8,1024]{1,0:T(8,128)S(1)} %collective-permute-done.11.after_ref, f32[2,32,1024]{2,1,0:T(8,128)S(1)} %get-tuple-element.35.wind_ref, ...), custom_call_target="tpu_custom_call" | custom-call | tf_op jit(solution)/shard_map/pallas_call | solution.py:602
  97.8 7.1 %all-to-all-start.2 = ((s16[16,160,128]{2,1,0:T(8,128)(2,1)}), s16[16,160,128]{2,1,0:T(8,128)(2,1)}, u32[]{:S(2)}, u32[]{:S(2)}) async-start(s16[16,160,128]{2,1,0:T(8,128)(2,1)} %copy-done.1), calls=%async_computation.2 | async-start | bytes 1310720 | tf_op jit(solution)/shard_map/all_to_all | solution.py:20
  108.5 7.6 %all-to-all-done.2.message_ref = s16[16,160,128]{2,1,0:T(8,128)(2,1)} async-done(((s16[16,160,128]{2,1,0:T(8,128)(2,1)}), s16[16,160,128]{2,1,0:T(8,128)(2,1)}, u32[]{:S(2)}, u32[]{:S(2)}) %all-to-all-start.2) | async-done | bytes 655392 | tf_op jit(solution)/shard_map/all_to_all | solution.py:20
  117.1 5.2 %shard_map.100 = (s16[8,144,256]{2,1,0:T(8,128)(2,1)S(1)}, f32[2,4,32,64]{3,2,1,0:T(8,128)S(1)}) custom-call(s32[1]{0:T(128)} %bitcast.side_ref, s16[16,160,128]{2,1,0:T(8,128)(2,1)} %all-to-all-done.2.message_ref, bf16[256,1024]{1,0:T(8,128)(2,1)S(1)} %copy-done.4, bf16[4,8,32,1024]{3,2,1,0:T(8,128)(2,1)S(1)} %copy-done, ...), custom_call_target="tpu_custom_call" | custom-call | tf_op jit(solution)/shard_map/pallas_call | solution.py:616
  123.1 7.9 %all-to-all-start.3 = ((s16[8,144,256]{2,1,0:T(8,128)(2,1)}), s16[8,144,256]{2,1,0:T(8,128)(2,1)S(1)}, u32[]{:S(2)}, u32[]{:S(2)}) async-start(s16[8,144,256]{2,1,0:T(8,128)(2,1)} %copy-done.7), calls=%async_computation.3 | async-start | bytes 1179648 | tf_op jit(solution)/shard_map/all_to_all | solution.py:20
  137.6 12.6 %all-to-all-done.3.message_ref = s16[8,144,256]{2,1,0:T(8,128)(2,1)S(1)} async-done(((s16[8,144,256]{2,1,0:T(8,128)(2,1)}), s16[8,144,256]{2,1,0:T(8,128)(2,1)S(1)}, u32[]{:S(2)}, u32[]{:S(2)}) %all-to-all-start.3) | async-done | bytes 589856 | tf_op jit(solution)/shard_map/all_to_all | solution.py:20
  150.2 1.4 shard_map.101
  151.6 3.5 %all-to-all-start.4 = ((f32[16,2,8,256]{3,2,1,0:T(8,128)}), f32[16,2,8,256]{3,2,1,0:T(8,128)S(1)}, u32[]{:S(2)}, u32[]{:S(2)}) async-start(f32[16,2,8,256]{3,2,1,0:T(8,128)} %shard_map.101), calls=%async_computation.4 | async-start | bytes 524288 | tf_op jit(solution)/shard_map/all_to_all | solution.py:20
  155.2 3.4 %collective-permute-start.14 = (f32[4,32,64]{2,1,0:T(8,128)S(1)}, f32[4,32,64]{2,1,0:T(8,128)S(1)}, u32[]{:S(2)}, u32[]{:S(2)}) collective-permute-start(f32[4,32,64]{2,1,0:T(8,128)S(1)} %get-tuple-element.53), channel_id=1, source_target_pairs={{0,1},{1,0},{2,3},{3,2},{4,5},{5,4},{6,7},{7,6},{8,9},{9,8},{10,11... | collective-permute-start | bytes 98312 | tf_op jit(solution)/shard_map/ppermute | solution.py:650
  158.6 2.5 %collective-permute-done.14 = f32[4,32,64]{2,1,0:T(8,128)S(1)} collective-permute-done((f32[4,32,64]{2,1,0:T(8,128)S(1)}, f32[4,32,64]{2,1,0:T(8,128)S(1)}, u32[]{:S(2)}, u32[]{:S(2)}) %collective-permute-start.14) | collective-permute-done | bytes 32800 | tf_op jit(solution)/shard_map/ppermute | solution.py:650
  161.8 7.8 %all-to-all-done.4 = f32[16,2,8,256]{3,2,1,0:T(8,128)S(1)} async-done(((f32[16,2,8,256]{3,2,1,0:T(8,128)}), f32[16,2,8,256]{3,2,1,0:T(8,128)S(1)}, u32[]{:S(2)}, u32[]{:S(2)}) %all-to-all-start.4) | async-done | bytes 262176 | tf_op jit(solution)/shard_map/all_to_all | solution.py:20
  (122 shorter events, 41.2 us)
Async XLA Ops:
  2.5 12.2 %collective-permute-start = (bf16[144,256]{1,0:T(8,128)(2,1)S(1)}, bf16[144,256]{1,0:T(8,128)(2,1)S(1)}, u32[]{:S(2)}, u32[]{:S(2)}) collective-permute-start(bf16[144,256]{1,0:T(8,128)(2,1)S(1)} %maximum_maximum_fusion), channel_id=1, source_target_pairs={{0,1},{1,0},{2,3},{3,2},{4,5},{5,4},{6,7},{7,6},{8,9},{9,8},{10,11... | collective-permute-start | bytes 221192 | tf_op jit(solution)/shard_map/ppermute | solution.py:464
  6.5 14.8 %copy-start = (bf16[4,8,32,1024]{3,2,1,0:T(8,128)(2,1)S(1)}, bf16[4,8,32,1024]{3,2,1,0:T(8,128)(2,1)}, u32[]{:S(2)}) copy-start(bf16[4,8,32,1024]{3,2,1,0:T(8,128)(2,1)} %own_hbm.3) | copy-start | bytes 6291460
  8.7 26.7 %all-to-all-start = ((f32[16,3,16,128]{3,2,1,0:T(8,128)}), f32[16,3,16,128]{3,2,1,0:T(8,128)S(1)}, u32[]{:S(2)}, u32[]{:S(2)}) async-start(f32[16,3,16,128]{3,2,1,0:T(8,128)} %bitcast.18), calls=%async_computation | async-start | bytes 786432 | tf_op jit(solution)/shard_map/all_to_all | solution.py:20
  15.4 9.6 %collective-permute-start.3 = (bf16[288,256]{1,0:T(8,128)(2,1)}, bf16[288,256]{1,0:T(8,128)(2,1)}, u32[]{:S(2)}, u32[]{:S(2)}) collective-permute-start(bf16[288,256]{1,0:T(8,128)(2,1)} %pad_maximum_fusion.refs_0_), channel_id=1, source_target_pairs={{2,0},{4,2},{6,4},{8,6},{10,8},{12,10},{14,12},{0,14},{3,1},{5,3},... | collective-permute-start | bytes 442376 | tf_op jit(solution)/shard_map/ppermute | solution.py:501
  21.2 7.4 %collective-permute-start.1 = (bf16[288,256]{1,0:T(8,128)(2,1)}, bf16[288,256]{1,0:T(8,128)(2,1)}, u32[]{:S(2)}, u32[]{:S(2)}) collective-permute-start(bf16[288,256]{1,0:T(8,128)(2,1)} %pad_maximum_fusion.refs_0_), channel_id=1, source_target_pairs={{0,2},{2,4},{4,6},{6,8},{8,10},{10,12},{12,14},{14,0},{1,3},{3,5},... | collective-permute-start | bytes 442376 | tf_op jit(solution)/shard_map/ppermute | solution.py:499
  22.3 27.8 %collective-permute-start.7 = (bf16[4,4,32,1024]{3,2,1,0:T(8,128)(2,1)}, bf16[4,4,32,1024]{3,2,1,0:T(8,128)(2,1)S(1)}, u32[]{:S(2)}, u32[]{:S(2)}) collective-permute-start(bf16[4,4,32,1024]{3,2,1,0:T(8,128)(2,1)} %constant_dynamic-slice_fusion.1), channel_id=1, source_target_pairs={{0,1},{1,0},{2,3},{3,2},{4,5},{5,4},{6,7},{7,6},{8,9},{9,8},{10,11... | collective-permute-start | bytes 3145736 | tf_op jit(solution)/shard_map/ppermute | solution.py:493
  25.0 6.7 %collective-permute-start.4 = (bf16[288,256]{1,0:T(8,128)(2,1)}, bf16[288,256]{1,0:T(8,128)(2,1)}, u32[]{:S(2)}, u32[]{:S(2)}) collective-permute-start(bf16[288,256]{1,0:T(8,128)(2,1)} %collective-permute-done.3.refs_1_), channel_id=1, source_target_pairs={{2,0},{4,2},{6,4},{8,6},{10,8},{12,10},{14,12},{0,14},{3,1},{5,3},... | collective-permute-start | bytes 442376 | tf_op jit(solution)/shard_map/ppermute | solution.py:501
  28.7 6.7 %collective-permute-start.2 = (bf16[288,256]{1,0:T(8,128)(2,1)}, bf16[288,256]{1,0:T(8,128)(2,1)}, u32[]{:S(2)}, u32[]{:S(2)}) collective-permute-start(bf16[288,256]{1,0:T(8,128)(2,1)} %collective-permute-done.1.refs_7_), channel_id=1, source_target_pairs={{0,2},{2,4},{4,6},{6,8},{8,10},{10,12},{12,14},{14,0},{1,3},{3,5},... | collective-permute-start | bytes 442376 | tf_op jit(solution)/shard_map/ppermute | solution.py:499
  35.3 6.7 %collective-permute-start.5 = (bf16[288,256]{1,0:T(8,128)(2,1)}, bf16[288,256]{1,0:T(8,128)(2,1)}, u32[]{:S(2)}, u32[]{:S(2)}) collective-permute-start(bf16[288,256]{1,0:T(8,128)(2,1)} %collective-permute-done.2.refs_6_), channel_id=1, source_target_pairs={{0,2},{2,4},{4,6},{6,8},{8,10},{10,12},{12,14},{14,0},{1,3},{3,5},... | collective-permute-start | bytes 442376 | tf_op jit(solution)/shard_map/ppermute | solution.py:499
  35.3 6.7 %collective-permute-start.6 = (bf16[288,256]{1,0:T(8,128)(2,1)}, bf16[288,256]{1,0:T(8,128)(2,1)S(1)}, u32[]{:S(2)}, u32[]{:S(2)}) collective-permute-start(bf16[288,256]{1,0:T(8,128)(2,1)} %collective-permute-done.4.refs_2_), channel_id=1, source_target_pairs={{2,0},{4,2},{6,4},{8,6},{10,8},{12,10},{14,12},{0,14},{3,1},{5,3},... | collective-permute-start | bytes 442376 | tf_op jit(solution)/shard_map/ppermute | solution.py:501
  39.3 25.9 %collective-permute-start.9 = (f32[16,2,16,128]{3,2,1,0:T(8,128)}, f32[16,2,16,128]{3,2,1,0:T(8,128)}, u32[]{:S(2)}, u32[]{:S(2)}) collective-permute-start(f32[16,2,16,128]{3,2,1,0:T(8,128)} %maximum_select_fusion), channel_id=1, source_target_pairs={{0,1},{1,0},{2,3},{3,2},{4,5},{5,4},{6,7},{7,6},{8,9},{9,8},{10,11... | collective-permute-start | bytes 786440 | tf_op jit(solution)/shard_map/ppermute | solution.py:505
  50.1 6.7 %collective-permute-start.8 = (bf16[288,256]{1,0:T(8,128)(2,1)}, bf16[288,256]{1,0:T(8,128)(2,1)}, u32[]{:S(2)}, u32[]{:S(2)}) collective-permute-start(bf16[288,256]{1,0:T(8,128)(2,1)} %collective-permute-done.5.refs_5_), channel_id=1, source_target_pairs={{0,2},{2,4},{4,6},{6,8},{8,10},{10,12},{12,14},{14,0},{1,3},{3,5},... | collective-permute-start | bytes 442376 | tf_op jit(solution)/shard_map/ppermute | solution.py:499
  56.8 1.0 copy-start.3
  57.8 0.9 copy-start.9
  64.4 0.8 copy-start.2
  65.2 10.2 %slice-start = ((bf16[288,256]{1,0:T(8,128)(2,1)}), bf16[32,256]{1,0:T(8,128)(2,1)S(1)}, s32[]{:S(2)}) async-start(bf16[288,256]{1,0:T(8,128)(2,1)} %copy-done.8), calls=%async_computation.5 | async-start | bytes 32768 | tf_op jit(solution)/shard_map/slice | solution.py:515
  65.2 18.8 %all-to-all-start.1 = ((s16[16,144,128]{2,1,0:T(8,128)(2,1)}), s16[16,144,128]{2,1,0:T(8,128)(2,1)}, u32[]{:S(2)}, u32[]{:S(2)}) async-start(s16[16,144,128]{2,1,0:T(8,128)(2,1)} %copy-done.2), calls=%async_computation.1 | async-start | bytes 1179648 | tf_op jit(solution)/shard_map/all_to_all | solution.py:20
  73.1 5.2 %copy-start.5 = (f32[16,3584]{1,0:T(8,128)}, f32[16,3584]{1,0:T(8,128)S(1)}, u32[]{:S(2)}) copy-start(f32[16,3584]{1,0:T(8,128)S(1)} %shard_map.97.local_ref) | copy-start | bytes 688132
  73.1 21.0 %copy-start.10 = (s32[2]{0:T(128)S(1)}, s32[2]{0:T(128)}, u32[]{:S(2)}) copy-start(s32[2]{0:T(128)} %pad_add_fusion.place_ref) | copy-start | bytes 28
  79.0 12.6 %collective-permute-start.13 = (f32[8,3584]{1,0:T(8,128)}, f32[8,3584]{1,0:T(8,128)S(1)}, u32[]{:S(2)}, u32[]{:S(2)}) collective-permute-start(f32[8,3584]{1,0:T(8,128)} %get-tuple-element.50), channel_id=1, source_target_pairs={{16,0},{17,1},{18,2},{19,3},{20,4},{21,5},{22,6},{23,7},{24,8},{25... | collective-permute-start | bytes 344072 | tf_op jit(solution)/shard_map/ppermute | solution.py:575
  81.0 10.6 %collective-permute-start.12 = (f32[8,3584]{1,0:T(8,128)}, f32[8,3584]{1,0:T(8,128)S(1)}, u32[]{:S(2)}, u32[]{:S(2)}) collective-permute-start(f32[8,3584]{1,0:T(8,128)} %get-tuple-element.51), channel_id=1, source_target_pairs={{0,16},{1,17},{2,18},{3,19},{4,20},{5,21},{6,22},{7,23},{8,24},{9,... | collective-permute-start | bytes 344072 | tf_op jit(solution)/shard_map/ppermute | solution.py:574
  85.3 7.9 %collective-permute-start.11 = (f32[8,1024]{1,0:T(8,128)S(1)}, f32[8,1024]{1,0:T(8,128)S(1)}, u32[]{:S(2)}, u32[]{:S(2)}) collective-permute-start(f32[8,1024]{1,0:T(8,128)S(1)} %get-tuple-element.58), channel_id=1, source_target_pairs={{16,0},{17,1},{18,2},{19,3},{20,4},{21,5},{22,6},{23,7},{24,8},{25... | collective-permute-start | bytes 98312 | tf_op jit(solution)/shard_map/ppermute | solution.py:598
  88.5 5.6 %collective-permute-start.10 = (f32[8,1024]{1,0:T(8,128)S(1)}, f32[8,1024]{1,0:T(8,128)S(1)}, u32[]{:S(2)}, u32[]{:S(2)}) collective-permute-start(f32[8,1024]{1,0:T(8,128)S(1)} %get-tuple-element.59), channel_id=1, source_target_pairs={{0,16},{1,17},{2,18},{3,19},{4,20},{5,21},{6,22},{7,23},{8,24},{9,... | collective-permute-start | bytes 98312 | tf_op jit(solution)/shard_map/ppermute | solution.py:597
  91.6 0.9 copy-start.6
  96.9 0.8 copy-start.1
  97.8 18.3 %all-to-all-start.2 = ((s16[16,160,128]{2,1,0:T(8,128)(2,1)}), s16[16,160,128]{2,1,0:T(8,128)(2,1)}, u32[]{:S(2)}, u32[]{:S(2)}) async-start(s16[16,160,128]{2,1,0:T(8,128)(2,1)} %copy-done.1), calls=%async_computation.2 | async-start | bytes 1310720 | tf_op jit(solution)/shard_map/all_to_all | solution.py:20
  116.1 1.0 copy-start.4
  122.3 0.8 copy-start.7
  123.1 27.1 %all-to-all-start.3 = ((s16[8,144,256]{2,1,0:T(8,128)(2,1)}), s16[8,144,256]{2,1,0:T(8,128)(2,1)S(1)}, u32[]{:S(2)}, u32[]{:S(2)}) async-start(s16[8,144,256]{2,1,0:T(8,128)(2,1)} %copy-done.7), calls=%async_computation.3 | async-start | bytes 1179648 | tf_op jit(solution)/shard_map/all_to_all | solution.py:20
  137.4 32.5 %copy-start.12 = (bf16[8,4,8,256]{3,2,1,0:T(8,128)(2,1)S(1)}, bf16[8,4,8,256]{3,2,1,0:T(8,128)(2,1)}, u32[]{:S(2)}) copy-start(bf16[8,4,8,256]{3,2,1,0:T(8,128)(2,1)} %param.8) | copy-start | bytes 393220
  151.6 17.9 %all-to-all-start.4 = ((f32[16,2,8,256]{3,2,1,0:T(8,128)}), f32[16,2,8,256]{3,2,1,0:T(8,128)S(1)}, u32[]{:S(2)}, u32[]{:S(2)}) async-start(f32[16,2,8,256]{3,2,1,0:T(8,128)} %shard_map.101), calls=%async_computation.4 | async-start | bytes 524288 | tf_op jit(solution)/shard_map/all_to_all | solution.py:20
  155.2 5.9 %collective-permute-start.14 = (f32[4,32,64]{2,1,0:T(8,128)S(1)}, f32[4,32,64]{2,1,0:T(8,128)S(1)}, u32[]{:S(2)}, u32[]{:S(2)}) collective-permute-start(f32[4,32,64]{2,1,0:T(8,128)S(1)} %get-tuple-element.53), channel_id=1, source_target_pairs={{0,1},{1,0},{2,3},{3,2},{4,5},{5,4},{6,7},{7,6},{8,9},{9,8},{10,11... | collective-permute-start | bytes 98312 | tf_op jit(solution)/shard_map/ppermute | solution.py:650
  (2 other events, 1.3 us)

commit v7 on v5

--- a/solution.py
+++ b/solution.py
@@ -30,6 +30,61 @@
     return jnp.dot(a, b, preferred_element_type=jnp.float32)
 
 
+def dot_last(a, b):
+    return lax.dot_general(a, b, (((1,), (1,)), ((), ())), preferred_element_type=jnp.float32)
+
+
+def row_codes(value):
+    largest = jnp.maximum(jnp.max(jnp.abs(value), axis=1, keepdims=True), 1e-30)
+    return jnp.ceil(jnp.log(largest) * (256.0 / LN2)) + 1.0
+
+
+def code_scale(codes):
+    return jnp.exp(codes * (LN2 / 256.0))
+
+
+def rounded(value, codes):
+    return jnp.round(value * (STEPS_16 / code_scale(codes)))
+
+
+def to_16(value):
+    return value.astype(jnp.int32).astype(jnp.int16)
+
+
+def from_16(value):
+    return value.astype(jnp.int32).astype(jnp.float32)
+
+
+def as_tiles(value):
+    rows, cols = value.shape
+    return jnp.concatenate(
+        [
+            value[t * 8 : (t + 1) * 8, at * 128 : (at + 1) * 128]
+            for t in range(rows // 8)
+            for at in range(cols // 128)
+        ],
+        axis=0,
+    )
+
+
+def from_tiles(value, row_tiles):
+    lane_tiles = value.shape[0] // 8 // row_tiles
+    rows = []
+    for t in range(row_tiles):
+        start = t * lane_tiles * 8
+        strips = [value[start + at * 8 : start + (at + 1) * 8] for at in range(lane_tiles)]
+        rows.append(jnp.concatenate(strips, axis=1))
+    return jnp.concatenate(rows, axis=0)
+
+
+def tile_scales(codes, lane_tiles):
+    scales = code_scale(codes) * (1.0 / STEPS_16)
+    parts = []
+    for t in range(scales.shape[0] // 8):
+        parts += [scales[t * 8 : (t + 1) * 8]] * lane_tiles
+    return jnp.concatenate(parts, axis=0)
+
+
 def member_rows(side, own_ref, other_ref, member, level):
     levels_here = other_ref.shape[1]
     own = own_ref[member, side * levels_here + level].astype(jnp.float32)
@@ -39,13 +94,27 @@
     return jnp.concatenate([low, high], axis=0)
 
 
-def localize_kernel(side_ref, columns_ref, lon_ref, own_ref, other_ref, *refs):
+def localize_kernel(place_ref, lon_ref, own_ref, other_ref, *refs):
     block_refs, sum_ref = refs[:-1], refs[-1]
     members, levels_here, row_count, lon_total = other_ref.shape
     tall = 2 * row_count
-    side = side_ref[0]
-    per_block = columns_ref.shape[1] // len(block_refs)
-    columns = columns_ref[...]
+    side = place_ref[0]
+    pairs = members * levels_here
+    lat_start = block_refs[0].shape[0] - row_count
+    per_block = lat_start // pairs
+    coarse_total = per_block * len(block_refs)
+    lat = block_refs[0][lat_start:].astype(jnp.float32)
+    half = row_count // 2
+    columns = jnp.concatenate(
+        [
+            lat[band * half : (band + 1) * half, part * coarse_total : (part + 1) * coarse_total]
+            for band in range(2)
+            for part in range(2)
+        ],
+        axis=0,
+    )
+    turn = (len(block_refs) - place_ref[1]) * per_block % coarse_total
+    columns = pltpu.roll(columns, turn, 1).astype(jnp.bfloat16)
     lon = lon_ref[...]
     for level in range(levels_here):
         narrow = []
@@ -61,16 +130,28 @@
             term = term * member_rows(side, own_ref, other_ref, member, level)
             total = term if total is None else total + term
         count = sum_ref.shape[0] // levels_here
-        sum_ref[level * count : (level + 1) * count] = total.reshape(count, tall // count, lon_total)
-
-
-def row_codes(value):
-    largest = jnp.maximum(jnp.max(jnp.abs(value), axis=1, keepdims=True), 1e-30)
-    return jnp.ceil(jnp.log(largest) * (256.0 / LN2)) + 1.0
-
-
-def code_scale(codes):
-    return jnp.exp(codes * (LN2 / 256.0))
+        piece_rows = tall // count
+        data = piece_rows * lon_total // 128
+        codes = row_codes(total)
+        total = rounded(total, codes)
+        for piece in range(count):
+            part = slice(piece * piece_rows, (piece + 1) * piece_rows)
+            sum_ref[level * count + piece, :data] = to_16(as_tiles(total[part]))
+            sum_ref[level * count + piece, data:] = to_16(
+                jnp.broadcast_to(codes[part], (piece_rows, 128))
+            )
+
+
+def add_kernel(scale, message_ref, out_ref):
+    sources, rows, _ = message_ref.shape
+    own_rows, lon_total = out_ref.shape
+    total = None
+    for source in range(sources):
+        value = from_16(message_ref[source, : rows - own_rows])
+        codes = from_16(message_ref[source, rows - own_rows :])
+        value = value * tile_scales(codes, lon_total // 128)
+        total = value if total is None else total + value
+    out_ref[...] = from_tiles(total, own_rows // 8) * scale
 
 
 def project_kernel(side_ref, adjoint_ref, lon_ref, own_ref, other_ref, out_ref, tile_ref):
@@ -105,7 +186,7 @@
         product = [
             member_rows(side, own_ref, other_ref, member, level) * adjoint for member in range(members)
         ]
-        projected = dot(two_terms(jnp.concatenate(product, axis=0)), lon)
+        projected = dot_last(two_terms(jnp.concatenate(product, axis=0)), lon)
         for member in range(members):
             at = member * tall
             value = projected[at : at + tall] + projected[at + members * tall : at + (members + 1) * tall]
@@ -155,10 +236,30 @@
             out_ref[band, p] = total[at : at + coarse_rows]
 
 
+def pack_kernel(cell_ref, value_ref, weight_ref, wind_ref, out_ref):
+    steps, levels, blocks, row_count = cell_ref.shape
+    peers, kinds, own_rows, lanes = out_ref.shape
+    levels_here = levels // (kinds - 1)
+    parts = row_count // own_rows
+    filler = jnp.zeros((lanes - 3 * steps * blocks, row_count), jnp.float32)
+    winds = jnp.concatenate([wind_ref[0], wind_ref[1]], axis=1)
+    for level in range(levels):
+        seen = [cell_ref[t, level].astype(jnp.float32) for t in range(steps)]
+        seen += [value_ref[t, level] for t in range(steps)]
+        seen += [weight_ref[t, level] for t in range(steps)]
+        rows = jnp.transpose(jnp.concatenate(seen + [filler], axis=0))
+        start, kind = level % levels_here * (peers // levels_here), level // levels_here
+        for peer in range(peers // levels_here):
+            at = peer % parts * own_rows
+            out_ref[start + peer, kind] = rows[at : at + own_rows]
+            if kind == 0:
+                out_ref[start + peer, kinds - 1] = winds[at : at + own_rows]
+
+
 def arrange_kernel(side_ref, own_ref, other_ref, out_ref):
     peers, _, row_count, lanes = own_ref.shape
     side = side_ref[0]
-    is_own = side_ref[1] == 1
+    is_own = side_ref[2] == 1
     lane = lax.broadcasted_iota(jnp.int32, (row_count, lanes), 1)
     width = lanes // 2
     pick = lambda peer, which, mine: jnp.where(is_own, own_ref[peer, mine], other_ref[peer, which])
@@ -212,8 +313,8 @@
 
 def stencil_kernel(place_ref, own_ref, before_ref, after_ref, wind_ref, gain_ref, value_ref, adjoint_ref):
     rows, cols = wind_ref.shape[1:]
-    first_row = place_ref[0]
-    last_row = place_ref[1]
+    first_row = place_ref[3]
+    last_row = place_ref[4]
     state = jnp.concatenate([before_ref[...], own_ref[...], after_ref[...]], axis=0)
     row = lax.broadcasted_iota(jnp.int32, (rows, cols), 0) + first_row
     col = lax.broadcasted_iota(jnp.int32, (rows, cols), 1)
@@ -310,7 +411,6 @@
     pairs = members_here * levels_here
     quarters = peers // levels_here
     own_rows = wide_count // quarters
-    member_scale = 1.0 / jnp.sqrt(jnp.float32(members_here * peers - 1))
     quarter = lax.axis_index("mem") % quarters
     ring = lax.axis_index("lat_0")
     first = lax.axis_index("lat_1") == 0
@@ -353,24 +453,23 @@
     ).reshape(sides * weight_rows, coarse_lons)
     both = jnp.concatenate([both, in_order(lat_rows, from_side[weight_rows:], 0)], axis=0)
 
-    packed = jnp.concatenate(
-        [observed_cell.astype(jnp.float32), observed_value, observed_weight], axis=0
-    )
-    kinds, _, _, block_count = packed.shape
+    kinds, block_count = 3 * STEPS, observed_cell.shape[3]
     lanes = 2 * col_count
-    packed = jnp.transpose(packed, (1, 2, 0, 3)).reshape(levels, row_count, kinds * block_count)
-    packed = jnp.pad(packed, ((0, 0), (0, 0), (0, lanes - kinds * block_count)))
-    winds = jnp.transpose(wind_field, (1, 0, 2)).reshape(1, row_count, lanes)
     parts = row_count // own_rows
-    packed = packed.reshape(sides, levels_here, 1, parts, own_rows, lanes)
-    winds = jnp.broadcast_to(
-        winds.reshape(1, 1, 1, parts, own_rows, lanes), (1, levels_here, 1, parts, own_rows, lanes)
-    )
-    packed = jnp.transpose(jnp.concatenate([packed, winds], axis=0), (1, 2, 3, 0, 4, 5))
-    packed = jnp.broadcast_to(
-        packed, (levels_here, quarters // parts, parts, sides + 1, own_rows, lanes)
-    )
-    packed = swapped(packed.reshape(peers, sides + 1, own_rows, lanes), "mem", 0)
+    whole = pl.BlockSpec(memory_space=pltpu.VMEM)
+    roomy = pltpu.CompilerParams(vmem_limit_bytes=24 * 1024 * 1024)
+    packed = pl.pallas_call(
+        pack_kernel,
+        out_shape=jax.ShapeDtypeStruct((peers, sides + 1, own_rows, lanes), jnp.float32),
+        in_specs=[whole] * 4,
+        out_specs=whole,
+        compiler_params=roomy,
+    )(
+        *[jnp.swapaxes(seen, 2, 3) for seen in (observed_cell, observed_value, observed_weight)],
+        wind_field,
+    )
+    _, packed = lax.optimization_barrier((from_side, packed))
+    packed = swapped(packed, "mem", 0)
 
     side = lax.axis_index("lat_1")
     other_members = lax.dynamic_slice_in_dim(
@@ -398,24 +497,27 @@
         rows = jnp.concatenate([rows[..., :coarse_total], rows[..., coarse_total:]], 1)
         return rows.reshape(1, wide_count, coarse_total)
 
-    columns = lat_of(both)[0].reshape(wide_count, rings, sides * coarse_rows)
-    columns = lax.dynamic_slice_in_dim(
-        jnp.concatenate([columns, columns], axis=1), ring, rings, axis=1
-    ).reshape(wide_count, coarse_total)
 
     scalars = pl.BlockSpec(memory_space=pltpu.SMEM)
-    whole = pl.BlockSpec(memory_space=pltpu.VMEM)
-    roomy = pltpu.CompilerParams(vmem_limit_bytes=48 * 1024 * 1024)
-    where_side = jnp.reshape(side, (1,)).astype(jnp.int32)
+    is_own = (quarter // parts == side).astype(jnp.int32)
+    place = jnp.stack(
+        [
+            side,
+            ring,
+            is_own,
+            ring * wide_count + quarter * own_rows - HALO,
+            jnp.int32(row_count * bands),
+        ]
+    ).astype(jnp.int32)
+    piece_rows = own_rows * lon_total // 128 + own_rows
     partial_sum = pl.pallas_call(
         localize_kernel,
-        out_shape=jax.ShapeDtypeStruct((peers, own_rows, lon_total), jnp.float32),
-        in_specs=[scalars] + [whole] * (4 + rings),
+        out_shape=jax.ShapeDtypeStruct((peers, piece_rows, 128), jnp.int16),
+        in_specs=[scalars] + [whole] * (3 + rings),
         out_specs=whole,
         compiler_params=roomy,
     )(
-        where_side,
-        columns,
+        place,
         lon_matrix,
         perturbations,
         other_members,
@@ -424,7 +526,6 @@
     partial_sum, packed, passed = lax.optimization_barrier((partial_sum, packed, passed))
     arrived = swapped(partial_sum, "mem", 0)
 
-    is_own = (quarter // parts == side).astype(jnp.int32)
     local = pl.pallas_call(
         arrange_kernel,
         out_shape=jax.ShapeDtypeStruct(
@@ -433,7 +534,7 @@
         in_specs=[scalars, whole, whole],
         out_specs=whole,
         compiler_params=roomy,
-    )(jnp.stack([side.astype(jnp.int32), is_own]), packed, passed)
+    )(place, packed, passed)
     local, *tied = lax.optimization_barrier((local, *[blocks[d] for d in range(rings)]))
     lat_ring = jnp.concatenate([lat_of(block) for block in tied], axis=0)
     lat_all = lax.dynamic_slice_in_dim(
@@ -456,13 +557,17 @@
         compiler_params=roomy,
     )(before, local, after)
 
-    own = arrived.sum(axis=0) * member_scale
+    scale = (members_here * peers - 1) ** -0.5
+    own = pl.pallas_call(
+        functools.partial(add_kernel, scale),
+        out_shape=jax.ShapeDtypeStruct((own_rows, lon_total), jnp.float32),
+        in_specs=[whole],
+        out_specs=whole,
+        compiler_params=roomy,
+    )(arrived)
 
     before = lax.ppermute(own[-HALO:], ALL, forward)
     after = lax.ppermute(own[:HALO], ALL, backward)
-    place = jnp.stack(
-        [ring * wide_count + quarter * own_rows - HALO, jnp.int32(row_count * bands)]
-    ).astype(jnp.int32)
     copies = pl.pallas_call(
         stencil_kernel,
         out_shape=jax.ShapeDtypeStruct((peers, own_rows * lon_total // 128 + 8, 128), jnp.float32),
@@ -481,10 +586,10 @@
         in_specs=[scalars] + [whole] * 4,
         out_specs=[whole] * 2,
         compiler_params=roomy,
-    )(where_side, adjoint_all, jnp.transpose(lon_matrix), perturbations, other_members)
+    )(place, adjoint_all, lon_matrix, perturbations, other_members)
     by_pair = swapped(projected, "lat_0", 0)
     full = pl.pallas_call(
-        functools.partial(gather_kernel, (members_here * peers - 1) ** -0.5),
+        functools.partial(gather_kernel, scale),
         out_shape=jax.ShapeDtypeStruct((bands, repeats, coarse_rows, coarse_lons), jnp.float32),
         in_specs=[whole] * 2,
         out_specs=whole,

time: 166 us -> 171 us (1.030)
  local copies, waits for them, and re-layouts: 33 us -> 37.3 us
  other arithmetic: 8.97 us -> 5.22 us
  starting transfers between devices: 61.3 us -> 64 us
    ppermute x4, waiting for transfers between devices: 4.17 us -> 11.7 us  [body(): rising = lax.ppermute(rising, 'lat_0', up)]
    ppermute x1, waiting for transfers between devices: 6.48 us -> 0.01 us  [body(): other_members = lax.ppermute(other_members, 'lat_1', across)]
    unnamed x39 -> x67, local copies, waits for them, and re-layouts: 17.5 us -> 23 us
    ppermute x4, starting transfers between devices: 0.01 us -> 3.92 us  [body(): rising = lax.ppermute(rising, 'lat_0', up)]
    ppermute x3, waiting for transfers between devices: 0.01 us -> 2.69 us  [body(): falling = lax.ppermute(falling, 'lat_0', down)]
    all_to_all x5, waiting for transfers between devices: 34.7 us -> 33 us  [swapped(): lax.all_to_all(value, axis, split_axis=dim, concat_axis=dim, tiled=True)]
    pallas_call x2 -> x4, Pallas kernels: 4.97 us -> 5.35 us  [the longest x1 3.6 us: body(): pl.pallas_call(localize_kernel, out_shape=jax.ShapeDtypeStruct((peers, pi...]
  transfers between devices with their start and end apart: 20 -> 20, of which waited for: 11 -> 11; matrix products, arithmetic and copies ran while one was open for 20% -> 14% of each run, Pallas kernels for 3% -> 4%
where the time goes in v7:
time: 171 us; the launch traced here: 170 us
  starting transfers between devices  64 us (37%)
  waiting for transfers between devices  50.9 us (30%)
  local copies, waits for them, and re-layouts  37.3 us (22%)
  Pallas kernels  11.4 us (7%)
  other arithmetic  5.22 us (3%)
    all_to_all x5, waiting for transfers between devices, swapped(): lax.all_to_all(value, axis, split_axis=dim, concat_axis=dim, tiled=True)  33 us
    all_to_all x5, starting transfers between devices, swapped(): lax.all_to_all(value, axis, split_axis=dim, concat_axis=dim, tiled=True)  28.9 us
    unnamed x67, local copies, waits for them, and re-layouts  23 us
    ppermute x4, waiting for transfers between devices, body(): rising = lax.ppermute(rising, 'lat_0', up)  11.7 us
    ppermute x3, starting transfers between devices, body(): falling = lax.ppermute(falling, 'lat_0', down)  11.2 us
    slice x8, local copies, waits for them, and re-layouts, lat_of(): block[sides * weight_rows:].reshape(sides, row_count // 2, coarse_lons)  5.78 us
    ppermute x4, starting transfers between devices, body(): rising = lax.ppermute(rising, 'lat_0', up)  3.92 us
    pallas_call x1, Pallas kernels, body(): pl.pallas_call(localize_kernel, out_shape=jax.ShapeDtypeStruct((peers, pi...  3.6 us
  transfers between devices with their start and end apart: 20, of which 11 were waited for; matrix products, arithmetic and copies ran while one was open for 14% of the time, Pallas kernels for 4%

profile of v7, /device:TPU:2, one launch (start us, length us, event | category | flops | bytes accessed | tf_op | source)
XLA Modules:
  0.0 169.8 jit_solution(13217478800132700691)
XLA Ops:
  3.8 2.1 %collective-permute-start.1 = (bf16[144,256]{1,0:T(8,128)(2,1)}, bf16[144,256]{1,0:T(8,128)(2,1)}, u32[]{:S(2)}, u32[]{:S(2)}) collective-permute-start(bf16[144,256]{1,0:T(8,128)(2,1)} %maximum_maximum_fusion), channel_id=1, source_target_pairs={{0,1},{1,0},{2,3},{3,2},{4,5},{5,4},{6,7},{7,6},{8,9},{9,8},{10,11... | collective-permute-start | bytes 221192 | tf_op jit(solution)/shard_map/ppermute | solution.py:450
  5.9 2.3 %constant_dynamic-slice_fusion.1 = bf16[4,4,32,1024]{3,2,1,0:T(8,128)(2,1)} fusion(bf16[4,8,32,1024]{3,2,1,0:T(8,128)(2,1)} %own_ref.3, s32[]{:T(128)S(6)} %select_n.85), kind=kLoop, calls=%fused_computation.37 | loop fusion | bytes 2097156 | tf_op jit(solution)/shard_map/dynamic_slice | solution.py:475
  8.2 1.4 collective-permute-start
  12.0 5.9 %all-to-all-start = ((f32[16,3,16,128]{3,2,1,0:T(8,128)}), f32[16,3,16,128]{3,2,1,0:T(8,128)S(1)}, u32[]{:S(2)}, u32[]{:S(2)}) async-start(f32[16,3,16,128]{3,2,1,0:T(8,128)} %copy-done.9), calls=%async_computation | async-start | bytes 786432 | tf_op jit(solution)/shard_map/all_to_all | solution.py:20
  19.8 2.0 %collective-permute-start.3 = (bf16[288,256]{1,0:T(8,128)(2,1)S(1)}, bf16[288,256]{1,0:T(8,128)(2,1)S(1)}, u32[]{:S(2)}, u32[]{:S(2)}) collective-permute-start(bf16[288,256]{1,0:T(8,128)(2,1)S(1)} %pad_maximum_fusion.refs_0_), channel_id=1, source_target_pairs={{0,2},{2,4},{4,6},{6,8},{8,10},{10,12},{12,14},{14,0},{1,3},{3,5},... | collective-permute-start | bytes 442376 | tf_op jit(solution)/shard_map/ppermute | solution.py:484
  21.8 4.0 %collective-permute-start.2 = (bf16[288,256]{1,0:T(8,128)(2,1)S(1)}, bf16[288,256]{1,0:T(8,128)(2,1)S(1)}, u32[]{:S(2)}, u32[]{:S(2)}) collective-permute-start(bf16[288,256]{1,0:T(8,128)(2,1)S(1)} %pad_maximum_fusion.refs_0_), channel_id=1, source_target_pairs={{2,0},{4,2},{6,4},{8,6},{10,8},{12,10},{14,12},{0,14},{3,1},{5,3},... | collective-permute-start | bytes 442376 | tf_op jit(solution)/shard_map/ppermute | solution.py:486
  26.5 3.4 %collective-permute-done.3.refs_7_ = bf16[288,256]{1,0:T(8,128)(2,1)S(1)} collective-permute-done((bf16[288,256]{1,0:T(8,128)(2,1)S(1)}, bf16[288,256]{1,0:T(8,128)(2,1)S(1)}, u32[]{:S(2)}, u32[]{:S(2)}) %collective-permute-start.3) | collective-permute-done | bytes 147488 | tf_op jit(solution)/shard_map/ppermute | solution.py:484
  30.6 3.2 %collective-permute-start.5 = (bf16[288,256]{1,0:T(8,128)(2,1)S(1)}, bf16[288,256]{1,0:T(8,128)(2,1)}, u32[]{:S(2)}, u32[]{:S(2)}) collective-permute-start(bf16[288,256]{1,0:T(8,128)(2,1)S(1)} %collective-permute-done.2.refs_1_), channel_id=1, source_target_pairs={{2,0},{4,2},{6,4},{8,6},{10,8},{12,10},{14,12},{0,14},{3,1},{5,3},... | collective-permute-start | bytes 442376 | tf_op jit(solution)/shard_map/ppermute | solution.py:486
  34.5 2.0 %collective-permute-done.4.refs_6_ = bf16[288,256]{1,0:T(8,128)(2,1)S(1)} collective-permute-done((bf16[288,256]{1,0:T(8,128)(2,1)S(1)}, bf16[288,256]{1,0:T(8,128)(2,1)S(1)}, u32[]{:S(2)}, u32[]{:S(2)}) %collective-permute-start.4) | collective-permute-done | bytes 147488 | tf_op jit(solution)/shard_map/ppermute | solution.py:484
  38.1 1.9 %collective-permute-start.7 = (bf16[288,256]{1,0:T(8,128)(2,1)}, bf16[288,256]{1,0:T(8,128)(2,1)}, u32[]{:S(2)}, u32[]{:S(2)}) collective-permute-start(bf16[288,256]{1,0:T(8,128)(2,1)} %copy-done.15), channel_id=1, source_target_pairs={{0,2},{2,4},{4,6},{6,8},{8,10},{10,12},{12,14},{14,0},{1,3},{3,5},... | collective-permute-start | bytes 442376 | tf_op jit(solution)/shard_map/ppermute | solution.py:484
  40.8 2.4 %collective-permute-start.9 = (f32[16,2,16,128]{3,2,1,0:T(8,128)}, f32[16,2,16,128]{3,2,1,0:T(8,128)}, u32[]{:S(2)}, u32[]{:S(2)}) collective-permute-start(f32[16,2,16,128]{3,2,1,0:T(8,128)} %maximum_select_fusion), channel_id=1, source_target_pairs={{0,1},{1,0},{2,3},{3,2},{4,5},{5,4},{6,7},{7,6},{8,9},{9,8},{10,11... | collective-permute-start | bytes 786440 | tf_op jit(solution)/shard_map/ppermute | solution.py:490
  43.2 3.9 %collective-permute-start.6 = (bf16[288,256]{1,0:T(8,128)(2,1)}, bf16[288,256]{1,0:T(8,128)(2,1)}, u32[]{:S(2)}, u32[]{:S(2)}) collective-permute-start(bf16[288,256]{1,0:T(8,128)(2,1)} %collective-permute-done.5.refs_2_), channel_id=1, source_target_pairs={{2,0},{4,2},{6,4},{8,6},{10,8},{12,10},{14,12},{0,14},{3,1},{5,3},... | collective-permute-start | bytes 442376 | tf_op jit(solution)/shard_map/ppermute | solution.py:486
  47.2 1.5 collective-permute-done.7.refs_5_
  48.8 2.7 %collective-permute-done.6.refs_3_ = bf16[288,256]{1,0:T(8,128)(2,1)} collective-permute-done((bf16[288,256]{1,0:T(8,128)(2,1)}, bf16[288,256]{1,0:T(8,128)(2,1)}, u32[]{:S(2)}, u32[]{:S(2)}) %collective-permute-start.6) | collective-permute-done | bytes 147488 | tf_op jit(solution)/shard_map/ppermute | solution.py:486
  51.5 4.8 %collective-permute-done.8.refs_4_ = bf16[288,256]{1,0:T(8,128)(2,1)} collective-permute-done((bf16[288,256]{1,0:T(8,128)(2,1)}, bf16[288,256]{1,0:T(8,128)(2,1)}, u32[]{:S(2)}, u32[]{:S(2)}) %collective-permute-start.8) | collective-permute-done | bytes 147488 | tf_op jit(solution)/shard_map/ppermute | solution.py:484
  60.9 3.6 %shard_map.96 = s16[16,144,128]{2,1,0:T(8,128)(2,1)S(1)} custom-call(s32[5]{0:T(128)S(1)} %stack.26.place_ref.side_ref, bf16[256,1024]{1,0:T(8,128)(2,1)S(1)} %copy-done.5, bf16[4,8,32,1024]{3,2,1,0:T(8,128)(2,1)S(1)} %copy-done, bf16[4,4,32,1024]{3,2,1,0:T(8,128)(2,1)S(1)} %collective-permute-done.other_ref, bf16[288,256]{1,0:T(8,128)(2,1)S(1)} %copy-done.11, ...), custom_call_target="tpu_custom_call" | custom-call | tf_op jit(solution)/shard_map/pallas_call | solution.py:513
  65.4 4.4 %all-to-all-start.1 = ((s16[16,144,128]{2,1,0:T(8,128)(2,1)}), s16[16,144,128]{2,1,0:T(8,128)(2,1)S(1)}, u32[]{:S(2)}, u32[]{:S(2)}) async-start(s16[16,144,128]{2,1,0:T(8,128)(2,1)} %copy-done.4), calls=%async_computation.1 | async-start | bytes 1179648 | tf_op jit(solution)/shard_map/all_to_all | solution.py:20
  69.8 1.4 shard_map.98.local_ref
  77.0 2.0 %collective-permute-start.13 = (f32[8,3584]{1,0:T(8,128)}, f32[8,3584]{1,0:T(8,128)S(1)}, u32[]{:S(2)}, u32[]{:S(2)}) collective-permute-start(f32[8,3584]{1,0:T(8,128)} %get-tuple-element.46), channel_id=1, source_target_pairs={{16,0},{17,1},{18,2},{19,3},{20,4},{21,5},{22,6},{23,7},{24,8},{25... | collective-permute-start | bytes 344072 | tf_op jit(solution)/shard_map/ppermute | solution.py:547
  79.0 2.3 %collective-permute-start.12 = (f32[8,3584]{1,0:T(8,128)S(1)}, f32[8,3584]{1,0:T(8,128)S(1)}, u32[]{:S(2)}, u32[]{:S(2)}) collective-permute-start(f32[8,3584]{1,0:T(8,128)S(1)} %get-tuple-element.47), channel_id=1, source_target_pairs={{0,16},{1,17},{2,18},{3,19},{4,20},{5,21},{6,22},{7,23},{8,24},{9,... | collective-permute-start | bytes 344072 | tf_op jit(solution)/shard_map/ppermute | solution.py:546
  82.2 3.3 %collective-permute-start.11 = (f32[8,1024]{1,0:T(8,128)S(1)}, f32[8,1024]{1,0:T(8,128)S(1)}, u32[]{:S(2)}, u32[]{:S(2)}) collective-permute-start(f32[8,1024]{1,0:T(8,128)S(1)} %get-tuple-element.54), channel_id=1, source_target_pairs={{16,0},{17,1},{18,2},{19,3},{20,4},{21,5},{22,6},{23,7},{24,8},{25... | collective-permute-start | bytes 98312 | tf_op jit(solution)/shard_map/ppermute | solution.py:570
  85.5 3.0 %collective-permute-start.10 = (f32[8,1024]{1,0:T(8,128)S(1)}, f32[8,1024]{1,0:T(8,128)S(1)}, u32[]{:S(2)}, u32[]{:S(2)}) collective-permute-start(f32[8,1024]{1,0:T(8,128)S(1)} %get-tuple-element.55), channel_id=1, source_target_pairs={{0,16},{1,17},{2,18},{3,19},{4,20},{5,21},{6,22},{7,23},{8,24},{9,... | collective-permute-start | bytes 98312 | tf_op jit(solution)/shard_map/ppermute | solution.py:569
  91.1 1.7 %shard_map.100 = f32[16,136,128]{2,1,0:T(8,128)S(1)} custom-call(s32[5]{0:T(128)S(1)} %stack.26.place_ref.side_ref, f32[16,1024]{1,0:T(8,128)S(1)} %shard_map.97.own_ref, f32[8,1024]{1,0:T(8,128)S(1)} %collective-permute-done.10.before_ref, f32[8,1024]{1,0:T(8,128)S(1)} %collective-permute-done.11.after_ref, f32[2,32,1024]{2,1,0:T(8,128)S(1)} %get-tuple-element.31.wind_ref, ...), custom_call_target="tpu_custom_call" | custom-call | tf_op jit(solution)/shard_map/pallas_call | solution.py:571
  93.8 7.0 %all-to-all-start.2 = ((f32[16,136,128]{2,1,0:T(8,128)}), f32[16,136,128]{2,1,0:T(8,128)S(1)}, u32[]{:S(2)}, u32[]{:S(2)}) async-start(f32[16,136,128]{2,1,0:T(8,128)} %copy-done.1), calls=%async_computation.2 | async-start | bytes 2228224 | tf_op jit(solution)/shard_map/all_to_all | solution.py:20
  105.2 11.7 %all-to-all-done.2.adjoint_ref = f32[16,136,128]{2,1,0:T(8,128)S(1)} async-done(((f32[16,136,128]{2,1,0:T(8,128)}), f32[16,136,128]{2,1,0:T(8,128)S(1)}, u32[]{:S(2)}, u32[]{:S(2)}) %all-to-all-start.2) | async-done | bytes 1114144 | tf_op jit(solution)/shard_map/all_to_all | solution.py:20
  119.2 2.2 %shard_map.101 = (s16[8,144,256]{2,1,0:T(8,128)(2,1)S(1)}, f32[2,4,32,64]{3,2,1,0:T(8,128)S(1)}) custom-call(s32[5]{0:T(128)S(1)} %stack.26.place_ref.side_ref, f32[16,136,128]{2,1,0:T(8,128)S(1)} %all-to-all-done.2.adjoint_ref, bf16[256,1024]{1,0:T(8,128)(2,1)S(1)} %copy-done.6, bf16[4,8,32,1024]{3,2,1,0:T(8,128)(2,1)S(1)} %copy-done, ...), custom_call_target="tpu_custom_call" | custom-call | tf_op jit(solution)/shard_map/pallas_call | solution.py:580
  122.2 8.0 %all-to-all-start.3 = ((s16[8,144,256]{2,1,0:T(8,128)(2,1)}), s16[8,144,256]{2,1,0:T(8,128)(2,1)S(1)}, u32[]{:S(2)}, u32[]{:S(2)}) async-start(s16[8,144,256]{2,1,0:T(8,128)(2,1)} %copy-done.12), calls=%async_computation.3 | async-start | bytes 1179648 | tf_op jit(solution)/shard_map/all_to_all | solution.py:20
  136.8 12.6 %all-to-all-done.3.message_ref = s16[8,144,256]{2,1,0:T(8,128)(2,1)S(1)} async-done(((s16[8,144,256]{2,1,0:T(8,128)(2,1)}), s16[8,144,256]{2,1,0:T(8,128)(2,1)S(1)}, u32[]{:S(2)}, u32[]{:S(2)}) %all-to-all-start.3) | async-done | bytes 589856 | tf_op jit(solution)/shard_map/all_to_all | solution.py:20
  150.8 3.5 %all-to-all-start.4 = ((f32[16,2,8,256]{3,2,1,0:T(8,128)}), f32[16,2,8,256]{3,2,1,0:T(8,128)S(1)}, u32[]{:S(2)}, u32[]{:S(2)}) async-start(f32[16,2,8,256]{3,2,1,0:T(8,128)} %shard_map.102), calls=%async_computation.4 | async-start | bytes 524288 | tf_op jit(solution)/shard_map/all_to_all | solution.py:20
  154.3 3.4 %collective-permute-start.14 = (f32[4,32,64]{2,1,0:T(8,128)S(1)}, f32[4,32,64]{2,1,0:T(8,128)S(1)}, u32[]{:S(2)}, u32[]{:S(2)}) collective-permute-start(f32[4,32,64]{2,1,0:T(8,128)S(1)} %get-tuple-element.49), channel_id=1, source_target_pairs={{0,1},{1,0},{2,3},{3,2},{4,5},{5,4},{6,7},{7,6},{8,9},{9,8},{10,11... | collective-permute-start | bytes 98312 | tf_op jit(solution)/shard_map/ppermute | solution.py:607
  157.7 2.5 %collective-permute-done.14 = f32[4,32,64]{2,1,0:T(8,128)S(1)} collective-permute-done((f32[4,32,64]{2,1,0:T(8,128)S(1)}, f32[4,32,64]{2,1,0:T(8,128)S(1)}, u32[]{:S(2)}, u32[]{:S(2)}) %collective-permute-start.14) | collective-permute-done | bytes 32800 | tf_op jit(solution)/shard_map/ppermute | solution.py:607
  160.9 7.8 %all-to-all-done.4 = f32[16,2,8,256]{3,2,1,0:T(8,128)S(1)} async-done(((f32[16,2,8,256]{3,2,1,0:T(8,128)}), f32[16,2,8,256]{3,2,1,0:T(8,128)S(1)}, u32[]{:S(2)}, u32[]{:S(2)}) %all-to-all-start.4) | async-done | bytes 262176 | tf_op jit(solution)/shard_map/all_to_all | solution.py:20
  (131 shorter events, 44.5 us)
Async XLA Ops:
  0.6 9.0 %copy-start.21 = (f32[4,8,32,8]{2,3,1,0:T(8,128)S(1)}, f32[4,8,32,8]{2,3,1,0:T(8,128)}, u32[]{:S(2)}) copy-start(f32[4,8,32,8]{2,3,1,0:T(8,128)} %param.15) | copy-start | bytes 98308
  0.6 9.0 %copy-start.20 = (f32[4,8,32,8]{2,3,1,0:T(8,128)S(1)}, f32[4,8,32,8]{2,3,1,0:T(8,128)}, u32[]{:S(2)}) copy-start(f32[4,8,32,8]{2,3,1,0:T(8,128)} %param.14) | copy-start | bytes 98308
  0.7 9.0 %copy-start.19 = (s32[4,8,32,8]{2,3,1,0:T(8,128)S(1)}, s32[4,8,32,8]{2,3,1,0:T(8,128)}, u32[]{:S(2)}) copy-start(s32[4,8,32,8]{2,3,1,0:T(8,128)} %param.13) | copy-start | bytes 98308
  1.4 4.5 %copy-start.24 = (bf16[16,128]{1,0:T(8,128)(2,1)}, bf16[16,128]{1,0:T(8,128)(2,1)S(1)}, u32[]{:S(2)}) copy-start(bf16[16,128]{1,0:T(8,128)(2,1)S(1)} %get-tuple-element.72) | copy-start | bytes 12292
  1.4 4.5 %copy-start.25 = (bf16[16,128]{1,0:T(8,128)(2,1)}, bf16[16,128]{1,0:T(8,128)(2,1)S(1)}, u32[]{:S(2)}) copy-start(bf16[16,128]{1,0:T(8,128)(2,1)S(1)} %get-tuple-element.73) | copy-start | bytes 12292
  3.8 6.8 %collective-permute-start.1 = (bf16[144,256]{1,0:T(8,128)(2,1)}, bf16[144,256]{1,0:T(8,128)(2,1)}, u32[]{:S(2)}, u32[]{:S(2)}) collective-permute-start(bf16[144,256]{1,0:T(8,128)(2,1)} %maximum_maximum_fusion), channel_id=1, source_target_pairs={{0,1},{1,0},{2,3},{3,2},{4,5},{5,4},{6,7},{7,6},{8,9},{9,8},{10,11... | collective-permute-start | bytes 221192 | tf_op jit(solution)/shard_map/ppermute | solution.py:450
  5.9 3.7 %copy-start.22 = (f32[2,32,64]{2,1,0:T(8,128)S(1)}, f32[2,32,64]{2,1,0:T(8,128)}, u32[]{:S(2)}) copy-start(f32[2,32,64]{2,1,0:T(8,128)} %wind_ref.1) | copy-start | bytes 49156
  8.2 48.0 %copy-start = (bf16[4,8,32,1024]{3,2,1,0:T(8,128)(2,1)S(1)}, bf16[4,8,32,1024]{3,2,1,0:T(8,128)(2,1)}, u32[]{:S(2)}) copy-start(bf16[4,8,32,1024]{3,2,1,0:T(8,128)(2,1)} %own_ref.3) | copy-start | bytes 6291460
  8.2 48.0 %collective-permute-start = (bf16[4,4,32,1024]{3,2,1,0:T(8,128)(2,1)}, bf16[4,4,32,1024]{3,2,1,0:T(8,128)(2,1)S(1)}, u32[]{:S(2)}, u32[]{:S(2)}) collective-permute-start(bf16[4,4,32,1024]{3,2,1,0:T(8,128)(2,1)} %constant_dynamic-slice_fusion.1), channel_id=1, source_target_pairs={{0,1},{1,0},{2,3},{3,2},{4,5},{5,4},{6,7},{7,6},{8,9},{9,8},{10,11... | collective-permute-start | bytes 3145736 | tf_op jit(solution)/shard_map/ppermute | solution.py:478
  12.0 26.1 %all-to-all-start = ((f32[16,3,16,128]{3,2,1,0:T(8,128)}), f32[16,3,16,128]{3,2,1,0:T(8,128)S(1)}, u32[]{:S(2)}, u32[]{:S(2)}) async-start(f32[16,3,16,128]{3,2,1,0:T(8,128)} %copy-done.9), calls=%async_computation | async-start | bytes 786432 | tf_op jit(solution)/shard_map/all_to_all | solution.py:20
  19.8 10.1 %collective-permute-start.3 = (bf16[288,256]{1,0:T(8,128)(2,1)S(1)}, bf16[288,256]{1,0:T(8,128)(2,1)S(1)}, u32[]{:S(2)}, u32[]{:S(2)}) collective-permute-start(bf16[288,256]{1,0:T(8,128)(2,1)S(1)} %pad_maximum_fusion.refs_0_), channel_id=1, source_target_pairs={{0,2},{2,4},{4,6},{6,8},{8,10},{10,12},{12,14},{14,0},{1,3},{3,5},... | collective-permute-start | bytes 442376 | tf_op jit(solution)/shard_map/ppermute | solution.py:484
  21.8 8.8 %collective-permute-start.2 = (bf16[288,256]{1,0:T(8,128)(2,1)S(1)}, bf16[288,256]{1,0:T(8,128)(2,1)S(1)}, u32[]{:S(2)}, u32[]{:S(2)}) collective-permute-start(bf16[288,256]{1,0:T(8,128)(2,1)S(1)} %pad_maximum_fusion.refs_0_), channel_id=1, source_target_pairs={{2,0},{4,2},{6,4},{8,6},{10,8},{12,10},{14,12},{0,14},{3,1},{5,3},... | collective-permute-start | bytes 442376 | tf_op jit(solution)/shard_map/ppermute | solution.py:486
  29.9 6.6 %collective-permute-start.4 = (bf16[288,256]{1,0:T(8,128)(2,1)S(1)}, bf16[288,256]{1,0:T(8,128)(2,1)S(1)}, u32[]{:S(2)}, u32[]{:S(2)}) collective-permute-start(bf16[288,256]{1,0:T(8,128)(2,1)S(1)} %collective-permute-done.3.refs_7_), channel_id=1, source_target_pairs={{0,2},{2,4},{4,6},{6,8},{8,10},{10,12},{12,14},{14,0},{1,3},{3,5},... | collective-permute-start | bytes 442376 | tf_op jit(solution)/shard_map/ppermute | solution.py:484
  30.6 6.6 %collective-permute-start.5 = (bf16[288,256]{1,0:T(8,128)(2,1)S(1)}, bf16[288,256]{1,0:T(8,128)(2,1)}, u32[]{:S(2)}, u32[]{:S(2)}) collective-permute-start(bf16[288,256]{1,0:T(8,128)(2,1)S(1)} %collective-permute-done.2.refs_1_), channel_id=1, source_target_pairs={{2,0},{4,2},{6,4},{8,6},{10,8},{12,10},{14,12},{0,14},{3,1},{5,3},... | collective-permute-start | bytes 442376 | tf_op jit(solution)/shard_map/ppermute | solution.py:486
  38.1 10.6 %collective-permute-start.7 = (bf16[288,256]{1,0:T(8,128)(2,1)}, bf16[288,256]{1,0:T(8,128)(2,1)}, u32[]{:S(2)}, u32[]{:S(2)}) collective-permute-start(bf16[288,256]{1,0:T(8,128)(2,1)} %copy-done.15), channel_id=1, source_target_pairs={{0,2},{2,4},{4,6},{6,8},{8,10},{10,12},{12,14},{14,0},{1,3},{3,5},... | collective-permute-start | bytes 442376 | tf_op jit(solution)/shard_map/ppermute | solution.py:484
  40.8 24.6 %collective-permute-start.9 = (f32[16,2,16,128]{3,2,1,0:T(8,128)}, f32[16,2,16,128]{3,2,1,0:T(8,128)}, u32[]{:S(2)}, u32[]{:S(2)}) collective-permute-start(f32[16,2,16,128]{3,2,1,0:T(8,128)} %maximum_select_fusion), channel_id=1, source_target_pairs={{0,1},{1,0},{2,3},{3,2},{4,5},{5,4},{6,7},{7,6},{8,9},{9,8},{10,11... | collective-permute-start | bytes 786440 | tf_op jit(solution)/shard_map/ppermute | solution.py:490
  43.2 8.2 %collective-permute-start.6 = (bf16[288,256]{1,0:T(8,128)(2,1)}, bf16[288,256]{1,0:T(8,128)(2,1)}, u32[]{:S(2)}, u32[]{:S(2)}) collective-permute-start(bf16[288,256]{1,0:T(8,128)(2,1)} %collective-permute-done.5.refs_2_), channel_id=1, source_target_pairs={{2,0},{4,2},{6,4},{8,6},{10,8},{12,10},{14,12},{0,14},{3,1},{5,3},... | collective-permute-start | bytes 442376 | tf_op jit(solution)/shard_map/ppermute | solution.py:486
  48.7 7.5 %collective-permute-start.8 = (bf16[288,256]{1,0:T(8,128)(2,1)}, bf16[288,256]{1,0:T(8,128)(2,1)}, u32[]{:S(2)}, u32[]{:S(2)}) collective-permute-start(bf16[288,256]{1,0:T(8,128)(2,1)} %collective-permute-done.7.refs_5_), channel_id=1, source_target_pairs={{0,2},{2,4},{4,6},{6,8},{8,10},{10,12},{12,14},{14,0},{1,3},{3,5},... | collective-permute-start | bytes 442376 | tf_op jit(solution)/shard_map/ppermute | solution.py:484
  56.2 1.0 copy-start.5
  60.9 3.6 %copy-start.2 = (bf16[4,4,32,1024]{3,2,1,0:T(8,128)(2,1)}, bf16[4,4,32,1024]{3,2,1,0:T(8,128)(2,1)S(1)}, u32[]{:S(2)}) copy-start(bf16[4,4,32,1024]{3,2,1,0:T(8,128)(2,1)S(1)} %collective-permute-done.other_ref) | copy-start | bytes 3145732
  65.4 16.6 %all-to-all-start.1 = ((s16[16,144,128]{2,1,0:T(8,128)(2,1)}), s16[16,144,128]{2,1,0:T(8,128)(2,1)S(1)}, u32[]{:S(2)}, u32[]{:S(2)}) async-start(s16[16,144,128]{2,1,0:T(8,128)(2,1)} %copy-done.4), calls=%async_computation.1 | async-start | bytes 1179648 | tf_op jit(solution)/shard_map/all_to_all | solution.py:20
  71.2 10.7 %copy-start.7 = (f32[16,3584]{1,0:T(8,128)}, f32[16,3584]{1,0:T(8,128)S(1)}, u32[]{:S(2)}) copy-start(f32[16,3584]{1,0:T(8,128)S(1)} %shard_map.98.local_ref) | copy-start | bytes 688132
  77.0 11.5 %collective-permute-start.13 = (f32[8,3584]{1,0:T(8,128)}, f32[8,3584]{1,0:T(8,128)S(1)}, u32[]{:S(2)}, u32[]{:S(2)}) collective-permute-start(f32[8,3584]{1,0:T(8,128)} %get-tuple-element.46), channel_id=1, source_target_pairs={{16,0},{17,1},{18,2},{19,3},{20,4},{21,5},{22,6},{23,7},{24,8},{25... | collective-permute-start | bytes 344072 | tf_op jit(solution)/shard_map/ppermute | solution.py:547
  79.0 9.5 %collective-permute-start.12 = (f32[8,3584]{1,0:T(8,128)S(1)}, f32[8,3584]{1,0:T(8,128)S(1)}, u32[]{:S(2)}, u32[]{:S(2)}) collective-permute-start(f32[8,3584]{1,0:T(8,128)S(1)} %get-tuple-element.47), channel_id=1, source_target_pairs={{0,16},{1,17},{2,18},{3,19},{4,20},{5,21},{6,22},{7,23},{8,24},{9,... | collective-permute-start | bytes 344072 | tf_op jit(solution)/shard_map/ppermute | solution.py:546
  82.2 7.9 %collective-permute-start.11 = (f32[8,1024]{1,0:T(8,128)S(1)}, f32[8,1024]{1,0:T(8,128)S(1)}, u32[]{:S(2)}, u32[]{:S(2)}) collective-permute-start(f32[8,1024]{1,0:T(8,128)S(1)} %get-tuple-element.54), channel_id=1, source_target_pairs={{16,0},{17,1},{18,2},{19,3},{20,4},{21,5},{22,6},{23,7},{24,8},{25... | collective-permute-start | bytes 98312 | tf_op jit(solution)/shard_map/ppermute | solution.py:570
  85.5 5.6 %collective-permute-start.10 = (f32[8,1024]{1,0:T(8,128)S(1)}, f32[8,1024]{1,0:T(8,128)S(1)}, u32[]{:S(2)}, u32[]{:S(2)}) collective-permute-start(f32[8,1024]{1,0:T(8,128)S(1)} %get-tuple-element.55), channel_id=1, source_target_pairs={{0,16},{1,17},{2,18},{3,19},{4,20},{5,21},{6,22},{7,23},{8,24},{9,... | collective-permute-start | bytes 98312 | tf_op jit(solution)/shard_map/ppermute | solution.py:569
  93.8 23.1 %all-to-all-start.2 = ((f32[16,136,128]{2,1,0:T(8,128)}), f32[16,136,128]{2,1,0:T(8,128)S(1)}, u32[]{:S(2)}, u32[]{:S(2)}) async-start(f32[16,136,128]{2,1,0:T(8,128)} %copy-done.1), calls=%async_computation.2 | async-start | bytes 2228224 | tf_op jit(solution)/shard_map/all_to_all | solution.py:20
  116.9 1.2 copy-start.3
  122.2 27.1 %all-to-all-start.3 = ((s16[8,144,256]{2,1,0:T(8,128)(2,1)}), s16[8,144,256]{2,1,0:T(8,128)(2,1)S(1)}, u32[]{:S(2)}, u32[]{:S(2)}) async-start(s16[8,144,256]{2,1,0:T(8,128)(2,1)} %copy-done.12), calls=%async_computation.3 | async-start | bytes 1179648 | tf_op jit(solution)/shard_map/all_to_all | solution.py:20
  136.6 32.5 %copy-start.23 = (bf16[8,4,8,256]{3,2,1,0:T(8,128)(2,1)S(1)}, bf16[8,4,8,256]{3,2,1,0:T(8,128)(2,1)}, u32[]{:S(2)}) copy-start(bf16[8,4,8,256]{3,2,1,0:T(8,128)(2,1)} %param.8) | copy-start | bytes 393220
  150.8 17.9 %all-to-all-start.4 = ((f32[16,2,8,256]{3,2,1,0:T(8,128)}), f32[16,2,8,256]{3,2,1,0:T(8,128)S(1)}, u32[]{:S(2)}, u32[]{:S(2)}) async-start(f32[16,2,8,256]{3,2,1,0:T(8,128)} %shard_map.102), calls=%async_computation.4 | async-start | bytes 524288 | tf_op jit(solution)/shard_map/all_to_all | solution.py:20
  154.3 5.9 %collective-permute-start.14 = (f32[4,32,64]{2,1,0:T(8,128)S(1)}, f32[4,32,64]{2,1,0:T(8,128)S(1)}, u32[]{:S(2)}, u32[]{:S(2)}) collective-permute-start(f32[4,32,64]{2,1,0:T(8,128)S(1)} %get-tuple-element.49), channel_id=1, source_target_pairs={{0,1},{1,0},{2,3},{3,2},{4,5},{5,4},{6,7},{7,6},{8,9},{9,8},{10,11... | collective-permute-start | bytes 98312 | tf_op jit(solution)/shard_map/ppermute | solution.py:607
  (14 other events, 11.7 us)

commit v8 on v5

--- a/solution.py
+++ b/solution.py
@@ -28,6 +28,57 @@
 
 def dot(a, b):
     return jnp.dot(a, b, preferred_element_type=jnp.float32)
+
+
+def row_codes(value):
+    largest = jnp.maximum(jnp.max(jnp.abs(value), axis=1, keepdims=True), 1e-30)
+    return jnp.ceil(jnp.log(largest) * (256.0 / LN2)) + 1.0
+
+
+def code_scale(codes):
+    return jnp.exp(codes * (LN2 / 256.0))
+
+
+def rounded(value, codes):
+    return jnp.round(value * (STEPS_16 / code_scale(codes)))
+
+
+def to_16(value):
+    return value.astype(jnp.int32).astype(jnp.int16)
+
+
+def from_16(value):
+    return value.astype(jnp.int32).astype(jnp.float32)
+
+
+def as_tiles(value):
+    rows, cols = value.shape
+    return jnp.concatenate(
+        [
+            value[t * 8 : (t + 1) * 8, at * 128 : (at + 1) * 128]
+            for t in range(rows // 8)
+            for at in range(cols // 128)
+        ],
+        axis=0,
+    )
+
+
+def from_tiles(value, row_tiles):
+    lane_tiles = value.shape[0] // 8 // row_tiles
+    rows = []
+    for t in range(row_tiles):
+        start = t * lane_tiles * 8
+        strips = [value[start + at * 8 : start + (at + 1) * 8] for at in range(lane_tiles)]
+        rows.append(jnp.concatenate(strips, axis=1))
+    return jnp.concatenate(rows, axis=0)
+
+
+def tile_scales(codes, lane_tiles):
+    scales = code_scale(codes) * (1.0 / STEPS_16)
+    parts = []
+    for t in range(scales.shape[0] // 8):
+        parts += [scales[t * 8 : (t + 1) * 8]] * lane_tiles
+    return jnp.concatenate(parts, axis=0)
 
 
 def member_rows(side, own_ref, other_ref, member, level):
@@ -61,16 +112,28 @@
             term = term * member_rows(side, own_ref, other_ref, member, level)
             total = term if total is None else total + term
         count = sum_ref.shape[0] // levels_here
-        sum_ref[level * count : (level + 1) * count] = total.reshape(count, tall // count, lon_total)
-
-
-def row_codes(value):
-    largest = jnp.maximum(jnp.max(jnp.abs(value), axis=1, keepdims=True), 1e-30)
-    return jnp.ceil(jnp.log(largest) * (256.0 / LN2)) + 1.0
-
-
-def code_scale(codes):
-    return jnp.exp(codes * (LN2 / 256.0))
+        piece_rows = tall // count
+        data = piece_rows * lon_total // 128
+        codes = row_codes(total)
+        total = rounded(total, codes)
+        for piece in range(count):
+            part = slice(piece * piece_rows, (piece + 1) * piece_rows)
+            sum_ref[level * count + piece, :data] = to_16(as_tiles(total[part]))
+            sum_ref[level * count + piece, data:] = to_16(
+                jnp.broadcast_to(codes[part], (piece_rows, 128))
+            )
+
+
+def add_kernel(scale, message_ref, out_ref):
+    sources, rows, _ = message_ref.shape
+    own_rows, lon_total = out_ref.shape
+    total = None
+    for source in range(sources):
+        value = from_16(message_ref[source, : rows - own_rows])
+        codes = from_16(message_ref[source, rows - own_rows :])
+        value = value * tile_scales(codes, lon_total // 128)
+        total = value if total is None else total + value
+    out_ref[...] = from_tiles(total, own_rows // 8) * scale
 
 
 def project_kernel(side_ref, adjoint_ref, lon_ref, own_ref, other_ref, out_ref, tile_ref):
@@ -310,7 +373,6 @@
     pairs = members_here * levels_here
     quarters = peers // levels_here
     own_rows = wide_count // quarters
-    member_scale = 1.0 / jnp.sqrt(jnp.float32(members_here * peers - 1))
     quarter = lax.axis_index("mem") % quarters
     ring = lax.axis_index("lat_0")
     first = lax.axis_index("lat_1") == 0
@@ -407,9 +469,10 @@
     whole = pl.BlockSpec(memory_space=pltpu.VMEM)
     roomy = pltpu.CompilerParams(vmem_limit_bytes=48 * 1024 * 1024)
     where_side = jnp.reshape(side, (1,)).astype(jnp.int32)
+    piece_rows = own_rows * lon_total // 128 + own_rows
     partial_sum = pl.pallas_call(
         localize_kernel,
-        out_shape=jax.ShapeDtypeStruct((peers, own_rows, lon_total), jnp.float32),
+        out_shape=jax.ShapeDtypeStruct((peers, piece_rows, 128), jnp.int16),
         in_specs=[scalars] + [whole] * (4 + rings),
         out_specs=whole,
         compiler_params=roomy,
@@ -456,7 +519,14 @@
         compiler_params=roomy,
     )(before, local, after)
 
-    own = arrived.sum(axis=0) * member_scale
+    scale = (members_here * peers - 1) ** -0.5
+    own = pl.pallas_call(
+        functools.partial(add_kernel, scale),
+        out_shape=jax.ShapeDtypeStruct((own_rows, lon_total), jnp.float32),
+        in_specs=[whole],
+        out_specs=whole,
+        compiler_params=roomy,
+    )(arrived)
 
     before = lax.ppermute(own[-HALO:], ALL, forward)
     after = lax.ppermute(own[:HALO], ALL, backward)
@@ -484,7 +554,7 @@
     )(where_side, adjoint_all, jnp.transpose(lon_matrix), perturbations, other_members)
     by_pair = swapped(projected, "lat_0", 0)
     full = pl.pallas_call(
-        functools.partial(gather_kernel, (members_here * peers - 1) ** -0.5),
+        functools.partial(gather_kernel, scale),
         out_shape=jax.ShapeDtypeStruct((bands, repeats, coarse_rows, coarse_lons), jnp.float32),
         in_specs=[whole] * 2,
         out_specs=whole,

time: 166 us -> 165 us (level)
    all_to_all x5, waiting for transfers between devices: 34.7 us -> 32.1 us  [swapped(): lax.all_to_all(value, axis, split_axis=dim, concat_axis=dim, tiled=True)]
    ppermute x3, starting transfers between devices: 12.4 us -> 10.4 us  [body(): falling = lax.ppermute(falling, 'lat_0', down)]
    ppermute x4, starting transfers between devices: 0.01 us -> 1.93 us  [body(): rising = lax.ppermute(rising, 'lat_0', up)]
    ppermute x1, waiting for transfers between devices: 0.01 us -> 1.86 us  [body(): before = lax.ppermute(own[-HALO:], ALL, forward)]
    all_to_all x5, starting transfers between devices: 28.5 us -> 30.3 us  [swapped(): lax.all_to_all(value, axis, split_axis=dim, concat_axis=dim, tiled=True)]
    pallas_call x2 -> x3, Pallas kernels: 4.97 us -> 5.29 us  [the longest x1 3.71 us: body(): pl.pallas_call(localize_kernel, out_shape=jax.ShapeDtypeStruct((peers, pi...]
  transfers between devices with their start and end apart: 20 -> 20, of which waited for: 11 -> 10; matrix products, arithmetic and copies ran while one was open for 20% -> 19% of each run, Pallas kernels for 3% -> 4%
where the time goes in v8:
time: 165 us; the launch traced here: 164 us
  starting transfers between devices  62.3 us (38%)
  waiting for transfers between devices  47.8 us (29%)
  local copies, waits for them, and re-layouts  34.1 us (21%)
  Pallas kernels  10.7 us (6%)
  other arithmetic  7.67 us (5%)
    all_to_all x5, waiting for transfers between devices, swapped(): lax.all_to_all(value, axis, split_axis=dim, concat_axis=dim, tiled=True)  32.1 us
    all_to_all x5, starting transfers between devices, swapped(): lax.all_to_all(value, axis, split_axis=dim, concat_axis=dim, tiled=True)  30.3 us
    unnamed x39, local copies, waits for them, and re-layouts  17.9 us
    ppermute x3, starting transfers between devices, body(): falling = lax.ppermute(falling, 'lat_0', down)  10.4 us
    ppermute x1, waiting for transfers between devices, body(): other_members = lax.ppermute(other_members, 'lat_1', across)  6.76 us
    slice x8, local copies, waits for them, and re-layouts, lat_of(): block[sides * weight_rows:].reshape(sides, row_count // 2, coarse_lons)  5.75 us
    ppermute x4, waiting for transfers between devices, body(): rising = lax.ppermute(rising, 'lat_0', up)  3.94 us
    pallas_call x1, Pallas kernels, body(): pl.pallas_call(localize_kernel, out_shape=jax.ShapeDtypeStruct((peers, pi...  3.71 us
  transfers between devices with their start and end apart: 20, of which 10 were waited for; matrix products, arithmetic and copies ran while one was open for 19% of the time, Pallas kernels for 4%

profile of v8, /device:TPU:2, one launch (start us, length us, event | category | flops | bytes accessed | tf_op | source)
XLA Modules:
  0.0 163.6 jit_solution(12035522075321794333)
XLA Ops:
  2.5 2.2 %collective-permute-start = (bf16[144,256]{1,0:T(8,128)(2,1)S(1)}, bf16[144,256]{1,0:T(8,128)(2,1)S(1)}, u32[]{:S(2)}, u32[]{:S(2)}) collective-permute-start(bf16[144,256]{1,0:T(8,128)(2,1)S(1)} %maximum_maximum_fusion), channel_id=1, source_target_pairs={{0,1},{1,0},{2,3},{3,2},{4,5},{5,4},{6,7},{7,6},{8,9},{9,8},{10,11... | collective-permute-start | bytes 221192 | tf_op jit(solution)/shard_map/ppermute | solution.py:412
  9.1 1.9 %collective-permute-start.3 = (bf16[288,256]{1,0:T(8,128)(2,1)}, bf16[288,256]{1,0:T(8,128)(2,1)}, u32[]{:S(2)}, u32[]{:S(2)}) collective-permute-start(bf16[288,256]{1,0:T(8,128)(2,1)} %pad_maximum_fusion.refs_0_), channel_id=1, source_target_pairs={{0,2},{2,4},{4,6},{6,8},{8,10},{10,12},{12,14},{14,0},{1,3},{3,5},... | collective-permute-start | bytes 442376 | tf_op jit(solution)/shard_map/ppermute | solution.py:447
  11.0 3.9 %collective-permute-start.2 = (bf16[288,256]{1,0:T(8,128)(2,1)}, bf16[288,256]{1,0:T(8,128)(2,1)}, u32[]{:S(2)}, u32[]{:S(2)}) collective-permute-start(bf16[288,256]{1,0:T(8,128)(2,1)} %pad_maximum_fusion.refs_0_), channel_id=1, source_target_pairs={{2,0},{4,2},{6,4},{8,6},{10,8},{12,10},{14,12},{0,14},{3,1},{5,3},... | collective-permute-start | bytes 442376 | tf_op jit(solution)/shard_map/ppermute | solution.py:449
  15.8 5.9 %all-to-all-start = ((f32[16,3,16,128]{3,2,1,0:T(8,128)}), f32[16,3,16,128]{3,2,1,0:T(8,128)S(1)}, u32[]{:S(2)}, u32[]{:S(2)}) async-start(f32[16,3,16,128]{3,2,1,0:T(8,128)} %bitcast.18), calls=%async_computation | async-start | bytes 786432 | tf_op jit(solution)/shard_map/all_to_all | solution.py:20
  22.9 2.1 %collective-permute-start.1 = (bf16[4,4,32,1024]{3,2,1,0:T(8,128)(2,1)}, bf16[4,4,32,1024]{3,2,1,0:T(8,128)(2,1)S(1)}, u32[]{:S(2)}, u32[]{:S(2)}) collective-permute-start(bf16[4,4,32,1024]{3,2,1,0:T(8,128)(2,1)} %constant_dynamic-slice_fusion.1), channel_id=1, source_target_pairs={{0,1},{1,0},{2,3},{3,2},{4,5},{5,4},{6,7},{7,6},{8,9},{9,8},{10,11... | collective-permute-start | bytes 3145736 | tf_op jit(solution)/shard_map/ppermute | solution.py:441
  25.0 3.2 %collective-permute-start.5 = (bf16[288,256]{1,0:T(8,128)(2,1)}, bf16[288,256]{1,0:T(8,128)(2,1)}, u32[]{:S(2)}, u32[]{:S(2)}) collective-permute-start(bf16[288,256]{1,0:T(8,128)(2,1)} %collective-permute-done.2.refs_1_), channel_id=1, source_target_pairs={{2,0},{4,2},{6,4},{8,6},{10,8},{12,10},{14,12},{0,14},{3,1},{5,3},... | collective-permute-start | bytes 442376 | tf_op jit(solution)/shard_map/ppermute | solution.py:449
  28.8 2.1 %copy.50 = bf16[256,1024]{0,1:T(8,128)(2,1)} copy(bf16[256,1024]{1,0:T(8,128)(2,1)} %lon_ref.1) | data formatting | bytes 1048576 | tf_op args[3]
  32.9 1.4 collective-permute-start.9
  34.3 3.2 %collective-permute-start.6 = (bf16[288,256]{1,0:T(8,128)(2,1)}, bf16[288,256]{1,0:T(8,128)(2,1)}, u32[]{:S(2)}, u32[]{:S(2)}) collective-permute-start(bf16[288,256]{1,0:T(8,128)(2,1)} %collective-permute-done.5.refs_2_), channel_id=1, source_target_pairs={{2,0},{4,2},{6,4},{8,6},{10,8},{12,10},{14,12},{0,14},{3,1},{5,3},... | collective-permute-start | bytes 442376 | tf_op jit(solution)/shard_map/ppermute | solution.py:449
  39.6 1.6 reshape_squeeze_reshape.3
  41.2 1.4 fusion
  43.4 2.1 %collective-permute-done.8.refs_4_ = bf16[288,256]{1,0:T(8,128)(2,1)} collective-permute-done((bf16[288,256]{1,0:T(8,128)(2,1)}, bf16[288,256]{1,0:T(8,128)(2,1)}, u32[]{:S(2)}, u32[]{:S(2)}) %collective-permute-start.8) | collective-permute-done | bytes 147488 | tf_op jit(solution)/shard_map/ppermute | solution.py:447
  45.5 6.8 %collective-permute-done.1.other_ref = bf16[4,4,32,1024]{3,2,1,0:T(8,128)(2,1)S(1)} collective-permute-done((bf16[4,4,32,1024]{3,2,1,0:T(8,128)(2,1)}, bf16[4,4,32,1024]{3,2,1,0:T(8,128)(2,1)S(1)}, u32[]{:S(2)}, u32[]{:S(2)}) %collective-permute-start.1) | collective-permute-done | bytes 1048608 | tf_op jit(solution)/shard_map/ppermute | solution.py:441
  53.3 3.7 %shard_map.95 = s16[16,144,128]{2,1,0:T(8,128)(2,1)S(1)} custom-call(s32[1]{0:T(128)} %bitcast.side_ref, bf16[64,128]{1,0:T(8,128)(2,1)S(1)} %copy.49.columns_ref, bf16[256,1024]{1,0:T(8,128)(2,1)S(1)} %copy-done.6, bf16[4,8,32,1024]{3,2,1,0:T(8,128)(2,1)S(1)} %copy-done, bf16[4,4,32,1024]{3,2,1,0:T(8,128)(2,1)S(1)} %collective-permute-done.1.other_ref, ...), custom_call_target="tpu_custom_call" | custom-call | tf_op jit(solution)/shard_map/pallas_call | solution.py:473
  57.8 5.7 %all-to-all-start.1 = ((s16[16,144,128]{2,1,0:T(8,128)(2,1)}), s16[16,144,128]{2,1,0:T(8,128)(2,1)S(1)}, u32[]{:S(2)}, u32[]{:S(2)}) async-start(s16[16,144,128]{2,1,0:T(8,128)(2,1)} %copy-done.4), calls=%async_computation.1 | async-start | bytes 1179648 | tf_op jit(solution)/shard_map/all_to_all | solution.py:20
  64.2 1.4 shard_map.97.local_ref
  71.4 2.0 %collective-permute-start.13 = (f32[8,3584]{1,0:T(8,128)}, f32[8,3584]{1,0:T(8,128)S(1)}, u32[]{:S(2)}, u32[]{:S(2)}) collective-permute-start(f32[8,3584]{1,0:T(8,128)} %get-tuple-element.44), channel_id=1, source_target_pairs={{16,0},{17,1},{18,2},{19,3},{20,4},{21,5},{22,6},{23,7},{24,8},{25... | collective-permute-start | bytes 344072 | tf_op jit(solution)/shard_map/ppermute | solution.py:509
  73.4 2.3 %collective-permute-start.12 = (f32[8,3584]{1,0:T(8,128)S(1)}, f32[8,3584]{1,0:T(8,128)S(1)}, u32[]{:S(2)}, u32[]{:S(2)}) collective-permute-start(f32[8,3584]{1,0:T(8,128)S(1)} %get-tuple-element.45), channel_id=1, source_target_pairs={{0,16},{1,17},{2,18},{3,19},{4,20},{5,21},{6,22},{7,23},{8,24},{9,... | collective-permute-start | bytes 344072 | tf_op jit(solution)/shard_map/ppermute | solution.py:508
  76.6 3.3 %collective-permute-start.11 = (f32[8,1024]{1,0:T(8,128)S(1)}, f32[8,1024]{1,0:T(8,128)S(1)}, u32[]{:S(2)}, u32[]{:S(2)}) collective-permute-start(f32[8,1024]{1,0:T(8,128)S(1)} %get-tuple-element.52), channel_id=1, source_target_pairs={{16,0},{17,1},{18,2},{19,3},{20,4},{21,5},{22,6},{23,7},{24,8},{25... | collective-permute-start | bytes 98312 | tf_op jit(solution)/shard_map/ppermute | solution.py:532
  79.8 3.0 %collective-permute-start.10 = (f32[8,1024]{1,0:T(8,128)S(1)}, f32[8,1024]{1,0:T(8,128)S(1)}, u32[]{:S(2)}, u32[]{:S(2)}) collective-permute-start(f32[8,1024]{1,0:T(8,128)S(1)} %get-tuple-element.53), channel_id=1, source_target_pairs={{0,16},{1,17},{2,18},{3,19},{4,20},{5,21},{6,22},{7,23},{8,24},{9,... | collective-permute-start | bytes 98312 | tf_op jit(solution)/shard_map/ppermute | solution.py:531
  83.5 1.9 %collective-permute-done.10.before_ref = f32[8,1024]{1,0:T(8,128)S(1)} collective-permute-done((f32[8,1024]{1,0:T(8,128)S(1)}, f32[8,1024]{1,0:T(8,128)S(1)}, u32[]{:S(2)}, u32[]{:S(2)}) %collective-permute-start.10) | collective-permute-done | bytes 32800 | tf_op jit(solution)/shard_map/ppermute | solution.py:531
  85.4 1.7 %shard_map.99 = f32[16,136,128]{2,1,0:T(8,128)S(1)} custom-call(s32[2]{0:T(128)S(1)} %copy-done.9, f32[16,1024]{1,0:T(8,128)S(1)} %shard_map.96.own_ref, f32[8,1024]{1,0:T(8,128)S(1)} %collective-permute-done.10.before_ref, f32[8,1024]{1,0:T(8,128)S(1)} %collective-permute-done.11.after_ref, f32[2,32,1024]{2,1,0:T(8,128)S(1)} %get-tuple-element.29.wind_ref, ...), custom_call_target="tpu_custom_call" | custom-call | tf_op jit(solution)/shard_map/pallas_call | solution.py:536
  88.1 6.2 %all-to-all-start.2 = ((f32[16,136,128]{2,1,0:T(8,128)}), f32[16,136,128]{2,1,0:T(8,128)S(1)}, u32[]{:S(2)}, u32[]{:S(2)}) async-start(f32[16,136,128]{2,1,0:T(8,128)} %copy-done.1), calls=%async_computation.2 | async-start | bytes 2228224 | tf_op jit(solution)/shard_map/all_to_all | solution.py:20
  98.7 11.7 %all-to-all-done.2.adjoint_ref = f32[16,136,128]{2,1,0:T(8,128)S(1)} async-done(((f32[16,136,128]{2,1,0:T(8,128)}), f32[16,136,128]{2,1,0:T(8,128)S(1)}, u32[]{:S(2)}, u32[]{:S(2)}) %all-to-all-start.2) | async-done | bytes 1114144 | tf_op jit(solution)/shard_map/all_to_all | solution.py:20
  112.7 1.7 %shard_map.100 = (s16[8,144,256]{2,1,0:T(8,128)(2,1)S(1)}, f32[2,4,32,64]{3,2,1,0:T(8,128)S(1)}) custom-call(s32[1]{0:T(128)} %bitcast.side_ref, f32[16,136,128]{2,1,0:T(8,128)S(1)} %all-to-all-done.2.adjoint_ref, bf16[1024,256]{1,0:T(8,128)(2,1)S(1)} %bitcast.88, bf16[4,8,32,1024]{3,2,1,0:T(8,128)(2,1)S(1)} %copy-done, bf16[4,4,32,1024]{3,2,1,0:T(8,128)(2,1)S(1)} %copy-done.3), custom_call_target="tpu_custom_call" | custom-call | tf_op jit(solution)/shard_map/pallas_call | solution.py:545
  115.2 8.8 %all-to-all-start.3 = ((s16[8,144,256]{2,1,0:T(8,128)(2,1)}), s16[8,144,256]{2,1,0:T(8,128)(2,1)S(1)}, u32[]{:S(2)}, u32[]{:S(2)}) async-start(s16[8,144,256]{2,1,0:T(8,128)(2,1)} %copy-done.7), calls=%async_computation.3 | async-start | bytes 1179648 | tf_op jit(solution)/shard_map/all_to_all | solution.py:20
  130.6 12.6 %all-to-all-done.3.message_ref = s16[8,144,256]{2,1,0:T(8,128)(2,1)S(1)} async-done(((s16[8,144,256]{2,1,0:T(8,128)(2,1)}), s16[8,144,256]{2,1,0:T(8,128)(2,1)S(1)}, u32[]{:S(2)}, u32[]{:S(2)}) %all-to-all-start.3) | async-done | bytes 589856 | tf_op jit(solution)/shard_map/all_to_all | solution.py:20
  143.2 1.4 shard_map.101
  144.6 3.5 %all-to-all-start.4 = ((f32[16,2,8,256]{3,2,1,0:T(8,128)}), f32[16,2,8,256]{3,2,1,0:T(8,128)S(1)}, u32[]{:S(2)}, u32[]{:S(2)}) async-start(f32[16,2,8,256]{3,2,1,0:T(8,128)} %shard_map.101), calls=%async_computation.4 | async-start | bytes 524288 | tf_op jit(solution)/shard_map/all_to_all | solution.py:20
  148.2 3.4 %collective-permute-start.14 = (f32[4,32,64]{2,1,0:T(8,128)S(1)}, f32[4,32,64]{2,1,0:T(8,128)S(1)}, u32[]{:S(2)}, u32[]{:S(2)}) collective-permute-start(f32[4,32,64]{2,1,0:T(8,128)S(1)} %get-tuple-element.47), channel_id=1, source_target_pairs={{0,1},{1,0},{2,3},{3,2},{4,5},{5,4},{6,7},{7,6},{8,9},{9,8},{10,11... | collective-permute-start | bytes 98312 | tf_op jit(solution)/shard_map/ppermute | solution.py:572
  151.6 2.5 %collective-permute-done.14 = f32[4,32,64]{2,1,0:T(8,128)S(1)} collective-permute-done((f32[4,32,64]{2,1,0:T(8,128)S(1)}, f32[4,32,64]{2,1,0:T(8,128)S(1)}, u32[]{:S(2)}, u32[]{:S(2)}) %collective-permute-start.14) | collective-permute-done | bytes 32800 | tf_op jit(solution)/shard_map/ppermute | solution.py:572
  154.8 7.8 %all-to-all-done.4 = f32[16,2,8,256]{3,2,1,0:T(8,128)S(1)} async-done(((f32[16,2,8,256]{3,2,1,0:T(8,128)}), f32[16,2,8,256]{3,2,1,0:T(8,128)S(1)}, u32[]{:S(2)}, u32[]{:S(2)}) %all-to-all-start.4) | async-done | bytes 262176 | tf_op jit(solution)/shard_map/all_to_all | solution.py:20
  (118 shorter events, 40.0 us)
Async XLA Ops:
  2.5 5.9 %collective-permute-start = (bf16[144,256]{1,0:T(8,128)(2,1)S(1)}, bf16[144,256]{1,0:T(8,128)(2,1)S(1)}, u32[]{:S(2)}, u32[]{:S(2)}) collective-permute-start(bf16[144,256]{1,0:T(8,128)(2,1)S(1)} %maximum_maximum_fusion), channel_id=1, source_target_pairs={{0,1},{1,0},{2,3},{3,2},{4,5},{5,4},{6,7},{7,6},{8,9},{9,8},{10,11... | collective-permute-start | bytes 221192 | tf_op jit(solution)/shard_map/ppermute | solution.py:412
  6.5 15.3 %copy-start = (bf16[4,8,32,1024]{3,2,1,0:T(8,128)(2,1)S(1)}, bf16[4,8,32,1024]{3,2,1,0:T(8,128)(2,1)}, u32[]{:S(2)}) copy-start(bf16[4,8,32,1024]{3,2,1,0:T(8,128)(2,1)} %own_ref.3) | copy-start | bytes 6291460
  9.1 15.9 %collective-permute-start.3 = (bf16[288,256]{1,0:T(8,128)(2,1)}, bf16[288,256]{1,0:T(8,128)(2,1)}, u32[]{:S(2)}, u32[]{:S(2)}) collective-permute-start(bf16[288,256]{1,0:T(8,128)(2,1)} %pad_maximum_fusion.refs_0_), channel_id=1, source_target_pairs={{0,2},{2,4},{4,6},{6,8},{8,10},{10,12},{12,14},{14,0},{1,3},{3,5},... | collective-permute-start | bytes 442376 | tf_op jit(solution)/shard_map/ppermute | solution.py:447
  11.0 14.0 %collective-permute-start.2 = (bf16[288,256]{1,0:T(8,128)(2,1)}, bf16[288,256]{1,0:T(8,128)(2,1)}, u32[]{:S(2)}, u32[]{:S(2)}) collective-permute-start(bf16[288,256]{1,0:T(8,128)(2,1)} %pad_maximum_fusion.refs_0_), channel_id=1, source_target_pairs={{2,0},{4,2},{6,4},{8,6},{10,8},{12,10},{14,12},{0,14},{3,1},{5,3},... | collective-permute-start | bytes 442376 | tf_op jit(solution)/shard_map/ppermute | solution.py:449
  15.8 16.3 %all-to-all-start = ((f32[16,3,16,128]{3,2,1,0:T(8,128)}), f32[16,3,16,128]{3,2,1,0:T(8,128)S(1)}, u32[]{:S(2)}, u32[]{:S(2)}) async-start(f32[16,3,16,128]{3,2,1,0:T(8,128)} %bitcast.18), calls=%async_computation | async-start | bytes 786432 | tf_op jit(solution)/shard_map/all_to_all | solution.py:20
  22.9 29.4 %collective-permute-start.1 = (bf16[4,4,32,1024]{3,2,1,0:T(8,128)(2,1)}, bf16[4,4,32,1024]{3,2,1,0:T(8,128)(2,1)S(1)}, u32[]{:S(2)}, u32[]{:S(2)}) collective-permute-start(bf16[4,4,32,1024]{3,2,1,0:T(8,128)(2,1)} %constant_dynamic-slice_fusion.1), channel_id=1, source_target_pairs={{0,1},{1,0},{2,3},{3,2},{4,5},{5,4},{6,7},{7,6},{8,9},{9,8},{10,11... | collective-permute-start | bytes 3145736 | tf_op jit(solution)/shard_map/ppermute | solution.py:441
  25.0 7.1 %collective-permute-start.4 = (bf16[288,256]{1,0:T(8,128)(2,1)}, bf16[288,256]{1,0:T(8,128)(2,1)}, u32[]{:S(2)}, u32[]{:S(2)}) collective-permute-start(bf16[288,256]{1,0:T(8,128)(2,1)} %collective-permute-done.3.refs_7_), channel_id=1, source_target_pairs={{0,2},{2,4},{4,6},{6,8},{8,10},{10,12},{12,14},{14,0},{1,3},{3,5},... | collective-permute-start | bytes 442376 | tf_op jit(solution)/shard_map/ppermute | solution.py:447
  25.0 7.1 %collective-permute-start.5 = (bf16[288,256]{1,0:T(8,128)(2,1)}, bf16[288,256]{1,0:T(8,128)(2,1)}, u32[]{:S(2)}, u32[]{:S(2)}) collective-permute-start(bf16[288,256]{1,0:T(8,128)(2,1)} %collective-permute-done.2.refs_1_), channel_id=1, source_target_pairs={{2,0},{4,2},{6,4},{8,6},{10,8},{12,10},{14,12},{0,14},{3,1},{5,3},... | collective-permute-start | bytes 442376 | tf_op jit(solution)/shard_map/ppermute | solution.py:449
  32.1 6.7 %collective-permute-start.7 = (bf16[288,256]{1,0:T(8,128)(2,1)}, bf16[288,256]{1,0:T(8,128)(2,1)}, u32[]{:S(2)}, u32[]{:S(2)}) collective-permute-start(bf16[288,256]{1,0:T(8,128)(2,1)} %collective-permute-done.4.refs_6_), channel_id=1, source_target_pairs={{0,2},{2,4},{4,6},{6,8},{8,10},{10,12},{12,14},{14,0},{1,3},{3,5},... | collective-permute-start | bytes 442376 | tf_op jit(solution)/shard_map/ppermute | solution.py:447
  32.9 24.9 %collective-permute-start.9 = (f32[16,2,16,128]{3,2,1,0:T(8,128)}, f32[16,2,16,128]{3,2,1,0:T(8,128)}, u32[]{:S(2)}, u32[]{:S(2)}) collective-permute-start(f32[16,2,16,128]{3,2,1,0:T(8,128)} %maximum_select_fusion), channel_id=1, source_target_pairs={{0,1},{1,0},{2,3},{3,2},{4,5},{5,4},{6,7},{7,6},{8,9},{9,8},{10,11... | collective-permute-start | bytes 786440 | tf_op jit(solution)/shard_map/ppermute | solution.py:453
  34.3 9.1 %collective-permute-start.6 = (bf16[288,256]{1,0:T(8,128)(2,1)}, bf16[288,256]{1,0:T(8,128)(2,1)}, u32[]{:S(2)}, u32[]{:S(2)}) collective-permute-start(bf16[288,256]{1,0:T(8,128)(2,1)} %collective-permute-done.5.refs_2_), channel_id=1, source_target_pairs={{2,0},{4,2},{6,4},{8,6},{10,8},{12,10},{14,12},{0,14},{3,1},{5,3},... | collective-permute-start | bytes 442376 | tf_op jit(solution)/shard_map/ppermute | solution.py:449
  38.8 6.7 %collective-permute-start.8 = (bf16[288,256]{1,0:T(8,128)(2,1)}, bf16[288,256]{1,0:T(8,128)(2,1)}, u32[]{:S(2)}, u32[]{:S(2)}) collective-permute-start(bf16[288,256]{1,0:T(8,128)(2,1)} %collective-permute-done.7.refs_5_), channel_id=1, source_target_pairs={{0,2},{2,4},{4,6},{6,8},{8,10},{10,12},{12,14},{14,0},{1,3},{3,5},... | collective-permute-start | bytes 442376 | tf_op jit(solution)/shard_map/ppermute | solution.py:447
  52.2 1.0 copy-start.6
  53.3 3.7 %copy-start.2 = (bf16[4,4,32,1024]{3,2,1,0:T(8,128)(2,1)}, bf16[4,4,32,1024]{3,2,1,0:T(8,128)(2,1)S(1)}, u32[]{:S(2)}) copy-start(bf16[4,4,32,1024]{3,2,1,0:T(8,128)(2,1)S(1)} %collective-permute-done.1.other_ref) | copy-start | bytes 3145732
  57.0 0.8 copy-start.4
  57.8 27.6 %copy-start.9 = (s32[2]{0:T(128)S(1)}, s32[2]{0:T(128)}, u32[]{:S(2)}) copy-start(s32[2]{0:T(128)} %pad_add_fusion.place_ref) | copy-start | bytes 28
  57.8 18.5 %all-to-all-start.1 = ((s16[16,144,128]{2,1,0:T(8,128)(2,1)}), s16[16,144,128]{2,1,0:T(8,128)(2,1)S(1)}, u32[]{:S(2)}, u32[]{:S(2)}) async-start(s16[16,144,128]{2,1,0:T(8,128)(2,1)} %copy-done.4), calls=%async_computation.1 | async-start | bytes 1179648 | tf_op jit(solution)/shard_map/all_to_all | solution.py:20
  63.6 0.6 copy-start.8
  71.4 11.5 %collective-permute-start.13 = (f32[8,3584]{1,0:T(8,128)}, f32[8,3584]{1,0:T(8,128)S(1)}, u32[]{:S(2)}, u32[]{:S(2)}) collective-permute-start(f32[8,3584]{1,0:T(8,128)} %get-tuple-element.44), channel_id=1, source_target_pairs={{16,0},{17,1},{18,2},{19,3},{20,4},{21,5},{22,6},{23,7},{24,8},{25... | collective-permute-start | bytes 344072 | tf_op jit(solution)/shard_map/ppermute | solution.py:509
  73.4 9.5 %collective-permute-start.12 = (f32[8,3584]{1,0:T(8,128)S(1)}, f32[8,3584]{1,0:T(8,128)S(1)}, u32[]{:S(2)}, u32[]{:S(2)}) collective-permute-start(f32[8,3584]{1,0:T(8,128)S(1)} %get-tuple-element.45), channel_id=1, source_target_pairs={{0,16},{1,17},{2,18},{3,19},{4,20},{5,21},{6,22},{7,23},{8,24},{9,... | collective-permute-start | bytes 344072 | tf_op jit(solution)/shard_map/ppermute | solution.py:508
  76.6 7.0 %collective-permute-start.11 = (f32[8,1024]{1,0:T(8,128)S(1)}, f32[8,1024]{1,0:T(8,128)S(1)}, u32[]{:S(2)}, u32[]{:S(2)}) collective-permute-start(f32[8,1024]{1,0:T(8,128)S(1)} %get-tuple-element.52), channel_id=1, source_target_pairs={{16,0},{17,1},{18,2},{19,3},{20,4},{21,5},{22,6},{23,7},{24,8},{25... | collective-permute-start | bytes 98312 | tf_op jit(solution)/shard_map/ppermute | solution.py:532
  79.8 5.6 %collective-permute-start.10 = (f32[8,1024]{1,0:T(8,128)S(1)}, f32[8,1024]{1,0:T(8,128)S(1)}, u32[]{:S(2)}, u32[]{:S(2)}) collective-permute-start(f32[8,1024]{1,0:T(8,128)S(1)} %get-tuple-element.53), channel_id=1, source_target_pairs={{0,16},{1,17},{2,18},{3,19},{4,20},{5,21},{6,22},{7,23},{8,24},{9,... | collective-permute-start | bytes 98312 | tf_op jit(solution)/shard_map/ppermute | solution.py:531
  87.1 1.0 copy-start.1
  88.1 22.3 %all-to-all-start.2 = ((f32[16,136,128]{2,1,0:T(8,128)}), f32[16,136,128]{2,1,0:T(8,128)S(1)}, u32[]{:S(2)}, u32[]{:S(2)}) async-start(f32[16,136,128]{2,1,0:T(8,128)} %copy-done.1), calls=%async_computation.2 | async-start | bytes 2228224 | tf_op jit(solution)/shard_map/all_to_all | solution.py:20
  110.4 1.2 copy-start.3
  111.6 1.0 copy-start.5
  114.4 0.8 copy-start.7
  115.2 28.0 %all-to-all-start.3 = ((s16[8,144,256]{2,1,0:T(8,128)(2,1)}), s16[8,144,256]{2,1,0:T(8,128)(2,1)S(1)}, u32[]{:S(2)}, u32[]{:S(2)}) async-start(s16[8,144,256]{2,1,0:T(8,128)(2,1)} %copy-done.7), calls=%async_computation.3 | async-start | bytes 1179648 | tf_op jit(solution)/shard_map/all_to_all | solution.py:20
  130.4 32.5 %copy-start.10 = (bf16[8,4,8,256]{3,2,1,0:T(8,128)(2,1)S(1)}, bf16[8,4,8,256]{3,2,1,0:T(8,128)(2,1)}, u32[]{:S(2)}) copy-start(bf16[8,4,8,256]{3,2,1,0:T(8,128)(2,1)} %param.8) | copy-start | bytes 393220
  144.6 17.9 %all-to-all-start.4 = ((f32[16,2,8,256]{3,2,1,0:T(8,128)}), f32[16,2,8,256]{3,2,1,0:T(8,128)S(1)}, u32[]{:S(2)}, u32[]{:S(2)}) async-start(f32[16,2,8,256]{3,2,1,0:T(8,128)} %shard_map.101), calls=%async_computation.4 | async-start | bytes 524288 | tf_op jit(solution)/shard_map/all_to_all | solution.py:20
  148.2 5.9 %collective-permute-start.14 = (f32[4,32,64]{2,1,0:T(8,128)S(1)}, f32[4,32,64]{2,1,0:T(8,128)S(1)}, u32[]{:S(2)}, u32[]{:S(2)}) collective-permute-start(f32[4,32,64]{2,1,0:T(8,128)S(1)} %get-tuple-element.47), channel_id=1, source_target_pairs={{0,1},{1,0},{2,3},{3,2},{4,5},{5,4},{6,7},{7,6},{8,9},{9,8},{10,11... | collective-permute-start | bytes 98312 | tf_op jit(solution)/shard_map/ppermute | solution.py:572

commit v9 on v8

--- a/solution.py
+++ b/solution.py
@@ -91,7 +91,7 @@
 
 
 def localize_kernel(side_ref, columns_ref, lon_ref, own_ref, other_ref, *refs):
-    block_refs, sum_ref = refs[:-1], refs[-1]
+    block_refs, sum_ref, lat_ref = refs[:-2], refs[-2], refs[-1]
     members, levels_here, row_count, lon_total = other_ref.shape
     tall = 2 * row_count
     side = side_ref[0]
@@ -122,6 +122,14 @@
             sum_ref[level * count + piece, data:] = to_16(
                 jnp.broadcast_to(codes[part], (piece_rows, 128))
             )
+    half = row_count // 2
+    for at, ref in enumerate(block_refs):
+        lat = ref[ref.shape[0] - row_count :]
+        for part in range(4):
+            rows = lat[part // 2 * half : (part // 2 + 1) * half]
+            lat_ref[at, part * half : (part + 1) * half] = rows[
+                :, part % 2 * lat_ref.shape[2] : (part % 2 + 1) * lat_ref.shape[2]
+            ]
 
 
 def add_kernel(scale, message_ref, out_ref):
@@ -470,11 +478,14 @@
     roomy = pltpu.CompilerParams(vmem_limit_bytes=48 * 1024 * 1024)
     where_side = jnp.reshape(side, (1,)).astype(jnp.int32)
     piece_rows = own_rows * lon_total // 128 + own_rows
-    partial_sum = pl.pallas_call(
+    partial_sum, lat_ring = pl.pallas_call(
         localize_kernel,
-        out_shape=jax.ShapeDtypeStruct((peers, piece_rows, 128), jnp.int16),
+        out_shape=[
+            jax.ShapeDtypeStruct((peers, piece_rows, 128), jnp.int16),
+            jax.ShapeDtypeStruct((rings, wide_count, coarse_total), jnp.bfloat16),
+        ],
         in_specs=[scalars] + [whole] * (4 + rings),
-        out_specs=whole,
+        out_specs=[whole] * 2,
         compiler_params=roomy,
     )(
         where_side,
@@ -497,14 +508,6 @@
         out_specs=whole,
         compiler_params=roomy,
     )(jnp.stack([side.astype(jnp.int32), is_own]), packed, passed)
-    local, *tied = lax.optimization_barrier((local, *[blocks[d] for d in range(rings)]))
-    lat_ring = jnp.concatenate([lat_of(block) for block in tied], axis=0)
-    lat_all = lax.dynamic_slice_in_dim(
-        jnp.concatenate([lat_ring, lat_ring], axis=0), rings - ring, rings, axis=0
-    )
-    repeats = pairs // rings
-    lat_all = jnp.broadcast_to(lat_all[:, None], (rings, repeats, wide_count, coarse_total))
-    lat_all = jnp.transpose(lat_all.reshape(rings * repeats * wide_count, coarse_total))
     before = lax.ppermute(local[-HALO:], ALL, forward)
     after = lax.ppermute(local[:HALO], ALL, backward)
     wide_rows = own_rows + 2 * HALO
@@ -542,6 +545,7 @@
     )(place, own, before, after, wide_wind, gains, values)
 
     adjoint_all = swapped(copies, "mem", 0)
+    repeats = pairs // rings
     projected, tiles = pl.pallas_call(
         project_kernel,
         out_shape=[
@@ -552,6 +556,12 @@
         out_specs=[whole] * 2,
         compiler_params=roomy,
     )(where_side, adjoint_all, jnp.transpose(lon_matrix), perturbations, other_members)
+    _, lat_ring = lax.optimization_barrier((projected, lat_ring))
+    lat_all = lax.dynamic_slice_in_dim(
+        jnp.concatenate([lat_ring, lat_ring], axis=0), rings - ring, rings, axis=0
+    )
+    lat_all = jnp.broadcast_to(lat_all[:, None], (rings, repeats, wide_count, coarse_total))
+    lat_all = jnp.transpose(lat_all.reshape(rings * repeats * wide_count, coarse_total))
     by_pair = swapped(projected, "lat_0", 0)
     full = pl.pallas_call(
         functools.partial(gather_kernel, scale),

time: 165 us -> 161 us (0.976)
  local copies, waits for them, and re-layouts: 34.1 us -> 18.5 us
  waiting for transfers between devices: 47.8 us -> 61.5 us
    all_to_all x5, waiting for transfers between devices: 32.1 us -> 43.9 us  [swapped(): lax.all_to_all(value, axis, split_axis=dim, concat_axis=dim, tiled=True)]
    unnamed x39 -> x30, local copies, waits for them, and re-layouts: 17.9 us -> 10.3 us
    slice x8 -> x0, local copies, waits for them, and re-layouts: 5.75 us -> none  [lat_of(): block[sides * weight_rows:].reshape(sides, row_count // 2, coarse_lons)]
    all_to_all x5, starting transfers between devices: 30.3 us -> 27.2 us  [swapped(): lax.all_to_all(value, axis, split_axis=dim, concat_axis=dim, tiled=True)]
    ppermute x1, waiting for transfers between devices: 6.76 us -> 9.39 us  [body(): other_members = lax.ppermute(other_members, 'lat_1', across)]
    ppermute x3, starting transfers between devices: 10.4 us -> 12.5 us  [body(): falling = lax.ppermute(falling, 'lat_0', down)]
    ppermute x1, waiting for transfers between devices: 1.86 us -> 0.01 us  [body(): before = lax.ppermute(own[-HALO:], ALL, forward)]
    ppermute x4, starting transfers between devices: 1.93 us -> 0.09 us  [body(): rising = lax.ppermute(rising, 'lat_0', up)]
  transfers between devices with their start and end apart: 20 -> 20, of which waited for: 10 -> 12; matrix products, arithmetic and copies ran while one was open for 19% -> 9% of each run, Pallas kernels for 4% -> 4%
where the time goes in v9:
time: 161 us; the launch traced here: 159 us
  waiting for transfers between devices  61.5 us (38%)
  starting transfers between devices  61.1 us (38%)
  local copies, waits for them, and re-layouts  18.5 us (11%)
  Pallas kernels  10.7 us (7%)
  other arithmetic  6.5 us (4%)
    all_to_all x5, waiting for transfers between devices, swapped(): lax.all_to_all(value, axis, split_axis=dim, concat_axis=dim, tiled=True)  43.9 us
    all_to_all x5, starting transfers between devices, swapped(): lax.all_to_all(value, axis, split_axis=dim, concat_axis=dim, tiled=True)  27.2 us
    ppermute x3, starting transfers between devices, body(): falling = lax.ppermute(falling, 'lat_0', down)  12.5 us
    unnamed x30, local copies, waits for them, and re-layouts  10.3 us
    ppermute x1, waiting for transfers between devices, body(): other_members = lax.ppermute(other_members, 'lat_1', across)  9.39 us
    ppermute x4, waiting for transfers between devices, body(): rising = lax.ppermute(rising, 'lat_0', up)  4.38 us
    ppermute x1, starting transfers between devices, body(): after = lax.ppermute(own[:HALO], ALL, backward)  3.72 us
    pallas_call x1, Pallas kernels, body(): pl.pallas_call(localize_kernel, out_shape=[jax.ShapeDtypeStruct((peers, p...  3.67 us
  transfers between devices with their start and end apart: 20, of which 12 were waited for; matrix products, arithmetic and copies ran while one was open for 9% of the time, Pallas kernels for 4%

profile of v9, /device:TPU:2, one launch (start us, length us, event | category | flops | bytes accessed | tf_op | source)
XLA Modules:
  0.0 159.3 jit_solution(17746332780405815057)
XLA Ops:
  2.5 2.2 %collective-permute-start = (bf16[144,256]{1,0:T(8,128)(2,1)S(1)}, bf16[144,256]{1,0:T(8,128)(2,1)S(1)}, u32[]{:S(2)}, u32[]{:S(2)}) collective-permute-start(bf16[144,256]{1,0:T(8,128)(2,1)S(1)} %maximum_maximum_fusion), channel_id=1, source_target_pairs={{0,1},{1,0},{2,3},{3,2},{4,5},{5,4},{6,7},{7,6},{8,9},{9,8},{10,11... | collective-permute-start | bytes 221192 | tf_op jit(solution)/shard_map/ppermute | solution.py:420
  8.5 5.9 %collective-permute-start.2 = (bf16[288,256]{1,0:T(8,128)(2,1)S(1)}, bf16[288,256]{1,0:T(8,128)(2,1)}, u32[]{:S(2)}, u32[]{:S(2)}) collective-permute-start(bf16[288,256]{1,0:T(8,128)(2,1)S(1)} %pad_maximum_fusion.refs_0_), channel_id=1, source_target_pairs={{2,0},{4,2},{6,4},{8,6},{10,8},{12,10},{14,12},{0,14},{3,1},{5,3},... | collective-permute-start | bytes 442376 | tf_op jit(solution)/shard_map/ppermute | solution.py:457
  15.3 5.9 %all-to-all-start = ((f32[16,3,16,128]{3,2,1,0:T(8,128)}), f32[16,3,16,128]{3,2,1,0:T(8,128)S(1)}, u32[]{:S(2)}, u32[]{:S(2)}) async-start(f32[16,3,16,128]{3,2,1,0:T(8,128)} %bitcast.18), calls=%async_computation | async-start | bytes 786432 | tf_op jit(solution)/shard_map/all_to_all | solution.py:20
  21.3 3.3 %collective-permute-start.5 = (bf16[288,256]{1,0:T(8,128)(2,1)}, bf16[288,256]{1,0:T(8,128)(2,1)}, u32[]{:S(2)}, u32[]{:S(2)}) collective-permute-start(bf16[288,256]{1,0:T(8,128)(2,1)} %collective-permute-done.2.refs_1_), channel_id=1, source_target_pairs={{2,0},{4,2},{6,4},{8,6},{10,8},{12,10},{14,12},{0,14},{3,1},{5,3},... | collective-permute-start | bytes 442376 | tf_op jit(solution)/shard_map/ppermute | solution.py:457
  25.7 2.1 %collective-permute-start.1 = (bf16[4,4,32,1024]{3,2,1,0:T(8,128)(2,1)}, bf16[4,4,32,1024]{3,2,1,0:T(8,128)(2,1)S(1)}, u32[]{:S(2)}, u32[]{:S(2)}) collective-permute-start(bf16[4,4,32,1024]{3,2,1,0:T(8,128)(2,1)} %constant_dynamic-slice_fusion), channel_id=1, source_target_pairs={{0,1},{1,0},{2,3},{3,2},{4,5},{5,4},{6,7},{7,6},{8,9},{9,8},{10,11... | collective-permute-start | bytes 3145736 | tf_op jit(solution)/shard_map/ppermute | solution.py:449
  30.3 2.1 %collective-permute-start.9 = (f32[16,2,16,128]{3,2,1,0:T(8,128)}, f32[16,2,16,128]{3,2,1,0:T(8,128)}, u32[]{:S(2)}, u32[]{:S(2)}) collective-permute-start(f32[16,2,16,128]{3,2,1,0:T(8,128)} %maximum_select_fusion), channel_id=1, source_target_pairs={{0,1},{1,0},{2,3},{3,2},{4,5},{5,4},{6,7},{7,6},{8,9},{9,8},{10,11... | collective-permute-start | bytes 786440 | tf_op jit(solution)/shard_map/ppermute | solution.py:461
  32.5 3.2 %collective-permute-start.6 = (bf16[288,256]{1,0:T(8,128)(2,1)}, bf16[288,256]{1,0:T(8,128)(2,1)}, u32[]{:S(2)}, u32[]{:S(2)}) collective-permute-start(bf16[288,256]{1,0:T(8,128)(2,1)} %collective-permute-done.5.refs_2_), channel_id=1, source_target_pairs={{2,0},{4,2},{6,4},{8,6},{10,8},{12,10},{14,12},{0,14},{3,1},{5,3},... | collective-permute-start | bytes 442376 | tf_op jit(solution)/shard_map/ppermute | solution.py:457
  35.7 1.5 collective-permute-done.7.refs_5_
  38.0 1.6 reshape_squeeze_reshape.3
  39.5 1.4 fusion.1
  41.8 2.3 %collective-permute-done.8.refs_4_ = bf16[288,256]{1,0:T(8,128)(2,1)} collective-permute-done((bf16[288,256]{1,0:T(8,128)(2,1)}, bf16[288,256]{1,0:T(8,128)(2,1)}, u32[]{:S(2)}, u32[]{:S(2)}) %collective-permute-start.8) | collective-permute-done | bytes 147488 | tf_op jit(solution)/shard_map/ppermute | solution.py:455
  44.1 9.4 %collective-permute-done.1.other_ref = bf16[4,4,32,1024]{3,2,1,0:T(8,128)(2,1)S(1)} collective-permute-done((bf16[4,4,32,1024]{3,2,1,0:T(8,128)(2,1)}, bf16[4,4,32,1024]{3,2,1,0:T(8,128)(2,1)S(1)}, u32[]{:S(2)}, u32[]{:S(2)}) %collective-permute-start.1) | collective-permute-done | bytes 1048608 | tf_op jit(solution)/shard_map/ppermute | solution.py:449
  55.4 3.7 %shard_map.95 = (s16[16,144,128]{2,1,0:T(8,128)(2,1)S(1)}, bf16[8,64,128]{2,1,0:T(8,128)(2,1)S(1)}) custom-call(s32[1]{0:T(128)} %bitcast.side_ref, bf16[64,128]{1,0:T(8,128)(2,1)S(1)} %copy.34.columns_ref, bf16[256,1024]{1,0:T(8,128)(2,1)S(1)} %copy-done.4, bf16[4,8,32,1024]{3,2,1,0:T(8,128)(2,1)S(1)} %copy-done, ...), custom_call_target="tpu_custom_call" | custom-call | tf_op jit(solution)/shard_map/pallas_call | solution.py:481
  60.6 5.7 %all-to-all-start.1 = ((s16[16,144,128]{2,1,0:T(8,128)(2,1)}), s16[16,144,128]{2,1,0:T(8,128)(2,1)S(1)}, u32[]{:S(2)}, u32[]{:S(2)}) async-start(s16[16,144,128]{2,1,0:T(8,128)(2,1)} %copy-done.8), calls=%async_computation.1 | async-start | bytes 1179648 | tf_op jit(solution)/shard_map/all_to_all | solution.py:20
  67.0 1.4 shard_map.97.local_ref
  68.4 2.1 %collective-permute-start.12 = (f32[8,3584]{1,0:T(8,128)S(1)}, f32[8,3584]{1,0:T(8,128)S(1)}, u32[]{:S(2)}, u32[]{:S(2)}) collective-permute-start(f32[8,3584]{1,0:T(8,128)S(1)} %get-tuple-element.33), channel_id=1, source_target_pairs={{0,16},{1,17},{2,18},{3,19},{4,20},{5,21},{6,22},{7,23},{8,24},{9,... | collective-permute-start | bytes 344072 | tf_op jit(solution)/shard_map/ppermute | solution.py:511
  70.5 3.5 %collective-permute-start.13 = (f32[8,3584]{1,0:T(8,128)S(1)}, f32[8,3584]{1,0:T(8,128)S(1)}, u32[]{:S(2)}, u32[]{:S(2)}) collective-permute-start(f32[8,3584]{1,0:T(8,128)S(1)} %get-tuple-element.32), channel_id=1, source_target_pairs={{16,0},{17,1},{18,2},{19,3},{20,4},{21,5},{22,6},{23,7},{24,8},{25... | collective-permute-start | bytes 344072 | tf_op jit(solution)/shard_map/ppermute | solution.py:512
  74.0 2.8 %all-to-all-done.1.message_ref = s16[16,144,128]{2,1,0:T(8,128)(2,1)S(1)} async-done(((s16[16,144,128]{2,1,0:T(8,128)(2,1)}), s16[16,144,128]{2,1,0:T(8,128)(2,1)S(1)}, u32[]{:S(2)}, u32[]{:S(2)}) %all-to-all-start.1) | async-done | bytes 589856 | tf_op jit(solution)/shard_map/all_to_all | solution.py:20
  77.0 2.0 %collective-permute-start.10 = (f32[8,1024]{1,0:T(8,128)S(1)}, f32[8,1024]{1,0:T(8,128)S(1)}, u32[]{:S(2)}, u32[]{:S(2)}) collective-permute-start(f32[8,1024]{1,0:T(8,128)S(1)} %get-tuple-element.41), channel_id=1, source_target_pairs={{0,16},{1,17},{2,18},{3,19},{4,20},{5,21},{6,22},{7,23},{8,24},{9,... | collective-permute-start | bytes 98312 | tf_op jit(solution)/shard_map/ppermute | solution.py:534
  79.0 3.7 %collective-permute-start.11 = (f32[8,1024]{1,0:T(8,128)S(1)}, f32[8,1024]{1,0:T(8,128)S(1)}, u32[]{:S(2)}, u32[]{:S(2)}) collective-permute-start(f32[8,1024]{1,0:T(8,128)S(1)} %get-tuple-element.40), channel_id=1, source_target_pairs={{16,0},{17,1},{18,2},{19,3},{20,4},{21,5},{22,6},{23,7},{24,8},{25... | collective-permute-start | bytes 98312 | tf_op jit(solution)/shard_map/ppermute | solution.py:535
  84.1 1.7 %shard_map.99 = f32[16,136,128]{2,1,0:T(8,128)S(1)} custom-call(s32[2]{0:T(128)S(1)} %pad_add_fusion.place_ref, f32[16,1024]{1,0:T(8,128)S(1)} %shard_map.96.own_ref, f32[8,1024]{1,0:T(8,128)S(1)} %collective-permute-done.10.before_ref, f32[8,1024]{1,0:T(8,128)S(1)} %collective-permute-done.11.after_ref, f32[2,32,1024]{2,1,0:T(8,128)S(1)} %get-tuple-element.23.wind_ref, ...), custom_call_target="tpu_custom_call" | custom-call | tf_op jit(solution)/shard_map/pallas_call | solution.py:539
  86.8 4.6 %all-to-all-start.2 = ((f32[16,136,128]{2,1,0:T(8,128)}), f32[16,136,128]{2,1,0:T(8,128)S(1)}, u32[]{:S(2)}, u32[]{:S(2)}) async-start(f32[16,136,128]{2,1,0:T(8,128)} %copy-done.1), calls=%async_computation.2 | async-start | bytes 2228224 | tf_op jit(solution)/shard_map/all_to_all | solution.py:20
  91.4 2.0 %copy.35 = bf16[256,1024]{0,1:T(8,128)(2,1)} copy(bf16[256,1024]{1,0:T(8,128)(2,1)} %lon_ref.1) | data formatting | bytes 1048576 | tf_op args[3]
  93.5 14.0 %all-to-all-done.2.adjoint_ref = f32[16,136,128]{2,1,0:T(8,128)S(1)} async-done(((f32[16,136,128]{2,1,0:T(8,128)}), f32[16,136,128]{2,1,0:T(8,128)S(1)}, u32[]{:S(2)}, u32[]{:S(2)}) %all-to-all-start.2) | async-done | bytes 1114144 | tf_op jit(solution)/shard_map/all_to_all | solution.py:20
  109.8 1.7 %shard_map.100 = (s16[8,144,256]{2,1,0:T(8,128)(2,1)S(1)}, f32[2,4,32,64]{3,2,1,0:T(8,128)S(1)}) custom-call(s32[1]{0:T(128)} %bitcast.side_ref, f32[16,136,128]{2,1,0:T(8,128)S(1)} %all-to-all-done.2.adjoint_ref, bf16[1024,256]{1,0:T(8,128)(2,1)S(1)} %bitcast.40, bf16[4,8,32,1024]{3,2,1,0:T(8,128)(2,1)S(1)} %copy-done, bf16[4,4,32,1024]{3,2,1,0:T(8,128)(2,1)S(1)} %copy-done.3), custom_call_target="tpu_custom_call" | custom-call | tf_op jit(solution)/shard_map/pallas_call | solution.py:549
  112.3 7.4 %all-to-all-start.3 = ((s16[8,144,256]{2,1,0:T(8,128)(2,1)}), s16[8,144,256]{2,1,0:T(8,128)(2,1)S(1)}, u32[]{:S(2)}, u32[]{:S(2)}) async-start(s16[8,144,256]{2,1,0:T(8,128)(2,1)} %copy-done.9), calls=%async_computation.3 | async-start | bytes 1179648 | tf_op jit(solution)/shard_map/all_to_all | solution.py:20
  120.0 18.9 %all-to-all-done.3.message_ref = s16[8,144,256]{2,1,0:T(8,128)(2,1)S(1)} async-done(((s16[8,144,256]{2,1,0:T(8,128)(2,1)}), s16[8,144,256]{2,1,0:T(8,128)(2,1)S(1)}, u32[]{:S(2)}, u32[]{:S(2)}) %all-to-all-start.3) | async-done | bytes 589856 | tf_op jit(solution)/shard_map/all_to_all | solution.py:20
  138.9 1.4 shard_map.101
  140.3 3.5 %all-to-all-start.4 = ((f32[16,2,8,256]{3,2,1,0:T(8,128)}), f32[16,2,8,256]{3,2,1,0:T(8,128)S(1)}, u32[]{:S(2)}, u32[]{:S(2)}) async-start(f32[16,2,8,256]{3,2,1,0:T(8,128)} %shard_map.101), calls=%async_computation.4 | async-start | bytes 524288 | tf_op jit(solution)/shard_map/all_to_all | solution.py:20
  143.8 3.5 %collective-permute-start.14 = (f32[4,32,64]{2,1,0:T(8,128)S(1)}, f32[4,32,64]{2,1,0:T(8,128)S(1)}, u32[]{:S(2)}, u32[]{:S(2)}) collective-permute-start(f32[4,32,64]{2,1,0:T(8,128)S(1)} %get-tuple-element.35), channel_id=1, source_target_pairs={{0,1},{1,0},{2,3},{3,2},{4,5},{5,4},{6,7},{7,6},{8,9},{9,8},{10,11... | collective-permute-start | bytes 98312 | tf_op jit(solution)/shard_map/ppermute | solution.py:582
  147.3 2.5 %collective-permute-done.14 = f32[4,32,64]{2,1,0:T(8,128)S(1)} collective-permute-done((f32[4,32,64]{2,1,0:T(8,128)S(1)}, f32[4,32,64]{2,1,0:T(8,128)S(1)}, u32[]{:S(2)}, u32[]{:S(2)}) %collective-permute-start.14) | collective-permute-done | bytes 32800 | tf_op jit(solution)/shard_map/ppermute | solution.py:582
  150.5 7.7 %all-to-all-done.4 = f32[16,2,8,256]{3,2,1,0:T(8,128)S(1)} async-done(((f32[16,2,8,256]{3,2,1,0:T(8,128)}), f32[16,2,8,256]{3,2,1,0:T(8,128)S(1)}, u32[]{:S(2)}, u32[]{:S(2)}) %all-to-all-start.4) | async-done | bytes 262176 | tf_op jit(solution)/shard_map/all_to_all | solution.py:20
  (84 shorter events, 23.3 us)
Async XLA Ops:
  2.5 5.9 %collective-permute-start = (bf16[144,256]{1,0:T(8,128)(2,1)S(1)}, bf16[144,256]{1,0:T(8,128)(2,1)S(1)}, u32[]{:S(2)}, u32[]{:S(2)}) collective-permute-start(bf16[144,256]{1,0:T(8,128)(2,1)S(1)} %maximum_maximum_fusion), channel_id=1, source_target_pairs={{0,1},{1,0},{2,3},{3,2},{4,5},{5,4},{6,7},{7,6},{8,9},{9,8},{10,11... | collective-permute-start | bytes 221192 | tf_op jit(solution)/shard_map/ppermute | solution.py:420
  6.5 18.2 %copy-start = (bf16[4,8,32,1024]{3,2,1,0:T(8,128)(2,1)S(1)}, bf16[4,8,32,1024]{3,2,1,0:T(8,128)(2,1)}, u32[]{:S(2)}) copy-start(bf16[4,8,32,1024]{3,2,1,0:T(8,128)(2,1)} %own_ref.3) | copy-start | bytes 6291460
  8.5 16.2 %copy-start.6 = (bf16[288,256]{1,0:T(8,128)(2,1)}, bf16[288,256]{1,0:T(8,128)(2,1)S(1)}, u32[]{:S(2)}) copy-start(bf16[288,256]{1,0:T(8,128)(2,1)S(1)} %pad_maximum_fusion.refs_0_) | copy-start | bytes 442372
  8.5 12.8 %collective-permute-start.2 = (bf16[288,256]{1,0:T(8,128)(2,1)S(1)}, bf16[288,256]{1,0:T(8,128)(2,1)}, u32[]{:S(2)}, u32[]{:S(2)}) collective-permute-start(bf16[288,256]{1,0:T(8,128)(2,1)S(1)} %pad_maximum_fusion.refs_0_), channel_id=1, source_target_pairs={{2,0},{4,2},{6,4},{8,6},{10,8},{12,10},{14,12},{0,14},{3,1},{5,3},... | collective-permute-start | bytes 442376 | tf_op jit(solution)/shard_map/ppermute | solution.py:457
  14.4 6.8 %collective-permute-start.3 = (bf16[288,256]{1,0:T(8,128)(2,1)S(1)}, bf16[288,256]{1,0:T(8,128)(2,1)}, u32[]{:S(2)}, u32[]{:S(2)}) collective-permute-start(bf16[288,256]{1,0:T(8,128)(2,1)S(1)} %pad_maximum_fusion.refs_0_), channel_id=1, source_target_pairs={{0,2},{2,4},{4,6},{6,8},{8,10},{10,12},{12,14},{14,0},{1,3},{3,5},... | collective-permute-start | bytes 442376 | tf_op jit(solution)/shard_map/ppermute | solution.py:455
  15.3 14.3 %all-to-all-start = ((f32[16,3,16,128]{3,2,1,0:T(8,128)}), f32[16,3,16,128]{3,2,1,0:T(8,128)S(1)}, u32[]{:S(2)}, u32[]{:S(2)}) async-start(f32[16,3,16,128]{3,2,1,0:T(8,128)} %bitcast.18), calls=%async_computation | async-start | bytes 786432 | tf_op jit(solution)/shard_map/all_to_all | solution.py:20
  21.2 7.8 %collective-permute-start.4 = (bf16[288,256]{1,0:T(8,128)(2,1)}, bf16[288,256]{1,0:T(8,128)(2,1)}, u32[]{:S(2)}, u32[]{:S(2)}) collective-permute-start(bf16[288,256]{1,0:T(8,128)(2,1)} %collective-permute-done.3.refs_7_), channel_id=1, source_target_pairs={{0,2},{2,4},{4,6},{6,8},{8,10},{10,12},{12,14},{14,0},{1,3},{3,5},... | collective-permute-start | bytes 442376 | tf_op jit(solution)/shard_map/ppermute | solution.py:455
  21.3 7.7 %collective-permute-start.5 = (bf16[288,256]{1,0:T(8,128)(2,1)}, bf16[288,256]{1,0:T(8,128)(2,1)}, u32[]{:S(2)}, u32[]{:S(2)}) collective-permute-start(bf16[288,256]{1,0:T(8,128)(2,1)} %collective-permute-done.2.refs_1_), channel_id=1, source_target_pairs={{2,0},{4,2},{6,4},{8,6},{10,8},{12,10},{14,12},{0,14},{3,1},{5,3},... | collective-permute-start | bytes 442376 | tf_op jit(solution)/shard_map/ppermute | solution.py:457
  25.7 27.8 %collective-permute-start.1 = (bf16[4,4,32,1024]{3,2,1,0:T(8,128)(2,1)}, bf16[4,4,32,1024]{3,2,1,0:T(8,128)(2,1)S(1)}, u32[]{:S(2)}, u32[]{:S(2)}) collective-permute-start(bf16[4,4,32,1024]{3,2,1,0:T(8,128)(2,1)} %constant_dynamic-slice_fusion), channel_id=1, source_target_pairs={{0,1},{1,0},{2,3},{3,2},{4,5},{5,4},{6,7},{7,6},{8,9},{9,8},{10,11... | collective-permute-start | bytes 3145736 | tf_op jit(solution)/shard_map/ppermute | solution.py:449
  29.6 7.7 %collective-permute-start.7 = (bf16[288,256]{1,0:T(8,128)(2,1)}, bf16[288,256]{1,0:T(8,128)(2,1)}, u32[]{:S(2)}, u32[]{:S(2)}) collective-permute-start(bf16[288,256]{1,0:T(8,128)(2,1)} %collective-permute-done.4.refs_6_), channel_id=1, source_target_pairs={{0,2},{2,4},{4,6},{6,8},{8,10},{10,12},{12,14},{14,0},{1,3},{3,5},... | collective-permute-start | bytes 442376 | tf_op jit(solution)/shard_map/ppermute | solution.py:455
  30.3 30.3 %collective-permute-start.9 = (f32[16,2,16,128]{3,2,1,0:T(8,128)}, f32[16,2,16,128]{3,2,1,0:T(8,128)}, u32[]{:S(2)}, u32[]{:S(2)}) collective-permute-start(f32[16,2,16,128]{3,2,1,0:T(8,128)} %maximum_select_fusion), channel_id=1, source_target_pairs={{0,1},{1,0},{2,3},{3,2},{4,5},{5,4},{6,7},{7,6},{8,9},{9,8},{10,11... | collective-permute-start | bytes 786440 | tf_op jit(solution)/shard_map/ppermute | solution.py:461
  32.5 9.3 %collective-permute-start.6 = (bf16[288,256]{1,0:T(8,128)(2,1)}, bf16[288,256]{1,0:T(8,128)(2,1)}, u32[]{:S(2)}, u32[]{:S(2)}) collective-permute-start(bf16[288,256]{1,0:T(8,128)(2,1)} %collective-permute-done.5.refs_2_), channel_id=1, source_target_pairs={{2,0},{4,2},{6,4},{8,6},{10,8},{12,10},{14,12},{0,14},{3,1},{5,3},... | collective-permute-start | bytes 442376 | tf_op jit(solution)/shard_map/ppermute | solution.py:457
  37.2 6.9 %collective-permute-start.8 = (bf16[288,256]{1,0:T(8,128)(2,1)}, bf16[288,256]{1,0:T(8,128)(2,1)}, u32[]{:S(2)}, u32[]{:S(2)}) collective-permute-start(bf16[288,256]{1,0:T(8,128)(2,1)} %collective-permute-done.7.refs_5_), channel_id=1, source_target_pairs={{0,2},{2,4},{4,6},{6,8},{8,10},{10,12},{12,14},{14,0},{1,3},{3,5},... | collective-permute-start | bytes 442376 | tf_op jit(solution)/shard_map/ppermute | solution.py:455
  53.5 1.0 copy-start.4
  54.5 0.9 copy-start.7
  55.4 3.7 %copy-start.2 = (bf16[4,4,32,1024]{3,2,1,0:T(8,128)(2,1)}, bf16[4,4,32,1024]{3,2,1,0:T(8,128)(2,1)S(1)}, u32[]{:S(2)}) copy-start(bf16[4,4,32,1024]{3,2,1,0:T(8,128)(2,1)S(1)} %collective-permute-done.1.other_ref) | copy-start | bytes 3145732
  59.1 0.8 copy-start.8
  60.6 16.2 %all-to-all-start.1 = ((s16[16,144,128]{2,1,0:T(8,128)(2,1)}), s16[16,144,128]{2,1,0:T(8,128)(2,1)S(1)}, u32[]{:S(2)}, u32[]{:S(2)}) async-start(s16[16,144,128]{2,1,0:T(8,128)(2,1)} %copy-done.8), calls=%async_computation.1 | async-start | bytes 1179648 | tf_op jit(solution)/shard_map/all_to_all | solution.py:20
  68.4 14.4 %collective-permute-start.12 = (f32[8,3584]{1,0:T(8,128)S(1)}, f32[8,3584]{1,0:T(8,128)S(1)}, u32[]{:S(2)}, u32[]{:S(2)}) collective-permute-start(f32[8,3584]{1,0:T(8,128)S(1)} %get-tuple-element.33), channel_id=1, source_target_pairs={{0,16},{1,17},{2,18},{3,19},{4,20},{5,21},{6,22},{7,23},{8,24},{9,... | collective-permute-start | bytes 344072 | tf_op jit(solution)/shard_map/ppermute | solution.py:511
  70.5 12.3 %collective-permute-start.13 = (f32[8,3584]{1,0:T(8,128)S(1)}, f32[8,3584]{1,0:T(8,128)S(1)}, u32[]{:S(2)}, u32[]{:S(2)}) collective-permute-start(f32[8,3584]{1,0:T(8,128)S(1)} %get-tuple-element.32), channel_id=1, source_target_pairs={{16,0},{17,1},{18,2},{19,3},{20,4},{21,5},{22,6},{23,7},{24,8},{25... | collective-permute-start | bytes 344072 | tf_op jit(solution)/shard_map/ppermute | solution.py:512
  77.0 6.5 %collective-permute-start.10 = (f32[8,1024]{1,0:T(8,128)S(1)}, f32[8,1024]{1,0:T(8,128)S(1)}, u32[]{:S(2)}, u32[]{:S(2)}) collective-permute-start(f32[8,1024]{1,0:T(8,128)S(1)} %get-tuple-element.41), channel_id=1, source_target_pairs={{0,16},{1,17},{2,18},{3,19},{4,20},{5,21},{6,22},{7,23},{8,24},{9,... | collective-permute-start | bytes 98312 | tf_op jit(solution)/shard_map/ppermute | solution.py:534
  79.0 5.1 %collective-permute-start.11 = (f32[8,1024]{1,0:T(8,128)S(1)}, f32[8,1024]{1,0:T(8,128)S(1)}, u32[]{:S(2)}, u32[]{:S(2)}) collective-permute-start(f32[8,1024]{1,0:T(8,128)S(1)} %get-tuple-element.40), channel_id=1, source_target_pairs={{16,0},{17,1},{18,2},{19,3},{20,4},{21,5},{22,6},{23,7},{24,8},{25... | collective-permute-start | bytes 98312 | tf_op jit(solution)/shard_map/ppermute | solution.py:535
  85.9 1.0 copy-start.1
  86.8 20.7 %all-to-all-start.2 = ((f32[16,136,128]{2,1,0:T(8,128)}), f32[16,136,128]{2,1,0:T(8,128)S(1)}, u32[]{:S(2)}, u32[]{:S(2)}) async-start(f32[16,136,128]{2,1,0:T(8,128)} %copy-done.1), calls=%async_computation.2 | async-start | bytes 2228224 | tf_op jit(solution)/shard_map/all_to_all | solution.py:20
  107.5 1.2 copy-start.3
  108.7 1.0 copy-start.5
  109.8 9.9 %copy-start.11 = (bf16[8,64,128]{2,1,0:T(8,128)(2,1)S(1)}, bf16[8,64,128]{2,1,0:T(8,128)(2,1)}, u32[]{:S(2)}) copy-start(bf16[8,64,128]{2,1,0:T(8,128)(2,1)} %copy-done.10) | copy-start | bytes 393220
  111.5 0.8 copy-start.9
  112.3 26.6 %all-to-all-start.3 = ((s16[8,144,256]{2,1,0:T(8,128)(2,1)}), s16[8,144,256]{2,1,0:T(8,128)(2,1)S(1)}, u32[]{:S(2)}, u32[]{:S(2)}) async-start(s16[8,144,256]{2,1,0:T(8,128)(2,1)} %copy-done.9), calls=%async_computation.3 | async-start | bytes 1179648 | tf_op jit(solution)/shard_map/all_to_all | solution.py:20
  119.8 38.8 %copy-start.13 = (bf16[8,4,8,256]{3,2,1,0:T(8,128)(2,1)S(1)}, bf16[8,4,8,256]{3,2,1,0:T(8,128)(2,1)}, u32[]{:S(2)}) copy-start(bf16[8,4,8,256]{3,2,1,0:T(8,128)(2,1)} %param.8) | copy-start | bytes 393220
  140.3 17.9 %all-to-all-start.4 = ((f32[16,2,8,256]{3,2,1,0:T(8,128)}), f32[16,2,8,256]{3,2,1,0:T(8,128)S(1)}, u32[]{:S(2)}, u32[]{:S(2)}) async-start(f32[16,2,8,256]{3,2,1,0:T(8,128)} %shard_map.101), calls=%async_computation.4 | async-start | bytes 524288 | tf_op jit(solution)/shard_map/all_to_all | solution.py:20
  143.8 6.0 %collective-permute-start.14 = (f32[4,32,64]{2,1,0:T(8,128)S(1)}, f32[4,32,64]{2,1,0:T(8,128)S(1)}, u32[]{:S(2)}, u32[]{:S(2)}) collective-permute-start(f32[4,32,64]{2,1,0:T(8,128)S(1)} %get-tuple-element.35), channel_id=1, source_target_pairs={{0,1},{1,0},{2,3},{3,2},{4,5},{5,4},{6,7},{7,6},{8,9},{9,8},{10,11... | collective-permute-start | bytes 98312 | tf_op jit(solution)/shard_map/ppermute | solution.py:582
  (2 other events, 1.3 us)

commit v10 on v9

--- a/solution.py
+++ b/solution.py
@@ -144,35 +144,33 @@
     out_ref[...] = from_tiles(total, own_rows // 8) * scale
 
 
-def project_kernel(side_ref, adjoint_ref, lon_ref, own_ref, other_ref, out_ref, tile_ref):
+def project_kernel(side_ref, message_ref, lon_ref, own_ref, other_ref, out_ref, tile_ref):
     members, levels_here, row_count, lon_total = other_ref.shape
     rings, _, coarse_lons = out_ref.shape
     tall = 2 * row_count
     side = side_ref[0]
     lon = lon_ref[...]
-    quarters = adjoint_ref.shape[0] // levels_here
-    row_tiles = tall // quarters // 8
+    quarters = message_ref.shape[0] // levels_here
+    own_rows = tall // quarters
     lane_tiles = lon_total // 128
+    data = own_rows * lane_tiles
+    width = tile_ref.shape[3]
     per_message = members * levels_here // rings
     row = lax.broadcasted_iota(jnp.int32, (tall, 128), 0)
     lane = lax.broadcasted_iota(jnp.int32, (tall, 128), 1)
     tails = [jnp.zeros((1, 128), jnp.float32) for _ in range(rings)]
     for level in range(levels_here):
-        strips = []
-        for at in range(lane_tiles):
-            strips.append(
-                jnp.concatenate(
-                    [
-                        adjoint_ref[
-                            level * quarters + q, (t * lane_tiles + at) * 8 : (t * lane_tiles + at + 1) * 8
-                        ]
-                        for q in range(quarters)
-                        for t in range(row_tiles)
-                    ],
-                    axis=0,
-                )
-            )
-        adjoint = jnp.concatenate(strips, axis=1)
+        pieces = []
+        for q in range(quarters):
+            value = from_16(message_ref[level * quarters + q, :data])
+            codes = from_16(message_ref[level * quarters + q, data : data + own_rows])
+            pieces.append(from_tiles(value * tile_scales(codes, lane_tiles), own_rows // 8))
+            tail = from_16(message_ref[level * quarters + q, data + own_rows :])
+            tile = tail[:8] * (code_scale(tail[8:]) * (1.0 / STEPS_16))
+            band, start = q * own_rows // row_count, q * own_rows % row_count
+            tile_ref[band, level, start : start + 8] = tile[:, :width]
+            tile_ref[band, level, start + 8 : start + 16] = tile[:, width:]
+        adjoint = jnp.concatenate(pieces, axis=0)
         product = [
             member_rows(side, own_ref, other_ref, member, level) * adjoint for member in range(members)
         ]
@@ -187,16 +185,10 @@
             out_ref[ring, place * tall : (place + 1) * tall] = whole.astype(jnp.int16)
             mark = jnp.where(lane == row + place * tall, codes, 0.0)
             tails[ring] = tails[ring] + jnp.sum(mark, axis=0, keepdims=True)
-        for q in range(quarters):
-            piece = adjoint_ref[level * quarters + q, row_tiles * lane_tiles * 8 :]
-            band, start = q * row_tiles * 8 // row_count, q * row_tiles * 8 % row_count
-            width = tile_ref.shape[3]
-            tile_ref[band, level, start : start + 8] = piece[:, :width]
-            tile_ref[band, level, start + 8 : start + 16] = piece[:, width:]
-    data = per_message * tall
+    end = per_message * tall
     for ring in range(rings):
         tail = jnp.broadcast_to(tails[ring], (16, 128)).astype(jnp.int32).astype(jnp.int16)
-        out_ref[ring, data : data + 16] = jnp.concatenate([tail] * (coarse_lons // 128), axis=1)
+        out_ref[ring, end : end + 16] = jnp.concatenate([tail] * (coarse_lons // 128), axis=1)
 
 
 def gather_kernel(scale, message_ref, lat_ref, out_ref):
@@ -281,7 +273,7 @@
         gain_ref[step] = jnp.where(hit, weight, 0.0)
 
 
-def stencil_kernel(place_ref, own_ref, before_ref, after_ref, wind_ref, gain_ref, value_ref, adjoint_ref):
+def stencil_kernel(place_ref, own_ref, before_ref, after_ref, wind_ref, gain_ref, value_ref, out_hbm, adjoint_ref, piece_ref, sems):
     rows, cols = wind_ref.shape[1:]
     first_row = place_ref[0]
     last_row = place_ref[1]
@@ -336,27 +328,41 @@
             + west(to_east * pushed)
         )
     adjoint = adjoint[HALO : rows - HALO]
-    row_tiles, lane_tiles = (rows - 2 * HALO) // 8, cols // 128
-    packed = jnp.concatenate(
-        [
-            adjoint[t * 8 : (t + 1) * 8, at * 128 : (at + 1) * 128]
-            for t in range(row_tiles)
-            for at in range(lane_tiles)
-        ],
-        axis=0,
-    )
-    count = adjoint_ref.shape[0]
+    own_rows = rows - 2 * HALO
+    data = own_rows * cols // 128
+    codes = row_codes(adjoint)
+    adjoint_ref[:data] = to_16(as_tiles(rounded(adjoint, codes)))
+    adjoint_ref[data:] = to_16(jnp.broadcast_to(codes, (own_rows, 128)))
+    count = out_hbm.shape[0]
+    copies = [
+        pltpu.make_async_copy(
+            adjoint_ref, out_hbm.at[copy, pl.ds(0, data + own_rows)], sems.at[copy]
+        )
+        for copy in range(count)
+    ]
+    for copy in copies:
+        copy.start()
     width = cols // count
     lane = lax.broadcasted_iota(jnp.int32, (8, 128), 1)
+    own = own_ref[...]
+    codes = row_codes(own)
+    own = rounded(own, codes)
+    codes = jnp.where(lane < width, codes[:8], codes[8:])
     for copy in range(count):
-        adjoint_ref[copy, : row_tiles * lane_tiles * 8] = packed
         strip = slice(copy * width // 128 * 128, copy * width // 128 * 128 + 128)
-        top, bottom = own_ref[0:8, strip], own_ref[8:16, strip]
+        top, bottom = own[0:8, strip], own[8:16, strip]
         if copy % 2 == 0:
             piece = jnp.where(lane < width, top, pltpu.roll(bottom, width, 1))
         else:
             piece = jnp.where(lane < width, pltpu.roll(top, width, 1), bottom)
-        adjoint_ref[copy, row_tiles * lane_tiles * 8 :] = piece
+        piece_ref[copy] = to_16(jnp.concatenate([piece, codes], axis=0))
+    last = pltpu.make_async_copy(
+        piece_ref, out_hbm.at[:, pl.ds(data + own_rows, 16)], sems.at[count]
+    )
+    last.start()
+    for copy in copies:
+        copy.wait()
+    last.wait()
 
 
 def body(
@@ -477,6 +483,7 @@
     whole = pl.BlockSpec(memory_space=pltpu.VMEM)
     roomy = pltpu.CompilerParams(vmem_limit_bytes=48 * 1024 * 1024)
     where_side = jnp.reshape(side, (1,)).astype(jnp.int32)
+    anywhere = pl.BlockSpec(memory_space=pl.ANY)
     piece_rows = own_rows * lon_total // 128 + own_rows
     partial_sum, lat_ring = pl.pallas_call(
         localize_kernel,
@@ -538,9 +545,14 @@
     ).astype(jnp.int32)
     copies = pl.pallas_call(
         stencil_kernel,
-        out_shape=jax.ShapeDtypeStruct((peers, own_rows * lon_total // 128 + 8, 128), jnp.float32),
+        out_shape=jax.ShapeDtypeStruct((peers, piece_rows + 16, 128), jnp.int16),
         in_specs=[scalars] + [whole] * 6,
-        out_specs=whole,
+        out_specs=anywhere,
+        scratch_shapes=[
+            pltpu.VMEM((piece_rows, 128), jnp.int16),
+            pltpu.VMEM((peers, 16, 128), jnp.int16),
+            pltpu.SemaphoreType.DMA((peers + 1,)),
+        ],
         compiler_params=roomy,
     )(place, own, before, after, wide_wind, gains, values)
 

time: 161 us -> 159 us (0.988)
  waiting for transfers between devices: 61.5 us -> 54.8 us
  Pallas kernels: 10.7 us -> 13.8 us
    all_to_all x5, waiting for transfers between devices: 43.9 us -> 37.9 us  [swapped(): lax.all_to_all(value, axis, split_axis=dim, concat_axis=dim, tiled=True)]
  transfers between devices with their start and end apart: 20 -> 20, of which waited for: 12 -> 11; matrix products, arithmetic and copies ran while one was open for 9% -> 9% of each run, Pallas kernels for 4% -> 4%
where the time goes in v10:
time: 159 us; the launch traced here: 157 us
  starting transfers between devices  61.9 us (39%)
  waiting for transfers between devices  54.8 us (34%)
  local copies, waits for them, and re-layouts  19.4 us (12%)
  Pallas kernels  13.8 us (9%)
  other arithmetic  6.5 us (4%)
    all_to_all x5, waiting for transfers between devices, swapped(): lax.all_to_all(value, axis, split_axis=dim, concat_axis=dim, tiled=True)  37.9 us
    all_to_all x5, starting transfers between devices, swapped(): lax.all_to_all(value, axis, split_axis=dim, concat_axis=dim, tiled=True)  28.1 us
    ppermute x3, starting transfers between devices, body(): falling = lax.ppermute(falling, 'lat_0', down)  12.5 us
    unnamed x30, local copies, waits for them, and re-layouts  10.6 us
    ppermute x1, waiting for transfers between devices, body(): other_members = lax.ppermute(other_members, 'lat_1', across)  9.37 us
    ppermute x4, waiting for transfers between devices, body(): rising = lax.ppermute(rising, 'lat_0', up)  4.4 us
    ppermute x1, starting transfers between devices, body(): after = lax.ppermute(own[:HALO], ALL, backward)  3.72 us
    ppermute x1, starting transfers between devices, body(): after = lax.ppermute(local[:HALO], ALL, backward)  3.51 us
  transfers between devices with their start and end apart: 20, of which 11 were waited for; matrix products, arithmetic and copies ran while one was open for 9% of the time, Pallas kernels for 4%

profile of v10, /device:TPU:2, one launch (start us, length us, event | category | flops | bytes accessed | tf_op | source)
XLA Modules:
  0.0 157.4 jit_solution(17166872119834045054)
XLA Ops:
  2.5 2.2 %collective-permute-start = (bf16[144,256]{1,0:T(8,128)(2,1)S(1)}, bf16[144,256]{1,0:T(8,128)(2,1)S(1)}, u32[]{:S(2)}, u32[]{:S(2)}) collective-permute-start(bf16[144,256]{1,0:T(8,128)(2,1)S(1)} %maximum_maximum_fusion), channel_id=1, source_target_pairs={{0,1},{1,0},{2,3},{3,2},{4,5},{5,4},{6,7},{7,6},{8,9},{9,8},{10,11... | collective-permute-start | bytes 221192 | tf_op jit(solution)/shard_map/ppermute | solution.py:426
  8.5 5.9 %collective-permute-start.2 = (bf16[288,256]{1,0:T(8,128)(2,1)S(1)}, bf16[288,256]{1,0:T(8,128)(2,1)}, u32[]{:S(2)}, u32[]{:S(2)}) collective-permute-start(bf16[288,256]{1,0:T(8,128)(2,1)S(1)} %pad_maximum_fusion.refs_0_), channel_id=1, source_target_pairs={{2,0},{4,2},{6,4},{8,6},{10,8},{12,10},{14,12},{0,14},{3,1},{5,3},... | collective-permute-start | bytes 442376 | tf_op jit(solution)/shard_map/ppermute | solution.py:463
  15.3 5.9 %all-to-all-start = ((f32[16,3,16,128]{3,2,1,0:T(8,128)}), f32[16,3,16,128]{3,2,1,0:T(8,128)S(1)}, u32[]{:S(2)}, u32[]{:S(2)}) async-start(f32[16,3,16,128]{3,2,1,0:T(8,128)} %bitcast.18), calls=%async_computation | async-start | bytes 786432 | tf_op jit(solution)/shard_map/all_to_all | solution.py:20
  21.3 3.3 %collective-permute-start.5 = (bf16[288,256]{1,0:T(8,128)(2,1)}, bf16[288,256]{1,0:T(8,128)(2,1)}, u32[]{:S(2)}, u32[]{:S(2)}) collective-permute-start(bf16[288,256]{1,0:T(8,128)(2,1)} %collective-permute-done.2.refs_1_), channel_id=1, source_target_pairs={{2,0},{4,2},{6,4},{8,6},{10,8},{12,10},{14,12},{0,14},{3,1},{5,3},... | collective-permute-start | bytes 442376 | tf_op jit(solution)/shard_map/ppermute | solution.py:463
  25.7 2.1 %collective-permute-start.1 = (bf16[4,4,32,1024]{3,2,1,0:T(8,128)(2,1)}, bf16[4,4,32,1024]{3,2,1,0:T(8,128)(2,1)S(1)}, u32[]{:S(2)}, u32[]{:S(2)}) collective-permute-start(bf16[4,4,32,1024]{3,2,1,0:T(8,128)(2,1)} %constant_dynamic-slice_fusion), channel_id=1, source_target_pairs={{0,1},{1,0},{2,3},{3,2},{4,5},{5,4},{6,7},{7,6},{8,9},{9,8},{10,11... | collective-permute-start | bytes 3145736 | tf_op jit(solution)/shard_map/ppermute | solution.py:455
  30.3 2.1 %collective-permute-start.9 = (f32[16,2,16,128]{3,2,1,0:T(8,128)}, f32[16,2,16,128]{3,2,1,0:T(8,128)}, u32[]{:S(2)}, u32[]{:S(2)}) collective-permute-start(f32[16,2,16,128]{3,2,1,0:T(8,128)} %maximum_select_fusion), channel_id=1, source_target_pairs={{0,1},{1,0},{2,3},{3,2},{4,5},{5,4},{6,7},{7,6},{8,9},{9,8},{10,11... | collective-permute-start | bytes 786440 | tf_op jit(solution)/shard_map/ppermute | solution.py:467
  32.4 3.2 %collective-permute-start.6 = (bf16[288,256]{1,0:T(8,128)(2,1)}, bf16[288,256]{1,0:T(8,128)(2,1)}, u32[]{:S(2)}, u32[]{:S(2)}) collective-permute-start(bf16[288,256]{1,0:T(8,128)(2,1)} %collective-permute-done.5.refs_2_), channel_id=1, source_target_pairs={{2,0},{4,2},{6,4},{8,6},{10,8},{12,10},{14,12},{0,14},{3,1},{5,3},... | collective-permute-start | bytes 442376 | tf_op jit(solution)/shard_map/ppermute | solution.py:463
  35.7 1.5 collective-permute-done.7.refs_5_
  38.0 1.6 reshape_squeeze_reshape.3
  39.5 1.4 fusion.1
  41.8 2.3 %collective-permute-done.8.refs_4_ = bf16[288,256]{1,0:T(8,128)(2,1)} collective-permute-done((bf16[288,256]{1,0:T(8,128)(2,1)}, bf16[288,256]{1,0:T(8,128)(2,1)}, u32[]{:S(2)}, u32[]{:S(2)}) %collective-permute-start.8) | collective-permute-done | bytes 147488 | tf_op jit(solution)/shard_map/ppermute | solution.py:461
  44.1 9.4 %collective-permute-done.1.other_ref = bf16[4,4,32,1024]{3,2,1,0:T(8,128)(2,1)S(1)} collective-permute-done((bf16[4,4,32,1024]{3,2,1,0:T(8,128)(2,1)}, bf16[4,4,32,1024]{3,2,1,0:T(8,128)(2,1)S(1)}, u32[]{:S(2)}, u32[]{:S(2)}) %collective-permute-start.1) | collective-permute-done | bytes 1048608 | tf_op jit(solution)/shard_map/ppermute | solution.py:455
  55.4 3.3 %shard_map.95 = (s16[16,144,128]{2,1,0:T(8,128)(2,1)S(1)}, bf16[8,64,128]{2,1,0:T(8,128)(2,1)S(1)}) custom-call(s32[1]{0:T(128)} %bitcast.side_ref, bf16[64,128]{1,0:T(8,128)(2,1)S(1)} %copy.34.columns_ref, bf16[256,1024]{1,0:T(8,128)(2,1)S(1)} %copy-done.2, bf16[4,8,32,1024]{3,2,1,0:T(8,128)(2,1)S(1)} %copy-done, ...), custom_call_target="tpu_custom_call" | custom-call | tf_op jit(solution)/shard_map/pallas_call | solution.py:488
  60.2 5.7 %all-to-all-start.1 = ((s16[16,144,128]{2,1,0:T(8,128)(2,1)}), s16[16,144,128]{2,1,0:T(8,128)(2,1)}, u32[]{:S(2)}, u32[]{:S(2)}) async-start(s16[16,144,128]{2,1,0:T(8,128)(2,1)} %copy-done.8), calls=%async_computation.1 | async-start | bytes 1179648 | tf_op jit(solution)/shard_map/all_to_all | solution.py:20
  66.6 1.4 shard_map.97.local_ref
  69.3 2.0 %collective-permute-start.12 = (f32[8,3584]{1,0:T(8,128)}, f32[8,3584]{1,0:T(8,128)S(1)}, u32[]{:S(2)}, u32[]{:S(2)}) collective-permute-start(f32[8,3584]{1,0:T(8,128)} %get-tuple-element.33), channel_id=1, source_target_pairs={{0,16},{1,17},{2,18},{3,19},{4,20},{5,21},{6,22},{7,23},{8,24},{9,... | collective-permute-start | bytes 344072 | tf_op jit(solution)/shard_map/ppermute | solution.py:518
  71.4 3.5 %collective-permute-start.13 = (f32[8,3584]{1,0:T(8,128)S(1)}, f32[8,3584]{1,0:T(8,128)S(1)}, u32[]{:S(2)}, u32[]{:S(2)}) collective-permute-start(f32[8,3584]{1,0:T(8,128)S(1)} %get-tuple-element.32), channel_id=1, source_target_pairs={{16,0},{17,1},{18,2},{19,3},{20,4},{21,5},{22,6},{23,7},{24,8},{25... | collective-permute-start | bytes 344072 | tf_op jit(solution)/shard_map/ppermute | solution.py:519
  74.9 1.6 %all-to-all-done.1.message_ref = s16[16,144,128]{2,1,0:T(8,128)(2,1)} async-done(((s16[16,144,128]{2,1,0:T(8,128)(2,1)}), s16[16,144,128]{2,1,0:T(8,128)(2,1)}, u32[]{:S(2)}, u32[]{:S(2)}) %all-to-all-start.1) | async-done | bytes 589856 | tf_op jit(solution)/shard_map/all_to_all | solution.py:20
  77.8 2.0 %collective-permute-start.10 = (f32[8,1024]{1,0:T(8,128)S(1)}, f32[8,1024]{1,0:T(8,128)S(1)}, u32[]{:S(2)}, u32[]{:S(2)}) collective-permute-start(f32[8,1024]{1,0:T(8,128)S(1)} %get-tuple-element.41), channel_id=1, source_target_pairs={{0,16},{1,17},{2,18},{3,19},{4,20},{5,21},{6,22},{7,23},{8,24},{9,... | collective-permute-start | bytes 98312 | tf_op jit(solution)/shard_map/ppermute | solution.py:541
  79.8 3.7 %collective-permute-start.11 = (f32[8,1024]{1,0:T(8,128)S(1)}, f32[8,1024]{1,0:T(8,128)S(1)}, u32[]{:S(2)}, u32[]{:S(2)}) collective-permute-start(f32[8,1024]{1,0:T(8,128)S(1)} %get-tuple-element.40), channel_id=1, source_target_pairs={{16,0},{17,1},{18,2},{19,3},{20,4},{21,5},{22,6},{23,7},{24,8},{25... | collective-permute-start | bytes 98312 | tf_op jit(solution)/shard_map/ppermute | solution.py:542
  85.2 2.8 %shard_map.99 = s16[16,160,128]{2,1,0:T(8,128)(2,1)S(1)} custom-call(s32[2]{0:T(128)S(1)} %pad_add_fusion.place_ref, f32[16,1024]{1,0:T(8,128)S(1)} %shard_map.96.own_ref, f32[8,1024]{1,0:T(8,128)S(1)} %collective-permute-done.10.before_ref, f32[8,1024]{1,0:T(8,128)S(1)} %collective-permute-done.11.after_ref, f32[2,32,1024]{2,1,0:T(8,128)S(1)} %get-tuple-element.23.wind_ref, ...), custom_call_target="tpu_custom_call" | custom-call | tf_op jit(solution)/shard_map/pallas_call | solution.py:546
  88.9 5.4 %all-to-all-start.2 = ((s16[16,160,128]{2,1,0:T(8,128)(2,1)}), s16[16,160,128]{2,1,0:T(8,128)(2,1)}, u32[]{:S(2)}, u32[]{:S(2)}) async-start(s16[16,160,128]{2,1,0:T(8,128)(2,1)} %copy-done.1), calls=%async_computation.2 | async-start | bytes 1310720 | tf_op jit(solution)/shard_map/all_to_all | solution.py:20
  94.3 2.0 %copy.35 = bf16[256,1024]{0,1:T(8,128)(2,1)} copy(bf16[256,1024]{1,0:T(8,128)(2,1)} %lon_ref.1) | data formatting | bytes 1048576 | tf_op args[3]
  96.4 9.2 %all-to-all-done.2.message_ref = s16[16,160,128]{2,1,0:T(8,128)(2,1)} async-done(((s16[16,160,128]{2,1,0:T(8,128)(2,1)}), s16[16,160,128]{2,1,0:T(8,128)(2,1)}, u32[]{:S(2)}, u32[]{:S(2)}) %all-to-all-start.2) | async-done | bytes 655392 | tf_op jit(solution)/shard_map/all_to_all | solution.py:20
  106.6 2.9 %shard_map.100 = (s16[8,144,256]{2,1,0:T(8,128)(2,1)S(1)}, f32[2,4,32,64]{3,2,1,0:T(8,128)S(1)}) custom-call(s32[1]{0:T(128)} %bitcast.side_ref, s16[16,160,128]{2,1,0:T(8,128)(2,1)} %all-to-all-done.2.message_ref, bf16[1024,256]{1,0:T(8,128)(2,1)S(1)} %bitcast.40, bf16[4,8,32,1024]{3,2,1,0:T(8,128)(2,1)S(1)} %copy-done, ...), custom_call_target="tpu_custom_call" | custom-call | tf_op jit(solution)/shard_map/pallas_call | solution.py:561
  110.4 7.5 %all-to-all-start.3 = ((s16[8,144,256]{2,1,0:T(8,128)(2,1)}), s16[8,144,256]{2,1,0:T(8,128)(2,1)S(1)}, u32[]{:S(2)}, u32[]{:S(2)}) async-start(s16[8,144,256]{2,1,0:T(8,128)(2,1)} %copy-done.9), calls=%async_computation.3 | async-start | bytes 1179648 | tf_op jit(solution)/shard_map/all_to_all | solution.py:20
  118.2 18.9 %all-to-all-done.3.message_ref = s16[8,144,256]{2,1,0:T(8,128)(2,1)S(1)} async-done(((s16[8,144,256]{2,1,0:T(8,128)(2,1)}), s16[8,144,256]{2,1,0:T(8,128)(2,1)S(1)}, u32[]{:S(2)}, u32[]{:S(2)}) %all-to-all-start.3) | async-done | bytes 589856 | tf_op jit(solution)/shard_map/all_to_all | solution.py:20
  137.0 1.4 shard_map.101
  138.4 3.5 %all-to-all-start.4 = ((f32[16,2,8,256]{3,2,1,0:T(8,128)}), f32[16,2,8,256]{3,2,1,0:T(8,128)S(1)}, u32[]{:S(2)}, u32[]{:S(2)}) async-start(f32[16,2,8,256]{3,2,1,0:T(8,128)} %shard_map.101), calls=%async_computation.4 | async-start | bytes 524288 | tf_op jit(solution)/shard_map/all_to_all | solution.py:20
  142.0 3.5 %collective-permute-start.14 = (f32[4,32,64]{2,1,0:T(8,128)S(1)}, f32[4,32,64]{2,1,0:T(8,128)S(1)}, u32[]{:S(2)}, u32[]{:S(2)}) collective-permute-start(f32[4,32,64]{2,1,0:T(8,128)S(1)} %get-tuple-element.35), channel_id=1, source_target_pairs={{0,1},{1,0},{2,3},{3,2},{4,5},{5,4},{6,7},{7,6},{8,9},{9,8},{10,11... | collective-permute-start | bytes 98312 | tf_op jit(solution)/shard_map/ppermute | solution.py:594
  145.5 2.5 %collective-permute-done.14 = f32[4,32,64]{2,1,0:T(8,128)S(1)} collective-permute-done((f32[4,32,64]{2,1,0:T(8,128)S(1)}, f32[4,32,64]{2,1,0:T(8,128)S(1)}, u32[]{:S(2)}, u32[]{:S(2)}) %collective-permute-start.14) | collective-permute-done | bytes 32800 | tf_op jit(solution)/shard_map/ppermute | solution.py:594
  148.7 7.7 %all-to-all-done.4 = f32[16,2,8,256]{3,2,1,0:T(8,128)S(1)} async-done(((f32[16,2,8,256]{3,2,1,0:T(8,128)}), f32[16,2,8,256]{3,2,1,0:T(8,128)S(1)}, u32[]{:S(2)}, u32[]{:S(2)}) %all-to-all-start.4) | async-done | bytes 262176 | tf_op jit(solution)/shard_map/all_to_all | solution.py:20
  (84 shorter events, 24.6 us)
Async XLA Ops:
  2.5 5.9 %collective-permute-start = (bf16[144,256]{1,0:T(8,128)(2,1)S(1)}, bf16[144,256]{1,0:T(8,128)(2,1)S(1)}, u32[]{:S(2)}, u32[]{:S(2)}) collective-permute-start(bf16[144,256]{1,0:T(8,128)(2,1)S(1)} %maximum_maximum_fusion), channel_id=1, source_target_pairs={{0,1},{1,0},{2,3},{3,2},{4,5},{5,4},{6,7},{7,6},{8,9},{9,8},{10,11... | collective-permute-start | bytes 221192 | tf_op jit(solution)/shard_map/ppermute | solution.py:426
  6.5 18.2 %copy-start = (bf16[4,8,32,1024]{3,2,1,0:T(8,128)(2,1)S(1)}, bf16[4,8,32,1024]{3,2,1,0:T(8,128)(2,1)}, u32[]{:S(2)}) copy-start(bf16[4,8,32,1024]{3,2,1,0:T(8,128)(2,1)} %own_ref.3) | copy-start | bytes 6291460
  8.5 16.1 %copy-start.6 = (bf16[288,256]{1,0:T(8,128)(2,1)}, bf16[288,256]{1,0:T(8,128)(2,1)S(1)}, u32[]{:S(2)}) copy-start(bf16[288,256]{1,0:T(8,128)(2,1)S(1)} %pad_maximum_fusion.refs_0_) | copy-start | bytes 442372
  8.5 12.8 %collective-permute-start.2 = (bf16[288,256]{1,0:T(8,128)(2,1)S(1)}, bf16[288,256]{1,0:T(8,128)(2,1)}, u32[]{:S(2)}, u32[]{:S(2)}) collective-permute-start(bf16[288,256]{1,0:T(8,128)(2,1)S(1)} %pad_maximum_fusion.refs_0_), channel_id=1, source_target_pairs={{2,0},{4,2},{6,4},{8,6},{10,8},{12,10},{14,12},{0,14},{3,1},{5,3},... | collective-permute-start | bytes 442376 | tf_op jit(solution)/shard_map/ppermute | solution.py:463
  14.4 6.8 %collective-permute-start.3 = (bf16[288,256]{1,0:T(8,128)(2,1)S(1)}, bf16[288,256]{1,0:T(8,128)(2,1)}, u32[]{:S(2)}, u32[]{:S(2)}) collective-permute-start(bf16[288,256]{1,0:T(8,128)(2,1)S(1)} %pad_maximum_fusion.refs_0_), channel_id=1, source_target_pairs={{0,2},{2,4},{4,6},{6,8},{8,10},{10,12},{12,14},{14,0},{1,3},{3,5},... | collective-permute-start | bytes 442376 | tf_op jit(solution)/shard_map/ppermute | solution.py:461
  15.3 14.3 %all-to-all-start = ((f32[16,3,16,128]{3,2,1,0:T(8,128)}), f32[16,3,16,128]{3,2,1,0:T(8,128)S(1)}, u32[]{:S(2)}, u32[]{:S(2)}) async-start(f32[16,3,16,128]{3,2,1,0:T(8,128)} %bitcast.18), calls=%async_computation | async-start | bytes 786432 | tf_op jit(solution)/shard_map/all_to_all | solution.py:20
  21.2 7.8 %collective-permute-start.4 = (bf16[288,256]{1,0:T(8,128)(2,1)}, bf16[288,256]{1,0:T(8,128)(2,1)}, u32[]{:S(2)}, u32[]{:S(2)}) collective-permute-start(bf16[288,256]{1,0:T(8,128)(2,1)} %collective-permute-done.3.refs_7_), channel_id=1, source_target_pairs={{0,2},{2,4},{4,6},{6,8},{8,10},{10,12},{12,14},{14,0},{1,3},{3,5},... | collective-permute-start | bytes 442376 | tf_op jit(solution)/shard_map/ppermute | solution.py:461
  21.3 7.7 %collective-permute-start.5 = (bf16[288,256]{1,0:T(8,128)(2,1)}, bf16[288,256]{1,0:T(8,128)(2,1)}, u32[]{:S(2)}, u32[]{:S(2)}) collective-permute-start(bf16[288,256]{1,0:T(8,128)(2,1)} %collective-permute-done.2.refs_1_), channel_id=1, source_target_pairs={{2,0},{4,2},{6,4},{8,6},{10,8},{12,10},{14,12},{0,14},{3,1},{5,3},... | collective-permute-start | bytes 442376 | tf_op jit(solution)/shard_map/ppermute | solution.py:463
  25.7 27.8 %collective-permute-start.1 = (bf16[4,4,32,1024]{3,2,1,0:T(8,128)(2,1)}, bf16[4,4,32,1024]{3,2,1,0:T(8,128)(2,1)S(1)}, u32[]{:S(2)}, u32[]{:S(2)}) collective-permute-start(bf16[4,4,32,1024]{3,2,1,0:T(8,128)(2,1)} %constant_dynamic-slice_fusion), channel_id=1, source_target_pairs={{0,1},{1,0},{2,3},{3,2},{4,5},{5,4},{6,7},{7,6},{8,9},{9,8},{10,11... | collective-permute-start | bytes 3145736 | tf_op jit(solution)/shard_map/ppermute | solution.py:455
  29.5 7.7 %collective-permute-start.7 = (bf16[288,256]{1,0:T(8,128)(2,1)}, bf16[288,256]{1,0:T(8,128)(2,1)}, u32[]{:S(2)}, u32[]{:S(2)}) collective-permute-start(bf16[288,256]{1,0:T(8,128)(2,1)} %collective-permute-done.4.refs_6_), channel_id=1, source_target_pairs={{0,2},{2,4},{4,6},{6,8},{8,10},{10,12},{12,14},{14,0},{1,3},{3,5},... | collective-permute-start | bytes 442376 | tf_op jit(solution)/shard_map/ppermute | solution.py:461
  30.3 29.9 %collective-permute-start.9 = (f32[16,2,16,128]{3,2,1,0:T(8,128)}, f32[16,2,16,128]{3,2,1,0:T(8,128)}, u32[]{:S(2)}, u32[]{:S(2)}) collective-permute-start(f32[16,2,16,128]{3,2,1,0:T(8,128)} %maximum_select_fusion), channel_id=1, source_target_pairs={{0,1},{1,0},{2,3},{3,2},{4,5},{5,4},{6,7},{7,6},{8,9},{9,8},{10,11... | collective-permute-start | bytes 786440 | tf_op jit(solution)/shard_map/ppermute | solution.py:467
  32.4 9.3 %collective-permute-start.6 = (bf16[288,256]{1,0:T(8,128)(2,1)}, bf16[288,256]{1,0:T(8,128)(2,1)}, u32[]{:S(2)}, u32[]{:S(2)}) collective-permute-start(bf16[288,256]{1,0:T(8,128)(2,1)} %collective-permute-done.5.refs_2_), channel_id=1, source_target_pairs={{2,0},{4,2},{6,4},{8,6},{10,8},{12,10},{14,12},{0,14},{3,1},{5,3},... | collective-permute-start | bytes 442376 | tf_op jit(solution)/shard_map/ppermute | solution.py:463
  37.2 6.9 %collective-permute-start.8 = (bf16[288,256]{1,0:T(8,128)(2,1)}, bf16[288,256]{1,0:T(8,128)(2,1)}, u32[]{:S(2)}, u32[]{:S(2)}) collective-permute-start(bf16[288,256]{1,0:T(8,128)(2,1)} %collective-permute-done.7.refs_5_), channel_id=1, source_target_pairs={{0,2},{2,4},{4,6},{6,8},{8,10},{10,12},{12,14},{14,0},{1,3},{3,5},... | collective-permute-start | bytes 442376 | tf_op jit(solution)/shard_map/ppermute | solution.py:461
  53.4 1.0 copy-start.2
  54.5 0.9 copy-start.7
  58.7 0.8 copy-start.8
  60.2 16.3 %all-to-all-start.1 = ((s16[16,144,128]{2,1,0:T(8,128)(2,1)}), s16[16,144,128]{2,1,0:T(8,128)(2,1)}, u32[]{:S(2)}, u32[]{:S(2)}) async-start(s16[16,144,128]{2,1,0:T(8,128)(2,1)} %copy-done.8), calls=%async_computation.1 | async-start | bytes 1179648 | tf_op jit(solution)/shard_map/all_to_all | solution.py:20
  68.7 0.7 copy-start.4
  69.3 14.2 %collective-permute-start.12 = (f32[8,3584]{1,0:T(8,128)}, f32[8,3584]{1,0:T(8,128)S(1)}, u32[]{:S(2)}, u32[]{:S(2)}) collective-permute-start(f32[8,3584]{1,0:T(8,128)} %get-tuple-element.33), channel_id=1, source_target_pairs={{0,16},{1,17},{2,18},{3,19},{4,20},{5,21},{6,22},{7,23},{8,24},{9,... | collective-permute-start | bytes 344072 | tf_op jit(solution)/shard_map/ppermute | solution.py:518
  71.4 12.2 %collective-permute-start.13 = (f32[8,3584]{1,0:T(8,128)S(1)}, f32[8,3584]{1,0:T(8,128)S(1)}, u32[]{:S(2)}, u32[]{:S(2)}) collective-permute-start(f32[8,3584]{1,0:T(8,128)S(1)} %get-tuple-element.32), channel_id=1, source_target_pairs={{16,0},{17,1},{18,2},{19,3},{20,4},{21,5},{22,6},{23,7},{24,8},{25... | collective-permute-start | bytes 344072 | tf_op jit(solution)/shard_map/ppermute | solution.py:519
  77.8 7.4 %collective-permute-start.10 = (f32[8,1024]{1,0:T(8,128)S(1)}, f32[8,1024]{1,0:T(8,128)S(1)}, u32[]{:S(2)}, u32[]{:S(2)}) collective-permute-start(f32[8,1024]{1,0:T(8,128)S(1)} %get-tuple-element.41), channel_id=1, source_target_pairs={{0,16},{1,17},{2,18},{3,19},{4,20},{5,21},{6,22},{7,23},{8,24},{9,... | collective-permute-start | bytes 98312 | tf_op jit(solution)/shard_map/ppermute | solution.py:541
  79.8 5.4 %collective-permute-start.11 = (f32[8,1024]{1,0:T(8,128)S(1)}, f32[8,1024]{1,0:T(8,128)S(1)}, u32[]{:S(2)}, u32[]{:S(2)}) collective-permute-start(f32[8,1024]{1,0:T(8,128)S(1)} %get-tuple-element.40), channel_id=1, source_target_pairs={{16,0},{17,1},{18,2},{19,3},{20,4},{21,5},{22,6},{23,7},{24,8},{25... | collective-permute-start | bytes 98312 | tf_op jit(solution)/shard_map/ppermute | solution.py:542
  83.6 0.9 copy-start.5
  88.1 0.9 copy-start.1
  88.9 16.7 %all-to-all-start.2 = ((s16[16,160,128]{2,1,0:T(8,128)(2,1)}), s16[16,160,128]{2,1,0:T(8,128)(2,1)}, u32[]{:S(2)}, u32[]{:S(2)}) async-start(s16[16,160,128]{2,1,0:T(8,128)(2,1)} %copy-done.1), calls=%async_computation.2 | async-start | bytes 1310720 | tf_op jit(solution)/shard_map/all_to_all | solution.py:20
  105.6 1.0 copy-start.3
  106.6 11.2 %copy-start.11 = (bf16[8,64,128]{2,1,0:T(8,128)(2,1)S(1)}, bf16[8,64,128]{2,1,0:T(8,128)(2,1)}, u32[]{:S(2)}) copy-start(bf16[8,64,128]{2,1,0:T(8,128)(2,1)} %copy-done.10) | copy-start | bytes 393220
  109.5 0.8 copy-start.9
  110.4 26.7 %all-to-all-start.3 = ((s16[8,144,256]{2,1,0:T(8,128)(2,1)}), s16[8,144,256]{2,1,0:T(8,128)(2,1)S(1)}, u32[]{:S(2)}, u32[]{:S(2)}) async-start(s16[8,144,256]{2,1,0:T(8,128)(2,1)} %copy-done.9), calls=%async_computation.3 | async-start | bytes 1179648 | tf_op jit(solution)/shard_map/all_to_all | solution.py:20
  117.9 38.8 %copy-start.13 = (bf16[8,4,8,256]{3,2,1,0:T(8,128)(2,1)S(1)}, bf16[8,4,8,256]{3,2,1,0:T(8,128)(2,1)}, u32[]{:S(2)}) copy-start(bf16[8,4,8,256]{3,2,1,0:T(8,128)(2,1)} %param.8) | copy-start | bytes 393220
  138.4 17.9 %all-to-all-start.4 = ((f32[16,2,8,256]{3,2,1,0:T(8,128)}), f32[16,2,8,256]{3,2,1,0:T(8,128)S(1)}, u32[]{:S(2)}, u32[]{:S(2)}) async-start(f32[16,2,8,256]{3,2,1,0:T(8,128)} %shard_map.101), calls=%async_computation.4 | async-start | bytes 524288 | tf_op jit(solution)/shard_map/all_to_all | solution.py:20
  142.0 6.0 %collective-permute-start.14 = (f32[4,32,64]{2,1,0:T(8,128)S(1)}, f32[4,32,64]{2,1,0:T(8,128)S(1)}, u32[]{:S(2)}, u32[]{:S(2)}) collective-permute-start(f32[4,32,64]{2,1,0:T(8,128)S(1)} %get-tuple-element.35), channel_id=1, source_target_pairs={{0,1},{1,0},{2,3},{3,2},{4,5},{5,4},{6,7},{7,6},{8,9},{9,8},{10,11... | collective-permute-start | bytes 98312 | tf_op jit(solution)/shard_map/ppermute | solution.py:594
  (2 other events, 1.3 us)

commit v11 on v10

--- a/solution.py
+++ b/solution.py
@@ -483,6 +483,21 @@
     whole = pl.BlockSpec(memory_space=pltpu.VMEM)
     roomy = pltpu.CompilerParams(vmem_limit_bytes=48 * 1024 * 1024)
     where_side = jnp.reshape(side, (1,)).astype(jnp.int32)
+    is_own = (quarter // parts == side).astype(jnp.int32)
+    local = pl.pallas_call(
+        arrange_kernel,
+        out_shape=jax.ShapeDtypeStruct(
+            (own_rows, 2 * lon_total + kinds * peers * block_count), jnp.float32
+        ),
+        in_specs=[scalars, whole, whole],
+        out_specs=whole,
+        compiler_params=roomy,
+    )(jnp.stack([side.astype(jnp.int32), is_own]), packed, passed)
+    seen_before = lax.ppermute(local[-HALO:], ALL, forward)
+    seen_after = lax.ppermute(local[:HALO], ALL, backward)
+    seen_before, seen_after, other_members = lax.optimization_barrier(
+        (seen_before, seen_after, other_members)
+    )
     anywhere = pl.BlockSpec(memory_space=pl.ANY)
     piece_rows = own_rows * lon_total // 128 + own_rows
     partial_sum, lat_ring = pl.pallas_call(
@@ -502,21 +517,8 @@
         other_members,
         *[blocks[d] for d in range(rings)],
     )
-    partial_sum, packed, passed = lax.optimization_barrier((partial_sum, packed, passed))
     arrived = swapped(partial_sum, "mem", 0)
 
-    is_own = (quarter // parts == side).astype(jnp.int32)
-    local = pl.pallas_call(
-        arrange_kernel,
-        out_shape=jax.ShapeDtypeStruct(
-            (own_rows, 2 * lon_total + kinds * peers * block_count), jnp.float32
-        ),
-        in_specs=[scalars, whole, whole],
-        out_specs=whole,
-        compiler_params=roomy,
-    )(jnp.stack([side.astype(jnp.int32), is_own]), packed, passed)
-    before = lax.ppermute(local[-HALO:], ALL, forward)
-    after = lax.ppermute(local[:HALO], ALL, backward)
     wide_rows = own_rows + 2 * HALO
     wide_wind, gains, values = pl.pallas_call(
         spread_kernel,
@@ -527,7 +529,7 @@
         in_specs=[whole] * 3,
         out_specs=[whole] * 3,
         compiler_params=roomy,
-    )(before, local, after)
+    )(seen_before, local, seen_after)
 
     scale = (members_here * peers - 1) ** -0.5
     own = pl.pallas_call(

time: 159 us -> 179 us (1.13)
  waiting for transfers between devices: 54.8 us -> 77.8 us
  other arithmetic: 6.5 us -> 4.64 us
    ppermute x1, waiting for transfers between devices: 0.01 us -> 20.1 us  [body(): passed = lax.ppermute(passed, 'lat_1', across)]
    ppermute x1, waiting for transfers between devices: 9.37 us -> 0.01 us  [body(): other_members = lax.ppermute(other_members, 'lat_1', across)]
    all_to_all x5, waiting for transfers between devices: 37.9 us -> 46.1 us  [swapped(): lax.all_to_all(value, axis, split_axis=dim, concat_axis=dim, tiled=True)]
    ppermute x4, waiting for transfers between devices: 4.4 us -> 7.4 us  [body(): rising = lax.ppermute(rising, 'lat_0', up)]
    ppermute x3, starting transfers between devices: 12.5 us -> 10.5 us  [body(): falling = lax.ppermute(falling, 'lat_0', down)]
    ppermute x4, starting transfers between devices: 0.09 us -> 2.01 us  [body(): rising = lax.ppermute(rising, 'lat_0', up)]
    unnamed x30 -> x34, local copies, waits for them, and re-layouts: 10.6 us -> 12.1 us
  transfers between devices with their start and end apart: 20 -> 20, of which waited for: 11 -> 11; matrix products, arithmetic and copies ran while one was open for 9% -> 6% of each run, Pallas kernels for 4% -> 1%
where the time goes in v11:
time: 179 us; the launch traced here: 178 us
  waiting for transfers between devices  77.8 us (43%)
  starting transfers between devices  61.7 us (34%)
  local copies, waits for them, and re-layouts  18.9 us (11%)
  Pallas kernels  13.7 us (8%)
  other arithmetic  4.64 us (3%)
    all_to_all x5, waiting for transfers between devices, swapped(): lax.all_to_all(value, axis, split_axis=dim, concat_axis=dim, tiled=True)  46.1 us
    all_to_all x5, starting transfers between devices, swapped(): lax.all_to_all(value, axis, split_axis=dim, concat_axis=dim, tiled=True)  29.5 us
    ppermute x1, waiting for transfers between devices, body(): passed = lax.ppermute(passed, 'lat_1', across)  20.1 us
    unnamed x34, local copies, waits for them, and re-layouts  12.1 us
    ppermute x3, starting transfers between devices, body(): falling = lax.ppermute(falling, 'lat_0', down)  10.5 us
    ppermute x4, waiting for transfers between devices, body(): rising = lax.ppermute(rising, 'lat_0', up)  7.4 us
    ppermute x1, starting transfers between devices, body(): after = lax.ppermute(own[:HALO], ALL, backward)  3.72 us
    ppermute x1, starting transfers between devices, body(): seen_after = lax.ppermute(local[:HALO], ALL, backward)  3.64 us
  transfers between devices with their start and end apart: 20, of which 11 were waited for; matrix products, arithmetic and copies ran while one was open for 6% of the time, Pallas kernels for 1%

profile of v11, /device:TPU:2, one launch (start us, length us, event | category | flops | bytes accessed | tf_op | source)
XLA Modules:
  0.0 177.7 jit_solution(4540354373195255463)
XLA Ops:
  2.5 2.2 %collective-permute-start = (bf16[144,256]{1,0:T(8,128)(2,1)S(1)}, bf16[144,256]{1,0:T(8,128)(2,1)S(1)}, u32[]{:S(2)}, u32[]{:S(2)}) collective-permute-start(bf16[144,256]{1,0:T(8,128)(2,1)S(1)} %maximum_maximum_fusion), channel_id=1, source_target_pairs={{0,1},{1,0},{2,3},{3,2},{4,5},{5,4},{6,7},{7,6},{8,9},{9,8},{10,11... | collective-permute-start | bytes 221192 | tf_op jit(solution)/shard_map/ppermute | solution.py:426
  8.6 5.9 %all-to-all-start = ((f32[16,3,16,128]{3,2,1,0:T(8,128)}), f32[16,3,16,128]{3,2,1,0:T(8,128)S(1)}, u32[]{:S(2)}, u32[]{:S(2)}) async-start(f32[16,3,16,128]{3,2,1,0:T(8,128)} %bitcast.19), calls=%async_computation | async-start | bytes 786432 | tf_op jit(solution)/shard_map/all_to_all | solution.py:20
  14.7 2.0 %collective-permute-start.1 = (bf16[288,256]{1,0:T(8,128)(2,1)S(1)}, bf16[288,256]{1,0:T(8,128)(2,1)}, u32[]{:S(2)}, u32[]{:S(2)}) collective-permute-start(bf16[288,256]{1,0:T(8,128)(2,1)S(1)} %pad_maximum_fusion.refs_0_), channel_id=1, source_target_pairs={{0,2},{2,4},{4,6},{6,8},{8,10},{10,12},{12,14},{14,0},{1,3},{3,5},... | collective-permute-start | bytes 442376 | tf_op jit(solution)/shard_map/ppermute | solution.py:461
  16.7 4.0 %collective-permute-start.3 = (bf16[288,256]{1,0:T(8,128)(2,1)S(1)}, bf16[288,256]{1,0:T(8,128)(2,1)}, u32[]{:S(2)}, u32[]{:S(2)}) collective-permute-start(bf16[288,256]{1,0:T(8,128)(2,1)S(1)} %pad_maximum_fusion.refs_0_), channel_id=1, source_target_pairs={{2,0},{4,2},{6,4},{8,6},{10,8},{12,10},{14,12},{0,14},{3,1},{5,3},... | collective-permute-start | bytes 442376 | tf_op jit(solution)/shard_map/ppermute | solution.py:463
  21.4 3.5 %collective-permute-done.1.refs_7_ = bf16[288,256]{1,0:T(8,128)(2,1)} collective-permute-done((bf16[288,256]{1,0:T(8,128)(2,1)S(1)}, bf16[288,256]{1,0:T(8,128)(2,1)}, u32[]{:S(2)}, u32[]{:S(2)}) %collective-permute-start.1) | collective-permute-done | bytes 147488 | tf_op jit(solution)/shard_map/ppermute | solution.py:461
  24.9 3.2 %collective-permute-start.4 = (bf16[288,256]{1,0:T(8,128)(2,1)}, bf16[288,256]{1,0:T(8,128)(2,1)}, u32[]{:S(2)}, u32[]{:S(2)}) collective-permute-start(bf16[288,256]{1,0:T(8,128)(2,1)} %collective-permute-done.3.refs_1_), channel_id=1, source_target_pairs={{2,0},{4,2},{6,4},{8,6},{10,8},{12,10},{14,12},{0,14},{3,1},{5,3},... | collective-permute-start | bytes 442376 | tf_op jit(solution)/shard_map/ppermute | solution.py:463
  29.2 1.4 collective-permute-start.8
  32.6 1.4 collective-permute-start.5
  34.8 3.2 %collective-permute-start.9 = (bf16[288,256]{1,0:T(8,128)(2,1)}, bf16[288,256]{1,0:T(8,128)(2,1)}, u32[]{:S(2)}, u32[]{:S(2)}) collective-permute-start(bf16[288,256]{1,0:T(8,128)(2,1)} %collective-permute-done.4.refs_2_), channel_id=1, source_target_pairs={{2,0},{4,2},{6,4},{8,6},{10,8},{12,10},{14,12},{0,14},{3,1},{5,3},... | collective-permute-start | bytes 442376 | tf_op jit(solution)/shard_map/ppermute | solution.py:463
  38.0 2.7 %collective-permute-done.10.refs_5_ = bf16[288,256]{1,0:T(8,128)(2,1)} collective-permute-done((bf16[288,256]{1,0:T(8,128)(2,1)}, bf16[288,256]{1,0:T(8,128)(2,1)}, u32[]{:S(2)}, u32[]{:S(2)}) %collective-permute-start.10) | collective-permute-done | bytes 147488 | tf_op jit(solution)/shard_map/ppermute | solution.py:461
  40.7 20.1 %collective-permute-done.5.other_ref = f32[16,2,16,128]{3,2,1,0:T(8,128)} collective-permute-done((f32[16,2,16,128]{3,2,1,0:T(8,128)}, f32[16,2,16,128]{3,2,1,0:T(8,128)}, u32[]{:S(2)}, u32[]{:S(2)}) %collective-permute-start.5) | collective-permute-done | bytes 262176 | tf_op jit(solution)/shard_map/ppermute | solution.py:467
  60.8 1.4 shard_map.95.local_ref
  63.6 1.9 %collective-permute-start.6 = (f32[8,3584]{1,0:T(8,128)}, f32[8,3584]{1,0:T(8,128)S(1)}, u32[]{:S(2)}, u32[]{:S(2)}) collective-permute-start(f32[8,3584]{1,0:T(8,128)} %get-tuple-element.33), channel_id=1, source_target_pairs={{0,16},{1,17},{2,18},{3,19},{4,20},{5,21},{6,22},{7,23},{8,24},{9,... | collective-permute-start | bytes 344072 | tf_op jit(solution)/shard_map/ppermute | solution.py:496
  65.6 3.6 %collective-permute-start.7 = (f32[8,3584]{1,0:T(8,128)}, f32[8,3584]{1,0:T(8,128)S(1)}, u32[]{:S(2)}, u32[]{:S(2)}) collective-permute-start(f32[8,3584]{1,0:T(8,128)} %get-tuple-element.32), channel_id=1, source_target_pairs={{16,0},{17,1},{18,2},{19,3},{20,4},{21,5},{22,6},{23,7},{24,8},{25... | collective-permute-start | bytes 344072 | tf_op jit(solution)/shard_map/ppermute | solution.py:497
  70.6 1.3 collective-permute-done.7.after_ref
  74.5 3.3 %shard_map.96 = (s16[16,144,128]{2,1,0:T(8,128)(2,1)S(1)}, bf16[8,64,128]{2,1,0:T(8,128)(2,1)S(1)}) custom-call(s32[1]{0:T(128)} %bitcast.side_ref, bf16[64,128]{1,0:T(8,128)(2,1)S(1)} %copy.34.columns_ref, bf16[256,1024]{1,0:T(8,128)(2,1)S(1)} %copy-done.2, bf16[4,8,32,1024]{3,2,1,0:T(8,128)(2,1)S(1)} %copy-done, ...), custom_call_target="tpu_custom_call" | custom-call | tf_op jit(solution)/shard_map/pallas_call | solution.py:503
  78.6 6.1 %all-to-all-start.1 = ((s16[16,144,128]{2,1,0:T(8,128)(2,1)}), s16[16,144,128]{2,1,0:T(8,128)(2,1)}, u32[]{:S(2)}, u32[]{:S(2)}) async-start(s16[16,144,128]{2,1,0:T(8,128)(2,1)} %copy-done.9), calls=%async_computation.1 | async-start | bytes 1179648 | tf_op jit(solution)/shard_map/all_to_all | solution.py:20
  84.8 10.5 %all-to-all-done.1.message_ref = s16[16,144,128]{2,1,0:T(8,128)(2,1)} async-done(((s16[16,144,128]{2,1,0:T(8,128)(2,1)}), s16[16,144,128]{2,1,0:T(8,128)(2,1)}, u32[]{:S(2)}, u32[]{:S(2)}) %all-to-all-start.1) | async-done | bytes 589856 | tf_op jit(solution)/shard_map/all_to_all | solution.py:20
  96.6 2.0 %collective-permute-start.12 = (f32[8,1024]{1,0:T(8,128)S(1)}, f32[8,1024]{1,0:T(8,128)S(1)}, u32[]{:S(2)}, u32[]{:S(2)}) collective-permute-start(f32[8,1024]{1,0:T(8,128)S(1)} %get-tuple-element.41), channel_id=1, source_target_pairs={{0,16},{1,17},{2,18},{3,19},{4,20},{5,21},{6,22},{7,23},{8,24},{9,... | collective-permute-start | bytes 98312 | tf_op jit(solution)/shard_map/ppermute | solution.py:543
  98.6 3.7 %collective-permute-start.13 = (f32[8,1024]{1,0:T(8,128)S(1)}, f32[8,1024]{1,0:T(8,128)S(1)}, u32[]{:S(2)}, u32[]{:S(2)}) collective-permute-start(f32[8,1024]{1,0:T(8,128)S(1)} %get-tuple-element.40), channel_id=1, source_target_pairs={{16,0},{17,1},{18,2},{19,3},{20,4},{21,5},{22,6},{23,7},{24,8},{25... | collective-permute-start | bytes 98312 | tf_op jit(solution)/shard_map/ppermute | solution.py:544
  104.9 2.8 %shard_map.99 = s16[16,160,128]{2,1,0:T(8,128)(2,1)S(1)} custom-call(s32[2]{0:T(128)S(1)} %pad_add_fusion.place_ref, f32[16,1024]{1,0:T(8,128)S(1)} %shard_map.97.own_ref, f32[8,1024]{1,0:T(8,128)S(1)} %collective-permute-done.12.before_ref, f32[8,1024]{1,0:T(8,128)S(1)} %collective-permute-done.13.after_ref, f32[2,32,1024]{2,1,0:T(8,128)S(1)} %get-tuple-element.23.wind_ref, ...), custom_call_target="tpu_custom_call" | custom-call | tf_op jit(solution)/shard_map/pallas_call | solution.py:548
  108.5 4.2 %all-to-all-start.2 = ((s16[16,160,128]{2,1,0:T(8,128)(2,1)}), s16[16,160,128]{2,1,0:T(8,128)(2,1)}, u32[]{:S(2)}, u32[]{:S(2)}) async-start(s16[16,160,128]{2,1,0:T(8,128)(2,1)} %copy-done.1), calls=%async_computation.2 | async-start | bytes 1310720 | tf_op jit(solution)/shard_map/all_to_all | solution.py:20
  112.7 2.0 %copy.35 = bf16[256,1024]{0,1:T(8,128)(2,1)} copy(bf16[256,1024]{1,0:T(8,128)(2,1)} %lon_ref.1) | data formatting | bytes 1048576 | tf_op args[3]
  114.8 8.9 %all-to-all-done.2.message_ref = s16[16,160,128]{2,1,0:T(8,128)(2,1)} async-done(((s16[16,160,128]{2,1,0:T(8,128)(2,1)}), s16[16,160,128]{2,1,0:T(8,128)(2,1)}, u32[]{:S(2)}, u32[]{:S(2)}) %all-to-all-start.2) | async-done | bytes 655392 | tf_op jit(solution)/shard_map/all_to_all | solution.py:20
  124.7 2.9 %shard_map.100 = (s16[8,144,256]{2,1,0:T(8,128)(2,1)S(1)}, f32[2,4,32,64]{3,2,1,0:T(8,128)S(1)}) custom-call(s32[1]{0:T(128)} %bitcast.side_ref, s16[16,160,128]{2,1,0:T(8,128)(2,1)} %all-to-all-done.2.message_ref, bf16[1024,256]{1,0:T(8,128)(2,1)S(1)} %bitcast.40, bf16[4,8,32,1024]{3,2,1,0:T(8,128)(2,1)S(1)} %copy-done, ...), custom_call_target="tpu_custom_call" | custom-call | tf_op jit(solution)/shard_map/pallas_call | solution.py:563
  128.4 9.7 %all-to-all-start.3 = ((s16[8,144,256]{2,1,0:T(8,128)(2,1)}), s16[8,144,256]{2,1,0:T(8,128)(2,1)S(1)}, u32[]{:S(2)}, u32[]{:S(2)}) async-start(s16[8,144,256]{2,1,0:T(8,128)(2,1)} %copy-done.8), calls=%async_computation.3 | async-start | bytes 1179648 | tf_op jit(solution)/shard_map/all_to_all | solution.py:20
  138.4 18.9 %all-to-all-done.3.message_ref = s16[8,144,256]{2,1,0:T(8,128)(2,1)S(1)} async-done(((s16[8,144,256]{2,1,0:T(8,128)(2,1)}), s16[8,144,256]{2,1,0:T(8,128)(2,1)S(1)}, u32[]{:S(2)}, u32[]{:S(2)}) %all-to-all-start.3) | async-done | bytes 589856 | tf_op jit(solution)/shard_map/all_to_all | solution.py:20
  157.3 1.4 shard_map.101
  158.7 3.5 %all-to-all-start.4 = ((f32[16,2,8,256]{3,2,1,0:T(8,128)}), f32[16,2,8,256]{3,2,1,0:T(8,128)S(1)}, u32[]{:S(2)}, u32[]{:S(2)}) async-start(f32[16,2,8,256]{3,2,1,0:T(8,128)} %shard_map.101), calls=%async_computation.4 | async-start | bytes 524288 | tf_op jit(solution)/shard_map/all_to_all | solution.py:20
  162.3 3.4 %collective-permute-start.14 = (f32[4,32,64]{2,1,0:T(8,128)S(1)}, f32[4,32,64]{2,1,0:T(8,128)S(1)}, u32[]{:S(2)}, u32[]{:S(2)}) collective-permute-start(f32[4,32,64]{2,1,0:T(8,128)S(1)} %get-tuple-element.35), channel_id=1, source_target_pairs={{0,1},{1,0},{2,3},{3,2},{4,5},{5,4},{6,7},{7,6},{8,9},{9,8},{10,11... | collective-permute-start | bytes 98312 | tf_op jit(solution)/shard_map/ppermute | solution.py:596
  165.7 2.5 %collective-permute-done.14 = f32[4,32,64]{2,1,0:T(8,128)S(1)} collective-permute-done((f32[4,32,64]{2,1,0:T(8,128)S(1)}, f32[4,32,64]{2,1,0:T(8,128)S(1)}, u32[]{:S(2)}, u32[]{:S(2)}) %collective-permute-start.14) | collective-permute-done | bytes 32800 | tf_op jit(solution)/shard_map/ppermute | solution.py:596
  168.9 7.8 %all-to-all-done.4 = f32[16,2,8,256]{3,2,1,0:T(8,128)S(1)} async-done(((f32[16,2,8,256]{3,2,1,0:T(8,128)}), f32[16,2,8,256]{3,2,1,0:T(8,128)S(1)}, u32[]{:S(2)}, u32[]{:S(2)}) %all-to-all-start.4) | async-done | bytes 262176 | tf_op jit(solution)/shard_map/all_to_all | solution.py:20
  (88 shorter events, 24.9 us)
Async XLA Ops:
  2.5 12.1 %collective-permute-start = (bf16[144,256]{1,0:T(8,128)(2,1)S(1)}, bf16[144,256]{1,0:T(8,128)(2,1)S(1)}, u32[]{:S(2)}, u32[]{:S(2)}) collective-permute-start(bf16[144,256]{1,0:T(8,128)(2,1)S(1)} %maximum_maximum_fusion), channel_id=1, source_target_pairs={{0,1},{1,0},{2,3},{3,2},{4,5},{5,4},{6,7},{7,6},{8,9},{9,8},{10,11... | collective-permute-start | bytes 221192 | tf_op jit(solution)/shard_map/ppermute | solution.py:426
  6.5 21.7 %copy-start = (bf16[4,8,32,1024]{3,2,1,0:T(8,128)(2,1)S(1)}, bf16[4,8,32,1024]{3,2,1,0:T(8,128)(2,1)}, u32[]{:S(2)}) copy-start(bf16[4,8,32,1024]{3,2,1,0:T(8,128)(2,1)} %own_ref.3) | copy-start | bytes 6291460
  8.6 23.2 %all-to-all-start = ((f32[16,3,16,128]{3,2,1,0:T(8,128)}), f32[16,3,16,128]{3,2,1,0:T(8,128)S(1)}, u32[]{:S(2)}, u32[]{:S(2)}) async-start(f32[16,3,16,128]{3,2,1,0:T(8,128)} %bitcast.19), calls=%async_computation | async-start | bytes 786432 | tf_op jit(solution)/shard_map/all_to_all | solution.py:20
  14.6 13.5 %copy-start.15 = (bf16[32,256]{1,0:T(8,128)(2,1)}, bf16[32,256]{1,0:T(8,128)(2,1)S(1)}, u32[]{:S(2)}) copy-start(bf16[32,256]{1,0:T(8,128)(2,1)S(1)} %maximum_select_fusion.3) | copy-start | bytes 49156
  14.7 10.2 %collective-permute-start.1 = (bf16[288,256]{1,0:T(8,128)(2,1)S(1)}, bf16[288,256]{1,0:T(8,128)(2,1)}, u32[]{:S(2)}, u32[]{:S(2)}) collective-permute-start(bf16[288,256]{1,0:T(8,128)(2,1)S(1)} %pad_maximum_fusion.refs_0_), channel_id=1, source_target_pairs={{0,2},{2,4},{4,6},{6,8},{8,10},{10,12},{12,14},{14,0},{1,3},{3,5},... | collective-permute-start | bytes 442376 | tf_op jit(solution)/shard_map/ppermute | solution.py:461
  16.7 8.2 %collective-permute-start.3 = (bf16[288,256]{1,0:T(8,128)(2,1)S(1)}, bf16[288,256]{1,0:T(8,128)(2,1)}, u32[]{:S(2)}, u32[]{:S(2)}) collective-permute-start(bf16[288,256]{1,0:T(8,128)(2,1)S(1)} %pad_maximum_fusion.refs_0_), channel_id=1, source_target_pairs={{2,0},{4,2},{6,4},{8,6},{10,8},{12,10},{14,12},{0,14},{3,1},{5,3},... | collective-permute-start | bytes 442376 | tf_op jit(solution)/shard_map/ppermute | solution.py:463
  24.9 6.9 %collective-permute-start.2 = (bf16[288,256]{1,0:T(8,128)(2,1)}, bf16[288,256]{1,0:T(8,128)(2,1)}, u32[]{:S(2)}, u32[]{:S(2)}) collective-permute-start(bf16[288,256]{1,0:T(8,128)(2,1)} %collective-permute-done.1.refs_7_), channel_id=1, source_target_pairs={{0,2},{2,4},{4,6},{6,8},{8,10},{10,12},{12,14},{14,0},{1,3},{3,5},... | collective-permute-start | bytes 442376 | tf_op jit(solution)/shard_map/ppermute | solution.py:461
  24.9 6.9 %collective-permute-start.4 = (bf16[288,256]{1,0:T(8,128)(2,1)}, bf16[288,256]{1,0:T(8,128)(2,1)}, u32[]{:S(2)}, u32[]{:S(2)}) collective-permute-start(bf16[288,256]{1,0:T(8,128)(2,1)} %collective-permute-done.3.refs_1_), channel_id=1, source_target_pairs={{2,0},{4,2},{6,4},{8,6},{10,8},{12,10},{14,12},{0,14},{3,1},{5,3},... | collective-permute-start | bytes 442376 | tf_op jit(solution)/shard_map/ppermute | solution.py:463
  29.2 43.3 %collective-permute-start.8 = (bf16[4,4,32,1024]{3,2,1,0:T(8,128)(2,1)}, bf16[4,4,32,1024]{3,2,1,0:T(8,128)(2,1)S(1)}, u32[]{:S(2)}, u32[]{:S(2)}) collective-permute-start(bf16[4,4,32,1024]{3,2,1,0:T(8,128)(2,1)} %constant_dynamic-slice_fusion), channel_id=1, source_target_pairs={{0,1},{1,0},{2,3},{3,2},{4,5},{5,4},{6,7},{7,6},{8,9},{9,8},{10,11... | collective-permute-start | bytes 3145736 | tf_op jit(solution)/shard_map/ppermute | solution.py:455
  32.6 28.2 %collective-permute-start.5 = (f32[16,2,16,128]{3,2,1,0:T(8,128)}, f32[16,2,16,128]{3,2,1,0:T(8,128)}, u32[]{:S(2)}, u32[]{:S(2)}) collective-permute-start(f32[16,2,16,128]{3,2,1,0:T(8,128)} %maximum_select_fusion), channel_id=1, source_target_pairs={{0,1},{1,0},{2,3},{3,2},{4,5},{5,4},{6,7},{7,6},{8,9},{9,8},{10,11... | collective-permute-start | bytes 786440 | tf_op jit(solution)/shard_map/ppermute | solution.py:467
  34.1 6.7 %collective-permute-start.10 = (bf16[288,256]{1,0:T(8,128)(2,1)}, bf16[288,256]{1,0:T(8,128)(2,1)}, u32[]{:S(2)}, u32[]{:S(2)}) collective-permute-start(bf16[288,256]{1,0:T(8,128)(2,1)} %collective-permute-done.2.refs_6_), channel_id=1, source_target_pairs={{0,2},{2,4},{4,6},{6,8},{8,10},{10,12},{12,14},{14,0},{1,3},{3,5},... | collective-permute-start | bytes 442376 | tf_op jit(solution)/shard_map/ppermute | solution.py:461
  34.8 37.7 %collective-permute-start.9 = (bf16[288,256]{1,0:T(8,128)(2,1)}, bf16[288,256]{1,0:T(8,128)(2,1)}, u32[]{:S(2)}, u32[]{:S(2)}) collective-permute-start(bf16[288,256]{1,0:T(8,128)(2,1)} %collective-permute-done.4.refs_2_), channel_id=1, source_target_pairs={{2,0},{4,2},{6,4},{8,6},{10,8},{12,10},{14,12},{0,14},{3,1},{5,3},... | collective-permute-start | bytes 442376 | tf_op jit(solution)/shard_map/ppermute | solution.py:463
  40.7 31.8 %collective-permute-start.11 = (bf16[288,256]{1,0:T(8,128)(2,1)}, bf16[288,256]{1,0:T(8,128)(2,1)}, u32[]{:S(2)}, u32[]{:S(2)}) collective-permute-start(bf16[288,256]{1,0:T(8,128)(2,1)} %collective-permute-done.10.refs_5_), channel_id=1, source_target_pairs={{0,2},{2,4},{4,6},{6,8},{8,10},{10,12},{12,14},{14,0},{1,3},{3,5},... | collective-permute-start | bytes 442376 | tf_op jit(solution)/shard_map/ppermute | solution.py:461
  63.6 6.3 %collective-permute-start.6 = (f32[8,3584]{1,0:T(8,128)}, f32[8,3584]{1,0:T(8,128)S(1)}, u32[]{:S(2)}, u32[]{:S(2)}) collective-permute-start(f32[8,3584]{1,0:T(8,128)} %get-tuple-element.33), channel_id=1, source_target_pairs={{0,16},{1,17},{2,18},{3,19},{4,20},{5,21},{6,22},{7,23},{8,24},{9,... | collective-permute-start | bytes 344072 | tf_op jit(solution)/shard_map/ppermute | solution.py:496
  65.6 6.3 %collective-permute-start.7 = (f32[8,3584]{1,0:T(8,128)}, f32[8,3584]{1,0:T(8,128)S(1)}, u32[]{:S(2)}, u32[]{:S(2)}) collective-permute-start(f32[8,3584]{1,0:T(8,128)} %get-tuple-element.32), channel_id=1, source_target_pairs={{16,0},{17,1},{18,2},{19,3},{20,4},{21,5},{22,6},{23,7},{24,8},{25... | collective-permute-start | bytes 344072 | tf_op jit(solution)/shard_map/ppermute | solution.py:497
  72.5 1.0 copy-start.2
  73.6 0.9 copy-start.7
  77.8 0.8 copy-start.9
  78.6 23.8 %copy-start.5 = (f32[16,3584]{1,0:T(8,128)S(1)}, f32[16,3584]{1,0:T(8,128)}, u32[]{:S(2)}) copy-start(f32[16,3584]{1,0:T(8,128)} %copy-done.4) | copy-start | bytes 688132
  78.6 16.7 %all-to-all-start.1 = ((s16[16,144,128]{2,1,0:T(8,128)(2,1)}), s16[16,144,128]{2,1,0:T(8,128)(2,1)}, u32[]{:S(2)}, u32[]{:S(2)}) async-start(s16[16,144,128]{2,1,0:T(8,128)(2,1)} %copy-done.9), calls=%async_computation.1 | async-start | bytes 1179648 | tf_op jit(solution)/shard_map/all_to_all | solution.py:20
  96.6 8.3 %collective-permute-start.12 = (f32[8,1024]{1,0:T(8,128)S(1)}, f32[8,1024]{1,0:T(8,128)S(1)}, u32[]{:S(2)}, u32[]{:S(2)}) collective-permute-start(f32[8,1024]{1,0:T(8,128)S(1)} %get-tuple-element.41), channel_id=1, source_target_pairs={{0,16},{1,17},{2,18},{3,19},{4,20},{5,21},{6,22},{7,23},{8,24},{9,... | collective-permute-start | bytes 98312 | tf_op jit(solution)/shard_map/ppermute | solution.py:543
  98.6 6.3 %collective-permute-start.13 = (f32[8,1024]{1,0:T(8,128)S(1)}, f32[8,1024]{1,0:T(8,128)S(1)}, u32[]{:S(2)}, u32[]{:S(2)}) collective-permute-start(f32[8,1024]{1,0:T(8,128)S(1)} %get-tuple-element.40), channel_id=1, source_target_pairs={{16,0},{17,1},{18,2},{19,3},{20,4},{21,5},{22,6},{23,7},{24,8},{25... | collective-permute-start | bytes 98312 | tf_op jit(solution)/shard_map/ppermute | solution.py:544
  102.4 0.9 copy-start.11
  103.3 0.9 copy-start.13
  107.7 0.8 copy-start.1
  108.5 15.1 %all-to-all-start.2 = ((s16[16,160,128]{2,1,0:T(8,128)(2,1)}), s16[16,160,128]{2,1,0:T(8,128)(2,1)}, u32[]{:S(2)}, u32[]{:S(2)}) async-start(s16[16,160,128]{2,1,0:T(8,128)(2,1)} %copy-done.1), calls=%async_computation.2 | async-start | bytes 1310720 | tf_op jit(solution)/shard_map/all_to_all | solution.py:20
  123.7 1.0 copy-start.3
  127.6 0.8 copy-start.8
  128.4 28.9 %all-to-all-start.3 = ((s16[8,144,256]{2,1,0:T(8,128)(2,1)}), s16[8,144,256]{2,1,0:T(8,128)(2,1)S(1)}, u32[]{:S(2)}, u32[]{:S(2)}) async-start(s16[8,144,256]{2,1,0:T(8,128)(2,1)} %copy-done.8), calls=%async_computation.3 | async-start | bytes 1179648 | tf_op jit(solution)/shard_map/all_to_all | solution.py:20
  138.2 38.8 %copy-start.14 = (bf16[8,4,8,256]{3,2,1,0:T(8,128)(2,1)S(1)}, bf16[8,4,8,256]{3,2,1,0:T(8,128)(2,1)}, u32[]{:S(2)}) copy-start(bf16[8,4,8,256]{3,2,1,0:T(8,128)(2,1)} %param.8) | copy-start | bytes 393220
  158.7 17.9 %all-to-all-start.4 = ((f32[16,2,8,256]{3,2,1,0:T(8,128)}), f32[16,2,8,256]{3,2,1,0:T(8,128)S(1)}, u32[]{:S(2)}, u32[]{:S(2)}) async-start(f32[16,2,8,256]{3,2,1,0:T(8,128)} %shard_map.101), calls=%async_computation.4 | async-start | bytes 524288 | tf_op jit(solution)/shard_map/all_to_all | solution.py:20
  162.3 5.9 %collective-permute-start.14 = (f32[4,32,64]{2,1,0:T(8,128)S(1)}, f32[4,32,64]{2,1,0:T(8,128)S(1)}, u32[]{:S(2)}, u32[]{:S(2)}) collective-permute-start(f32[4,32,64]{2,1,0:T(8,128)S(1)} %get-tuple-element.35), channel_id=1, source_target_pairs={{0,1},{1,0},{2,3},{3,2},{4,5},{5,4},{6,7},{7,6},{8,9},{9,8},{10,11... | collective-permute-start | bytes 98312 | tf_op jit(solution)/shard_map/ppermute | solution.py:596
  (4 other events, 2.6 us)

commit v12 on v10

--- a/solution.py
+++ b/solution.py
@@ -250,7 +250,10 @@
 def spread_kernel(before_ref, local_ref, after_ref, wind_ref, gain_ref, value_ref):
     _, rows, cols = wind_ref.shape
     lanes = cols // OBLK
-    local = jnp.concatenate([before_ref[...], local_ref[...], after_ref[...]], axis=0)
+    width = local_ref.shape[1]
+    local = jnp.concatenate(
+        [before_ref[:, :width], local_ref[...], after_ref[:, :width]], axis=0
+    )
     wind_ref[0] = local[:, :cols]
     wind_ref[1] = local[:, cols : 2 * cols]
     sights = [local[:, 2 * cols + k * lanes : 2 * cols + (k + 1) * lanes] for k in range(3 * STEPS)]
@@ -277,7 +280,8 @@
     rows, cols = wind_ref.shape[1:]
     first_row = place_ref[0]
     last_row = place_ref[1]
-    state = jnp.concatenate([before_ref[...], own_ref[...], after_ref[...]], axis=0)
+    skip = before_ref.shape[1] - cols
+    state = jnp.concatenate([before_ref[:, skip:], own_ref[...], after_ref[:, skip:]], axis=0)
     row = lax.broadcasted_iota(jnp.int32, (rows, cols), 0) + first_row
     col = lax.broadcasted_iota(jnp.int32, (rows, cols), 1)
     inside = ((row >= 0) & (row < last_row)).astype(jnp.float32)
@@ -515,8 +519,17 @@
         out_specs=whole,
         compiler_params=roomy,
     )(jnp.stack([side.astype(jnp.int32), is_own]), packed, passed)
-    before = lax.ppermute(local[-HALO:], ALL, forward)
-    after = lax.ppermute(local[:HALO], ALL, backward)
+    scale = (members_here * peers - 1) ** -0.5
+    own = pl.pallas_call(
+        functools.partial(add_kernel, scale),
+        out_shape=jax.ShapeDtypeStruct((own_rows, lon_total), jnp.float32),
+        in_specs=[whole],
+        out_specs=whole,
+        compiler_params=roomy,
+    )(arrived)
+
+    before = lax.ppermute(jnp.concatenate([local[-HALO:], own[-HALO:]], axis=1), ALL, forward)
+    after = lax.ppermute(jnp.concatenate([local[:HALO], own[:HALO]], axis=1), ALL, backward)
     wide_rows = own_rows + 2 * HALO
     wide_wind, gains, values = pl.pallas_call(
         spread_kernel,
@@ -529,17 +542,6 @@
         compiler_params=roomy,
     )(before, local, after)
 
-    scale = (members_here * peers - 1) ** -0.5
-    own = pl.pallas_call(
-        functools.partial(add_kernel, scale),
-        out_shape=jax.ShapeDtypeStruct((own_rows, lon_total), jnp.float32),
-        in_specs=[whole],
-        out_specs=whole,
-        compiler_params=roomy,
-    )(arrived)
-
-    before = lax.ppermute(own[-HALO:], ALL, forward)
-    after = lax.ppermute(own[:HALO], ALL, backward)
     place = jnp.stack(
         [ring * wide_count + quarter * own_rows - HALO, jnp.int32(row_count * bands)]
     ).astype(jnp.int32)

time: 159 us -> 162 us (1.019)
  waiting for transfers between devices: 54.8 us -> 63.8 us
  starting transfers between devices: 61.9 us -> 55.4 us
    all_to_all x5, waiting for transfers between devices: 37.9 us -> 44.1 us  [swapped(): lax.all_to_all(value, axis, split_axis=dim, concat_axis=dim, tiled=True)]
    ppermute x4 -> x2, starting transfers between devices: 11.3 us -> 5.72 us  [the longest x1 3.71 us: body(): lax.ppermute(jnp.concatenate([local[:HALO], own[:HALO]], axis=1), ALL, ba...]
    ppermute x4 -> x2, waiting for transfers between devices: 0.01 us -> 2.7 us  [the longest x1 2.54 us: body(): lax.ppermute(jnp.concatenate([local[:HALO], own[:HALO]], axis=1), ALL, ba...]
  transfers between devices with their start and end apart: 20 -> 18, of which waited for: 11 -> 13; matrix products, arithmetic and copies ran while one was open for 9% -> 9% of each run, Pallas kernels for 4% -> 3%
where the time goes in v12:
time: 162 us; the launch traced here: 160 us
  waiting for transfers between devices  63.8 us (39%)
  starting transfers between devices  55.4 us (34%)
  local copies, waits for them, and re-layouts  18.7 us (12%)
  Pallas kernels  13.8 us (9%)
  other arithmetic  7.8 us (5%)
    all_to_all x5, waiting for transfers between devices, swapped(): lax.all_to_all(value, axis, split_axis=dim, concat_axis=dim, tiled=True)  44.1 us
    all_to_all x5, starting transfers between devices, swapped(): lax.all_to_all(value, axis, split_axis=dim, concat_axis=dim, tiled=True)  27.2 us
    ppermute x3, starting transfers between devices, body(): falling = lax.ppermute(falling, 'lat_0', down)  12.5 us
    unnamed x30, local copies, waits for them, and re-layouts  10.5 us
    ppermute x1, waiting for transfers between devices, body(): other_members = lax.ppermute(other_members, 'lat_1', across)  9.37 us
    ppermute x4, waiting for transfers between devices, body(): rising = lax.ppermute(rising, 'lat_0', up)  4.46 us
    ppermute x1, starting transfers between devices, body(): lax.ppermute(jnp.concatenate([local[:HALO], own[:HALO]], axis=1), ALL, ba...  3.71 us
    ppermute x1, starting transfers between devices, body(): increment = in_order(kept, lax.ppermute(sent, 'lat_1', across), 0)  3.5 us
  transfers between devices with their start and end apart: 18, of which 13 were waited for; matrix products, arithmetic and copies ran while one was open for 9% of the time, Pallas kernels for 3%

profile of v12, /device:TPU:2, one launch (start us, length us, event | category | flops | bytes accessed | tf_op | source)
XLA Modules:
  0.0 160.5 jit_solution(74215730195469673)
XLA Ops:
  2.5 2.2 %collective-permute-start = (bf16[144,256]{1,0:T(8,128)(2,1)S(1)}, bf16[144,256]{1,0:T(8,128)(2,1)S(1)}, u32[]{:S(2)}, u32[]{:S(2)}) collective-permute-start(bf16[144,256]{1,0:T(8,128)(2,1)S(1)} %maximum_maximum_fusion), channel_id=1, source_target_pairs={{0,1},{1,0},{2,3},{3,2},{4,5},{5,4},{6,7},{7,6},{8,9},{9,8},{10,11... | collective-permute-start | bytes 221192 | tf_op jit(solution)/shard_map/ppermute | solution.py:430
  8.5 5.9 %collective-permute-start.2 = (bf16[288,256]{1,0:T(8,128)(2,1)S(1)}, bf16[288,256]{1,0:T(8,128)(2,1)}, u32[]{:S(2)}, u32[]{:S(2)}) collective-permute-start(bf16[288,256]{1,0:T(8,128)(2,1)S(1)} %pad_maximum_fusion.refs_0_), channel_id=1, source_target_pairs={{2,0},{4,2},{6,4},{8,6},{10,8},{12,10},{14,12},{0,14},{3,1},{5,3},... | collective-permute-start | bytes 442376 | tf_op jit(solution)/shard_map/ppermute | solution.py:467
  15.3 5.9 %all-to-all-start = ((f32[16,3,16,128]{3,2,1,0:T(8,128)}), f32[16,3,16,128]{3,2,1,0:T(8,128)S(1)}, u32[]{:S(2)}, u32[]{:S(2)}) async-start(f32[16,3,16,128]{3,2,1,0:T(8,128)} %bitcast.18), calls=%async_computation | async-start | bytes 786432 | tf_op jit(solution)/shard_map/all_to_all | solution.py:20
  21.3 3.3 %collective-permute-start.5 = (bf16[288,256]{1,0:T(8,128)(2,1)}, bf16[288,256]{1,0:T(8,128)(2,1)}, u32[]{:S(2)}, u32[]{:S(2)}) collective-permute-start(bf16[288,256]{1,0:T(8,128)(2,1)} %collective-permute-done.2.refs_1_), channel_id=1, source_target_pairs={{2,0},{4,2},{6,4},{8,6},{10,8},{12,10},{14,12},{0,14},{3,1},{5,3},... | collective-permute-start | bytes 442376 | tf_op jit(solution)/shard_map/ppermute | solution.py:467
  25.7 2.1 %collective-permute-start.1 = (bf16[4,4,32,1024]{3,2,1,0:T(8,128)(2,1)}, bf16[4,4,32,1024]{3,2,1,0:T(8,128)(2,1)S(1)}, u32[]{:S(2)}, u32[]{:S(2)}) collective-permute-start(bf16[4,4,32,1024]{3,2,1,0:T(8,128)(2,1)} %constant_dynamic-slice_fusion), channel_id=1, source_target_pairs={{0,1},{1,0},{2,3},{3,2},{4,5},{5,4},{6,7},{7,6},{8,9},{9,8},{10,11... | collective-permute-start | bytes 3145736 | tf_op jit(solution)/shard_map/ppermute | solution.py:459
  30.3 2.1 %collective-permute-start.9 = (f32[16,2,16,128]{3,2,1,0:T(8,128)}, f32[16,2,16,128]{3,2,1,0:T(8,128)}, u32[]{:S(2)}, u32[]{:S(2)}) collective-permute-start(f32[16,2,16,128]{3,2,1,0:T(8,128)} %maximum_select_fusion), channel_id=1, source_target_pairs={{0,1},{1,0},{2,3},{3,2},{4,5},{5,4},{6,7},{7,6},{8,9},{9,8},{10,11... | collective-permute-start | bytes 786440 | tf_op jit(solution)/shard_map/ppermute | solution.py:471
  32.4 3.2 %collective-permute-start.6 = (bf16[288,256]{1,0:T(8,128)(2,1)}, bf16[288,256]{1,0:T(8,128)(2,1)}, u32[]{:S(2)}, u32[]{:S(2)}) collective-permute-start(bf16[288,256]{1,0:T(8,128)(2,1)} %collective-permute-done.5.refs_2_), channel_id=1, source_target_pairs={{2,0},{4,2},{6,4},{8,6},{10,8},{12,10},{14,12},{0,14},{3,1},{5,3},... | collective-permute-start | bytes 442376 | tf_op jit(solution)/shard_map/ppermute | solution.py:467
  35.7 1.5 collective-permute-done.7.refs_5_
  38.0 1.5 reshape_squeeze_reshape.3
  39.5 1.4 fusion.1
  41.8 2.3 %collective-permute-done.8.refs_4_ = bf16[288,256]{1,0:T(8,128)(2,1)} collective-permute-done((bf16[288,256]{1,0:T(8,128)(2,1)}, bf16[288,256]{1,0:T(8,128)(2,1)}, u32[]{:S(2)}, u32[]{:S(2)}) %collective-permute-start.8) | collective-permute-done | bytes 147488 | tf_op jit(solution)/shard_map/ppermute | solution.py:465
  44.1 9.4 %collective-permute-done.1.other_ref = bf16[4,4,32,1024]{3,2,1,0:T(8,128)(2,1)S(1)} collective-permute-done((bf16[4,4,32,1024]{3,2,1,0:T(8,128)(2,1)}, bf16[4,4,32,1024]{3,2,1,0:T(8,128)(2,1)S(1)}, u32[]{:S(2)}, u32[]{:S(2)}) %collective-permute-start.1) | collective-permute-done | bytes 1048608 | tf_op jit(solution)/shard_map/ppermute | solution.py:459
  55.4 3.3 %shard_map.95 = (s16[16,144,128]{2,1,0:T(8,128)(2,1)S(1)}, bf16[8,64,128]{2,1,0:T(8,128)(2,1)S(1)}) custom-call(s32[1]{0:T(128)} %bitcast.side_ref, bf16[64,128]{1,0:T(8,128)(2,1)S(1)} %copy.34.columns_ref, bf16[256,1024]{1,0:T(8,128)(2,1)S(1)} %copy-done.2, bf16[4,8,32,1024]{3,2,1,0:T(8,128)(2,1)S(1)} %copy-done, ...), custom_call_target="tpu_custom_call" | custom-call | tf_op jit(solution)/shard_map/pallas_call | solution.py:492
  60.2 5.7 %all-to-all-start.1 = ((s16[16,144,128]{2,1,0:T(8,128)(2,1)}), s16[16,144,128]{2,1,0:T(8,128)(2,1)}, u32[]{:S(2)}, u32[]{:S(2)}) async-start(s16[16,144,128]{2,1,0:T(8,128)(2,1)} %copy-done.9), calls=%async_computation.1 | async-start | bytes 1179648 | tf_op jit(solution)/shard_map/all_to_all | solution.py:20
  66.5 1.4 shard_map.97.local_ref
  68.6 7.8 %all-to-all-done.1.message_ref = s16[16,144,128]{2,1,0:T(8,128)(2,1)} async-done(((s16[16,144,128]{2,1,0:T(8,128)(2,1)}), s16[16,144,128]{2,1,0:T(8,128)(2,1)}, u32[]{:S(2)}, u32[]{:S(2)}) %all-to-all-start.1) | async-done | bytes 589856 | tf_op jit(solution)/shard_map/all_to_all | solution.py:20
  76.5 1.3 shard_map.96.own_ref
  78.4 2.0 %collective-permute-start.10 = (f32[8,4608]{1,0:T(8,128)}, f32[8,4608]{1,0:T(8,128)S(1)}, u32[]{:S(2)}, u32[]{:S(2)}) collective-permute-start(f32[8,4608]{1,0:T(8,128)} %pad_maximum_fusion.1), channel_id=1, source_target_pairs={{0,16},{1,17},{2,18},{3,19},{4,20},{5,21},{6,22},{7,23},{8,24},{9,... | collective-permute-start | bytes 442376 | tf_op jit(solution)/shard_map/ppermute | solution.py:531
  81.1 3.7 %collective-permute-start.11 = (f32[8,4608]{1,0:T(8,128)}, f32[8,4608]{1,0:T(8,128)S(1)}, u32[]{:S(2)}, u32[]{:S(2)}) collective-permute-start(f32[8,4608]{1,0:T(8,128)} %pad_maximum_fusion.2), channel_id=1, source_target_pairs={{16,0},{17,1},{18,2},{19,3},{20,4},{21,5},{22,6},{23,7},{24,8},{25... | collective-permute-start | bytes 442376 | tf_op jit(solution)/shard_map/ppermute | solution.py:532
  85.1 2.5 %collective-permute-done.11.after_ref = f32[8,4608]{1,0:T(8,128)S(1)} collective-permute-done((f32[8,4608]{1,0:T(8,128)}, f32[8,4608]{1,0:T(8,128)S(1)}, u32[]{:S(2)}, u32[]{:S(2)}) %collective-permute-start.11) | collective-permute-done | bytes 147488 | tf_op jit(solution)/shard_map/ppermute | solution.py:532
  89.2 2.8 %shard_map.99 = s16[16,160,128]{2,1,0:T(8,128)(2,1)S(1)} custom-call(s32[2]{0:T(128)S(1)} %pad_add_fusion.place_ref, f32[16,1024]{1,0:T(8,128)S(1)} %shard_map.96.own_ref, f32[8,4608]{1,0:T(8,128)S(1)} %collective-permute-done.10.before_ref, f32[8,4608]{1,0:T(8,128)S(1)} %collective-permute-done.11.after_ref, f32[2,32,1024]{2,1,0:T(8,128)S(1)} %get-tuple-element.23.wind_ref, ...), custom_call_target="tpu_custom_call" | custom-call | tf_op jit(solution)/shard_map/pallas_call | solution.py:548
  92.9 4.3 %all-to-all-start.2 = ((s16[16,160,128]{2,1,0:T(8,128)(2,1)}), s16[16,160,128]{2,1,0:T(8,128)(2,1)}, u32[]{:S(2)}, u32[]{:S(2)}) async-start(s16[16,160,128]{2,1,0:T(8,128)(2,1)} %copy-done.1), calls=%async_computation.2 | async-start | bytes 1310720 | tf_op jit(solution)/shard_map/all_to_all | solution.py:20
  97.2 2.0 %copy.35 = bf16[256,1024]{0,1:T(8,128)(2,1)} copy(bf16[256,1024]{1,0:T(8,128)(2,1)} %lon_ref.1) | data formatting | bytes 1048576 | tf_op args[3]
  99.3 9.2 %all-to-all-done.2.message_ref = s16[16,160,128]{2,1,0:T(8,128)(2,1)} async-done(((s16[16,160,128]{2,1,0:T(8,128)(2,1)}), s16[16,160,128]{2,1,0:T(8,128)(2,1)}, u32[]{:S(2)}, u32[]{:S(2)}) %all-to-all-start.2) | async-done | bytes 655392 | tf_op jit(solution)/shard_map/all_to_all | solution.py:20
  109.5 2.9 %shard_map.100 = (s16[8,144,256]{2,1,0:T(8,128)(2,1)S(1)}, f32[2,4,32,64]{3,2,1,0:T(8,128)S(1)}) custom-call(s32[1]{0:T(128)} %bitcast.side_ref, s16[16,160,128]{2,1,0:T(8,128)(2,1)} %all-to-all-done.2.message_ref, bf16[1024,256]{1,0:T(8,128)(2,1)S(1)} %bitcast.40, bf16[4,8,32,1024]{3,2,1,0:T(8,128)(2,1)S(1)} %copy-done, ...), custom_call_target="tpu_custom_call" | custom-call | tf_op jit(solution)/shard_map/pallas_call | solution.py:563
  113.3 7.6 %all-to-all-start.3 = ((s16[8,144,256]{2,1,0:T(8,128)(2,1)}), s16[8,144,256]{2,1,0:T(8,128)(2,1)S(1)}, u32[]{:S(2)}, u32[]{:S(2)}) async-start(s16[8,144,256]{2,1,0:T(8,128)(2,1)} %copy-done.8), calls=%async_computation.3 | async-start | bytes 1179648 | tf_op jit(solution)/shard_map/all_to_all | solution.py:20
  121.2 18.9 %all-to-all-done.3.message_ref = s16[8,144,256]{2,1,0:T(8,128)(2,1)S(1)} async-done(((s16[8,144,256]{2,1,0:T(8,128)(2,1)}), s16[8,144,256]{2,1,0:T(8,128)(2,1)S(1)}, u32[]{:S(2)}, u32[]{:S(2)}) %all-to-all-start.3) | async-done | bytes 589856 | tf_op jit(solution)/shard_map/all_to_all | solution.py:20
  140.1 1.4 shard_map.101
  141.5 3.5 %all-to-all-start.4 = ((f32[16,2,8,256]{3,2,1,0:T(8,128)}), f32[16,2,8,256]{3,2,1,0:T(8,128)S(1)}, u32[]{:S(2)}, u32[]{:S(2)}) async-start(f32[16,2,8,256]{3,2,1,0:T(8,128)} %shard_map.101), calls=%async_computation.4 | async-start | bytes 524288 | tf_op jit(solution)/shard_map/all_to_all | solution.py:20
  145.0 3.5 %collective-permute-start.12 = (f32[4,32,64]{2,1,0:T(8,128)S(1)}, f32[4,32,64]{2,1,0:T(8,128)S(1)}, u32[]{:S(2)}, u32[]{:S(2)}) collective-permute-start(f32[4,32,64]{2,1,0:T(8,128)S(1)} %get-tuple-element.35), channel_id=1, source_target_pairs={{0,1},{1,0},{2,3},{3,2},{4,5},{5,4},{6,7},{7,6},{8,9},{9,8},{10,11... | collective-permute-start | bytes 98312 | tf_op jit(solution)/shard_map/ppermute | solution.py:596
  148.5 2.5 %collective-permute-done.12 = f32[4,32,64]{2,1,0:T(8,128)S(1)} collective-permute-done((f32[4,32,64]{2,1,0:T(8,128)S(1)}, f32[4,32,64]{2,1,0:T(8,128)S(1)}, u32[]{:S(2)}, u32[]{:S(2)}) %collective-permute-start.12) | collective-permute-done | bytes 32800 | tf_op jit(solution)/shard_map/ppermute | solution.py:596
  151.7 7.7 %all-to-all-done.4 = f32[16,2,8,256]{3,2,1,0:T(8,128)S(1)} async-done(((f32[16,2,8,256]{3,2,1,0:T(8,128)}), f32[16,2,8,256]{3,2,1,0:T(8,128)S(1)}, u32[]{:S(2)}, u32[]{:S(2)}) %all-to-all-start.4) | async-done | bytes 262176 | tf_op jit(solution)/shard_map/all_to_all | solution.py:20
  (82 shorter events, 24.2 us)
Async XLA Ops:
  2.5 5.9 %collective-permute-start = (bf16[144,256]{1,0:T(8,128)(2,1)S(1)}, bf16[144,256]{1,0:T(8,128)(2,1)S(1)}, u32[]{:S(2)}, u32[]{:S(2)}) collective-permute-start(bf16[144,256]{1,0:T(8,128)(2,1)S(1)} %maximum_maximum_fusion), channel_id=1, source_target_pairs={{0,1},{1,0},{2,3},{3,2},{4,5},{5,4},{6,7},{7,6},{8,9},{9,8},{10,11... | collective-permute-start | bytes 221192 | tf_op jit(solution)/shard_map/ppermute | solution.py:430
  6.5 18.2 %copy-start = (bf16[4,8,32,1024]{3,2,1,0:T(8,128)(2,1)S(1)}, bf16[4,8,32,1024]{3,2,1,0:T(8,128)(2,1)}, u32[]{:S(2)}) copy-start(bf16[4,8,32,1024]{3,2,1,0:T(8,128)(2,1)} %own_ref.3) | copy-start | bytes 6291460
  8.5 16.1 %copy-start.6 = (bf16[288,256]{1,0:T(8,128)(2,1)}, bf16[288,256]{1,0:T(8,128)(2,1)S(1)}, u32[]{:S(2)}) copy-start(bf16[288,256]{1,0:T(8,128)(2,1)S(1)} %pad_maximum_fusion.refs_0_) | copy-start | bytes 442372
  8.5 12.8 %collective-permute-start.2 = (bf16[288,256]{1,0:T(8,128)(2,1)S(1)}, bf16[288,256]{1,0:T(8,128)(2,1)}, u32[]{:S(2)}, u32[]{:S(2)}) collective-permute-start(bf16[288,256]{1,0:T(8,128)(2,1)S(1)} %pad_maximum_fusion.refs_0_), channel_id=1, source_target_pairs={{2,0},{4,2},{6,4},{8,6},{10,8},{12,10},{14,12},{0,14},{3,1},{5,3},... | collective-permute-start | bytes 442376 | tf_op jit(solution)/shard_map/ppermute | solution.py:467
  14.4 6.8 %collective-permute-start.3 = (bf16[288,256]{1,0:T(8,128)(2,1)S(1)}, bf16[288,256]{1,0:T(8,128)(2,1)}, u32[]{:S(2)}, u32[]{:S(2)}) collective-permute-start(bf16[288,256]{1,0:T(8,128)(2,1)S(1)} %pad_maximum_fusion.refs_0_), channel_id=1, source_target_pairs={{0,2},{2,4},{4,6},{6,8},{8,10},{10,12},{12,14},{14,0},{1,3},{3,5},... | collective-permute-start | bytes 442376 | tf_op jit(solution)/shard_map/ppermute | solution.py:465
  15.3 14.3 %all-to-all-start = ((f32[16,3,16,128]{3,2,1,0:T(8,128)}), f32[16,3,16,128]{3,2,1,0:T(8,128)S(1)}, u32[]{:S(2)}, u32[]{:S(2)}) async-start(f32[16,3,16,128]{3,2,1,0:T(8,128)} %bitcast.18), calls=%async_computation | async-start | bytes 786432 | tf_op jit(solution)/shard_map/all_to_all | solution.py:20
  21.2 7.8 %collective-permute-start.4 = (bf16[288,256]{1,0:T(8,128)(2,1)}, bf16[288,256]{1,0:T(8,128)(2,1)}, u32[]{:S(2)}, u32[]{:S(2)}) collective-permute-start(bf16[288,256]{1,0:T(8,128)(2,1)} %collective-permute-done.3.refs_7_), channel_id=1, source_target_pairs={{0,2},{2,4},{4,6},{6,8},{8,10},{10,12},{12,14},{14,0},{1,3},{3,5},... | collective-permute-start | bytes 442376 | tf_op jit(solution)/shard_map/ppermute | solution.py:465
  21.3 7.7 %collective-permute-start.5 = (bf16[288,256]{1,0:T(8,128)(2,1)}, bf16[288,256]{1,0:T(8,128)(2,1)}, u32[]{:S(2)}, u32[]{:S(2)}) collective-permute-start(bf16[288,256]{1,0:T(8,128)(2,1)} %collective-permute-done.2.refs_1_), channel_id=1, source_target_pairs={{2,0},{4,2},{6,4},{8,6},{10,8},{12,10},{14,12},{0,14},{3,1},{5,3},... | collective-permute-start | bytes 442376 | tf_op jit(solution)/shard_map/ppermute | solution.py:467
  25.7 27.8 %collective-permute-start.1 = (bf16[4,4,32,1024]{3,2,1,0:T(8,128)(2,1)}, bf16[4,4,32,1024]{3,2,1,0:T(8,128)(2,1)S(1)}, u32[]{:S(2)}, u32[]{:S(2)}) collective-permute-start(bf16[4,4,32,1024]{3,2,1,0:T(8,128)(2,1)} %constant_dynamic-slice_fusion), channel_id=1, source_target_pairs={{0,1},{1,0},{2,3},{3,2},{4,5},{5,4},{6,7},{7,6},{8,9},{9,8},{10,11... | collective-permute-start | bytes 3145736 | tf_op jit(solution)/shard_map/ppermute | solution.py:459
  29.5 7.7 %collective-permute-start.7 = (bf16[288,256]{1,0:T(8,128)(2,1)}, bf16[288,256]{1,0:T(8,128)(2,1)}, u32[]{:S(2)}, u32[]{:S(2)}) collective-permute-start(bf16[288,256]{1,0:T(8,128)(2,1)} %collective-permute-done.4.refs_6_), channel_id=1, source_target_pairs={{0,2},{2,4},{4,6},{6,8},{8,10},{10,12},{12,14},{14,0},{1,3},{3,5},... | collective-permute-start | bytes 442376 | tf_op jit(solution)/shard_map/ppermute | solution.py:465
  30.3 29.9 %collective-permute-start.9 = (f32[16,2,16,128]{3,2,1,0:T(8,128)}, f32[16,2,16,128]{3,2,1,0:T(8,128)}, u32[]{:S(2)}, u32[]{:S(2)}) collective-permute-start(f32[16,2,16,128]{3,2,1,0:T(8,128)} %maximum_select_fusion), channel_id=1, source_target_pairs={{0,1},{1,0},{2,3},{3,2},{4,5},{5,4},{6,7},{7,6},{8,9},{9,8},{10,11... | collective-permute-start | bytes 786440 | tf_op jit(solution)/shard_map/ppermute | solution.py:471
  32.4 9.3 %collective-permute-start.6 = (bf16[288,256]{1,0:T(8,128)(2,1)}, bf16[288,256]{1,0:T(8,128)(2,1)}, u32[]{:S(2)}, u32[]{:S(2)}) collective-permute-start(bf16[288,256]{1,0:T(8,128)(2,1)} %collective-permute-done.5.refs_2_), channel_id=1, source_target_pairs={{2,0},{4,2},{6,4},{8,6},{10,8},{12,10},{14,12},{0,14},{3,1},{5,3},... | collective-permute-start | bytes 442376 | tf_op jit(solution)/shard_map/ppermute | solution.py:467
  37.2 6.9 %collective-permute-start.8 = (bf16[288,256]{1,0:T(8,128)(2,1)}, bf16[288,256]{1,0:T(8,128)(2,1)}, u32[]{:S(2)}, u32[]{:S(2)}) collective-permute-start(bf16[288,256]{1,0:T(8,128)(2,1)} %collective-permute-done.7.refs_5_), channel_id=1, source_target_pairs={{0,2},{2,4},{4,6},{6,8},{8,10},{10,12},{12,14},{14,0},{1,3},{3,5},... | collective-permute-start | bytes 442376 | tf_op jit(solution)/shard_map/ppermute | solution.py:465
  53.5 1.0 copy-start.2
  54.5 0.9 copy-start.7
  58.7 0.8 copy-start.9
  59.5 0.7 copy-start.10
  60.2 16.3 %all-to-all-start.1 = ((s16[16,144,128]{2,1,0:T(8,128)(2,1)}), s16[16,144,128]{2,1,0:T(8,128)(2,1)}, u32[]{:S(2)}, u32[]{:S(2)}) async-start(s16[16,144,128]{2,1,0:T(8,128)(2,1)} %copy-done.9), calls=%async_computation.1 | async-start | bytes 1179648 | tf_op jit(solution)/shard_map/all_to_all | solution.py:20
  65.9 0.6 copy-start.12
  68.0 0.7 copy-start.4
  78.4 6.7 %collective-permute-start.10 = (f32[8,4608]{1,0:T(8,128)}, f32[8,4608]{1,0:T(8,128)S(1)}, u32[]{:S(2)}, u32[]{:S(2)}) collective-permute-start(f32[8,4608]{1,0:T(8,128)} %pad_maximum_fusion.1), channel_id=1, source_target_pairs={{0,16},{1,17},{2,18},{3,19},{4,20},{5,21},{6,22},{7,23},{8,24},{9,... | collective-permute-start | bytes 442376 | tf_op jit(solution)/shard_map/ppermute | solution.py:531
  81.1 6.5 %collective-permute-start.11 = (f32[8,4608]{1,0:T(8,128)}, f32[8,4608]{1,0:T(8,128)S(1)}, u32[]{:S(2)}, u32[]{:S(2)}) collective-permute-start(f32[8,4608]{1,0:T(8,128)} %pad_maximum_fusion.2), channel_id=1, source_target_pairs={{16,0},{17,1},{18,2},{19,3},{20,4},{21,5},{22,6},{23,7},{24,8},{25... | collective-permute-start | bytes 442376 | tf_op jit(solution)/shard_map/ppermute | solution.py:532
  87.6 0.9 copy-start.5
  92.0 0.9 copy-start.1
  92.9 15.6 %all-to-all-start.2 = ((s16[16,160,128]{2,1,0:T(8,128)(2,1)}), s16[16,160,128]{2,1,0:T(8,128)(2,1)}, u32[]{:S(2)}, u32[]{:S(2)}) async-start(s16[16,160,128]{2,1,0:T(8,128)(2,1)} %copy-done.1), calls=%async_computation.2 | async-start | bytes 1310720 | tf_op jit(solution)/shard_map/all_to_all | solution.py:20
  108.5 1.0 copy-start.3
  109.5 11.4 %copy-start.11 = (bf16[8,64,128]{2,1,0:T(8,128)(2,1)S(1)}, bf16[8,64,128]{2,1,0:T(8,128)(2,1)}, u32[]{:S(2)}) copy-start(bf16[8,64,128]{2,1,0:T(8,128)(2,1)} %copy-done.10) | copy-start | bytes 393220
  112.4 0.8 copy-start.8
  113.3 26.8 %all-to-all-start.3 = ((s16[8,144,256]{2,1,0:T(8,128)(2,1)}), s16[8,144,256]{2,1,0:T(8,128)(2,1)S(1)}, u32[]{:S(2)}, u32[]{:S(2)}) async-start(s16[8,144,256]{2,1,0:T(8,128)(2,1)} %copy-done.8), calls=%async_computation.3 | async-start | bytes 1179648 | tf_op jit(solution)/shard_map/all_to_all | solution.py:20
  121.0 38.8 %copy-start.13 = (bf16[8,4,8,256]{3,2,1,0:T(8,128)(2,1)S(1)}, bf16[8,4,8,256]{3,2,1,0:T(8,128)(2,1)}, u32[]{:S(2)}) copy-start(bf16[8,4,8,256]{3,2,1,0:T(8,128)(2,1)} %param.8) | copy-start | bytes 393220
  141.5 17.9 %all-to-all-start.4 = ((f32[16,2,8,256]{3,2,1,0:T(8,128)}), f32[16,2,8,256]{3,2,1,0:T(8,128)S(1)}, u32[]{:S(2)}, u32[]{:S(2)}) async-start(f32[16,2,8,256]{3,2,1,0:T(8,128)} %shard_map.101), calls=%async_computation.4 | async-start | bytes 524288 | tf_op jit(solution)/shard_map/all_to_all | solution.py:20
  145.0 6.0 %collective-permute-start.12 = (f32[4,32,64]{2,1,0:T(8,128)S(1)}, f32[4,32,64]{2,1,0:T(8,128)S(1)}, u32[]{:S(2)}, u32[]{:S(2)}) collective-permute-start(f32[4,32,64]{2,1,0:T(8,128)S(1)} %get-tuple-element.35), channel_id=1, source_target_pairs={{0,1},{1,0},{2,3},{3,2},{4,5},{5,4},{6,7},{7,6},{8,9},{9,8},{10,11... | collective-permute-start | bytes 98312 | tf_op jit(solution)/shard_map/ppermute | solution.py:596
